TPU v7x, 32 devices: a whole 2x2x4 slice. The times are simulated.
32 devices in a mesh: dp: 8 (over z, y), fsdp: 4 (over x, core).
Axes of the slice: x: 2, y: 2, z: 4, core: 2. Of those that a mesh axis runs over, the one named last changes fastest.
Arguments:
- tokens: bfloat16 [8192, 768], P(('dp', 'fsdp')), may hold values from -6 to 6
- cotangent: bfloat16 [8192, 768], P(('dp', 'fsdp')), may hold values from -6 to 6
- counts: int32 [8, 4], replicated, may hold values from 128 to 256, as said below
- lengths: int32 [8, 8], replicated, may hold values from 1 to 1017, as said below
- weight_qkv: float32 [768, 2304], P(('dp', 'fsdp')), may hold values from -0.3125 to 0.3125
- weight_out: float32 [768, 768], P(('dp', 'fsdp')), may hold values from -0.21875 to 0.21875
- weight_in: float32 [768, 2304], P(('dp', 'fsdp')), may hold values from -0.21875 to 0.21875
- weight_down: float32 [768, 1152], P(('dp', 'fsdp')), may hold values from -0.1875 to 0.1875
- norm_gains: float32 [2, 768], P(None, ('dp', 'fsdp')), may hold values from 0.5 to 1.5
- first_qkv: float32 [768, 2304], P(('dp', 'fsdp')), may hold values from -448 to 448
- first_out: float32 [768, 768], P(('dp', 'fsdp')), may hold values from -320 to 320
- first_in: float32 [768, 2304], P(('dp', 'fsdp')), may hold values from -256 to 256
- first_down: float32 [768, 1152], P(('dp', 'fsdp')), may hold values from -256 to 256
- first_gains: float32 [2, 768], P(None, ('dp', 'fsdp')), may hold values from -768 to 768
- second_qkv: float32 [768, 2304], P(('dp', 'fsdp')), may hold values from 6144 to 24576
- second_out: float32 [768, 768], P(('dp', 'fsdp')), may hold values from 3072 to 12288
- second_in: float32 [768, 2304], P(('dp', 'fsdp')), may hold values from 2211 to 8847
- second_down: float32 [768, 1152], P(('dp', 'fsdp')), may hold values from 2211 to 8847
- second_gains: float32 [2, 768], P(None, ('dp', 'fsdp')), may hold values from 15728 to 62914
- average_qkv: float32 [768, 2304], P(('dp', 'fsdp')), may hold values from -0.3125 to 0.3125
- average_out: float32 [768, 768], P(('dp', 'fsdp')), may hold values from -0.21875 to 0.21875
- average_in: float32 [768, 2304], P(('dp', 'fsdp')), may hold values from -0.21875 to 0.21875
- average_down: float32 [768, 1152], P(('dp', 'fsdp')), may hold values from -0.1875 to 0.1875
- average_gains: float32 [2, 768], P(None, ('dp', 'fsdp')), may hold values from 0.5 to 1.5
Outputs:
- block_out: bfloat16 [8192, 768], P(('dp', 'fsdp'))
- grad_tokens: float32 [8192, 768], P(('dp', 'fsdp'))
- momentum_qkv: float32 [768, 2304], P(('dp', 'fsdp'))
- momentum_out: float32 [768, 768], P(('dp', 'fsdp'))
- momentum_in: float32 [768, 2304], P(('dp', 'fsdp'))
- momentum_down: float32 [768, 1152], P(('dp', 'fsdp'))
- momentum_gains: float32 [2, 768], P(None, ('dp', 'fsdp'))
- variance_qkv: float32 [768, 2304], P(('dp', 'fsdp'))
- variance_out: float32 [768, 768], P(('dp', 'fsdp'))
- variance_in: float32 [768, 2304], P(('dp', 'fsdp'))
- variance_down: float32 [768, 1152], P(('dp', 'fsdp'))
- variance_gains: float32 [2, 768], P(None, ('dp', 'fsdp'))
- master_qkv: float32 [768, 2304], P(('dp', 'fsdp'))
- master_out: float32 [768, 768], P(('dp', 'fsdp'))
- master_in: float32 [768, 2304], P(('dp', 'fsdp'))
- master_down: float32 [768, 1152], P(('dp', 'fsdp'))
- master_gains: float32 [2, 768], P(None, ('dp', 'fsdp'))
- smooth_qkv: float32 [768, 2304], P(('dp', 'fsdp'))
- smooth_out: float32 [768, 768], P(('dp', 'fsdp'))
- smooth_in: float32 [768, 2304], P(('dp', 'fsdp'))
- smooth_down: float32 [768, 1152], P(('dp', 'fsdp'))
- smooth_gains: float32 [2, 768], P(None, ('dp', 'fsdp'))
- halfcopy_qkv: bfloat16 [768, 2304], P(('dp', 'fsdp'))
- halfcopy_out: bfloat16 [768, 768], P(('dp', 'fsdp'))
- halfcopy_in: bfloat16 [768, 2304], P(('dp', 'fsdp'))
- halfcopy_down: bfloat16 [768, 1152], P(('dp', 'fsdp'))
- halfcopy_gains: bfloat16 [2, 768], P(None, ('dp', 'fsdp'))
Inputs may be any that keep to these rules, and one draw needn't show every extreme that they name: counts[g, f] live tokens fill the first rows of device f of pack g; in every pack some device holds exactly 256, and in one pack, drawn from the seed, every device does. lengths[g] are the lengths of the documents laid in order over the live tokens of pack g and add up to the sum of counts[g]; one of them, at an index drawn from the seed, begins on the pack's first device and ends on its last; the others are at most 16 tokens, and in the pack whose devices are all full they are 1.
All inputs are finite; a program needn't handle non-finite values.
Results may differ from a plain program's by a relative error of at most 0.017.
The roundings to bfloat16 on the way count: a program that leaves them out, or rounds other values in their place, can miss the bound.
Values may be sent and summed in bfloat16 or wider, within the bound.
No kernel may reach another device: no remote copies, remote signals or barrier semaphores. Data moves between devices by JAX's collectives and lax.ppermute only.
A program may use at most 128 MiB of HBM per device.

v0:
```python
import jax
import jax.numpy as jnp
from jax import lax
from jax.sharding import PartitionSpec as P

HEADS = 12
HD = 64
STEP = 6


NORM_EPS = 1e-05
ROTARY_BASE = 160000.0
BETA_FIRST = 0.5
BETA_SECOND = 0.5
ADAM_EPS = 1e-08
WEIGHT_DECAY = 0.01
MATRIX_RATE = 0.04
GAIN_RATE = 0.5
AVERAGE_KEEP = 0.6
MASKED = -1e30


def group_layout(count_row, length_row, slots):
    devices_here = count_row.shape[0]
    places = jnp.arange(devices_here * slots, dtype=jnp.int32)
    holder = places // slots
    within = places - holder * slots
    before = jnp.cumsum(count_row) - count_row
    choose = (holder[:, None] == jnp.arange(devices_here, dtype=jnp.int32)[None, :]).astype(
        jnp.int32
    )
    offset = jnp.sum(choose * before[None, :], axis=1) + within
    limits = jnp.sum(choose * count_row[None, :], axis=1)
    living = within < limits
    doc_ends = jnp.cumsum(length_row)
    passed = offset[:, None] >= doc_ends[None, :]
    document = jnp.sum(passed.astype(jnp.int32), axis=1)
    begins = jnp.max(jnp.where(passed, doc_ends[None, :], 0), axis=1)
    number_docs = length_row.shape[0]
    document = jnp.where(living, document, number_docs)
    position = jnp.where(living, offset - begins, 0)
    return (document, position, living)


def rotary_tables(position, head_size):
    half_size = head_size // 2
    speeds = ROTARY_BASE ** (-(jnp.arange(half_size, dtype=jnp.float32) * (2.0 / head_size)))
    angles = position.astype(jnp.float32)[:, None] * speeds[None, :]
    return (jnp.cos(angles), jnp.sin(angles))


def rotate(heads_in, cosine_table, sine_table):
    half_size = heads_in.shape[-1] // 2
    leading = heads_in[..., :half_size]
    latter = heads_in[..., half_size:]
    cos_wide = cosine_table[:, None, :]
    sin_wide = sine_table[:, None, :]
    return jnp.concatenate(
        [leading * cos_wide - latter * sin_wide, latter * cos_wide + leading * sin_wide], axis=-1
    )


def rotate_back(grads_in, cosine_table, sine_table):
    half_size = grads_in.shape[-1] // 2
    leading = grads_in[..., :half_size]
    latter = grads_in[..., half_size:]
    cos_wide = cosine_table[:, None, :]
    sin_wide = sine_table[:, None, :]
    return jnp.concatenate(
        [leading * cos_wide + latter * sin_wide, latter * cos_wide - leading * sin_wide], axis=-1
    )


def norm_parts(values_in):
    center = values_in - jnp.mean(values_in, axis=-1, keepdims=True)
    inverse = lax.rsqrt(jnp.mean(center * center, axis=-1, keepdims=True) + NORM_EPS)
    return (center * inverse, inverse)


def norm_back(upstream, normed, inverse):
    return inverse * (
        upstream
        - jnp.mean(upstream, axis=-1, keepdims=True)
        - normed * jnp.mean(upstream * normed, axis=-1, keepdims=True)
    )


def block_scores(queries, key_block, doc_query, doc_key, score_scale):
    scores = (
        jnp.einsum("qhd,khd->hqk", queries, key_block, preferred_element_type=jnp.float32)
        * score_scale
    )
    return jnp.where(doc_query[None, :, None] == doc_key[None, None, :], scores, MASKED)


def contract_rows(left_side, right_side):
    return lax.dot_general(
        left_side, right_side, (((0,), (0,)), ((), ())), preferred_element_type=jnp.float32
    )


def contract_cols(left_side, right_side):
    return lax.dot_general(
        left_side, right_side, (((1,), (1,)), ((), ())), preferred_element_type=jnp.float32
    )


def adam_update(master, first_old, second_old, average_old, gradient, step_rate):
    first_new = BETA_FIRST * first_old + (1.0 - BETA_FIRST) * gradient
    second_new = BETA_SECOND * second_old + (1.0 - BETA_SECOND) * gradient * gradient
    first_fix = first_new / (1.0 - BETA_FIRST**STEP)
    second_fix = second_new / (1.0 - BETA_SECOND**STEP)
    master_new = master - step_rate * (
        first_fix / (jnp.sqrt(second_fix) + ADAM_EPS) + WEIGHT_DECAY * master
    )
    average_new = AVERAGE_KEEP * average_old + (1.0 - AVERAGE_KEEP) * master_new
    return (first_new, second_new, master_new, average_new, master_new.astype(jnp.bfloat16))


def body(
    tokens,
    cotangent,
    counts,
    lengths,
    weight_qkv,
    weight_out,
    weight_in,
    weight_down,
    norm_gains,
    first_qkv,
    first_out,
    first_in,
    first_down,
    first_gains,
    second_qkv,
    second_out,
    second_in,
    second_down,
    second_gains,
    average_qkv,
    average_out,
    average_in,
    average_down,
    average_gains,
):
    slots = tokens.shape[0]
    model_width = tokens.shape[1]
    hidden_units = weight_down.shape[1]
    head_count = HEADS
    head_size = HD
    score_scale = 1.0 / head_size**0.5
    heads_shape = (slots, head_count, head_size)
    group_row = lax.axis_index("dp")
    own_place = lax.axis_index("fsdp")
    count_row = lax.dynamic_index_in_dim(counts, group_row, 0, keepdims=False)
    length_row = lax.dynamic_index_in_dim(lengths, group_row, 0, keepdims=False)
    doc_all, position_all, living_all = group_layout(count_row, length_row, slots)
    doc_mine = lax.dynamic_slice_in_dim(doc_all, own_place * slots, slots)
    position_mine = lax.dynamic_slice_in_dim(position_all, own_place * slots, slots)
    living_mine = lax.dynamic_slice_in_dim(living_all, own_place * slots, slots)
    cosine_table, sine_table = rotary_tables(position_mine, head_size)
    living_col = living_mine[:, None]
    copies = (
        weight_qkv.astype(jnp.bfloat16),
        weight_out.astype(jnp.bfloat16),
        weight_in.astype(jnp.bfloat16),
        weight_down.astype(jnp.bfloat16),
        norm_gains.astype(jnp.bfloat16),
    )
    qkv_full, out_full, in_full, down_full, gain_full = (
        lax.all_gather(copies[0], ("dp", "fsdp"), axis=0, tiled=True),
        lax.all_gather(copies[1], ("dp", "fsdp"), axis=0, tiled=True),
        lax.all_gather(copies[2], ("dp", "fsdp"), axis=0, tiled=True),
        lax.all_gather(copies[3], ("dp", "fsdp"), axis=0, tiled=True),
        lax.all_gather(copies[4], ("dp", "fsdp"), axis=1, tiled=True),
    )
    tokens_f = tokens.astype(jnp.float32)
    normed_one, inverse_one = norm_parts(tokens_f)
    gain_one = gain_full[0].astype(jnp.float32)
    gain_two = gain_full[1].astype(jnp.float32)
    normed1_low = (normed_one * gain_one).astype(jnp.bfloat16)
    mixed_qkv = jnp.dot(normed1_low, qkv_full, preferred_element_type=jnp.float32)
    queries16 = rotate(
        mixed_qkv[:, :model_width].reshape(heads_shape), cosine_table, sine_table
    ).astype(jnp.bfloat16)
    keys16 = rotate(
        mixed_qkv[:, model_width : 2 * model_width].reshape(heads_shape), cosine_table, sine_table
    ).astype(jnp.bfloat16)
    key_flat = keys16.reshape(slots, model_width)
    value_flat = mixed_qkv[:, 2 * model_width :].astype(jnp.bfloat16)
    key_rows, value_rows = (
        lax.all_gather(key_flat, "fsdp", axis=0, tiled=True),
        lax.all_gather(value_flat, "fsdp", axis=0, tiled=True),
    )
    group_rows = key_rows.shape[0]
    block_rows = 512
    count_blocks = group_rows // block_rows
    blocks_shape = (count_blocks, block_rows, head_count, head_size)
    doc_blocks = doc_all.reshape(count_blocks, block_rows)
    key_blocks = key_rows.reshape(blocks_shape)
    value_blocks = value_rows.reshape(blocks_shape)

    def max_sum(state_now, pieces):
        run_peak, run_total = state_now
        scores = block_scores(queries16, pieces[0], doc_mine, pieces[1], score_scale)
        new_peak = jnp.maximum(run_peak, jnp.max(scores, axis=-1))
        run_total = run_total * jnp.exp(run_peak - new_peak) + jnp.sum(
            jnp.exp(scores - new_peak[:, :, None]), axis=-1
        )
        return ((new_peak, run_total), None)

    start_state = (
        jnp.full((head_count, slots), MASKED, jnp.float32),
        jnp.zeros((head_count, slots), jnp.float32),
    )
    (run_peak, run_total), unused_max = lax.scan(max_sum, start_state, (key_blocks, doc_blocks))
    log_total = run_peak + jnp.log(run_total)

    def weigh_values(accum, pieces):
        scores = block_scores(queries16, pieces[0], doc_mine, pieces[2], score_scale)
        probs16 = jnp.exp(scores - log_total[:, :, None]).astype(jnp.bfloat16)
        return (
            accum
            + jnp.einsum("hqk,khd->qhd", probs16, pieces[1], preferred_element_type=jnp.float32),
            None,
        )

    attended, unused_out = lax.scan(
        weigh_values, jnp.zeros(heads_shape, jnp.float32), (key_blocks, value_blocks, doc_blocks)
    )
    attended16 = attended.reshape(slots, model_width).astype(jnp.bfloat16)
    middle = tokens_f + jnp.dot(attended16, out_full, preferred_element_type=jnp.float32)
    normed_two, inverse_two = norm_parts(middle)
    normed2_low = (normed_two * gain_two).astype(jnp.bfloat16)
    gate_up = jnp.dot(normed2_low, in_full, preferred_element_type=jnp.float32)
    act_half = gate_up[:, :hidden_units]
    gate_half = gate_up[:, hidden_units:]
    activated16 = (jax.nn.gelu(act_half, approximate=False) * gate_half).astype(jnp.bfloat16)
    branch_two = contract_cols(activated16, down_full)
    block_out = jnp.where(living_col, middle + branch_two, 0.0).astype(jnp.bfloat16)
    qkv_back, out_back, in_back, down_back, gain_back = (
        lax.all_gather(copies[0], ("dp", "fsdp"), axis=0, tiled=True),
        lax.all_gather(copies[1], ("dp", "fsdp"), axis=0, tiled=True),
        lax.all_gather(copies[2], ("dp", "fsdp"), axis=0, tiled=True),
        lax.all_gather(copies[3], ("dp", "fsdp"), axis=0, tiled=True),
        lax.all_gather(copies[4], ("dp", "fsdp"), axis=1, tiled=True),
    )
    key_again, value_again = (
        lax.all_gather(key_flat, "fsdp", axis=0, tiled=True),
        lax.all_gather(value_flat, "fsdp", axis=0, tiled=True),
    )
    gain_one_back = gain_back[0].astype(jnp.float32)
    gain_two_back = gain_back[1].astype(jnp.float32)
    dout = jnp.where(living_col, cotangent.astype(jnp.float32), 0.0)
    dym16 = dout.astype(jnp.bfloat16)
    grad_down = contract_rows(dym16, activated16)
    dact = jnp.dot(dym16, down_back, preferred_element_type=jnp.float32)
    unused_gate, gate_pull = jax.vjp(
        lambda front_part, rear_part: jax.nn.gelu(front_part, approximate=False) * rear_part,
        act_half,
        gate_half,
    )
    dfront, drear = gate_pull(dact)
    dgate16 = jnp.concatenate([dfront, drear], axis=1).astype(jnp.bfloat16)
    grad_in = contract_rows(normed2_low, dgate16)
    dnormed_two = contract_cols(dgate16, in_back)
    grad_gain_two = jnp.sum(dnormed_two * normed_two, axis=0)
    dmiddle = dout + norm_back(dnormed_two * gain_two_back, normed_two, inverse_two)
    dbranch16 = dmiddle.astype(jnp.bfloat16)
    grad_out = contract_rows(attended16, dbranch16)
    dattn16 = contract_cols(dbranch16, out_back).astype(jnp.bfloat16).reshape(heads_shape)
    row_delta = jnp.sum(dattn16.astype(jnp.float32) * attended, axis=-1).T
    back_keys = key_again.reshape(blocks_shape)
    back_values = value_again.reshape(blocks_shape)

    def back_block(dquery_sum, pieces):
        key_block, value_block, doc_block = pieces
        scores = block_scores(queries16, key_block, doc_mine, doc_block, score_scale)
        probs = jnp.exp(scores - log_total[:, :, None])
        probs16 = probs.astype(jnp.bfloat16)
        dvalue_block = jnp.einsum(
            "hqk,qhd->khd", probs16, dattn16, preferred_element_type=jnp.float32
        )
        dprobs = jnp.einsum(
            "qhd,khd->hqk", dattn16, value_block, preferred_element_type=jnp.float32
        )
        dscores16 = (probs * (dprobs - row_delta[:, :, None])).astype(jnp.bfloat16)
        dquery_sum = dquery_sum + jnp.einsum(
            "hqk,khd->qhd", dscores16, key_block, preferred_element_type=jnp.float32
        )
        dkey_block = jnp.einsum(
            "hqk,qhd->khd", dscores16, queries16, preferred_element_type=jnp.float32
        )
        return (dquery_sum, (dkey_block, dvalue_block))

    dquery_sum, (dkey_blocks, dvalue_blocks) = lax.scan(
        back_block, jnp.zeros(heads_shape, jnp.float32), (back_keys, back_values, doc_blocks)
    )
    dkey_mine, dvalue_mine = (
        lax.psum_scatter(
            (dkey_blocks.reshape(group_rows, model_width) * score_scale).astype(jnp.bfloat16),
            "fsdp",
            scatter_dimension=0,
            tiled=True,
        ).astype(jnp.float32),
        lax.psum_scatter(
            dvalue_blocks.reshape(group_rows, model_width).astype(jnp.bfloat16),
            "fsdp",
            scatter_dimension=0,
            tiled=True,
        ).astype(jnp.float32),
    )
    dquery_pre = rotate_back(dquery_sum * score_scale, cosine_table, sine_table).reshape(
        slots, model_width
    )
    dkey_pre = rotate_back(dkey_mine.reshape(heads_shape), cosine_table, sine_table).reshape(
        slots, model_width
    )
    dmixed16 = jnp.concatenate([dquery_pre, dkey_pre, dvalue_mine], axis=1).astype(jnp.bfloat16)
    grad_qkv = contract_rows(normed1_low, dmixed16)
    dnormed_one = contract_cols(dmixed16, qkv_back)
    grad_gain_one = jnp.sum(dnormed_one * normed_one, axis=0)
    grad_tokens = dmiddle + norm_back(dnormed_one * gain_one_back, normed_one, inverse_one)
    grad_gains = jnp.stack([grad_gain_one, grad_gain_two], axis=0)
    reduced = (
        lax.psum_scatter(grad_qkv, ("dp", "fsdp"), scatter_dimension=0, tiled=True),
        lax.psum_scatter(grad_out, ("dp", "fsdp"), scatter_dimension=0, tiled=True),
        lax.psum_scatter(grad_in, ("dp", "fsdp"), scatter_dimension=0, tiled=True),
        lax.psum_scatter(grad_down, ("dp", "fsdp"), scatter_dimension=0, tiled=True),
        lax.psum_scatter(grad_gains, ("dp", "fsdp"), scatter_dimension=1, tiled=True),
    )
    masters = (weight_qkv, weight_out, weight_in, weight_down, norm_gains)
    firsts = (first_qkv, first_out, first_in, first_down, first_gains)
    seconds = (second_qkv, second_out, second_in, second_down, second_gains)
    averages = (average_qkv, average_out, average_in, average_down, average_gains)
    rates = (MATRIX_RATE, MATRIX_RATE, MATRIX_RATE, MATRIX_RATE, GAIN_RATE)
    updated = [
        adam_update(
            masters[which],
            firsts[which],
            seconds[which],
            averages[which],
            reduced[which],
            rates[which],
        )
        for which in range(5)
    ]
    return (
        block_out,
        grad_tokens,
        updated[0][0],
        updated[1][0],
        updated[2][0],
        updated[3][0],
        updated[4][0],
        updated[0][1],
        updated[1][1],
        updated[2][1],
        updated[3][1],
        updated[4][1],
        updated[0][2],
        updated[1][2],
        updated[2][2],
        updated[3][2],
        updated[4][2],
        updated[0][3],
        updated[1][3],
        updated[2][3],
        updated[3][3],
        updated[4][3],
        updated[0][4],
        updated[1][4],
        updated[2][4],
        updated[3][4],
        updated[4][4],
    )


def solution(mesh):
    return jax.shard_map(
        body,
        mesh=mesh,
        in_specs=(
            P(("dp", "fsdp"), None),
            P(("dp", "fsdp"), None),
            P(),
            P(),
            P(("dp", "fsdp"), None),
            P(("dp", "fsdp"), None),
            P(("dp", "fsdp"), None),
            P(("dp", "fsdp"), None),
            P(None, ("dp", "fsdp")),
            P(("dp", "fsdp"), None),
            P(("dp", "fsdp"), None),
            P(("dp", "fsdp"), None),
            P(("dp", "fsdp"), None),
            P(None, ("dp", "fsdp")),
            P(("dp", "fsdp"), None),
            P(("dp", "fsdp"), None),
            P(("dp", "fsdp"), None),
            P(("dp", "fsdp"), None),
            P(None, ("dp", "fsdp")),
            P(("dp", "fsdp"), None),
            P(("dp", "fsdp"), None),
            P(("dp", "fsdp"), None),
            P(("dp", "fsdp"), None),
            P(None, ("dp", "fsdp")),
        ),
        out_specs=(
            P(("dp", "fsdp"), None),
            P(("dp", "fsdp"), None),
            P(("dp", "fsdp"), None),
            P(("dp", "fsdp"), None),
            P(("dp", "fsdp"), None),
            P(("dp", "fsdp"), None),
            P(None, ("dp", "fsdp")),
            P(("dp", "fsdp"), None),
            P(("dp", "fsdp"), None),
            P(("dp", "fsdp"), None),
            P(("dp", "fsdp"), None),
            P(None, ("dp", "fsdp")),
            P(("dp", "fsdp"), None),
            P(("dp", "fsdp"), None),
            P(("dp", "fsdp"), None),
            P(("dp", "fsdp"), None),
            P(None, ("dp", "fsdp")),
            P(("dp", "fsdp"), None),
            P(("dp", "fsdp"), None),
            P(("dp", "fsdp"), None),
            P(("dp", "fsdp"), None),
            P(None, ("dp", "fsdp")),
            P(("dp", "fsdp"), None),
            P(("dp", "fsdp"), None),
            P(("dp", "fsdp"), None),
            P(("dp", "fsdp"), None),
            P(None, ("dp", "fsdp")),
        ),
        check_vma=False,
    )
```

profile of v0, /device:TPU:9, one launch (start us, length us, event | category | flops | bytes accessed | tf_op | source)
XLA Modules:
  0.0 872.0 jit_solution(15720795662652246476)
XLA Ops:
  7.3 1.6 convert_element_type.114
  10.7 35.6 %all-gather = bf16[32,24,2]{1,2,0:T(2,128)(2,1)S(1)} all-gather(bf16[1,24,2]{1,2,0:T(2,128)(2,1)S(1)} %convert_bitcast_fusion), channel_id=1, replica_groups=mesh['dp'=8,'fsdp'=4] {'dp','fsdp'}, dimensions={0}, use_global_device_ids=true | all-gather | bytes 3168 | tf_op jit(solution)/shard_map/all_gather | solution.py:175
  49.4 1.2 fusion.76
  51.5 21.3 %all-gather.8.cloned.1.call-done = bf16[768,2304]{1,0:T(8,128)(2,1)} async-done(((bf16[24,2304]{1,0:T(8,128)(2,1)}), bf16[768,2304]{1,0:T(8,128)(2,1)}) %all-gather.8.cloned.1.call-update) | async-done | bytes 3538960 | tf_op jit(solution)/shard_map/all_gather | solution.py:171
  72.8 3.2 fusion.110
  76.0 1.3 fusion.125
  77.2 1.4 copy.103
  78.6 2.3 copy.102
  80.9 2.1 subtract_convert_fusion.2
  87.8 15.4 %all-gather.12.cloned.1.call-done = bf16[1024,768]{0,1:T(8,128)(2,1)} async-done(((bf16[256,768]{0,1:T(8,128)(2,1)}), bf16[1024,768]{0,1:T(8,128)(2,1)}) %all-gather.12.cloned.1.call-update) | async-done | bytes 1572880 | tf_op jit(solution)/shard_map/all_gather | solution.py:192
  103.2 3.8 reshape.364
  107.1 1.7 copy.106
  108.8 5.4 while.39
  110.2 1.3 exponential_reduce_fusion.2
  112.9 1.3 exponential_reduce_fusion.2
  114.2 10.8 %all-gather.10.cloned.1.call-done = bf16[1024,768]{1,0:T(8,128)(2,1)} async-done(((bf16[256,768]{1,0:T(8,128)(2,1)}), bf16[1024,768]{1,0:T(8,128)(2,1)}) %all-gather.10.cloned.1.call-update) | async-done | bytes 1572880 | tf_op jit(solution)/shard_map/all_gather | solution.py:193
  125.0 2.6 copy.101
  127.7 3.8 reshape.360
  131.5 2.9 copy.105
  134.4 9.0 %while.40 = (s32[]{:T(128)}, f32[256,12,64]{0,2,1:T(8,128)}, bf16[2,512,12,64]{1,3,2,0:T(8,128)(2,1)}, s32[256]{0:T(256)S(1)}, s32[2,512]{1,0:T(2,128)S(1)}, /*i...) while((s32[]{:T(128)}, f32[256,12,64]{0,2,1:T(8,128)}, ...), condition=%wide.region_13.14_spmd.clone, body=%wide.region_12.13_spmd.clone.sunk | while | flops 409468928 | bytes 3826298 | solution.py:228
  134.6 4.2 fusion.175
  138.9 4.4 fusion.175
  143.5 1.9 convert_element_type.118
  145.4 36.1 %all-gather.14.cloned.1.call-done = bf16[768,768]{1,0:T(8,128)(2,1)} async-done(((bf16[24,768]{1,0:T(8,128)(2,1)}), bf16[768,768]{1,0:T(8,128)(2,1)}) %all-gather.14.cloned.1.call-update) | async-done | bytes 1179664 | tf_op jit(solution)/shard_map/all_gather | solution.py:172
  181.5 2.1 fusion.126
  185.0 59.3 %all-gather.16.cloned.1.call-done = bf16[768,2304]{1,0:T(8,128)(2,1)} async-done(((bf16[24,2304]{1,0:T(8,128)(2,1)}), bf16[768,2304]{1,0:T(8,128)(2,1)}) %all-gather.16.cloned.1.call-update) | async-done | bytes 3538960 | tf_op jit(solution)/shard_map/all_gather | solution.py:173
  244.3 4.7 fusion.112
  248.9 52.7 %all-gather.18.cloned.1.call-done = bf16[768,1152]{1,0:T(8,128)(2,1)} async-done(((bf16[24,1152]{1,0:T(8,128)(2,1)}), bf16[768,1152]{1,0:T(8,128)(2,1)}) %all-gather.18.cloned.1.call-update) | async-done | bytes 1769488 | tf_op jit(solution)/shard_map/all_gather | solution.py:174
  301.6 5.6 add_convert_fusion
  308.2 1.5 copy-done.11
  309.8 1.8 multiply_reduce_fusion
  312.9 1.3 convolution_convert_fusion
  314.1 1.9 copy.107
  316.1 1.9 multiply_reduce_fusion.1
  318.0 20.4 %while.41 = (s32[]{:T(128)}, f32[256,12,64]{0,2,1:T(8,128)S(1)}, f32[2,512,12,64]{1,3,2,0:T(8,128)}, bf16[2,512,12,64]{1,3,2,0:T(8,128)(2,1)}, bf16[2,512,12,64]...) while((s32[]{:T(128)}, f32[256,12,64]{0,2,1:T(8,128)S(1)}, ...), condition=%wide.region_20.21_spmd.clone, body=%wide.region_19.20_spmd.clone.sunk | while | flops 1022885888 | bytes 83123584 | solution.py:296
  319.9 1.7 bitcast_dynamic-update-slice_fusion.5
  321.6 2.1 fusion.187
  326.7 1.7 copy-done.13
  330.0 1.7 bitcast_dynamic-update-slice_fusion.5
  331.7 2.1 fusion.187
  336.8 1.7 copy-done.13
  338.5 2.3 multiply_convert_fusion
  340.8 1.6 copy.110
  342.4 1.6 copy.118
  344.1 1.3 copy-done.21
  345.4 1.6 copy.111
  347.1 1.7 copy.119
  350.2 1.9 fusion.84
  353.3 2.6 fusion.87
  357.0 5.2 fusion.78
  363.2 8.6 reduce-scatter.10.cloned.1.call-done
  373.4 29.3 %reduce-scatter.12.cloned.1.call-done = bf16[256,768]{0,1:T(8,128)(2,1)} async-done(((bf16[1024,768]{0,1:T(8,128)(2,1)}), bf16[256,768]{0,1:T(8,128)(2,1)}) %reduce-scatter.12.cloned.1.call-update) | async-done | bytes 393232 | tf_op jit(solution)/shard_map/reduce_scatter | solution.py:306
  402.7 5.2 fusion.80
  408.7 3.1 fusion.56
  411.9 2.5 fusion.75
  414.3 38.6 %all-reduce.1 = f32[2,768]{1,0:T(2,128)S(1)} all-reduce(f32[2,768]{1,0:T(2,128)S(1)} %pad_maximum_fusion.10), channel_id=8, replica_groups=mesh['dp'=8,'fsdp'=4] {'dp','fsdp'}, use_global_device_ids=true, to_apply=%region_31.32.clone | all-reduce | flops 1536 | bytes 12288
  454.2 51.2 %reduce-scatter.16.cloned.1.call-done = f32[24,768]{1,0:T(8,128)} async-done(((f32[768,768]{1,0:T(8,128)}), f32[24,768]{1,0:T(8,128)}) %reduce-scatter.16.cloned.1.call-update) | async-done | bytes 73744 | tf_op jit(solution)/shard_map/reduce_scatter | solution.py:327
  505.4 1.6 fusion.119
  508.8 104.6 %reduce-scatter.20.cloned.1.call-done = f32[24,1152]{1,0:T(8,128)} async-done(((f32[768,1152]{1,0:T(8,128)}), f32[24,1152]{1,0:T(8,128)}) %reduce-scatter.20.cloned.1.call-update) | async-done | bytes 110608
  613.4 1.6 fusion.115
  615.7 122.5 %reduce-scatter.18.cloned.1.call-done = f32[24,2304]{1,0:T(8,128)} async-done(((f32[768,2304]{1,0:T(8,128)}), f32[24,2304]{1,0:T(8,128)}) %reduce-scatter.18.cloned.1.call-update) | async-done | bytes 221200 | tf_op jit(solution)/shard_map/reduce_scatter | solution.py:328
  738.2 1.8 fusion.117
  740.8 121.3 %reduce-scatter.14.cloned.1.call-done = f32[24,2304]{1,0:T(8,128)} async-done(((f32[768,2304]{1,0:T(8,128)}), f32[24,2304]{1,0:T(8,128)}) %reduce-scatter.14.cloned.1.call-update) | async-done | bytes 221200 | tf_op jit(solution)/shard_map/reduce_scatter | solution.py:326
  862.1 1.8 fusion.121
  (276 shorter events, 38.3 us)
Async XLA Ops:
  7.2 65.6 %copy-start.2 = (bf16[256,768]{1,0:T(8,128)(2,1)S(1)}, bf16[256,768]{1,0:T(8,128)(2,1)}, u32[]{:S(2)}) copy-start(bf16[256,768]{1,0:T(8,128)(2,1)} %param.30) | copy-start | bytes 1179652
  7.2 65.5 %all-gather.8.cloned.1.call-start = ((), (), s32[]{:S(2)}) async-start(), calls=%async_computation.6 | async-start | bytes 3649536 | tf_op jit(solution)/shard_map/all_gather | solution.py:171
  8.9 94.3 %all-gather.12.cloned.1.call-start = ((), (), s32[]{:S(2)}) async-start(), calls=%async_computation.8 | async-start | bytes 1966080 | tf_op jit(solution)/shard_map/all_gather | solution.py:192
  49.4 26.6 %copy-start.54 = (f32[256]{0:T(256)}, f32[256]{0:T(256)S(1)}, u32[]{:S(2)}) copy-start(f32[256]{0:T(256)S(1)} %broadcast_multiply_fusion.6) | copy-start | bytes 3076
  50.6 25.3 %copy-start.59 = (f32[256]{0:T(256)}, f32[256]{0:T(256)S(1)}, u32[]{:S(2)}) copy-start(f32[256]{0:T(256)S(1)} %add_rsqrt_fusion.1) | copy-start | bytes 3076
  77.2 3.7 copy-start.35
  77.2 3.7 copy-start.37
  83.0 2.5 copy-start.24
  83.0 3.2 copy-start.32
  83.1 3.9 copy-start.69
  83.1 4.7 copy-start.29
  83.1 4.7 copy-start.30
  83.9 41.1 %all-gather.10.cloned.1.call-start = ((), (), s32[]{:S(2)}) async-start(), calls=%async_computation.7 | async-start | bytes 1966080 | tf_op jit(solution)/shard_map/all_gather | solution.py:193
  84.8 96.8 %all-gather.14.cloned.1.call-start = ((), (), s32[]{:S(2)}) async-start(), calls=%async_computation.9 | async-start | bytes 1216512 | tf_op jit(solution)/shard_map/all_gather | solution.py:172
  85.5 158.8 %all-gather.16.cloned.1.call-start = ((), (), s32[]{:S(2)}) async-start(), calls=%async_computation.10 | async-start | bytes 3649536 | tf_op jit(solution)/shard_map/all_gather | solution.py:173
  86.2 215.4 %all-gather.18.cloned.1.call-start = ((), (), s32[]{:S(2)}) async-start(), calls=%async_computation.11 | async-start | bytes 1824768 | tf_op jit(solution)/shard_map/all_gather | solution.py:174
  86.9 284.9 %reduce-scatter.10.cloned.1.call-start = ((), (), s32[]{:S(2)}) async-start(), calls=%async_computation.12 | async-start | bytes 1966080 | tf_op jit(solution)/shard_map/reduce_scatter | solution.py:300
  143.5 38.1 %copy-start.64 = (f32[12,256]{1,0:T(8,128)}, f32[12,256]{1,0:T(8,128)S(1)}, u32[]{:S(2)}) copy-start(f32[12,256]{1,0:T(8,128)S(1)} %get-tuple-element.812) | copy-start | bytes 36868
  301.6 5.6 copy-start.6
  307.1 2.6 copy-start.11
  307.2 2.6 copy-start.57
  307.2 2.6 copy-start.61
  308.2 3.3 copy-start.15
  309.8 1.8 copy-start.66
  321.6 2.1 copy-start.20
  323.7 1.9 copy-start.12
  331.7 2.1 copy-start.20
  333.8 1.9 copy-start.12
  344.1 58.7 %reduce-scatter.12.cloned.1.call-start = ((), (), s32[]{:S(2)}) async-start(), calls=%async_computation.13 | async-start | bytes 1966080 | tf_op jit(solution)/shard_map/reduce_scatter | solution.py:306
  348.8 156.6 %reduce-scatter.16.cloned.1.call-start = ((), (), s32[]{:S(2)}) async-start(), calls=%async_computation.15 | async-start | bytes 2433024 | tf_op jit(solution)/shard_map/reduce_scatter | solution.py:327
  352.1 261.3 %reduce-scatter.20.cloned.1.call-start = ((), (), s32[]{:S(2)}) async-start(), calls=%async_computation.17 | async-start | bytes 3649536
  356.0 382.3 %reduce-scatter.18.cloned.1.call-start = ((), (), s32[]{:S(2)}) async-start(), calls=%async_computation.16 | async-start | bytes 7299072 | tf_op jit(solution)/shard_map/reduce_scatter | solution.py:328
  362.2 10.8 %copy-start.36 = (f32[256,32]{0,1:T(8,128)S(1)}, f32[256,32]{0,1:T(8,128)}, u32[]{:S(2)}) copy-start(f32[256,32]{0,1:T(8,128)} %get-tuple-element.478) | copy-start | bytes 98308
  362.2 10.8 %copy-start.38 = (f32[256,32]{0,1:T(8,128)S(1)}, f32[256,32]{0,1:T(8,128)}, u32[]{:S(2)}) copy-start(f32[256,32]{0,1:T(8,128)} %get-tuple-element.479) | copy-start | bytes 98308
  362.2 499.9 %reduce-scatter.14.cloned.1.call-start = ((), (), s32[]{:S(2)}) async-start(), calls=%async_computation.14 | async-start | bytes 7299072 | tf_op jit(solution)/shard_map/reduce_scatter | solution.py:326
  373.1 29.6 %copy-start.3 = (bf16[256,768]{1,0:T(8,128)(2,1)S(1)}, bf16[256,768]{1,0:T(8,128)(2,1)}, u32[]{:S(2)}) copy-start(bf16[256,768]{1,0:T(8,128)(2,1)} %param.30) | copy-start | bytes 1179652
  373.1 29.6 %copy-start.55 = (f32[256]{0:T(256)S(1)}, f32[256]{0:T(256)}, u32[]{:S(2)}) copy-start(f32[256]{0:T(256)} %copy-done.54) | copy-start | bytes 3076
  373.1 29.6 %copy-start.60 = (f32[256]{0:T(256)S(1)}, f32[256]{0:T(256)}, u32[]{:S(2)}) copy-start(f32[256]{0:T(256)} %copy-done.59) | copy-start | bytes 3076
  408.7 3.1 copy-start.9
  411.8 41.2 %copy-start.73 = (f32[2,24]{1,0:T(2,128)S(1)}, f32[2,24]{1,0:T(2,128)}, u32[]{:S(2)}) copy-start(f32[2,24]{1,0:T(2,128)} %param.38) | copy-start | bytes 580
  411.8 41.2 %copy-start.74 = (f32[2,24]{1,0:T(2,128)S(1)}, f32[2,24]{1,0:T(2,128)}, u32[]{:S(2)}) copy-start(f32[2,24]{1,0:T(2,128)} %param.48) | copy-start | bytes 580
  411.8 41.2 %copy-start.75 = (f32[2,24]{1,0:T(2,128)S(1)}, f32[2,24]{1,0:T(2,128)}, u32[]{:S(2)}) copy-start(f32[2,24]{1,0:T(2,128)} %param.43) | copy-start | bytes 580
  411.8 41.8 %copy-start.72 = (f32[2,24]{1,0:T(2,128)S(1)}, f32[2,24]{1,0:T(2,128)}, u32[]{:S(2)}) copy-start(f32[2,24]{1,0:T(2,128)} %param.53) | copy-start | bytes 580
  411.8 93.5 %copy-start.41 = (f32[24,768]{1,0:T(8,128)S(1)}, f32[24,768]{1,0:T(8,128)}, u32[]{:S(2)}) copy-start(f32[24,768]{1,0:T(8,128)} %param.35) | copy-start | bytes 221188
  411.8 93.5 %copy-start.51 = (f32[24,768]{1,0:T(8,128)S(1)}, f32[24,768]{1,0:T(8,128)}, u32[]{:S(2)}) copy-start(f32[24,768]{1,0:T(8,128)} %param.45) | copy-start | bytes 221188
  411.8 93.5 %copy-start.52 = (f32[24,768]{1,0:T(8,128)S(1)}, f32[24,768]{1,0:T(8,128)}, u32[]{:S(2)}) copy-start(f32[24,768]{1,0:T(8,128)} %param.40) | copy-start | bytes 221188
  411.8 95.1 %copy-start.53 = (f32[24,768]{1,0:T(8,128)S(1)}, f32[24,768]{1,0:T(8,128)}, u32[]{:S(2)}) copy-start(f32[24,768]{1,0:T(8,128)} %param.50) | copy-start | bytes 221188
  453.6 55.2 %copy-start.71 = (f32[2,24]{1,0:T(2,128)}, f32[2,24]{1,0:T(2,128)S(1)}, u32[]{:S(2)}) copy-start(f32[2,24]{1,0:T(2,128)S(1)} %get-tuple-element.437) | copy-start | bytes 580
  506.9 108.1 %copy-start.39 = (f32[24,768]{1,0:T(8,128)}, f32[24,768]{1,0:T(8,128)S(1)}, u32[]{:S(2)}) copy-start(f32[24,768]{1,0:T(8,128)S(1)} %get-tuple-element.449) | copy-start | bytes 221188
  506.9 106.5 %copy-start.33 = (f32[24,1152]{1,0:T(8,128)S(1)}, f32[24,1152]{1,0:T(8,128)}, u32[]{:S(2)}) copy-start(f32[24,1152]{1,0:T(8,128)} %param.37) | copy-start | bytes 331780
  506.9 106.5 %copy-start.48 = (f32[24,1152]{1,0:T(8,128)S(1)}, f32[24,1152]{1,0:T(8,128)}, u32[]{:S(2)}) copy-start(f32[24,1152]{1,0:T(8,128)} %param.47) | copy-start | bytes 331780
  506.9 106.5 %copy-start.49 = (f32[24,1152]{1,0:T(8,128)S(1)}, f32[24,1152]{1,0:T(8,128)}, u32[]{:S(2)}) copy-start(f32[24,1152]{1,0:T(8,128)} %param.42) | copy-start | bytes 331780
  507.6 107.5 %copy-start.50 = (f32[24,1152]{1,0:T(8,128)S(1)}, f32[24,1152]{1,0:T(8,128)}, u32[]{:S(2)}) copy-start(f32[24,1152]{1,0:T(8,128)} %param.52) | copy-start | bytes 331780
  507.6 230.6 %copy-start.25 = (f32[24,2304]{1,0:T(8,128)S(1)}, f32[24,2304]{1,0:T(8,128)}, u32[]{:S(2)}) copy-start(f32[24,2304]{1,0:T(8,128)} %param.36) | copy-start | bytes 663556
  507.6 230.6 %copy-start.42 = (f32[24,2304]{1,0:T(8,128)S(1)}, f32[24,2304]{1,0:T(8,128)}, u32[]{:S(2)}) copy-start(f32[24,2304]{1,0:T(8,128)} %param.46) | copy-start | bytes 663556
  507.6 230.6 %copy-start.43 = (f32[24,2304]{1,0:T(8,128)S(1)}, f32[24,2304]{1,0:T(8,128)}, u32[]{:S(2)}) copy-start(f32[24,2304]{1,0:T(8,128)} %param.41) | copy-start | bytes 663556
  508.8 231.3 %copy-start.46 = (f32[24,2304]{1,0:T(8,128)S(1)}, f32[24,2304]{1,0:T(8,128)}, u32[]{:S(2)}) copy-start(f32[24,2304]{1,0:T(8,128)} %param.51) | copy-start | bytes 663556
  508.8 353.3 %copy-start.26 = (f32[24,2304]{1,0:T(8,128)S(1)}, f32[24,2304]{1,0:T(8,128)}, u32[]{:S(2)}) copy-start(f32[24,2304]{1,0:T(8,128)} %param.34) | copy-start | bytes 663556
  508.8 353.3 %copy-start.44 = (f32[24,2304]{1,0:T(8,128)S(1)}, f32[24,2304]{1,0:T(8,128)}, u32[]{:S(2)}) copy-start(f32[24,2304]{1,0:T(8,128)} %param.44) | copy-start | bytes 663556
  508.8 353.3 %copy-start.45 = (f32[24,2304]{1,0:T(8,128)S(1)}, f32[24,2304]{1,0:T(8,128)}, u32[]{:S(2)}) copy-start(f32[24,2304]{1,0:T(8,128)} %param.39) | copy-start | bytes 663556
  615.1 248.9 %copy-start.34 = (f32[24,1152]{1,0:T(8,128)}, f32[24,1152]{1,0:T(8,128)S(1)}, u32[]{:S(2)}) copy-start(f32[24,1152]{1,0:T(8,128)S(1)} %get-tuple-element.441) | copy-start | bytes 331780
  738.2 126.5 %copy-start.1 = (s32[8,8]{1,0:T(8,128)S(1)}, s32[8,8]{1,0:T(8,128)}, u32[]{:S(2)}) copy-start(s32[8,8]{1,0:T(8,128)} %param.33) | copy-start | bytes 772
  740.1 124.7 %copy-start.27 = (f32[24,2304]{1,0:T(8,128)}, f32[24,2304]{1,0:T(8,128)S(1)}, u32[]{:S(2)}) copy-start(f32[24,2304]{1,0:T(8,128)S(1)} %get-tuple-element.445) | copy-start | bytes 663556
  740.1 123.9 %copy-start.47 = (f32[24,2304]{1,0:T(8,128)S(1)}, f32[24,2304]{1,0:T(8,128)}, u32[]{:S(2)}) copy-start(f32[24,2304]{1,0:T(8,128)} %param.49) | copy-start | bytes 663556
  (32 other events, 42.1 us)
Sparse Core Ops, SparseCore 0:
  11.5 61.1 all-gather.7
  84.0 19.1 all-gather.11
  105.4 19.5 all-gather.9
  128.4 53.1 all-gather.13
  184.8 59.3 all-gather.15
  247.5 54.0 all-gather.17
  344.2 27.6 reduce-scatter.9
  374.5 28.1 reduce-scatter.11
  408.0 97.2 reduce-scatter.15
  511.5 101.8 reduce-scatter.19
  620.0 118.1 reduce-scatter.17
  743.7 118.3 reduce-scatter.13
where the time goes:
time: 884 us; the launch traced here: 872 us
  waiting for transfers between devices  633 us (72%)
  blocking collectives  74.2 us (8%)
  matrix products  63.1 us (7%)
  local copies, waits for them, and re-layouts  45.8 us (5%)
  other arithmetic  38.8 us (4%)
  between operations  15.3 us (2%)
    reduce_scatter x1, waiting for transfers between devices, body(): lax.psum_scatter(grad_in, ('dp', 'fsdp'), scatter_dimension=0, tiled=True)  122 us
    reduce_scatter x1, waiting for transfers between devices, body(): lax.psum_scatter(grad_qkv, ('dp', 'fsdp'), scatter_dimension=0, tiled=True)  121 us
    unnamed x13, waiting for transfers between devices  105 us
    all_gather x1, waiting for transfers between devices, body(): lax.all_gather(copies[2], ('dp', 'fsdp'), axis=0, tiled=True)  59.3 us
    all_gather x1, waiting for transfers between devices, body(): lax.all_gather(copies[3], ('dp', 'fsdp'), axis=0, tiled=True)  52.7 us
    reduce_scatter x1, waiting for transfers between devices, body(): lax.psum_scatter(grad_out, ('dp', 'fsdp'), scatter_dimension=0, tiled=True)  51.2 us
    unnamed x1, blocking collectives  38.6 us
    all_gather x1, waiting for transfers between devices, body(): lax.all_gather(copies[1], ('dp', 'fsdp'), axis=0, tiled=True)  36.1 us
  transfers between devices with their start and end apart: 12, of which 12 were waited for; matrix products, arithmetic and copies ran while one was open for 10% of the time, Pallas kernels for 0%

commit v1 on v0

--- a/solution.py
+++ b/solution.py
@@ -1,6 +1,8 @@
 import jax
 import jax.numpy as jnp
 from jax import lax
+from jax.experimental import pallas as pl
+from jax.experimental.pallas import tpu as pltpu
 from jax.sharding import PartitionSpec as P
 
 HEADS = 12
@@ -117,7 +119,7 @@
     return (first_new, second_new, master_new, average_new, master_new.astype(jnp.bfloat16))
 
 
-def body(
+def general_body(
     tokens,
     cotangent,
     counts,
@@ -376,64 +378,613 @@
     )
 
 
+BF = jnp.bfloat16
+F32 = jnp.float32
+AXES = ("dp", "fsdp")
+VMEM_LIMIT = 50 * 1024 * 1024
+
+
+def xperm(value, mask):
+    count = lax.axis_size("dp") * lax.axis_size("fsdp")
+    return lax.ppermute(value, AXES, [(i, i ^ mask) for i in range(count)])
+
+
+def dot_nn(a, b):
+    return jnp.dot(a, b, preferred_element_type=F32)
+
+
+def dot_nt(a, b):
+    return lax.dot_general(a, b, (((1,), (1,)), ((), ())), preferred_element_type=F32)
+
+
+def dot_tn(a, b):
+    return lax.dot_general(a, b, (((0,), (0,)), ((), ())), preferred_element_type=F32)
+
+
+def split_columns(first, second):
+    src = lax.broadcasted_iota(jnp.int32, (first, second), 0)
+    col = lax.broadcasted_iota(jnp.int32, (1, second), 1)
+    part = col // 256
+    inner = col % 256
+    half = inner // 128
+    lane = inner % 128
+    rotary = jnp.where(lane < 96, 192 * part + 64 * (lane // 32) + 32 * half + lane % 32, -1)
+    plain = jnp.where(inner < 192, 384 + inner, -1)
+    want = jnp.where(part < 2, rotary, plain)
+    return (src == want).astype(F32).astype(BF)
+
+
+def head_lanes(width, head):
+    lane = lax.broadcasted_iota(jnp.int32, (1, width), 1) % 128
+    return (lane >= 32 * head) & (lane < 32 * head + 32)
+
+
+def value_lanes(width, head):
+    lane = lax.broadcasted_iota(jnp.int32, (1, width), 1)
+    return (lane >= 64 * head) & (lane < 64 * head + 64)
+
+
+def forward_kernel(
+    ids, t0, t1, t2, t3, cos, sin, docq, dock, w0, w1, w2, w3, w4, w5, w6, w7,
+    n16, q8, key, val, att, a0, a1, a2, a3, prob, gain, wide, wscr, sems,
+):
+    step = pl.program_id(0)
+
+    @pl.when(step == 0)
+    def _():
+        copies = []
+        for k, piece in enumerate((w0, w1, w2, w3, w4, w5, w6, w7)):
+            at = pl.multiple_of(96 * (ids[1] ^ k), 96)
+            copies.append(pltpu.make_async_copy(piece, wscr.at[pl.ds(at, 96)], sems.at[k]))
+            copies[-1].start()
+        for copy in copies:
+            copy.wait()
+        weight = wscr[...]
+        wide[...] = dot_nn(weight, split_columns(640, 768)).astype(BF)
+        row = lax.broadcasted_iota(jnp.int32, (8, 640), 0)
+        col = lax.broadcasted_iota(jnp.int32, (8, 640), 1)
+        pick = ((col == row + 576) & (row < 2)).astype(F32).astype(BF)
+        gain[...] = dot_nt(pick, weight)
+        gain_row = gain[0:1, :]
+        for i, piece in enumerate((t0, t1, t2, t3)):
+            rows = slice(256 * i, 256 * i + 256)
+            x = piece[...].astype(F32)
+            center = x - jnp.mean(x, axis=-1, keepdims=True)
+            inverse = lax.rsqrt(jnp.mean(center * center, axis=-1, keepdims=True) + NORM_EPS)
+            normed = (center * inverse * gain_row).astype(BF)
+            n16[rows, :] = normed
+            mixed = dot_nn(normed, wide[...])
+            c, s = cos[rows, :], sin[rows, :]
+            qa, qb = mixed[:, :128], mixed[:, 128:256]
+            ka, kb = mixed[:, 256:384], mixed[:, 384:512]
+            q8[rows, :128] = ((qa * c - qb * s).astype(BF).astype(F32) * 0.125).astype(BF)
+            q8[rows, 128:] = ((qb * c + qa * s).astype(BF).astype(F32) * 0.125).astype(BF)
+            key[rows, :128] = (ka * c - kb * s).astype(BF)
+            key[rows, 128:] = (kb * c + ka * s).astype(BF)
+            val[rows, :] = mixed[:, 512:].astype(BF)
+
+    rows = pl.ds(pl.multiple_of(step * 256, 256), 256)
+    queries = q8[rows, :]
+    keys = key[...]
+    values = val[...]
+    same = docq[rows, :] == dock[...]
+    total = jnp.zeros((256, 256), F32)
+    zero = jnp.zeros((), BF)
+    for h in range(3):
+        scores = dot_nt(jnp.where(head_lanes(256, h), queries, zero), keys)
+        scores = jnp.where(same, scores, MASKED)
+        peak = jnp.max(scores, axis=-1, keepdims=True)
+        weights = jnp.exp(scores - peak)
+        scale = 1.0 / jnp.sum(weights, axis=-1, keepdims=True)
+        weights16 = (weights * scale).astype(BF)
+        prob[h] = weights16
+        total += dot_nn(weights16, jnp.where(value_lanes(256, h), values, zero))
+    att[...] = total[:, :192]
+    low = total[:, :192].astype(BF)
+    for i, out in enumerate((a0, a1, a2, a3)):
+
+        @pl.when(step == i)
+        def _():
+            out[...] = low
+
+
+def full(shape):
+    return pl.BlockSpec(shape, lambda *_: (0,) * len(shape))
+
+
+SMEM = pl.BlockSpec(memory_space=pltpu.SMEM)
+ANY = pl.BlockSpec(memory_space=pl.ANY)
+
+
+def shaped(shape, dtype):
+    return jax.ShapeDtypeStruct(shape, dtype)
+
+
+def forward_attention(ids, token_pieces, cos, sin, docs, w_pieces):
+    return pl.pallas_call(
+        forward_kernel,
+        grid=(4,),
+        in_specs=[SMEM]
+        + [full((256, 768))] * 4
+        + [full((1024, 128))] * 2
+        + [full((1024, 1)), full((1, 1024))]
+        + [ANY] * 8,
+        out_specs=[
+            full((1024, 768)),
+            full((1024, 256)),
+            full((1024, 256)),
+            full((1024, 256)),
+            pl.BlockSpec((256, 192), lambda i: (i, 0)),
+            full((256, 192)),
+            full((256, 192)),
+            full((256, 192)),
+            full((256, 192)),
+            pl.BlockSpec((3, 256, 1024), lambda i: (0, i, 0)),
+            full((8, 768)),
+            full((768, 768)),
+        ],
+        out_shape=[
+            shaped((1024, 768), BF),
+            shaped((1024, 256), BF),
+            shaped((1024, 256), BF),
+            shaped((1024, 256), BF),
+            shaped((1024, 192), F32),
+            shaped((256, 192), BF),
+            shaped((256, 192), BF),
+            shaped((256, 192), BF),
+            shaped((256, 192), BF),
+            shaped((3, 1024, 1024), BF),
+            shaped((8, 768), F32),
+            shaped((768, 768), BF),
+        ],
+        scratch_shapes=[pltpu.VMEM((768, 640), BF), pltpu.SemaphoreType.DMA((8,))],
+        compiler_params=pltpu.CompilerParams(vmem_limit_bytes=VMEM_LIMIT),
+        cost_estimate=pl.CostEstimate(flops=6 * 10**9, bytes_accessed=16 * 10**6, transcendentals=3 * 10**6),
+        name="forward_attention",
+    )(ids, *token_pieces, cos, sin, docs[:, None], docs[None, :], *w_pieces)
+
+
+def erf_pair(x):
+    cdf = 0.5 * (1.0 + lax.erf(x * (0.5**0.5)))
+    density = jnp.exp(-0.5 * x * x) * (1.0 / (2.0 * 3.141592653589793) ** 0.5)
+    return cdf, density
+
+
+SLOTS = 16
+
+
+def feed_kernel(*refs):
+    ids, tok, cot, live, gain, a0, a1, a2, a3 = refs[:9]
+    first = refs[9 : 9 + SLOTS]
+    last = refs[9 + SLOTS : 9 + 2 * SLOTS]
+    (block, dmid, d0, d1, d2, d3, act16, n2low, dgate, dbr, ggain, w_in, w_out, w_down, sems) = refs[
+        9 + 2 * SLOTS :
+    ]
+    f, core, chip = ids[0], ids[2], ids[3]
+    copies = []
+
+    def load(source, target):
+        copies.append(pltpu.make_async_copy(source, target, sems.at[len(copies)]))
+        copies[-1].start()
+
+    places = []
+    for owner in range(2):
+        half = core if owner == 0 else 1 - core
+        for group in range(8):
+            for j in range(2):
+                kx, ky, kz = (group >> 1) & 1, (group >> 2) & 1, (group & 1) * 2 + j
+                mask = kz * 4 + ky * 2 + kx
+                at = pl.multiple_of(48 * (chip ^ mask), 48)
+                places.append((owner * 8 + group, j, half, pl.ds(at, 48)))
+    for which, j, half, rows in places:
+        load(first[which].at[j, :, pl.ds(1152, 384)], w_out.at[half, rows])
+    for which, j, half, rows in places:
+        load(first[which].at[j, :, pl.ds(0, 1152)], w_in.at[half, rows])
+    for which, j, half, rows in places:
+        load(last[which].at[j], w_down.at[half, rows])
+    for copy in copies[:32]:
+        copy.wait()
+    tok_f = tok[...].astype(F32)
+    pieces = [a[...] for a in (a0, a1, a2, a3)]
+    heads = [pl.ds(pl.multiple_of(192 * (f ^ k), 192), 192) for k in range(4)]
+    left = jnp.zeros((256, 384), F32)
+    right = jnp.zeros((256, 384), F32)
+    for k in range(4):
+        left += dot_nn(pieces[k], w_out[0, heads[k], :])
+        right += dot_nn(pieces[k], w_out[1, heads[k], :])
+    middle = tok_f + jnp.concatenate([left, right], axis=1)
+    center = middle - jnp.mean(middle, axis=-1, keepdims=True)
+    inverse = lax.rsqrt(jnp.mean(center * center, axis=-1, keepdims=True) + NORM_EPS)
+    normed = center * inverse
+    gain_row = gain[1:2, :]
+    low = (normed * gain_row).astype(BF)
+    n2low[...] = low
+    for copy in copies[32:64]:
+        copy.wait()
+    act = dot_nn(low, w_in[0])
+    gate = dot_nn(low, w_in[1])
+    cdf, density = erf_pair(act)
+    gelu = act * cdf
+    active = (gelu * gate).astype(BF)
+    act16[...] = active
+    for copy in copies[64:]:
+        copy.wait()
+    alive = live[...]
+    dout = jnp.where(alive > 0.5, cot[...].astype(F32), 0.0)
+    dym = dout.astype(BF)
+    dact = jnp.concatenate([dot_nn(dym, w_down[0]), dot_nn(dym, w_down[1, :, :512])], axis=1)
+    dg_front = (dact * gate * (cdf + act * density)).astype(BF)
+    dg_rear = (dact * gelu).astype(BF)
+    dgate[:, :1152] = dg_front
+    dgate[:, 1152:] = dg_rear
+    dnormed = dot_nt(dg_front, w_in[0]) + dot_nt(dg_rear, w_in[1])
+    ggain[...] = jnp.broadcast_to(jnp.sum(dnormed * normed, axis=0, keepdims=True), (8, 768))
+    up = dnormed * gain_row
+    dmiddle = dout + inverse * (
+        up
+        - jnp.mean(up, axis=-1, keepdims=True)
+        - normed * jnp.mean(up * normed, axis=-1, keepdims=True)
+    )
+    dmid[...] = dmiddle
+    dbranch = dmiddle.astype(BF)
+    dbr[...] = dbranch
+    for k, out in enumerate((d0, d1, d2, d3)):
+        out[...] = (
+            dot_nt(dbranch[:, :384], w_out[0, heads[k], :]) + dot_nt(dbranch[:, 384:], w_out[1, heads[k], :])
+        ).astype(BF)
+    branch = dot_nt(active[:, :640], w_down[0]) + dot_nt(active[:, 640:], w_down[1, :, :512])
+    block[...] = jnp.where(alive > 0.5, middle + branch, 0.0).astype(BF)
+
+
+def feed_forward(ids, tokens, cotangent, live, gain, att_pieces, first, last):
+    return pl.pallas_call(
+        feed_kernel,
+        in_specs=[SMEM] + [pl.BlockSpec(memory_space=pltpu.VMEM)] * 8 + [ANY] * (2 * SLOTS),
+        out_specs=[pl.BlockSpec(memory_space=pltpu.VMEM)] * 11,
+        out_shape=[
+            shaped((256, 768), BF),
+            shaped((256, 768), F32),
+            shaped((256, 192), BF),
+            shaped((256, 192), BF),
+            shaped((256, 192), BF),
+            shaped((256, 192), BF),
+            shaped((256, 1152), BF),
+            shaped((256, 768), BF),
+            shaped((256, 2304), BF),
+            shaped((256, 768), BF),
+            shaped((8, 768), F32),
+        ],
+        scratch_shapes=[
+            pltpu.VMEM((2, 768, 1152), BF),
+            pltpu.VMEM((2, 768, 384), BF),
+            pltpu.VMEM((2, 768, 640), BF),
+            pltpu.SemaphoreType.DMA((96,)),
+        ],
+        compiler_params=pltpu.CompilerParams(vmem_limit_bytes=VMEM_LIMIT),
+        cost_estimate=pl.CostEstimate(flops=5 * 10**9, bytes_accessed=12 * 10**6, transcendentals=10**6),
+        name="feed_forward",
+    )(ids, tokens, cotangent, live, gain, *att_pieces, *first, *last)
+
+
+CHUNK = 2176
+
+
+def feed_grad_kernel(
+    ids, cot, live, act16, n2low, dgate, dbr, a0, a1, a2, a3,
+    s0, s1, s2, s3, k0, k1, k2, k3, grads, sems,
+):
+    f, core, chip = ids[0], ids[2], ids[3]
+    dym = jnp.where(live[...] > 0.5, cot[...].astype(F32), 0.0).astype(BF)
+    gdown = dot_tn(dym, act16[...])
+    grads[0, :, 1536:2176] = gdown[:, :640].astype(BF)
+    grads[1, :, 1536:2048] = gdown[:, 640:].astype(BF)
+    grads[1, :, 2048:2176] = jnp.zeros((768, 128), BF)
+    low = n2low[...]
+    grads[0, :, :1152] = dot_tn(low, dgate[:, :1152]).astype(BF)
+    grads[1, :, :1152] = dot_tn(low, dgate[:, 1152:]).astype(BF)
+    branch = dbr[...]
+    for k, piece in enumerate((a0, a1, a2, a3)):
+        rows = pl.ds(pl.multiple_of(192 * (f ^ k), 192), 192)
+        gout = dot_tn(piece[...], branch).astype(BF)
+        grads[0, rows, 1152:1536] = gout[:, :384]
+        grads[1, rows, 1152:1536] = gout[:, 384:]
+    copies = []
+    for group in (3, 1, 2, 0):
+        for kz in range(4):
+            at = pl.multiple_of(48 * (chip ^ (kz * 4 + group)), 48)
+            for half, target in ((1 - core, (s0, s1, s2, s3)[group]), (core, (k0, k1, k2, k3)[group])):
+                copies.append(
+                    pltpu.make_async_copy(grads.at[half, pl.ds(at, 48)], target.at[kz], sems.at[len(copies)])
+                )
+                copies[-1].start()
+    for copy in copies:
+        copy.wait()
+
+
+def feed_gradients(ids, cotangent, live, act16, n2low, dgate, dbr, att_pieces):
+    return pl.pallas_call(
+        feed_grad_kernel,
+        in_specs=[SMEM] + [pl.BlockSpec(memory_space=pltpu.VMEM)] * 10,
+        out_specs=[ANY] * 8,
+        out_shape=[shaped((4, 48, CHUNK), BF)] * 8,
+        scratch_shapes=[pltpu.VMEM((2, 768, CHUNK), BF), pltpu.SemaphoreType.DMA((32,))],
+        compiler_params=pltpu.CompilerParams(vmem_limit_bytes=VMEM_LIMIT),
+        cost_estimate=pl.CostEstimate(flops=3 * 10**9, bytes_accessed=12 * 10**6, transcendentals=0),
+        name="feed_gradients",
+    )(ids, cotangent, live, act16, n2low, dgate, dbr, *att_pieces)
+
+
+def backward_kernel(
+    ids, t0, t1, t2, t3, cos, sin, n16, q8, key, val, att, prob, d0, d1, d2, d3, gain, wide, ggain,
+    dn0, dn1, dn2, dn3, far, near, dq, dkt, dvt, grads, sems,
+):
+    step = pl.program_id(0)
+
+    @pl.when(step == 0)
+    def _():
+        dkt[...] = jnp.zeros((256, 1024), F32)
+        dvt[...] = jnp.zeros((256, 1024), F32)
+
+    rows = pl.ds(pl.multiple_of(step * 256, 256), 256)
+    zero = jnp.zeros((), BF)
+    keys = key[...]
+    values = val[...]
+    dattn = d0[...]
+    for i, piece in ((1, d1), (2, d2), (3, d3)):
+        dattn = jnp.where(step == i, piece[...], dattn)
+    dattn = jnp.concatenate([dattn, jnp.zeros((256, 64), BF)], axis=1)
+    product = dattn[:, :192].astype(F32) * att[...]
+    queries_t = q8[rows, :].T
+    dattn_t = dattn.T
+    total = jnp.zeros((256, 256), F32)
+    for h in range(3):
+        weights = prob[h]
+        dprob = dot_nt(jnp.where(value_lanes(256, h), dattn, zero), values)
+        delta = jnp.sum(jnp.where(value_lanes(192, h), product, 0.0), axis=-1, keepdims=True)
+        dscores = (weights.astype(F32) * (dprob - delta)).astype(BF)
+        total += dot_nn(dscores, jnp.where(head_lanes(256, h), keys, zero))
+        q_head = jnp.concatenate([queries_t[32 * h : 32 * h + 32], queries_t[128 + 32 * h : 160 + 32 * h]], axis=0)
+        dk_head = dot_nn(q_head, dscores)
+        dkt[32 * h : 32 * h + 32, :] += dk_head[:32]
+        dkt[128 + 32 * h : 160 + 32 * h, :] += dk_head[32:]
+        dvt[64 * h : 64 * h + 64, :] += dot_nn(dattn_t[64 * h : 64 * h + 64], weights)
+    c, s = cos[rows, :], sin[rows, :]
+    dqa, dqb = total[:, :128] * 0.125, total[:, 128:] * 0.125
+    dq[rows, :128] = (dqa * c + dqb * s).astype(BF)
+    dq[rows, 128:256] = (dqb * c - dqa * s).astype(BF)
+
+    @pl.when(step == 3)
+    def _():
+        dk = dkt[...].T
+        ca, sa = cos[...], sin[...]
+        dq[:, 256:384] = (dk[:, :128] * ca + dk[:, 128:] * sa).astype(BF)
+        dq[:, 384:512] = (dk[:, 128:] * ca - dk[:, :128] * sa).astype(BF)
+        dq[:, 512:768] = dvt[...].T.astype(BF)
+        ggain1 = jnp.zeros((1, 768), F32)
+        for i, (piece, out) in enumerate(((t0, dn0), (t1, dn1), (t2, dn2), (t3, dn3))):
+            part = dot_nt(dq[256 * i : 256 * i + 256, :], wide[...])
+            x = piece[...].astype(F32)
+            center = x - jnp.mean(x, axis=-1, keepdims=True)
+            inverse = lax.rsqrt(jnp.mean(center * center, axis=-1, keepdims=True) + NORM_EPS)
+            ggain1 += jnp.sum(part * (center * inverse), axis=0, keepdims=True)
+            out[...] = part.astype(BF)
+        wide_grad = dot_tn(n16[...], dq[...]).astype(BF)
+        natural = dot_nt(wide_grad, split_columns(640, 768))
+        gains = jnp.concatenate([ggain1, ggain[0:1, :], jnp.zeros((126, 768), F32)], axis=0)
+        column = jnp.concatenate([natural[:, :512], natural[:, 512:576], gains.T[:, :64]], axis=1)
+        grads[...] = column.astype(BF)
+        copies = []
+        for ky, target in ((1, far), (0, near)):
+            for kz in range(4):
+                at = pl.multiple_of(96 * (ids[1] ^ (kz * 2 + ky)), 96)
+                copies.append(
+                    pltpu.make_async_copy(grads.at[pl.ds(at, 96)], target.at[kz], sems.at[len(copies)])
+                )
+                copies[-1].start()
+        for copy in copies:
+            copy.wait()
+
+
+def backward_attention(ids, token_pieces, cos, sin, n16, q8, key, val, att, prob, d_pieces, gain, wide, ggain):
+    return pl.pallas_call(
+        backward_kernel,
+        grid=(4,),
+        in_specs=[SMEM]
+        + [full((256, 768))] * 4
+        + [full((1024, 128))] * 2
+        + [full((1024, 768))]
+        + [full((1024, 256))] * 3
+        + [pl.BlockSpec((256, 192), lambda i: (i, 0))]
+        + [pl.BlockSpec((3, 256, 1024), lambda i: (0, i, 0))]
+        + [full((256, 192))] * 4
+        + [full((8, 768)), full((768, 768)), full((8, 768))],
+        out_specs=[full((256, 768))] * 4 + [ANY, ANY],
+        out_shape=[shaped((256, 768), BF)] * 4 + [shaped((4, 96, 640), BF)] * 2,
+        scratch_shapes=[
+            pltpu.VMEM((1024, 768), BF),
+            pltpu.VMEM((256, 1024), F32),
+            pltpu.VMEM((256, 1024), F32),
+            pltpu.VMEM((768, 640), BF),
+            pltpu.SemaphoreType.DMA((8,)),
+        ],
+        compiler_params=pltpu.CompilerParams(vmem_limit_bytes=VMEM_LIMIT),
+        cost_estimate=pl.CostEstimate(flops=8 * 10**9, bytes_accessed=16 * 10**6, transcendentals=0),
+        name="backward_attention",
+    )(ids, *token_pieces, cos, sin, n16, q8, key, val, att, prob, *d_pieces, gain, wide, ggain)
+
+
+def pack_layout(count_row, length_row, slots, own_place):
+    devices_here = count_row.shape[0]
+    places = jnp.arange(devices_here * slots, dtype=jnp.int32)
+    holder = (places // slots) ^ own_place
+    within = places % slots
+    before = jnp.cumsum(count_row) - count_row
+    choose = (holder[:, None] == jnp.arange(devices_here, dtype=jnp.int32)[None, :]).astype(jnp.int32)
+    offset = jnp.sum(choose * before[None, :], axis=1) + within
+    limits = jnp.sum(choose * count_row[None, :], axis=1)
+    living = within < limits
+    doc_ends = jnp.cumsum(length_row)
+    passed = offset[:, None] >= doc_ends[None, :]
+    document = jnp.sum(passed.astype(jnp.int32), axis=1)
+    begins = jnp.max(jnp.where(passed, doc_ends[None, :], 0), axis=1)
+    document = jnp.where(living, document, length_row.shape[0])
+    position = jnp.where(living, offset - begins, 0)
+    return document, position, living
+
+
+def by_place(pieces, low_bit, high_bit):
+    a, b, c, d = pieces
+    t0, t1 = jnp.where(low_bit, b, a), jnp.where(low_bit, a, b)
+    t2, t3 = jnp.where(low_bit, d, c), jnp.where(low_bit, c, d)
+    return [
+        jnp.where(high_bit, t2, t0),
+        jnp.where(high_bit, t3, t1),
+        jnp.where(high_bit, t0, t2),
+        jnp.where(high_bit, t1, t3),
+    ]
+
+
+def gather_halves(halves, core):
+    mine = jnp.where(core == 0, halves[0], halves[1])
+    other = jnp.where(core == 0, halves[1], halves[0])
+    came = xperm(other, 1)
+    lower, upper = jnp.where(core == 0, mine, came), jnp.where(core == 0, came, mine)
+    own = jnp.concatenate([lower, upper], axis=0)
+    z1, z2, z3 = xperm(own, 8), xperm(own, 16), xperm(own, 24)
+    p0, p1 = jnp.stack([own, z1]), jnp.stack([z2, z3])
+    x0, y0 = xperm(p0, 2), xperm(p0, 4)
+    x1, y1 = xperm(p1, 2), xperm(p1, 4)
+    xy0 = xperm(y0, 2)
+    xy1 = xperm(x1, 4)
+    held = [p0, p1, x0, x1, y0, y1, xy0, xy1]
+    return held + [xperm(piece, 1) for piece in held]
+
+
+def fast_body(
+    tokens, cotangent, counts, lengths,
+    weight_qkv, weight_out, weight_in, weight_down, norm_gains,
+    first_qkv, first_out, first_in, first_down, first_gains,
+    second_qkv, second_out, second_in, second_down, second_gains,
+    average_qkv, average_out, average_in, average_down, average_gains,
+):
+    slots = tokens.shape[0]
+    group_row = lax.axis_index("dp")
+    own_place = lax.axis_index("fsdp")
+    core, side = own_place & 1, own_place >> 1
+    chip = group_row * 2 + side
+    ids = jnp.stack([own_place, group_row, core, chip]).astype(jnp.int32)
+
+    qkv16 = weight_qkv.astype(BF)
+    blocks = qkv16.reshape(24, 3, 4, 192).transpose(2, 0, 1, 3).reshape(4, 24, 576)
+    gain_cols = jnp.concatenate([norm_gains.T.astype(BF), jnp.zeros((24, 62), BF)], axis=1)
+    blocks = jnp.concatenate([blocks, jnp.broadcast_to(gain_cols[None], (4, 24, 64))], axis=2)
+    sends = [lax.dynamic_index_in_dim(blocks, own_place ^ k, 0, keepdims=False) for k in range(4)]
+    came = [sends[0]] + [xperm(sends[k], k) for k in (1, 2, 3)]
+    rows_here = jnp.concatenate(by_place(came, core == 1, side == 1), axis=0)
+    column = [rows_here, xperm(rows_here, 8), xperm(rows_here, 16), xperm(rows_here, 24)]
+    w_pieces = []
+    for piece in column:
+        w_pieces += [piece, xperm(piece, 4)]
+
+    tok_x, tok_c = xperm(tokens, 2), xperm(tokens, 1)
+    token_pieces = [tokens, tok_c, tok_x, xperm(tok_x, 1)]
+
+    in16, out16, down16 = weight_in.astype(BF), weight_out.astype(BF), weight_down.astype(BF)
+    down16 = jnp.pad(down16, ((0, 0), (0, 128)))
+    first = gather_halves(
+        [
+            jnp.concatenate([in16[:, 1152 * h : 1152 * h + 1152], out16[:, 384 * h : 384 * h + 384]], axis=1)
+            for h in range(2)
+        ],
+        core,
+    )
+    last = gather_halves([down16[:, 640 * h : 640 * h + 640] for h in range(2)], core)
+
+    count_row = lax.dynamic_index_in_dim(counts, group_row, 0, keepdims=False)
+    length_row = lax.dynamic_index_in_dim(lengths, group_row, 0, keepdims=False)
+    docs, position, living = pack_layout(count_row, length_row, slots, own_place)
+    speeds = ROTARY_BASE ** (-(jnp.arange(HD // 2, dtype=F32) * (2.0 / HD)))
+    angles = position.astype(F32)[:, None] * jnp.tile(speeds, 4)[None, :]
+    cos, sin = jnp.cos(angles), jnp.sin(angles)
+    live = living[:slots, None].astype(F32)
+
+    n16, q8, key, val, att, a0, a1, a2, a3, prob, gain, wide = forward_attention(
+        ids, token_pieces, cos, sin, docs, w_pieces
+    )
+    att_pieces = [a0, xperm(a1, 1), xperm(a2, 2), xperm(a3, 3)]
+    block_out, dmiddle, d0, d1, d2, d3, act16, n2low, dgate, dbr, ggain = feed_forward(
+        ids, tokens, cotangent, live, gain, att_pieces, first, last
+    )
+    d_pieces = [d0, xperm(d1, 1), xperm(d2, 2), xperm(d3, 3)]
+    s0, s1, s2, s3, k0, k1, k2, k3 = feed_gradients(
+        ids, cotangent, live, act16, n2low, dgate, dbr, att_pieces
+    )
+
+    def add(*parts):
+        total = parts[0].astype(F32)
+        for part in parts[1:]:
+            total = total + part.astype(F32)
+        return total.astype(BF)
+
+    e3 = add(k3, xperm(s3, 1))
+    e1 = add(k1, xperm(s1, 1))
+    e2 = add(k2, xperm(s2, 1))
+    e0 = add(k0, xperm(s0, 1))
+    to_y = xperm(e3[:2], 2)
+    to_x = xperm(e3[2:], 4)
+    x0 = xperm(e1[:2], 2)
+    y1 = xperm(e2[2:], 4)
+    y0 = xperm(add(e2[:2], to_y), 4)
+    x1 = xperm(add(e1[2:], to_x), 2)
+    f0 = add(e0[:2], x0, y0)
+    f1 = add(e0[2:], x1, y1)
+    chip_rows = add(f0[0], xperm(f0[1], 8), xperm(f1[0], 16), xperm(f1[1], 24))
+    lower, upper = chip_rows[:24], chip_rows[24:]
+    mine, other = jnp.where(core == 0, lower, upper), jnp.where(core == 0, upper, lower)
+    came = xperm(other, 1)
+    half0 = jnp.where(core == 0, mine, came).astype(F32)
+    half1 = jnp.where(core == 0, came, mine).astype(F32)
+    grad_in = jnp.concatenate([half0[:, :1152], half1[:, :1152]], axis=1)
+    grad_out = jnp.concatenate([half0[:, 1152:1536], half1[:, 1152:1536]], axis=1)
+    grad_down = jnp.concatenate([half0[:, 1536:2176], half1[:, 1536:2048]], axis=1)
+
+    dn0, dn1, dn2, dn3, far, near = backward_attention(
+        ids, token_pieces, cos, sin, n16, q8, key, val, att, prob, d_pieces, gain, wide, ggain
+    )
+    e = add(near, xperm(far, 4))
+    dp_rows = add(e[0], xperm(e[1], 8), xperm(e[2], 16), xperm(e[3], 24)).reshape(4, 24, 640)
+    sends = [lax.dynamic_index_in_dim(dp_rows, own_place ^ k, 0, keepdims=False) for k in range(4)]
+    came = [sends[0]] + [xperm(sends[k], k) for k in (1, 2, 3)]
+    placed = jnp.stack(by_place([piece.astype(F32) for piece in came], core == 1, side == 1))
+    grad_qkv = placed[:, :, :576].reshape(4, 24, 3, 192).transpose(1, 2, 0, 3).reshape(24, 2304)
+    grad_gains = jnp.sum(placed[:, :, 576:578], axis=0).T
+
+    own_sum, x_sum = add(dn0, xperm(dn1, 1)), add(dn2, xperm(dn3, 1))
+    dnormed = own_sum.astype(F32) + xperm(x_sum, 2).astype(F32)
+    normed, inverse = norm_parts(tokens.astype(F32))
+    grad_tokens = dmiddle + norm_back(dnormed * gain[0:1, :], normed, inverse)
+
+    masters = (weight_qkv, weight_out, weight_in, weight_down, norm_gains)
+    firsts = (first_qkv, first_out, first_in, first_down, first_gains)
+    seconds = (second_qkv, second_out, second_in, second_down, second_gains)
+    averages = (average_qkv, average_out, average_in, average_down, average_gains)
+    rates = (MATRIX_RATE, MATRIX_RATE, MATRIX_RATE, MATRIX_RATE, GAIN_RATE)
+    grads = (grad_qkv, grad_out, grad_in, grad_down, grad_gains)
+    updated = [
+        adam_update(masters[i], firsts[i], seconds[i], averages[i], grads[i], rates[i]) for i in range(5)
+    ]
+    return (block_out, grad_tokens) + tuple(updated[i][j] for j in range(5) for i in range(5))
+
+
 def solution(mesh):
+    sizes = dict(mesh.shape)
+    body = fast_body if sizes == {"dp": 8, "fsdp": 4} else general_body
+    rows, columns = P(("dp", "fsdp"), None), P(None, ("dp", "fsdp"))
+    weights = (rows,) * 4 + (columns,)
     return jax.shard_map(
         body,
         mesh=mesh,
-        in_specs=(
-            P(("dp", "fsdp"), None),
-            P(("dp", "fsdp"), None),
-            P(),
-            P(),
-            P(("dp", "fsdp"), None),
-            P(("dp", "fsdp"), None),
-            P(("dp", "fsdp"), None),
-            P(("dp", "fsdp"), None),
-            P(None, ("dp", "fsdp")),
-            P(("dp", "fsdp"), None),
-            P(("dp", "fsdp"), None),
-            P(("dp", "fsdp"), None),
-            P(("dp", "fsdp"), None),
-            P(None, ("dp", "fsdp")),
-            P(("dp", "fsdp"), None),
-            P(("dp", "fsdp"), None),
-            P(("dp", "fsdp"), None),
-            P(("dp", "fsdp"), None),
-            P(None, ("dp", "fsdp")),
-            P(("dp", "fsdp"), None),
-            P(("dp", "fsdp"), None),
-            P(("dp", "fsdp"), None),
-            P(("dp", "fsdp"), None),
-            P(None, ("dp", "fsdp")),
-        ),
-        out_specs=(
-            P(("dp", "fsdp"), None),
-            P(("dp", "fsdp"), None),
-            P(("dp", "fsdp"), None),
-            P(("dp", "fsdp"), None),
-            P(("dp", "fsdp"), None),
-            P(("dp", "fsdp"), None),
-            P(None, ("dp", "fsdp")),
-            P(("dp", "fsdp"), None),
-            P(("dp", "fsdp"), None),
-            P(("dp", "fsdp"), None),
-            P(("dp", "fsdp"), None),
-            P(None, ("dp", "fsdp")),
-            P(("dp", "fsdp"), None),
-            P(("dp", "fsdp"), None),
-            P(("dp", "fsdp"), None),
-            P(("dp", "fsdp"), None),
-            P(None, ("dp", "fsdp")),
-            P(("dp", "fsdp"), None),
-            P(("dp", "fsdp"), None),
-            P(("dp", "fsdp"), None),
-            P(("dp", "fsdp"), None),
-            P(None, ("dp", "fsdp")),
-            P(("dp", "fsdp"), None),
-            P(("dp", "fsdp"), None),
-            P(("dp", "fsdp"), None),
-            P(("dp", "fsdp"), None),
-            P(None, ("dp", "fsdp")),
-        ),
+        in_specs=(rows, rows, P(), P()) + weights * 4,
+        out_specs=(rows, rows) + weights * 5,
         check_vma=False,
     )

time: 884 us -> 292 us (0.33)
  waiting for transfers between devices: 633 us -> 91.2 us
  blocking collectives: 74.2 us -> 0 us
  starting transfers between devices: 0.75 us -> 73 us
  matrix products: 63.1 us -> 0 us
  Pallas kernels: 0 us -> 53.2 us
  between operations: 15.3 us -> 1.78 us
    reduce_scatter x5 -> x0, waiting for transfers between devices: 333 us -> none  [the longest x1 122 us: body(): lax.psum_scatter(grad_in, ('dp', 'fsdp'), scatter_dimension=0, tiled=True)]
    all_gather x6 -> x0, waiting for transfers between devices: 196 us -> none  [the longest x1 59.3 us: body(): lax.all_gather(copies[2], ('dp', 'fsdp'), axis=0, tiled=True)]
    unnamed x13 -> x0, waiting for transfers between devices: 105 us -> none
    ppermute x0 -> x79, waiting for transfers between devices: none -> 91.2 us  [xperm(): return lax.ppermute(value, AXES, [(i, i ^ mask) for i in range(count)])]
    ppermute x0 -> x79, starting transfers between devices: none -> 73 us  [xperm(): return lax.ppermute(value, AXES, [(i, i ^ mask) for i in range(count)])]
    dot_general x26 -> x0, matrix products: 63.1 us -> none  [the longest x4 15 us: contract_rows(): lax.dot_general(left_side, right_side, (((0,), (0,)), ((), ())), preferre...]
    pallas_call x0 -> x4, Pallas kernels: none -> 53.2 us  [the longest x1 17.6 us: forward_attention(): pl.pallas_call(forward_kernel, grid=(4,), in_specs=[SMEM] + [full((256, 7...]
    unnamed x1 -> x0, blocking collectives: 38.6 us -> none
  transfers between devices with their start and end apart: 12 -> 79, of which waited for: 12 -> 19; matrix products, arithmetic and copies ran while one was open for 10% -> 11% of each run, Pallas kernels for 0% -> 9%
where the time goes in v1:
time: 292 us; the launch traced here: 287 us
  waiting for transfers between devices  91.2 us (31%)
  starting transfers between devices  73 us (25%)
  Pallas kernels  53.2 us (18%)
  local copies, waits for them, and re-layouts  37.5 us (13%)
  other arithmetic  30.7 us (11%)
    ppermute x79, waiting for transfers between devices, xperm(): return lax.ppermute(value, AXES, [(i, i ^ mask) for i in range(count)])  91.2 us
    ppermute x79, starting transfers between devices, xperm(): return lax.ppermute(value, AXES, [(i, i ^ mask) for i in range(count)])  73 us
    unnamed x177, local copies, waits for them, and re-layouts  28.7 us
    pallas_call x1, Pallas kernels, forward_attention(): pl.pallas_call(forward_kernel, grid=(4,), in_specs=[SMEM] + [full((256, 7...  17.6 us
    pallas_call x1, Pallas kernels, backward_attention(): pl.pallas_call(backward_kernel, grid=(4,), in_specs=[SMEM] + [full((256,...  15.8 us
    pallas_call x1, Pallas kernels, feed_forward(): pl.pallas_call(feed_kernel, in_specs=[SMEM] + [pl.BlockSpec(memory_space=...  13 us
    convert_element_type x11, other arithmetic, add(): return total.astype(BF)  8.37 us
    pallas_call x1, Pallas kernels, feed_gradients(): pl.pallas_call(feed_grad_kernel, in_specs=[SMEM] + [pl.BlockSpec(memory_s...  6.89 us
  transfers between devices with their start and end apart: 79, of which 19 were waited for; matrix products, arithmetic and copies ran while one was open for 11% of the time, Pallas kernels for 9%

profile of v1, /device:TPU:9, one launch (start us, length us, event | category | flops | bytes accessed | tf_op | source)
XLA Modules:
  0.0 287.3 jit_solution(3445504170255970365)
XLA Ops:
  1.6 0.9 convert_element_type.226
  3.1 1.8 collective-permute-start.3
  8.1 1.3 collective-permute-start.6
  9.6 2.3 collective-permute-start.9
  11.9 1.4 collective-permute-start.35
  13.3 4.1 %collective-permute-done.35 = bf16[48,640]{1,0:T(8,128)(2,1)S(1)} collective-permute-done((bf16[48,640]{1,0:T(8,128)(2,1)S(1)}, bf16[48,640]{1,0:T(8,128)(2,1)S(1)}, u32[]{:S(2)}, u32[]{:S(2)}) %collective-permute-start.35) | collective-permute-done | bytes 61472 | tf_op jit(solution)/shard_map/ppermute | solution.py:389
  17.5 1.0 collective-permute-start.11
  18.5 1.2 collective-permute-done.37
  20.6 5.9 %collective-permute-done.36 = bf16[48,640]{1,0:T(8,128)(2,1)S(1)} collective-permute-done((bf16[48,640]{1,0:T(8,128)(2,1)S(1)}, bf16[48,640]{1,0:T(8,128)(2,1)S(1)}, u32[]{:S(2)}, u32[]{:S(2)}) %collective-permute-start.36) | collective-permute-done | bytes 61472 | tf_op jit(solution)/shard_map/ppermute | solution.py:389
  26.5 1.1 collective-permute-start.38
  28.3 1.2 collective-permute-start.41
  29.5 4.8 %collective-permute-start.44 = (bf16[2,48,640]{2,1,0:T(8,128)(2,1)S(1)}, bf16[2,48,640]{2,1,0:T(8,128)(2,1)S(1)}, u32[]{:S(2)}, u32[]{:S(2)}) collective-permute-start(bf16[2,48,640]{2,1,0:T(8,128)(2,1)S(1)} %pad_maximum_fusion.6.refs_25_), channel_id=1, source_target_pairs={{0,1},{1,0},{2,3},{3,2},{4,5},{5,4},{6,7},{7,6},{8,9},{9,8},{10,11... | collective-permute-start | bytes 368648 | tf_op jit(solution)/shard_map/ppermute | solution.py:389
  34.3 1.5 collective-permute-start.17
  36.7 1.3 collective-permute-start.18
  38.0 2.8 collective-permute-start.45
  41.5 1.2 collective-permute-start.8
  44.0 1.2 collective-permute-start.12
  45.9 1.8 collective-permute-done.18
  48.6 4.6 %collective-permute-start.46 = (bf16[2,48,640]{2,1,0:T(8,128)(2,1)S(1)}, bf16[2,48,640]{2,1,0:T(8,128)(2,1)S(1)}, u32[]{:S(2)}, u32[]{:S(2)}) collective-permute-start(bf16[2,48,640]{2,1,0:T(8,128)(2,1)S(1)} %collective-permute-done.38.refs_27_), channel_id=1, source_target_pairs={{0,1},{1,0},{2,3},{3,2},{4,5},{5,4},{6,7},{7,6},{8,9},{9,8},{10,11... | collective-permute-start | bytes 368648 | tf_op jit(solution)/shard_map/ppermute | solution.py:389
  66.3 1.4 collective-permute-start.23
  67.7 1.2 collective-permute-start.26
  68.9 3.1 %multiply_sine_fusion = (f32[1024,128]{1,0:T(8,128)}, f32[1024,128]{1,0:T(8,128)}) fusion(f32[128]{0:T(128)S(1)} %mul.254, f32[1024]{0:T(1024)S(1)} %get-tuple-element.183), kind=kLoop, calls=%fused_computation.24 | loop fusion | flops 131072 | bytes 1053184 | tf_op jit(solution)/shard_map/sin | solution.py:908
  72.0 2.0 collective-permute-start.2
  74.0 4.1 %collective-permute-done.21.refs_12_ = bf16[2,48,1536]{2,1,0:T(8,128)(2,1)} collective-permute-done((bf16[2,48,1536]{2,1,0:T(8,128)(2,1)S(1)}, bf16[2,48,1536]{2,1,0:T(8,128)(2,1)}, u32[]{:S(2)}, u32[]{:S(2)}) %collective-permute-start.21) | collective-permute-done | bytes 294944 | tf_op jit(solution)/shard_map/ppermute | solution.py:389
  78.2 1.3 collective-permute-start.27
  80.3 1.2 collective-permute-start.28
  81.6 1.0 copy.110
  82.7 1.0 copy.109
  83.7 2.1 fusion.14.docq
  86.3 2.2 collective-permute-done.24.refs_15_
  93.7 17.6 %forward_attention.1 = (bf16[1024,768]{1,0:T(8,128)(2,1)}, bf16[1024,256]{1,0:T(8,128)(2,1)S(1)}, bf16[1024,256]{1,0:T(8,128)(2,1)}, bf16[1024,256]{1,0:T(8,128)...) custom-call(s32[4]{0:T(128)S(1)} %pad_add_fusion.ids.refs_0_, ...), custom_call_target="tpu_custom_call" | custom-call | flops 6000000000 | bytes 16000000 | tf_op jit(solution)/shard_map/forward_attention/pallas_call | solution.py:504
  113.9 1.0 collective-permute-start.15
  115.1 3.2 %collective-permute-done.14.refs_7_.a2 = bf16[256,192]{1,0:T(8,128)(2,1)S(1)} collective-permute-done((bf16[256,192]{1,0:T(8,128)(2,1)S(1)}, bf16[256,192]{1,0:T(8,128)(2,1)S(1)}, u32[]{:S(2)}, u32[]{:S(2)}) %collective-permute-start.14) | collective-permute-done | bytes 98336 | tf_op jit(solution)/shard_map/ppermute | solution.py:389
  118.3 3.0 %collective-permute-done.15.refs_8_.a3 = bf16[256,192]{1,0:T(8,128)(2,1)S(1)} collective-permute-done((bf16[256,192]{1,0:T(8,128)(2,1)S(1)}, bf16[256,192]{1,0:T(8,128)(2,1)S(1)}, u32[]{:S(2)}, u32[]{:S(2)}) %collective-permute-start.15) | collective-permute-done | bytes 98336 | tf_op jit(solution)/shard_map/ppermute | solution.py:389
  134.9 13.0 %feed_forward.1 = (bf16[256,768]{1,0:T(8,128)(2,1)}, f32[256,768]{1,0:T(8,128)}, bf16[256,192]{1,0:T(8,128)(2,1)S(1)}, bf16[256,192]{1,0:T(8,128)(2,1)S(1)}, bf1...) custom-call(s32[4]{0:T(128)S(1)} %pad_add_fusion.ids.refs_0_, ...), custom_call_target="tpu_custom_call" | custom-call | flops 5000000000 | bytes 12000000 | tf_op jit(solution)/shard_map/feed_forward/pallas_call | solution.py:640
  148.9 1.2 collective-permute-start.54
  150.3 2.8 collective-permute-done.53.d2
  153.0 3.2 %collective-permute-done.54.d3 = bf16[256,192]{1,0:T(8,128)(2,1)S(1)} collective-permute-done((bf16[256,192]{1,0:T(8,128)(2,1)S(1)}, bf16[256,192]{1,0:T(8,128)(2,1)S(1)}, u32[]{:S(2)}, u32[]{:S(2)}) %collective-permute-start.54) | collective-permute-done | bytes 98336 | tf_op jit(solution)/shard_map/ppermute | solution.py:389
  156.2 15.8 %backward_attention.1 = (bf16[256,768]{1,0:T(8,128)(2,1)S(1)}, bf16[256,768]{1,0:T(8,128)(2,1)S(1)}, bf16[256,768]{1,0:T(8,128)(2,1)S(1)}, bf16[256,768]{1,0:T(8...) custom-call(s32[4]{0:T(128)S(1)} %pad_add_fusion.ids.refs_0_, bf16[256,768]{1,0:T(8,128)(2,1)S(1)} %copy-done.3, ...), custom_call_target="tpu_custom_call" | custom-call | flops 8000000000 | bytes 16000000 | tf_op jit(solution)/shard_map/backward_attention/pallas_call | solution.py:789
  172.8 12.4 %collective-permute-done.58 = bf16[4,96,640]{2,1,0:T(8,128)(2,1)S(1)} collective-permute-done((bf16[4,96,640]{2,1,0:T(8,128)(2,1)}, bf16[4,96,640]{2,1,0:T(8,128)(2,1)S(1)}, u32[]{:S(2)}, u32[]{:S(2)}) %collective-permute-start.58) | collective-permute-done | bytes 491552 | tf_op jit(solution)/shard_map/ppermute | solution.py:389
  185.2 1.2 add_convert_fusion.4
  186.5 3.8 %collective-permute-start.60 = (bf16[96,640]{1,0:T(8,128)(2,1)S(1)}, bf16[96,640]{1,0:T(8,128)(2,1)S(1)}, u32[]{:S(2)}, u32[]{:S(2)}) collective-permute-start(bf16[96,640]{1,0:T(8,128)(2,1)S(1)} %get-tuple-element.191), channel_id=1, source_target_pairs={{0,16},{1,17},{2,18},{3,19},{4,20},{5,21},{6,22},{7,23},{8,24},{9,... | collective-permute-start | bytes 368648 | tf_op jit(solution)/shard_map/ppermute | solution.py:389
  190.4 6.9 %feed_gradients.1 = (bf16[4,48,2176]{2,1,0:T(8,128)(2,1)S(1)}, bf16[4,48,2176]{2,1,0:T(8,128)(2,1)S(1)}, bf16[4,48,2176]{2,1,0:T(8,128)(2,1)}, bf16[4,48,2176]{2...) custom-call(s32[4]{0:T(128)S(1)} %pad_add_fusion.ids.refs_0_, ...), custom_call_target="tpu_custom_call" | custom-call | flops 3000000000 | bytes 12000000 | tf_op jit(solution)/shard_map/feed_gradients/pallas_call | solution.py:705
  197.3 1.4 collective-permute-start.69
  199.7 1.3 collective-permute-start.62
  201.9 1.4 collective-permute-start.66
  205.0 1.9 reshape.242
  206.9 1.9 copy.114
  208.8 1.8 reshape.243
  210.7 2.3 fusion.55
  214.2 1.7 multiply_add_fusion.3
  216.6 1.4 add_convert_fusion
  218.9 1.5 add_convert_fusion.2
  221.3 1.4 add_convert_fusion.1
  222.7 12.4 %collective-permute-done.70 = bf16[2,48,2176]{2,1,0:T(8,128)(2,1)S(1)} collective-permute-done((bf16[2,48,2176]{2,1,0:T(8,128)(2,1)S(1)}, bf16[2,48,2176]{2,1,0:T(8,128)(2,1)S(1)}, u32[]{:S(2)}, u32[]{:S(2)}) %collective-permute-start.70) | collective-permute-done | bytes 417824 | tf_op jit(solution)/shard_map/ppermute | solution.py:389
  235.7 8.4 %collective-permute-done.73 = bf16[2,48,2176]{2,1,0:T(8,128)(2,1)S(1)} collective-permute-done((bf16[2,48,2176]{2,1,0:T(8,128)(2,1)S(1)}, bf16[2,48,2176]{2,1,0:T(8,128)(2,1)S(1)}, u32[]{:S(2)}, u32[]{:S(2)}) %collective-permute-start.73) | collective-permute-done | bytes 417824 | tf_op jit(solution)/shard_map/ppermute | solution.py:389
  244.8 1.0 collective-permute-start.71
  246.6 1.4 add_convert_fusion.3
  248.4 3.9 %collective-permute-done.75 = bf16[2,48,2176]{2,1,0:T(8,128)(2,1)S(1)} collective-permute-done((bf16[2,48,2176]{2,1,0:T(8,128)(2,1)S(1)}, bf16[2,48,2176]{2,1,0:T(8,128)(2,1)S(1)}, u32[]{:S(2)}, u32[]{:S(2)}) %collective-permute-start.75) | collective-permute-done | bytes 417824 | tf_op jit(solution)/shard_map/ppermute | solution.py:389
  252.3 9.0 %collective-permute-done.71 = bf16[2,48,2176]{2,1,0:T(8,128)(2,1)S(1)} collective-permute-done((bf16[2,48,2176]{2,1,0:T(8,128)(2,1)S(1)}, bf16[2,48,2176]{2,1,0:T(8,128)(2,1)S(1)}, u32[]{:S(2)}, u32[]{:S(2)}) %collective-permute-start.71) | collective-permute-done | bytes 417824 | tf_op jit(solution)/shard_map/ppermute | solution.py:389
  262.3 3.5 %collective-permute-start.76 = (bf16[48,2176]{1,0:T(8,128)(2,1)S(1)}, bf16[48,2176]{1,0:T(8,128)(2,1)S(1)}, u32[]{:S(2)}, u32[]{:S(2)}) collective-permute-start(bf16[48,2176]{1,0:T(8,128)(2,1)S(1)} %get-tuple-element.192), channel_id=1, source_target_pairs={{0,16},{1,17},{2,18},{3,19},{4,20},{5,21},{6,22},{7,23},{8,24},{9,... | collective-permute-start | bytes 626696 | tf_op jit(solution)/shard_map/ppermute | solution.py:389
  266.3 12.1 %collective-permute-done.76 = bf16[48,2176]{1,0:T(8,128)(2,1)S(1)} collective-permute-done((bf16[48,2176]{1,0:T(8,128)(2,1)S(1)}, bf16[48,2176]{1,0:T(8,128)(2,1)S(1)}, u32[]{:S(2)}, u32[]{:S(2)}) %collective-permute-start.76) | collective-permute-done | bytes 208928 | tf_op jit(solution)/shard_map/ppermute | solution.py:389
  278.6 2.7 collective-permute-start.78
  281.3 1.3 fusion.7
  (372 shorter events, 64.7 us)
Async XLA Ops:
  6.4 6.9 %collective-permute-start.16 = (bf16[24,1536]{1,0:T(8,128)(2,1)S(1)}, bf16[24,1536]{1,0:T(8,128)(2,1)S(1)}, u32[]{:S(2)}, u32[]{:S(2)}) collective-permute-start(bf16[24,1536]{1,0:T(8,128)(2,1)S(1)} %broadcast_select_fusion.4), channel_id=1, source_target_pairs={{0,1},{1,0},{2,3},{3,2},{4,5},{5,4},{6,7},{7,6},{8,9},{9,8},{10,11... | collective-permute-start | bytes 221192 | tf_op jit(solution)/shard_map/ppermute | solution.py:389
  6.8 5.1 %collective-permute-start.34 = (bf16[24,640]{1,0:T(8,128)(2,1)S(1)}, bf16[24,640]{1,0:T(8,128)(2,1)S(1)}, u32[]{:S(2)}, u32[]{:S(2)}) collective-permute-start(bf16[24,640]{1,0:T(8,128)(2,1)S(1)} %broadcast_select_fusion.8), channel_id=1, source_target_pairs={{0,1},{1,0},{2,3},{3,2},{4,5},{5,4},{6,7},{7,6},{8,9},{9,8},{10,11... | collective-permute-start | bytes 92168 | tf_op jit(solution)/shard_map/ppermute | solution.py:389
  8.1 19.5 %collective-permute-start.6 = (bf16[96,640]{1,0:T(8,128)(2,1)S(1)}, bf16[96,640]{1,0:T(8,128)(2,1)S(1)}, u32[]{:S(2)}, u32[]{:S(2)}) collective-permute-start(bf16[96,640]{1,0:T(8,128)(2,1)S(1)} %pad_maximum_fusion.5.w0), channel_id=1, source_target_pairs={{0,4},{1,5},{2,6},{3,7},{4,0},{5,1},{6,2},{7,3},{8,12},{9,13},{10,... | collective-permute-start | bytes 368648 | tf_op jit(solution)/shard_map/ppermute | solution.py:389
  9.4 18.5 %collective-permute-start.7 = (bf16[96,640]{1,0:T(8,128)(2,1)S(1)}, bf16[96,640]{1,0:T(8,128)(2,1)S(1)}, u32[]{:S(2)}, u32[]{:S(2)}) collective-permute-start(bf16[96,640]{1,0:T(8,128)(2,1)S(1)} %pad_maximum_fusion.5.w0), channel_id=1, source_target_pairs={{0,8},{1,9},{2,10},{3,11},{4,12},{5,13},{6,14},{7,15},{8,0},{9,1},... | collective-permute-start | bytes 368648 | tf_op jit(solution)/shard_map/ppermute | solution.py:389
  9.6 18.7 %collective-permute-start.9 = (bf16[96,640]{1,0:T(8,128)(2,1)S(1)}, bf16[96,640]{1,0:T(8,128)(2,1)S(1)}, u32[]{:S(2)}, u32[]{:S(2)}) collective-permute-start(bf16[96,640]{1,0:T(8,128)(2,1)S(1)} %pad_maximum_fusion.5.w0), channel_id=1, source_target_pairs={{0,16},{1,17},{2,18},{3,19},{4,20},{5,21},{6,22},{7,23},{8,24},{9,... | collective-permute-start | bytes 368648 | tf_op jit(solution)/shard_map/ppermute | solution.py:389
  11.9 5.5 %collective-permute-start.35 = (bf16[48,640]{1,0:T(8,128)(2,1)S(1)}, bf16[48,640]{1,0:T(8,128)(2,1)S(1)}, u32[]{:S(2)}, u32[]{:S(2)}) collective-permute-start(bf16[48,640]{1,0:T(8,128)(2,1)S(1)} %get-tuple-element.219), channel_id=1, source_target_pairs={{0,8},{1,9},{2,10},{3,11},{4,12},{5,13},{6,14},{7,15},{8,0},{9,1},... | collective-permute-start | bytes 184328 | tf_op jit(solution)/shard_map/ppermute | solution.py:389
  13.3 6.4 %collective-permute-start.37 = (bf16[48,640]{1,0:T(8,128)(2,1)S(1)}, bf16[48,640]{1,0:T(8,128)(2,1)S(1)}, u32[]{:S(2)}, u32[]{:S(2)}) collective-permute-start(bf16[48,640]{1,0:T(8,128)(2,1)S(1)} %get-tuple-element.219), channel_id=1, source_target_pairs={{0,24},{1,25},{2,26},{3,27},{4,28},{5,29},{6,30},{7,31},{8,16},{9,... | collective-permute-start | bytes 184328 | tf_op jit(solution)/shard_map/ppermute | solution.py:389
  17.5 12.1 %collective-permute-start.11 = (bf16[96,640]{1,0:T(8,128)(2,1)S(1)}, bf16[96,640]{1,0:T(8,128)(2,1)S(1)}, u32[]{:S(2)}, u32[]{:S(2)}) collective-permute-start(bf16[96,640]{1,0:T(8,128)(2,1)S(1)} %pad_maximum_fusion.5.w0), channel_id=1, source_target_pairs={{0,24},{1,25},{2,26},{3,27},{4,28},{5,29},{6,30},{7,31},{8,16},{9,... | collective-permute-start | bytes 368648 | tf_op jit(solution)/shard_map/ppermute | solution.py:389
  19.7 6.8 %collective-permute-start.36 = (bf16[48,640]{1,0:T(8,128)(2,1)S(1)}, bf16[48,640]{1,0:T(8,128)(2,1)S(1)}, u32[]{:S(2)}, u32[]{:S(2)}) collective-permute-start(bf16[48,640]{1,0:T(8,128)(2,1)S(1)} %get-tuple-element.219), channel_id=1, source_target_pairs={{0,16},{1,17},{2,18},{3,19},{4,20},{5,21},{6,22},{7,23},{8,24},{9,... | collective-permute-start | bytes 184328 | tf_op jit(solution)/shard_map/ppermute | solution.py:389
  26.5 7.8 %collective-permute-start.38 = (bf16[2,48,640]{2,1,0:T(8,128)(2,1)S(1)}, bf16[2,48,640]{2,1,0:T(8,128)(2,1)S(1)}, u32[]{:S(2)}, u32[]{:S(2)}) collective-permute-start(bf16[2,48,640]{2,1,0:T(8,128)(2,1)S(1)} %pad_maximum_fusion.6.refs_25_), channel_id=1, source_target_pairs={{0,2},{1,3},{2,0},{3,1},{4,6},{5,7},{6,4},{7,5},{8,10},{9,11},{10,... | collective-permute-start | bytes 368648 | tf_op jit(solution)/shard_map/ppermute | solution.py:389
  27.6 9.1 %collective-permute-start.40 = (bf16[2,48,640]{2,1,0:T(8,128)(2,1)S(1)}, bf16[2,48,640]{2,1,0:T(8,128)(2,1)S(1)}, u32[]{:S(2)}, u32[]{:S(2)}) collective-permute-start(bf16[2,48,640]{2,1,0:T(8,128)(2,1)S(1)} %pad_maximum_fusion.6.refs_25_), channel_id=1, source_target_pairs={{0,4},{1,5},{2,6},{3,7},{4,0},{5,1},{6,2},{7,3},{8,12},{9,13},{10,... | collective-permute-start | bytes 368648 | tf_op jit(solution)/shard_map/ppermute | solution.py:389
  27.9 8.0 %collective-permute-start.39 = (bf16[2,48,640]{2,1,0:T(8,128)(2,1)S(1)}, bf16[2,48,640]{2,1,0:T(8,128)(2,1)S(1)}, u32[]{:S(2)}, u32[]{:S(2)}) collective-permute-start(bf16[2,48,640]{2,1,0:T(8,128)(2,1)S(1)} %pad_maximum_fusion.7.refs_26_), channel_id=1, source_target_pairs={{0,2},{1,3},{2,0},{3,1},{4,6},{5,7},{6,4},{7,5},{8,10},{9,11},{10,... | collective-permute-start | bytes 368648 | tf_op jit(solution)/shard_map/ppermute | solution.py:389
  28.3 9.7 %collective-permute-start.41 = (bf16[2,48,640]{2,1,0:T(8,128)(2,1)S(1)}, bf16[2,48,640]{2,1,0:T(8,128)(2,1)S(1)}, u32[]{:S(2)}, u32[]{:S(2)}) collective-permute-start(bf16[2,48,640]{2,1,0:T(8,128)(2,1)S(1)} %pad_maximum_fusion.7.refs_26_), channel_id=1, source_target_pairs={{0,4},{1,5},{2,6},{3,7},{4,0},{5,1},{6,2},{7,3},{8,12},{9,13},{10,... | collective-permute-start | bytes 368648 | tf_op jit(solution)/shard_map/ppermute | solution.py:389
  29.5 11.3 %collective-permute-start.44 = (bf16[2,48,640]{2,1,0:T(8,128)(2,1)S(1)}, bf16[2,48,640]{2,1,0:T(8,128)(2,1)S(1)}, u32[]{:S(2)}, u32[]{:S(2)}) collective-permute-start(bf16[2,48,640]{2,1,0:T(8,128)(2,1)S(1)} %pad_maximum_fusion.6.refs_25_), channel_id=1, source_target_pairs={{0,1},{1,0},{2,3},{3,2},{4,5},{5,4},{6,7},{7,6},{8,9},{9,8},{10,11... | collective-permute-start | bytes 368648 | tf_op jit(solution)/shard_map/ppermute | solution.py:389
  34.3 9.7 %collective-permute-start.17 = (bf16[48,1536]{1,0:T(8,128)(2,1)S(1)}, bf16[48,1536]{1,0:T(8,128)(2,1)S(1)}, u32[]{:S(2)}, u32[]{:S(2)}) collective-permute-start(bf16[48,1536]{1,0:T(8,128)(2,1)S(1)} %get-tuple-element.207), channel_id=1, source_target_pairs={{0,8},{1,9},{2,10},{3,11},{4,12},{5,13},{6,14},{7,15},{8,0},{9,1},... | collective-permute-start | bytes 442376 | tf_op jit(solution)/shard_map/ppermute | solution.py:389
  35.9 9.4 %collective-permute-start.19 = (bf16[48,1536]{1,0:T(8,128)(2,1)S(1)}, bf16[48,1536]{1,0:T(8,128)(2,1)S(1)}, u32[]{:S(2)}, u32[]{:S(2)}) collective-permute-start(bf16[48,1536]{1,0:T(8,128)(2,1)S(1)} %get-tuple-element.207), channel_id=1, source_target_pairs={{0,24},{1,25},{2,26},{3,27},{4,28},{5,29},{6,30},{7,31},{8,16},{9,... | collective-permute-start | bytes 442376 | tf_op jit(solution)/shard_map/ppermute | solution.py:389
  36.7 11.0 %collective-permute-start.18 = (bf16[48,1536]{1,0:T(8,128)(2,1)S(1)}, bf16[48,1536]{1,0:T(8,128)(2,1)S(1)}, u32[]{:S(2)}, u32[]{:S(2)}) collective-permute-start(bf16[48,1536]{1,0:T(8,128)(2,1)S(1)} %get-tuple-element.207), channel_id=1, source_target_pairs={{0,16},{1,17},{2,18},{3,19},{4,20},{5,21},{6,22},{7,23},{8,24},{9,... | collective-permute-start | bytes 442376 | tf_op jit(solution)/shard_map/ppermute | solution.py:389
  38.0 5.1 %collective-permute-start.45 = (bf16[2,48,640]{2,1,0:T(8,128)(2,1)S(1)}, bf16[2,48,640]{2,1,0:T(8,128)(2,1)S(1)}, u32[]{:S(2)}, u32[]{:S(2)}) collective-permute-start(bf16[2,48,640]{2,1,0:T(8,128)(2,1)S(1)} %pad_maximum_fusion.7.refs_26_), channel_id=1, source_target_pairs={{0,1},{1,0},{2,3},{3,2},{4,5},{5,4},{6,7},{7,6},{8,9},{9,8},{10,11... | collective-permute-start | bytes 368648 | tf_op jit(solution)/shard_map/ppermute | solution.py:389
  41.5 6.5 %collective-permute-start.8 = (bf16[96,640]{1,0:T(8,128)(2,1)S(1)}, bf16[96,640]{1,0:T(8,128)(2,1)S(1)}, u32[]{:S(2)}, u32[]{:S(2)}) collective-permute-start(bf16[96,640]{1,0:T(8,128)(2,1)S(1)} %collective-permute-done.7.w2), channel_id=1, source_target_pairs={{0,4},{1,5},{2,6},{3,7},{4,0},{5,1},{6,2},{7,3},{8,12},{9,13},{10,... | collective-permute-start | bytes 368648 | tf_op jit(solution)/shard_map/ppermute | solution.py:389
  43.8 10.1 %collective-permute-start.10 = (bf16[96,640]{1,0:T(8,128)(2,1)S(1)}, bf16[96,640]{1,0:T(8,128)(2,1)S(1)}, u32[]{:S(2)}, u32[]{:S(2)}) collective-permute-start(bf16[96,640]{1,0:T(8,128)(2,1)S(1)} %collective-permute-done.9.w4), channel_id=1, source_target_pairs={{0,4},{1,5},{2,6},{3,7},{4,0},{5,1},{6,2},{7,3},{8,12},{9,13},{10,... | collective-permute-start | bytes 368648 | tf_op jit(solution)/shard_map/ppermute | solution.py:389
  44.0 10.5 %collective-permute-start.12 = (bf16[96,640]{1,0:T(8,128)(2,1)S(1)}, bf16[96,640]{1,0:T(8,128)(2,1)S(1)}, u32[]{:S(2)}, u32[]{:S(2)}) collective-permute-start(bf16[96,640]{1,0:T(8,128)(2,1)S(1)} %collective-permute-done.11.w6), channel_id=1, source_target_pairs={{0,4},{1,5},{2,6},{3,7},{4,0},{5,1},{6,2},{7,3},{8,12},{9,13},{10,... | collective-permute-start | bytes 368648 | tf_op jit(solution)/shard_map/ppermute | solution.py:389
  45.3 10.8 %collective-permute-start.42 = (bf16[2,48,640]{2,1,0:T(8,128)(2,1)S(1)}, bf16[2,48,640]{2,1,0:T(8,128)(2,1)S(1)}, u32[]{:S(2)}, u32[]{:S(2)}) collective-permute-start(bf16[2,48,640]{2,1,0:T(8,128)(2,1)S(1)} %collective-permute-done.40.refs_29_), channel_id=1, source_target_pairs={{0,2},{1,3},{2,0},{3,1},{4,6},{5,7},{6,4},{7,5},{8,10},{9,11},{10,... | collective-permute-start | bytes 368648 | tf_op jit(solution)/shard_map/ppermute | solution.py:389
  47.8 9.7 %collective-permute-start.43 = (bf16[2,48,640]{2,1,0:T(8,128)(2,1)S(1)}, bf16[2,48,640]{2,1,0:T(8,128)(2,1)S(1)}, u32[]{:S(2)}, u32[]{:S(2)}) collective-permute-start(bf16[2,48,640]{2,1,0:T(8,128)(2,1)S(1)} %collective-permute-done.39.refs_28_), channel_id=1, source_target_pairs={{0,4},{1,5},{2,6},{3,7},{4,0},{5,1},{6,2},{7,3},{8,12},{9,13},{10,... | collective-permute-start | bytes 368648 | tf_op jit(solution)/shard_map/ppermute | solution.py:389
  48.6 9.5 %collective-permute-start.46 = (bf16[2,48,640]{2,1,0:T(8,128)(2,1)S(1)}, bf16[2,48,640]{2,1,0:T(8,128)(2,1)S(1)}, u32[]{:S(2)}, u32[]{:S(2)}) collective-permute-start(bf16[2,48,640]{2,1,0:T(8,128)(2,1)S(1)} %collective-permute-done.38.refs_27_), channel_id=1, source_target_pairs={{0,1},{1,0},{2,3},{3,2},{4,5},{5,4},{6,7},{7,6},{8,9},{9,8},{10,11... | collective-permute-start | bytes 368648 | tf_op jit(solution)/shard_map/ppermute | solution.py:389
  54.6 10.8 %collective-permute-start = (bf16[256,768]{1,0:T(8,128)(2,1)S(1)}, bf16[256,768]{1,0:T(8,128)(2,1)S(1)}, u32[]{:S(2)}, u32[]{:S(2)}) collective-permute-start(bf16[256,768]{1,0:T(8,128)(2,1)S(1)} %copy-done.2), channel_id=1, source_target_pairs={{0,1},{1,0},{2,3},{3,2},{4,5},{5,4},{6,7},{7,6},{8,9},{9,8},{10,11... | collective-permute-start | bytes 1179656 | tf_op jit(solution)/shard_map/ppermute | solution.py:389
  55.2 10.2 %collective-permute-start.1 = (bf16[256,768]{1,0:T(8,128)(2,1)S(1)}, bf16[256,768]{1,0:T(8,128)(2,1)S(1)}, u32[]{:S(2)}, u32[]{:S(2)}) collective-permute-start(bf16[256,768]{1,0:T(8,128)(2,1)S(1)} %copy-done.2), channel_id=1, source_target_pairs={{0,2},{1,3},{2,0},{3,1},{4,6},{5,7},{6,4},{7,5},{8,10},{9,11},{10,... | collective-permute-start | bytes 1179656 | tf_op jit(solution)/shard_map/ppermute | solution.py:389
  58.8 5.0 %collective-permute-start.49 = (bf16[2,48,640]{2,1,0:T(8,128)(2,1)S(1)}, bf16[2,48,640]{2,1,0:T(8,128)(2,1)S(1)}, u32[]{:S(2)}, u32[]{:S(2)}) collective-permute-start(bf16[2,48,640]{2,1,0:T(8,128)(2,1)S(1)} %collective-permute-done.41.refs_30_), channel_id=1, source_target_pairs={{0,1},{1,0},{2,3},{3,2},{4,5},{5,4},{6,7},{7,6},{8,9},{9,8},{10,11... | collective-permute-start | bytes 368648 | tf_op jit(solution)/shard_map/ppermute | solution.py:389
  61.5 10.4 %collective-permute-start.20 = (bf16[2,48,1536]{2,1,0:T(8,128)(2,1)S(1)}, bf16[2,48,1536]{2,1,0:T(8,128)(2,1)S(1)}, u32[]{:S(2)}, u32[]{:S(2)}) collective-permute-start(bf16[2,48,1536]{2,1,0:T(8,128)(2,1)S(1)} %pad_maximum_fusion.refs_9_), channel_id=1, source_target_pairs={{0,2},{1,3},{2,0},{3,1},{4,6},{5,7},{6,4},{7,5},{8,10},{9,11},{10,... | collective-permute-start | bytes 884744 | tf_op jit(solution)/shard_map/ppermute | solution.py:389
  65.4 14.1 %collective-permute-start.22 = (bf16[2,48,1536]{2,1,0:T(8,128)(2,1)S(1)}, bf16[2,48,1536]{2,1,0:T(8,128)(2,1)}, u32[]{:S(2)}, u32[]{:S(2)}) collective-permute-start(bf16[2,48,1536]{2,1,0:T(8,128)(2,1)S(1)} %pad_maximum_fusion.refs_9_), channel_id=1, source_target_pairs={{0,4},{1,5},{2,6},{3,7},{4,0},{5,1},{6,2},{7,3},{8,12},{9,13},{10,... | collective-permute-start | bytes 884744 | tf_op jit(solution)/shard_map/ppermute | solution.py:389
  65.5 12.7 %collective-permute-start.21 = (bf16[2,48,1536]{2,1,0:T(8,128)(2,1)S(1)}, bf16[2,48,1536]{2,1,0:T(8,128)(2,1)}, u32[]{:S(2)}, u32[]{:S(2)}) collective-permute-start(bf16[2,48,1536]{2,1,0:T(8,128)(2,1)S(1)} %pad_maximum_fusion.1.refs_10_), channel_id=1, source_target_pairs={{0,2},{1,3},{2,0},{3,1},{4,6},{5,7},{6,4},{7,5},{8,10},{9,11},{10,... | collective-permute-start | bytes 884744 | tf_op jit(solution)/shard_map/ppermute | solution.py:389
  66.3 14.0 %collective-permute-start.23 = (bf16[2,48,1536]{2,1,0:T(8,128)(2,1)S(1)}, bf16[2,48,1536]{2,1,0:T(8,128)(2,1)}, u32[]{:S(2)}, u32[]{:S(2)}) collective-permute-start(bf16[2,48,1536]{2,1,0:T(8,128)(2,1)S(1)} %pad_maximum_fusion.1.refs_10_), channel_id=1, source_target_pairs={{0,4},{1,5},{2,6},{3,7},{4,0},{5,1},{6,2},{7,3},{8,12},{9,13},{10,... | collective-permute-start | bytes 884744 | tf_op jit(solution)/shard_map/ppermute | solution.py:389
  67.7 12.6 %collective-permute-start.26 = (bf16[2,48,1536]{2,1,0:T(8,128)(2,1)S(1)}, bf16[2,48,1536]{2,1,0:T(8,128)(2,1)S(1)}, u32[]{:S(2)}, u32[]{:S(2)}) collective-permute-start(bf16[2,48,1536]{2,1,0:T(8,128)(2,1)S(1)} %pad_maximum_fusion.refs_9_), channel_id=1, source_target_pairs={{0,1},{1,0},{2,3},{3,2},{4,5},{5,4},{6,7},{7,6},{8,9},{9,8},{10,11... | collective-permute-start | bytes 884744 | tf_op jit(solution)/shard_map/ppermute | solution.py:389
  72.0 13.8 %collective-permute-start.2 = (bf16[256,768]{1,0:T(8,128)(2,1)S(1)}, bf16[256,768]{1,0:T(8,128)(2,1)S(1)}, u32[]{:S(2)}, u32[]{:S(2)}) collective-permute-start(bf16[256,768]{1,0:T(8,128)(2,1)S(1)} %collective-permute-done.1.t2), channel_id=1, source_target_pairs={{0,1},{1,0},{2,3},{3,2},{4,5},{5,4},{6,7},{7,6},{8,9},{9,8},{10,11... | collective-permute-start | bytes 1179656 | tf_op jit(solution)/shard_map/ppermute | solution.py:389
  78.2 7.6 %collective-permute-start.27 = (bf16[2,48,1536]{2,1,0:T(8,128)(2,1)S(1)}, bf16[2,48,1536]{2,1,0:T(8,128)(2,1)}, u32[]{:S(2)}, u32[]{:S(2)}) collective-permute-start(bf16[2,48,1536]{2,1,0:T(8,128)(2,1)S(1)} %pad_maximum_fusion.1.refs_10_), channel_id=1, source_target_pairs={{0,1},{1,0},{2,3},{3,2},{4,5},{5,4},{6,7},{7,6},{8,9},{9,8},{10,11... | collective-permute-start | bytes 884744 | tf_op jit(solution)/shard_map/ppermute | solution.py:389
  79.5 9.0 %collective-permute-start.24 = (bf16[2,48,1536]{2,1,0:T(8,128)(2,1)}, bf16[2,48,1536]{2,1,0:T(8,128)(2,1)}, u32[]{:S(2)}, u32[]{:S(2)}) collective-permute-start(bf16[2,48,1536]{2,1,0:T(8,128)(2,1)} %collective-permute-done.22.refs_13_), channel_id=1, source_target_pairs={{0,2},{1,3},{2,0},{3,1},{4,6},{5,7},{6,4},{7,5},{8,10},{9,11},{10,... | collective-permute-start | bytes 884744 | tf_op jit(solution)/shard_map/ppermute | solution.py:389
  80.3 8.9 %collective-permute-start.25 = (bf16[2,48,1536]{2,1,0:T(8,128)(2,1)}, bf16[2,48,1536]{2,1,0:T(8,128)(2,1)}, u32[]{:S(2)}, u32[]{:S(2)}) collective-permute-start(bf16[2,48,1536]{2,1,0:T(8,128)(2,1)} %collective-permute-done.21.refs_12_), channel_id=1, source_target_pairs={{0,4},{1,5},{2,6},{3,7},{4,0},{5,1},{6,2},{7,3},{8,12},{9,13},{10,... | collective-permute-start | bytes 884744 | tf_op jit(solution)/shard_map/ppermute | solution.py:389
  80.3 9.7 %collective-permute-start.28 = (bf16[2,48,1536]{2,1,0:T(8,128)(2,1)S(1)}, bf16[2,48,1536]{2,1,0:T(8,128)(2,1)}, u32[]{:S(2)}, u32[]{:S(2)}) collective-permute-start(bf16[2,48,1536]{2,1,0:T(8,128)(2,1)S(1)} %collective-permute-done.20.refs_11_), channel_id=1, source_target_pairs={{0,1},{1,0},{2,3},{3,2},{4,5},{5,4},{6,7},{7,6},{8,9},{9,8},{10,11... | collective-permute-start | bytes 884744 | tf_op jit(solution)/shard_map/ppermute | solution.py:389
  85.8 27.0 %collective-permute-start.29 = (bf16[2,48,1536]{2,1,0:T(8,128)(2,1)}, bf16[2,48,1536]{2,1,0:T(8,128)(2,1)S(1)}, u32[]{:S(2)}, u32[]{:S(2)}) collective-permute-start(bf16[2,48,1536]{2,1,0:T(8,128)(2,1)} %collective-permute-done.21.refs_12_), channel_id=1, source_target_pairs={{0,1},{1,0},{2,3},{3,2},{4,5},{5,4},{6,7},{7,6},{8,9},{9,8},{10,11... | collective-permute-start | bytes 884744 | tf_op jit(solution)/shard_map/ppermute | solution.py:389
  85.8 27.5 %collective-permute-start.30 = (bf16[2,48,1536]{2,1,0:T(8,128)(2,1)}, bf16[2,48,1536]{2,1,0:T(8,128)(2,1)S(1)}, u32[]{:S(2)}, u32[]{:S(2)}) collective-permute-start(bf16[2,48,1536]{2,1,0:T(8,128)(2,1)} %collective-permute-done.22.refs_13_), channel_id=1, source_target_pairs={{0,1},{1,0},{2,3},{3,2},{4,5},{5,4},{6,7},{7,6},{8,9},{9,8},{10,11... | collective-permute-start | bytes 884744 | tf_op jit(solution)/shard_map/ppermute | solution.py:389
  88.5 25.4 %collective-permute-start.31 = (bf16[2,48,1536]{2,1,0:T(8,128)(2,1)}, bf16[2,48,1536]{2,1,0:T(8,128)(2,1)S(1)}, u32[]{:S(2)}, u32[]{:S(2)}) collective-permute-start(bf16[2,48,1536]{2,1,0:T(8,128)(2,1)} %collective-permute-done.23.refs_14_), channel_id=1, source_target_pairs={{0,1},{1,0},{2,3},{3,2},{4,5},{5,4},{6,7},{7,6},{8,9},{9,8},{10,11... | collective-permute-start | bytes 884744 | tf_op jit(solution)/shard_map/ppermute | solution.py:389
  89.3 32.0 %collective-permute-start.32 = (bf16[2,48,1536]{2,1,0:T(8,128)(2,1)}, bf16[2,48,1536]{2,1,0:T(8,128)(2,1)}, u32[]{:S(2)}, u32[]{:S(2)}) collective-permute-start(bf16[2,48,1536]{2,1,0:T(8,128)(2,1)} %collective-permute-done.24.refs_15_), channel_id=1, source_target_pairs={{0,1},{1,0},{2,3},{3,2},{4,5},{5,4},{6,7},{7,6},{8,9},{9,8},{10,11... | collective-permute-start | bytes 884744 | tf_op jit(solution)/shard_map/ppermute | solution.py:389
  90.1 31.2 %collective-permute-start.33 = (bf16[2,48,1536]{2,1,0:T(8,128)(2,1)}, bf16[2,48,1536]{2,1,0:T(8,128)(2,1)}, u32[]{:S(2)}, u32[]{:S(2)}) collective-permute-start(bf16[2,48,1536]{2,1,0:T(8,128)(2,1)} %collective-permute-done.25.refs_16_), channel_id=1, source_target_pairs={{0,1},{1,0},{2,3},{3,2},{4,5},{5,4},{6,7},{7,6},{8,9},{9,8},{10,11... | collective-permute-start | bytes 884744 | tf_op jit(solution)/shard_map/ppermute | solution.py:389
  113.2 5.1 %collective-permute-start.14 = (bf16[256,192]{1,0:T(8,128)(2,1)S(1)}, bf16[256,192]{1,0:T(8,128)(2,1)S(1)}, u32[]{:S(2)}, u32[]{:S(2)}) collective-permute-start(bf16[256,192]{1,0:T(8,128)(2,1)S(1)} %get-tuple-element.67), channel_id=1, source_target_pairs={{0,2},{1,3},{2,0},{3,1},{4,6},{5,7},{6,4},{7,5},{8,10},{9,11},{10,... | collective-permute-start | bytes 294920 | tf_op jit(solution)/shard_map/ppermute | solution.py:389
  113.9 7.4 %collective-permute-start.15 = (bf16[256,192]{1,0:T(8,128)(2,1)S(1)}, bf16[256,192]{1,0:T(8,128)(2,1)S(1)}, u32[]{:S(2)}, u32[]{:S(2)}) collective-permute-start(bf16[256,192]{1,0:T(8,128)(2,1)S(1)} %get-tuple-element.68), channel_id=1, source_target_pairs={{0,3},{1,2},{2,1},{3,0},{4,7},{5,6},{6,5},{7,4},{8,11},{9,10},{10,... | collective-permute-start | bytes 294920 | tf_op jit(solution)/shard_map/ppermute | solution.py:389
  148.9 7.4 %collective-permute-start.54 = (bf16[256,192]{1,0:T(8,128)(2,1)S(1)}, bf16[256,192]{1,0:T(8,128)(2,1)S(1)}, u32[]{:S(2)}, u32[]{:S(2)}) collective-permute-start(bf16[256,192]{1,0:T(8,128)(2,1)S(1)} %get-tuple-element.80), channel_id=1, source_target_pairs={{0,3},{1,2},{2,1},{3,0},{4,7},{5,6},{6,5},{7,4},{8,11},{9,10},{10,... | collective-permute-start | bytes 294920 | tf_op jit(solution)/shard_map/ppermute | solution.py:389
  172.1 13.1 %collective-permute-start.58 = (bf16[4,96,640]{2,1,0:T(8,128)(2,1)}, bf16[4,96,640]{2,1,0:T(8,128)(2,1)S(1)}, u32[]{:S(2)}, u32[]{:S(2)}) collective-permute-start(bf16[4,96,640]{2,1,0:T(8,128)(2,1)} %get-tuple-element.88), channel_id=1, source_target_pairs={{0,4},{1,5},{2,6},{3,7},{4,0},{5,1},{6,2},{7,3},{8,12},{9,13},{10,... | collective-permute-start | bytes 1474568 | tf_op jit(solution)/shard_map/ppermute | solution.py:389
  172.5 28.6 %collective-permute-start.56 = (bf16[256,768]{1,0:T(8,128)(2,1)S(1)}, bf16[256,768]{1,0:T(8,128)(2,1)S(1)}, u32[]{:S(2)}, u32[]{:S(2)}) collective-permute-start(bf16[256,768]{1,0:T(8,128)(2,1)S(1)} %get-tuple-element.86), channel_id=1, source_target_pairs={{0,1},{1,0},{2,3},{3,2},{4,5},{5,4},{6,7},{7,6},{8,9},{9,8},{10,11... | collective-permute-start | bytes 1179656 | tf_op jit(solution)/shard_map/ppermute | solution.py:389
  186.4 12.3 %collective-permute-start.61 = (bf16[96,640]{1,0:T(8,128)(2,1)S(1)}, bf16[96,640]{1,0:T(8,128)(2,1)S(1)}, u32[]{:S(2)}, u32[]{:S(2)}) collective-permute-start(bf16[96,640]{1,0:T(8,128)(2,1)S(1)} %get-tuple-element.190), channel_id=1, source_target_pairs={{0,24},{1,25},{2,26},{3,27},{4,28},{5,29},{6,30},{7,31},{8,16},{9,... | collective-permute-start | bytes 368648 | tf_op jit(solution)/shard_map/ppermute | solution.py:389
  186.5 12.3 %collective-permute-start.60 = (bf16[96,640]{1,0:T(8,128)(2,1)S(1)}, bf16[96,640]{1,0:T(8,128)(2,1)S(1)}, u32[]{:S(2)}, u32[]{:S(2)}) collective-permute-start(bf16[96,640]{1,0:T(8,128)(2,1)S(1)} %get-tuple-element.191), channel_id=1, source_target_pairs={{0,16},{1,17},{2,18},{3,19},{4,20},{5,21},{6,22},{7,23},{8,24},{9,... | collective-permute-start | bytes 368648 | tf_op jit(solution)/shard_map/ppermute | solution.py:389
  190.4 8.5 %collective-permute-start.59 = (bf16[96,640]{1,0:T(8,128)(2,1)S(1)}, bf16[96,640]{1,0:T(8,128)(2,1)S(1)}, u32[]{:S(2)}, u32[]{:S(2)}) collective-permute-start(bf16[96,640]{1,0:T(8,128)(2,1)S(1)} %get-tuple-element.189), channel_id=1, source_target_pairs={{0,8},{1,9},{2,10},{3,11},{4,12},{5,13},{6,14},{7,15},{8,0},{9,1},... | collective-permute-start | bytes 368648 | tf_op jit(solution)/shard_map/ppermute | solution.py:389
  197.3 18.5 %collective-permute-start.69 = (bf16[4,48,2176]{2,1,0:T(8,128)(2,1)}, bf16[4,48,2176]{2,1,0:T(8,128)(2,1)}, u32[]{:S(2)}, u32[]{:S(2)}) collective-permute-start(bf16[4,48,2176]{2,1,0:T(8,128)(2,1)} %get-tuple-element.100), channel_id=1, source_target_pairs={{0,1},{1,0},{2,3},{3,2},{4,5},{5,4},{6,7},{7,6},{8,9},{9,8},{10,11... | collective-permute-start | bytes 2506760 | tf_op jit(solution)/shard_map/ppermute | solution.py:389
  198.7 21.7 %collective-permute-start.68 = (bf16[4,48,2176]{2,1,0:T(8,128)(2,1)}, bf16[4,48,2176]{2,1,0:T(8,128)(2,1)}, u32[]{:S(2)}, u32[]{:S(2)}) collective-permute-start(bf16[4,48,2176]{2,1,0:T(8,128)(2,1)} %get-tuple-element.98), channel_id=1, source_target_pairs={{0,1},{1,0},{2,3},{3,2},{4,5},{5,4},{6,7},{7,6},{8,9},{9,8},{10,11... | collective-permute-start | bytes 2506760 | tf_op jit(solution)/shard_map/ppermute | solution.py:389
  201.9 16.2 %collective-permute-start.66 = (bf16[4,48,2176]{2,1,0:T(8,128)(2,1)S(1)}, bf16[4,48,2176]{2,1,0:T(8,128)(2,1)}, u32[]{:S(2)}, u32[]{:S(2)}) collective-permute-start(bf16[4,48,2176]{2,1,0:T(8,128)(2,1)S(1)} %get-tuple-element.96), channel_id=1, source_target_pairs={{0,1},{1,0},{2,3},{3,2},{4,5},{5,4},{6,7},{7,6},{8,9},{9,8},{10,11... | collective-permute-start | bytes 2506760 | tf_op jit(solution)/shard_map/ppermute | solution.py:389
  203.6 42.2 %collective-permute-start.65 = (bf16[4,48,2176]{2,1,0:T(8,128)(2,1)S(1)}, bf16[4,48,2176]{2,1,0:T(8,128)(2,1)}, u32[]{:S(2)}, u32[]{:S(2)}) collective-permute-start(bf16[4,48,2176]{2,1,0:T(8,128)(2,1)S(1)} %get-tuple-element.94), channel_id=1, source_target_pairs={{0,1},{1,0},{2,3},{3,2},{4,5},{5,4},{6,7},{7,6},{8,9},{9,8},{10,11... | collective-permute-start | bytes 2506760 | tf_op jit(solution)/shard_map/ppermute | solution.py:389
  204.1 40.8 %collective-permute-start.55 = (bf16[256,768]{1,0:T(8,128)(2,1)S(1)}, bf16[256,768]{1,0:T(8,128)(2,1)S(1)}, u32[]{:S(2)}, u32[]{:S(2)}) collective-permute-start(bf16[256,768]{1,0:T(8,128)(2,1)S(1)} %get-tuple-element.84), channel_id=1, source_target_pairs={{0,1},{1,0},{2,3},{3,2},{4,5},{5,4},{6,7},{7,6},{8,9},{9,8},{10,11... | collective-permute-start | bytes 1179656 | tf_op jit(solution)/shard_map/ppermute | solution.py:389
  215.9 32.1 %collective-permute-start.57 = (bf16[256,768]{1,0:T(8,128)(2,1)S(1)}, bf16[256,768]{1,0:T(8,128)(2,1)S(1)}, u32[]{:S(2)}, u32[]{:S(2)}) collective-permute-start(bf16[256,768]{1,0:T(8,128)(2,1)S(1)} %copy-done.65), channel_id=1, source_target_pairs={{0,2},{1,3},{2,0},{3,1},{4,6},{5,7},{6,4},{7,5},{8,10},{9,11},{10,... | collective-permute-start | bytes 1179656 | tf_op jit(solution)/shard_map/ppermute | solution.py:389
  218.1 16.9 %collective-permute-start.70 = (bf16[2,48,2176]{2,1,0:T(8,128)(2,1)S(1)}, bf16[2,48,2176]{2,1,0:T(8,128)(2,1)S(1)}, u32[]{:S(2)}, u32[]{:S(2)}) collective-permute-start(bf16[2,48,2176]{2,1,0:T(8,128)(2,1)S(1)} %get-tuple-element.187), channel_id=1, source_target_pairs={{0,2},{1,3},{2,0},{3,1},{4,6},{5,7},{6,4},{7,5},{8,10},{9,11},{10,... | collective-permute-start | bytes 1253384 | tf_op jit(solution)/shard_map/ppermute | solution.py:389
  220.4 27.9 %collective-permute-start.67 = (bf16[2,48,2176]{2,1,0:T(8,128)(2,1)S(1)}, bf16[2,48,2176]{2,1,0:T(8,128)(2,1)S(1)}, u32[]{:S(2)}, u32[]{:S(2)}) collective-permute-start(bf16[2,48,2176]{2,1,0:T(8,128)(2,1)S(1)} %slice.148), channel_id=1, source_target_pairs={{0,2},{1,3},{2,0},{3,1},{4,6},{5,7},{6,4},{7,5},{8,10},{9,11},{10,... | collective-permute-start | bytes 1253384 | tf_op jit(solution)/shard_map/ppermute | solution.py:389
  235.1 9.0 %collective-permute-start.73 = (bf16[2,48,2176]{2,1,0:T(8,128)(2,1)S(1)}, bf16[2,48,2176]{2,1,0:T(8,128)(2,1)S(1)}, u32[]{:S(2)}, u32[]{:S(2)}) collective-permute-start(bf16[2,48,2176]{2,1,0:T(8,128)(2,1)S(1)} %get-tuple-element.188), channel_id=1, source_target_pairs={{0,4},{1,5},{2,6},{3,7},{4,0},{5,1},{6,2},{7,3},{8,12},{9,13},{10,... | collective-permute-start | bytes 1253384 | tf_op jit(solution)/shard_map/ppermute | solution.py:389
  244.1 8.1 %collective-permute-start.75 = (bf16[2,48,2176]{2,1,0:T(8,128)(2,1)S(1)}, bf16[2,48,2176]{2,1,0:T(8,128)(2,1)S(1)}, u32[]{:S(2)}, u32[]{:S(2)}) collective-permute-start(bf16[2,48,2176]{2,1,0:T(8,128)(2,1)S(1)} %slice.156), channel_id=1, source_target_pairs={{0,4},{1,5},{2,6},{3,7},{4,0},{5,1},{6,2},{7,3},{8,12},{9,13},{10,... | collective-permute-start | bytes 1253384 | tf_op jit(solution)/shard_map/ppermute | solution.py:389
  244.8 16.4 %collective-permute-start.71 = (bf16[2,48,2176]{2,1,0:T(8,128)(2,1)S(1)}, bf16[2,48,2176]{2,1,0:T(8,128)(2,1)S(1)}, u32[]{:S(2)}, u32[]{:S(2)}) collective-permute-start(bf16[2,48,2176]{2,1,0:T(8,128)(2,1)S(1)} %add_convert_fusion.8), channel_id=1, source_target_pairs={{0,4},{1,5},{2,6},{3,7},{4,0},{5,1},{6,2},{7,3},{8,12},{9,13},{10,... | collective-permute-start | bytes 1253384 | tf_op jit(solution)/shard_map/ppermute | solution.py:389
  245.8 15.4 %collective-permute-start.74 = (bf16[2,48,2176]{2,1,0:T(8,128)(2,1)S(1)}, bf16[2,48,2176]{2,1,0:T(8,128)(2,1)S(1)}, u32[]{:S(2)}, u32[]{:S(2)}) collective-permute-start(bf16[2,48,2176]{2,1,0:T(8,128)(2,1)S(1)} %add_convert_fusion.6), channel_id=1, source_target_pairs={{0,2},{1,3},{2,0},{3,1},{4,6},{5,7},{6,4},{7,5},{8,10},{9,11},{10,... | collective-permute-start | bytes 1253384 | tf_op jit(solution)/shard_map/ppermute | solution.py:389
  262.3 16.2 %collective-permute-start.76 = (bf16[48,2176]{1,0:T(8,128)(2,1)S(1)}, bf16[48,2176]{1,0:T(8,128)(2,1)S(1)}, u32[]{:S(2)}, u32[]{:S(2)}) collective-permute-start(bf16[48,2176]{1,0:T(8,128)(2,1)S(1)} %get-tuple-element.192), channel_id=1, source_target_pairs={{0,16},{1,17},{2,18},{3,19},{4,20},{5,21},{6,22},{7,23},{8,24},{9,... | collective-permute-start | bytes 626696 | tf_op jit(solution)/shard_map/ppermute | solution.py:389
  265.8 12.7 %collective-permute-start.72 = (bf16[48,2176]{1,0:T(8,128)(2,1)S(1)}, bf16[48,2176]{1,0:T(8,128)(2,1)S(1)}, u32[]{:S(2)}, u32[]{:S(2)}) collective-permute-start(bf16[48,2176]{1,0:T(8,128)(2,1)S(1)} %slice_bitcast_fusion.2), channel_id=1, source_target_pairs={{0,8},{1,9},{2,10},{3,11},{4,12},{5,13},{6,14},{7,15},{8,0},{9,1},... | collective-permute-start | bytes 626696 | tf_op jit(solution)/shard_map/ppermute | solution.py:389
  (103 other events, 622.0 us)

commit v2 on v1

--- a/solution.py
+++ b/solution.py
@@ -1,3 +1,5 @@
+import functools
+
 import jax
 import jax.numpy as jnp
 from jax import lax
@@ -381,7 +383,7 @@
 BF = jnp.bfloat16
 F32 = jnp.float32
 AXES = ("dp", "fsdp")
-VMEM_LIMIT = 50 * 1024 * 1024
+VMEM_LIMIT = 60 * 1024 * 1024
 
 
 def xperm(value, mask):
@@ -424,50 +426,95 @@
     return (lane >= 64 * head) & (lane < 64 * head + 64)
 
 
-def forward_kernel(
-    ids, t0, t1, t2, t3, cos, sin, docq, dock, w0, w1, w2, w3, w4, w5, w6, w7,
-    n16, q8, key, val, att, a0, a1, a2, a3, prob, gain, wide, wscr, sems,
+def prologue_kernel(
+    ids, wq, w_out, w_in, w_down, gains, own, near, far, mine_in, other_in, mine_rest, other_rest
 ):
-    step = pl.program_id(0)
-
-    @pl.when(step == 0)
-    def _():
-        copies = []
-        for k, piece in enumerate((w0, w1, w2, w3, w4, w5, w6, w7)):
-            at = pl.multiple_of(96 * (ids[1] ^ k), 96)
-            copies.append(pltpu.make_async_copy(piece, wscr.at[pl.ds(at, 96)], sems.at[k]))
-            copies[-1].start()
-        for copy in copies:
-            copy.wait()
-        weight = wscr[...]
-        wide[...] = dot_nn(weight, split_columns(640, 768)).astype(BF)
-        row = lax.broadcasted_iota(jnp.int32, (8, 640), 0)
-        col = lax.broadcasted_iota(jnp.int32, (8, 640), 1)
-        pick = ((col == row + 576) & (row < 2)).astype(F32).astype(BF)
-        gain[...] = dot_nt(pick, weight)
-        gain_row = gain[0:1, :]
-        for i, piece in enumerate((t0, t1, t2, t3)):
-            rows = slice(256 * i, 256 * i + 256)
-            x = piece[...].astype(F32)
-            center = x - jnp.mean(x, axis=-1, keepdims=True)
-            inverse = lax.rsqrt(jnp.mean(center * center, axis=-1, keepdims=True) + NORM_EPS)
-            normed = (center * inverse * gain_row).astype(BF)
-            n16[rows, :] = normed
-            mixed = dot_nn(normed, wide[...])
-            c, s = cos[rows, :], sin[rows, :]
-            qa, qb = mixed[:, :128], mixed[:, 128:256]
-            ka, kb = mixed[:, 256:384], mixed[:, 384:512]
-            q8[rows, :128] = ((qa * c - qb * s).astype(BF).astype(F32) * 0.125).astype(BF)
-            q8[rows, 128:] = ((qb * c + qa * s).astype(BF).astype(F32) * 0.125).astype(BF)
-            key[rows, :128] = (ka * c - kb * s).astype(BF)
-            key[rows, 128:] = (kb * c + ka * s).astype(BF)
-            val[rows, :] = mixed[:, 512:].astype(BF)
-
-    rows = pl.ds(pl.multiple_of(step * 256, 256), 256)
-    queries = q8[rows, :]
+    f, core = ids[0], ids[2]
+    row = lax.broadcasted_iota(jnp.int32, (24, 24), 0)
+    col = lax.broadcasted_iota(jnp.int32, (24, 24), 1)
+    parts = []
+    for j in range(2):
+        spread = jnp.where(row == col, gains[j : j + 1, :], 0.0)
+        parts.append(jnp.sum(spread, axis=-1, keepdims=True))
+    lane = lax.broadcasted_iota(jnp.int32, (24, 64), 1)
+    columns = jnp.where(lane == 0, parts[0], jnp.where(lane == 1, parts[1], 0.0))
+    blocks = []
+    for j in range(4):
+        pieces = [wq[:, 768 * part + 192 * j : 768 * part + 192 * j + 192] for part in range(3)]
+        blocks.append(jnp.concatenate(pieces + [columns], axis=1))
+    for k, out in enumerate((own, near, far.at[0], far.at[1])):
+        place = f ^ k
+        low = jnp.where(place == 0, blocks[0], blocks[1])
+        high = jnp.where(place == 2, blocks[2], blocks[3])
+        out[...] = jnp.where(place < 2, low, high).astype(BF)
+    left, right = w_in[:, :1152], w_in[:, 1152:]
+    mine_in[...] = jnp.where(core == 0, left, right).astype(BF)
+    other_in[...] = jnp.where(core == 0, right, left).astype(BF)
+    left = jnp.concatenate([w_out[:, :384], w_down[:, :640]], axis=1)
+    right = jnp.concatenate([w_out[:, 384:], w_down[:, 640:], jnp.zeros((24, 128), F32)], axis=1)
+    mine_rest[...] = jnp.where(core == 0, left, right).astype(BF)
+    other_rest[...] = jnp.where(core == 0, right, left).astype(BF)
+
+
+def assemble_kernel(ids, q0, q1, q2, q3, mine_rest, came_rest, mine_in, came_in, rows, rest, into):
+    f, core = ids[0], ids[2]
+    pieces = [q[...].astype(F32) for q in (q0, q1, q2, q3)]
+    ordered = []
+    for place in range(4):
+        k = f ^ place
+        low = jnp.where(k == 0, pieces[0], pieces[1])
+        high = jnp.where(k == 2, pieces[2], pieces[3])
+        ordered.append(jnp.where(k < 2, low, high))
+    rows[...] = jnp.concatenate(ordered, axis=0).astype(BF)
+    for mine, came, out in ((mine_rest, came_rest, rest), (mine_in, came_in, into)):
+        one, two = mine[...].astype(F32), came[...].astype(F32)
+        out[...] = jnp.concatenate(
+            [jnp.where(core == 0, one, two), jnp.where(core == 0, two, one)], axis=0
+        ).astype(BF)
+
+
+def project_kernel(
+    ids, t0, t1, t2, t3, cos, sin, w0, w1, w2, w3,
+    n16, q8, key, val, gain, wide, wscr, sems,
+):
+    copies = []
+    pieces = (w0, w1, w2.at[0], w3.at[0], w2.at[1], w3.at[1], w2.at[2], w3.at[2])
+    for k, piece in enumerate(pieces):
+        at = pl.multiple_of(96 * (ids[1] ^ k), 96)
+        copies.append(pltpu.make_async_copy(piece, wscr.at[pl.ds(at, 96)], sems.at[k]))
+        copies[-1].start()
+    for copy in copies:
+        copy.wait()
+    weight = wscr[...]
+    wide[...] = dot_nn(weight, split_columns(640, 768)).astype(BF)
+    row = lax.broadcasted_iota(jnp.int32, (8, 640), 0)
+    col = lax.broadcasted_iota(jnp.int32, (8, 640), 1)
+    pick = ((col == row + 576) & (row < 2)).astype(F32).astype(BF)
+    gain[...] = dot_nt(pick, weight)
+    gain_row = gain[0:1, :]
+    for i, piece in enumerate((t0, t1, t2, t3)):
+        rows = slice(256 * i, 256 * i + 256)
+        x = piece[...].astype(F32)
+        center = x - jnp.mean(x, axis=-1, keepdims=True)
+        inverse = lax.rsqrt(jnp.mean(center * center, axis=-1, keepdims=True) + NORM_EPS)
+        normed = (center * inverse * gain_row).astype(BF)
+        n16[rows, :] = normed
+        mixed = dot_nn(normed, wide[...])
+        c, s = cos[rows, :], sin[rows, :]
+        qa, qb = mixed[:, :128], mixed[:, 128:256]
+        ka, kb = mixed[:, 256:384], mixed[:, 384:512]
+        q8[rows, :128] = ((qa * c - qb * s).astype(BF).astype(F32) * 0.125).astype(BF)
+        q8[rows, 128:] = ((qb * c + qa * s).astype(BF).astype(F32) * 0.125).astype(BF)
+        key[rows, :128] = (ka * c - kb * s).astype(BF)
+        key[rows, 128:] = (kb * c + ka * s).astype(BF)
+        val[rows, :] = mixed[:, 512:].astype(BF)
+
+
+def attend_kernel(q8, key, val, docq, dock, att, low, prob):
+    queries = q8[...]
     keys = key[...]
     values = val[...]
-    same = docq[rows, :] == dock[...]
+    same = docq[...] == dock[...]
     total = jnp.zeros((256, 256), F32)
     zero = jnp.zeros((), BF)
     for h in range(3):
@@ -480,68 +527,91 @@
         prob[h] = weights16
         total += dot_nn(weights16, jnp.where(value_lanes(256, h), values, zero))
     att[...] = total[:, :192]
-    low = total[:, :192].astype(BF)
-    for i, out in enumerate((a0, a1, a2, a3)):
-
-        @pl.when(step == i)
-        def _():
-            out[...] = low
+    low[0] = total[:, :192].astype(BF)
 
 
 def full(shape):
     return pl.BlockSpec(shape, lambda *_: (0,) * len(shape))
 
 
+VM = pl.BlockSpec(memory_space=pltpu.VMEM)
 SMEM = pl.BlockSpec(memory_space=pltpu.SMEM)
-ANY = pl.BlockSpec(memory_space=pl.ANY)
+ANY = pl.BlockSpec(memory_space=pltpu.HBM)
 
 
 def shaped(shape, dtype):
     return jax.ShapeDtypeStruct(shape, dtype)
 
 
-def forward_attention(ids, token_pieces, cos, sin, docs, w_pieces):
+def prologue(ids, weight_qkv, weight_out, weight_in, weight_down, norm_gains):
     return pl.pallas_call(
-        forward_kernel,
-        grid=(4,),
-        in_specs=[SMEM]
-        + [full((256, 768))] * 4
-        + [full((1024, 128))] * 2
-        + [full((1024, 1)), full((1, 1024))]
-        + [ANY] * 8,
-        out_specs=[
-            full((1024, 768)),
-            full((1024, 256)),
-            full((1024, 256)),
-            full((1024, 256)),
-            pl.BlockSpec((256, 192), lambda i: (i, 0)),
-            full((256, 192)),
-            full((256, 192)),
-            full((256, 192)),
-            full((256, 192)),
-            pl.BlockSpec((3, 256, 1024), lambda i: (0, i, 0)),
-            full((8, 768)),
-            full((768, 768)),
-        ],
+        prologue_kernel,
+        in_specs=[SMEM] + [VM] * 5,
+        out_specs=[VM] * 7,
+        out_shape=[shaped((24, 640), BF)] * 2 + [shaped((2, 24, 640), BF)] + [shaped((24, 1152), BF)] * 2 + [shaped((24, 1024), BF)] * 2,
+        compiler_params=pltpu.CompilerParams(vmem_limit_bytes=VMEM_LIMIT),
+        cost_estimate=pl.CostEstimate(flops=10**6, bytes_accessed=10**6, transcendentals=0),
+        name="prologue",
+    )(ids, weight_qkv, weight_out, weight_in, weight_down, norm_gains)
+
+
+def assemble(ids, *pieces):
+    return pl.pallas_call(
+        assemble_kernel,
+        in_specs=[SMEM] + [VM] * 8,
+        out_specs=[VM] * 3,
+        out_shape=[shaped((96, 640), BF), shaped((48, 1024), BF), shaped((48, 1152), BF)],
+        compiler_params=pltpu.CompilerParams(vmem_limit_bytes=VMEM_LIMIT),
+        cost_estimate=pl.CostEstimate(flops=10**6, bytes_accessed=10**6, transcendentals=0),
+        name="assemble",
+    )(ids, *pieces)
+
+
+def project(ids, token_pieces, cos, sin, w_pieces):
+    return pl.pallas_call(
+        project_kernel,
+        in_specs=[SMEM] + [VM] * 6 + [ANY] * 4,
+        out_specs=[VM] * 6,
         out_shape=[
             shaped((1024, 768), BF),
             shaped((1024, 256), BF),
             shaped((1024, 256), BF),
             shaped((1024, 256), BF),
-            shaped((1024, 192), F32),
-            shaped((256, 192), BF),
-            shaped((256, 192), BF),
-            shaped((256, 192), BF),
-            shaped((256, 192), BF),
-            shaped((3, 1024, 1024), BF),
             shaped((8, 768), F32),
             shaped((768, 768), BF),
         ],
         scratch_shapes=[pltpu.VMEM((768, 640), BF), pltpu.SemaphoreType.DMA((8,))],
         compiler_params=pltpu.CompilerParams(vmem_limit_bytes=VMEM_LIMIT),
-        cost_estimate=pl.CostEstimate(flops=6 * 10**9, bytes_accessed=16 * 10**6, transcendentals=3 * 10**6),
-        name="forward_attention",
-    )(ids, *token_pieces, cos, sin, docs[:, None], docs[None, :], *w_pieces)
+        cost_estimate=pl.CostEstimate(flops=3 * 10**9, bytes_accessed=8 * 10**6, transcendentals=0),
+        name="project",
+    )(ids, *token_pieces, cos, sin, *w_pieces)
+
+
+def attend(base, q8, key, val, docs):
+    return pl.pallas_call(
+        attend_kernel,
+        grid=(2,),
+        in_specs=[
+            pl.BlockSpec((256, 256), lambda i: (base + i, 0)),
+            full((1024, 256)),
+            full((1024, 256)),
+            pl.BlockSpec((256, 1), lambda i: (base + i, 0)),
+            full((1, 1024)),
+        ],
+        out_specs=[
+            pl.BlockSpec((256, 192), lambda i: (i, 0)),
+            pl.BlockSpec((1, 256, 192), lambda i: (i, 0, 0)),
+            pl.BlockSpec((3, 256, 1024), lambda i: (0, i, 0)),
+        ],
+        out_shape=[
+            shaped((512, 192), F32),
+            shaped((2, 256, 192), BF),
+            shaped((3, 512, 1024), BF),
+        ],
+        compiler_params=pltpu.CompilerParams(vmem_limit_bytes=VMEM_LIMIT),
+        cost_estimate=pl.CostEstimate(flops=3 * 10**9, bytes_accessed=8 * 10**6, transcendentals=2 * 10**6),
+        name="attend",
+    )(q8, key, val, docs[:, None], docs[None, :])
 
 
 def erf_pair(x):
@@ -550,48 +620,46 @@
     return cdf, density
 
 
-SLOTS = 16
+SLOTS = 10
+PLACES = [(0, kz, kz * 4) for kz in range(4)]
+PLACES += [(1, kz, kz * 4 + 1) for kz in range(4)]
+PLACES += [(2, kz, kz * 4 + 2) for kz in range(4)]
+PLACES += [(3, kz, kz * 4 + 3) for kz in range(2)]
+PLACES += [(4, kz - 2, kz * 4 + 3) for kz in range(2, 4)]
+
+
+def load_halves(held, target, core, chip, sems):
+    copies = []
+    for owner in range(2):
+        half = core if owner == 0 else 1 - core
+        for which, slot, mask in PLACES:
+            at = pl.multiple_of(48 * (chip ^ mask), 48)
+            copies.append(
+                pltpu.make_async_copy(
+                    held[owner * 5 + which].at[slot], target.at[half, pl.ds(at, 48)], sems.at[len(copies)]
+                )
+            )
+            copies[-1].start()
+    return copies
 
 
 def feed_kernel(*refs):
     ids, tok, cot, live, gain, a0, a1, a2, a3 = refs[:9]
-    first = refs[9 : 9 + SLOTS]
-    last = refs[9 + SLOTS : 9 + 2 * SLOTS]
-    (block, dmid, d0, d1, d2, d3, act16, n2low, dgate, dbr, ggain, w_in, w_out, w_down, sems) = refs[
-        9 + 2 * SLOTS :
-    ]
+    held_rest, held_in = refs[9 : 9 + SLOTS], refs[9 + SLOTS : 9 + 2 * SLOTS]
+    (block, dmid, d_near, d_far, act16, n2low, dgate, dbr, ggain, w_rest, w_in, sems) = refs[9 + 2 * SLOTS :]
     f, core, chip = ids[0], ids[2], ids[3]
-    copies = []
-
-    def load(source, target):
-        copies.append(pltpu.make_async_copy(source, target, sems.at[len(copies)]))
-        copies[-1].start()
-
-    places = []
-    for owner in range(2):
-        half = core if owner == 0 else 1 - core
-        for group in range(8):
-            for j in range(2):
-                kx, ky, kz = (group >> 1) & 1, (group >> 2) & 1, (group & 1) * 2 + j
-                mask = kz * 4 + ky * 2 + kx
-                at = pl.multiple_of(48 * (chip ^ mask), 48)
-                places.append((owner * 8 + group, j, half, pl.ds(at, 48)))
-    for which, j, half, rows in places:
-        load(first[which].at[j, :, pl.ds(1152, 384)], w_out.at[half, rows])
-    for which, j, half, rows in places:
-        load(first[which].at[j, :, pl.ds(0, 1152)], w_in.at[half, rows])
-    for which, j, half, rows in places:
-        load(last[which].at[j], w_down.at[half, rows])
-    for copy in copies[:32]:
-        copy.wait()
+    rest_copies = load_halves(held_rest, w_rest, core, chip, sems.at[0])
+    in_copies = load_halves(held_in, w_in, core, chip, sems.at[1])
     tok_f = tok[...].astype(F32)
     pieces = [a[...] for a in (a0, a1, a2, a3)]
     heads = [pl.ds(pl.multiple_of(192 * (f ^ k), 192), 192) for k in range(4)]
+    for copy in rest_copies:
+        copy.wait()
     left = jnp.zeros((256, 384), F32)
     right = jnp.zeros((256, 384), F32)
     for k in range(4):
-        left += dot_nn(pieces[k], w_out[0, heads[k], :])
-        right += dot_nn(pieces[k], w_out[1, heads[k], :])
+        left += dot_nn(pieces[k], w_rest[0, heads[k], :384])
+        right += dot_nn(pieces[k], w_rest[1, heads[k], :384])
     middle = tok_f + jnp.concatenate([left, right], axis=1)
     center = middle - jnp.mean(middle, axis=-1, keepdims=True)
     inverse = lax.rsqrt(jnp.mean(center * center, axis=-1, keepdims=True) + NORM_EPS)
@@ -599,7 +667,7 @@
     gain_row = gain[1:2, :]
     low = (normed * gain_row).astype(BF)
     n2low[...] = low
-    for copy in copies[32:64]:
+    for copy in in_copies:
         copy.wait()
     act = dot_nn(low, w_in[0])
     gate = dot_nn(low, w_in[1])
@@ -607,12 +675,10 @@
     gelu = act * cdf
     active = (gelu * gate).astype(BF)
     act16[...] = active
-    for copy in copies[64:]:
-        copy.wait()
     alive = live[...]
     dout = jnp.where(alive > 0.5, cot[...].astype(F32), 0.0)
     dym = dout.astype(BF)
-    dact = jnp.concatenate([dot_nn(dym, w_down[0]), dot_nn(dym, w_down[1, :, :512])], axis=1)
+    dact = jnp.concatenate([dot_nn(dym, w_rest[0, :, 384:1024]), dot_nn(dym, w_rest[1, :, 384:896])], axis=1)
     dg_front = (dact * gate * (cdf + act * density)).astype(BF)
     dg_rear = (dact * gelu).astype(BF)
     dgate[:, :1152] = dg_front
@@ -628,26 +694,24 @@
     dmid[...] = dmiddle
     dbranch = dmiddle.astype(BF)
     dbr[...] = dbranch
-    for k, out in enumerate((d0, d1, d2, d3)):
-        out[...] = (
-            dot_nt(dbranch[:, :384], w_out[0, heads[k], :]) + dot_nt(dbranch[:, 384:], w_out[1, heads[k], :])
+    for k in range(4):
+        (d_near, d_far)[k // 2][k % 2] = (
+            dot_nt(dbranch[:, :384], w_rest[0, heads[k], :384]) + dot_nt(dbranch[:, 384:], w_rest[1, heads[k], :384])
         ).astype(BF)
-    branch = dot_nt(active[:, :640], w_down[0]) + dot_nt(active[:, 640:], w_down[1, :, :512])
+    branch = dot_nt(active[:, :640], w_rest[0, :, 384:1024]) + dot_nt(active[:, 640:], w_rest[1, :, 384:896])
     block[...] = jnp.where(alive > 0.5, middle + branch, 0.0).astype(BF)
 
 
-def feed_forward(ids, tokens, cotangent, live, gain, att_pieces, first, last):
+def feed_forward(ids, tokens, cotangent, live, gain, att_pieces, held_rest, held_in):
     return pl.pallas_call(
         feed_kernel,
-        in_specs=[SMEM] + [pl.BlockSpec(memory_space=pltpu.VMEM)] * 8 + [ANY] * (2 * SLOTS),
-        out_specs=[pl.BlockSpec(memory_space=pltpu.VMEM)] * 11,
+        in_specs=[SMEM] + [VM] * 8 + [ANY] * (2 * SLOTS),
+        out_specs=[VM] * 9,
         out_shape=[
             shaped((256, 768), BF),
             shaped((256, 768), F32),
-            shaped((256, 192), BF),
-            shaped((256, 192), BF),
-            shaped((256, 192), BF),
-            shaped((256, 192), BF),
+            shaped((2, 256, 192), BF),
+            shaped((2, 256, 192), BF),
             shaped((256, 1152), BF),
             shaped((256, 768), BF),
             shaped((256, 2304), BF),
@@ -655,86 +719,87 @@
             shaped((8, 768), F32),
         ],
         scratch_shapes=[
+            pltpu.VMEM((2, 768, 1024), BF),
             pltpu.VMEM((2, 768, 1152), BF),
-            pltpu.VMEM((2, 768, 384), BF),
-            pltpu.VMEM((2, 768, 640), BF),
-            pltpu.SemaphoreType.DMA((96,)),
+            pltpu.SemaphoreType.DMA((2, 32)),
         ],
         compiler_params=pltpu.CompilerParams(vmem_limit_bytes=VMEM_LIMIT),
         cost_estimate=pl.CostEstimate(flops=5 * 10**9, bytes_accessed=12 * 10**6, transcendentals=10**6),
         name="feed_forward",
-    )(ids, tokens, cotangent, live, gain, *att_pieces, *first, *last)
-
-
-CHUNK = 2176
-
-
-def feed_grad_kernel(
-    ids, cot, live, act16, n2low, dgate, dbr, a0, a1, a2, a3,
-    s0, s1, s2, s3, k0, k1, k2, k3, grads, sems,
+    )(ids, tokens, cotangent, live, gain, *att_pieces, *held_rest, *held_in)
+
+
+def store_chunks(grads, far_sent, sent, far_kept, kept, core, chip, sems):
+    copies = []
+    for group in (3, 0, 1, 2):
+        for kz in range(4):
+            at = pl.multiple_of(48 * (chip ^ (kz * 4 + group)), 48)
+            for half, far, near in ((1 - core, far_sent, sent), (core, far_kept, kept)):
+                target = far.at[kz] if group == 3 else near.at[group * 4 + kz]
+                copies.append(pltpu.make_async_copy(grads.at[half, pl.ds(at, 48)], target, sems.at[len(copies)]))
+                copies[-1].start()
+    for copy in copies:
+        copy.wait()
+
+
+def grad_in_kernel(ids, n2low, dgate, far_sent, sent, far_kept, kept, grads, sems):
+    low = n2low[...]
+    grads[0] = dot_tn(low, dgate[:, :1152]).astype(BF)
+    grads[1] = dot_tn(low, dgate[:, 1152:]).astype(BF)
+    store_chunks(grads, far_sent, sent, far_kept, kept, ids[2], ids[3], sems)
+
+
+def grad_rest_kernel(
+    ids, cot, live, act16, dbr, a0, a1, a2, a3, far_sent, sent, far_kept, kept, grads, sems
 ):
-    f, core, chip = ids[0], ids[2], ids[3]
+    f = ids[0]
     dym = jnp.where(live[...] > 0.5, cot[...].astype(F32), 0.0).astype(BF)
     gdown = dot_tn(dym, act16[...])
-    grads[0, :, 1536:2176] = gdown[:, :640].astype(BF)
-    grads[1, :, 1536:2048] = gdown[:, 640:].astype(BF)
-    grads[1, :, 2048:2176] = jnp.zeros((768, 128), BF)
-    low = n2low[...]
-    grads[0, :, :1152] = dot_tn(low, dgate[:, :1152]).astype(BF)
-    grads[1, :, :1152] = dot_tn(low, dgate[:, 1152:]).astype(BF)
+    grads[0, :, 384:1024] = gdown[:, :640].astype(BF)
+    grads[1, :, 384:896] = gdown[:, 640:].astype(BF)
+    grads[1, :, 896:1024] = jnp.zeros((768, 128), BF)
     branch = dbr[...]
     for k, piece in enumerate((a0, a1, a2, a3)):
         rows = pl.ds(pl.multiple_of(192 * (f ^ k), 192), 192)
         gout = dot_tn(piece[...], branch).astype(BF)
-        grads[0, rows, 1152:1536] = gout[:, :384]
-        grads[1, rows, 1152:1536] = gout[:, 384:]
-    copies = []
-    for group in (3, 1, 2, 0):
-        for kz in range(4):
-            at = pl.multiple_of(48 * (chip ^ (kz * 4 + group)), 48)
-            for half, target in ((1 - core, (s0, s1, s2, s3)[group]), (core, (k0, k1, k2, k3)[group])):
-                copies.append(
-                    pltpu.make_async_copy(grads.at[half, pl.ds(at, 48)], target.at[kz], sems.at[len(copies)])
-                )
-                copies[-1].start()
-    for copy in copies:
-        copy.wait()
-
-
-def feed_gradients(ids, cotangent, live, act16, n2low, dgate, dbr, att_pieces):
+        grads[0, rows, :384] = gout[:, :384]
+        grads[1, rows, :384] = gout[:, 384:]
+    store_chunks(grads, far_sent, sent, far_kept, kept, ids[2], ids[3], sems)
+
+
+def chunk_call(kernel, name, width, ids, *operands):
     return pl.pallas_call(
-        feed_grad_kernel,
-        in_specs=[SMEM] + [pl.BlockSpec(memory_space=pltpu.VMEM)] * 10,
-        out_specs=[ANY] * 8,
-        out_shape=[shaped((4, 48, CHUNK), BF)] * 8,
-        scratch_shapes=[pltpu.VMEM((2, 768, CHUNK), BF), pltpu.SemaphoreType.DMA((32,))],
+        kernel,
+        in_specs=[SMEM] + [VM] * len(operands),
+        out_specs=[ANY] * 4,
+        out_shape=[shaped((4, 48, width), BF), shaped((12, 48, width), BF)] * 2,
+        scratch_shapes=[pltpu.VMEM((2, 768, width), BF), pltpu.SemaphoreType.DMA((32,))],
         compiler_params=pltpu.CompilerParams(vmem_limit_bytes=VMEM_LIMIT),
-        cost_estimate=pl.CostEstimate(flops=3 * 10**9, bytes_accessed=12 * 10**6, transcendentals=0),
-        name="feed_gradients",
-    )(ids, cotangent, live, act16, n2low, dgate, dbr, *att_pieces)
-
-
-def backward_kernel(
-    ids, t0, t1, t2, t3, cos, sin, n16, q8, key, val, att, prob, d0, d1, d2, d3, gain, wide, ggain,
-    dn0, dn1, dn2, dn3, far, near, dq, dkt, dvt, grads, sems,
-):
+        cost_estimate=pl.CostEstimate(flops=15 * 10**8, bytes_accessed=8 * 10**6, transcendentals=0),
+        name=name,
+    )(ids, *operands)
+
+
+def backward_kernel(*refs, resumed):
+    cos, sin, q8, key, val, att, prob, first, second = refs[:9]
+    refs = refs[9:]
+    if resumed:
+        dkt_in, dvt_in, refs = refs[0], refs[1], refs[2:]
+    dq, dkt, dvt = refs
     step = pl.program_id(0)
 
     @pl.when(step == 0)
     def _():
-        dkt[...] = jnp.zeros((256, 1024), F32)
-        dvt[...] = jnp.zeros((256, 1024), F32)
-
-    rows = pl.ds(pl.multiple_of(step * 256, 256), 256)
+        dkt[...] = dkt_in[...] if resumed else jnp.zeros((256, 1024), F32)
+        dvt[...] = dvt_in[...] if resumed else jnp.zeros((256, 1024), F32)
+
     zero = jnp.zeros((), BF)
     keys = key[...]
     values = val[...]
-    dattn = d0[...]
-    for i, piece in ((1, d1), (2, d2), (3, d3)):
-        dattn = jnp.where(step == i, piece[...], dattn)
+    dattn = jnp.where(step == 0, first[...], second[...])
     dattn = jnp.concatenate([dattn, jnp.zeros((256, 64), BF)], axis=1)
     product = dattn[:, :192].astype(F32) * att[...]
-    queries_t = q8[rows, :].T
+    queries_t = q8[...].T
     dattn_t = dattn.T
     total = jnp.zeros((256, 256), F32)
     for h in range(3):
@@ -748,69 +813,85 @@
         dkt[32 * h : 32 * h + 32, :] += dk_head[:32]
         dkt[128 + 32 * h : 160 + 32 * h, :] += dk_head[32:]
         dvt[64 * h : 64 * h + 64, :] += dot_nn(dattn_t[64 * h : 64 * h + 64], weights)
-    c, s = cos[rows, :], sin[rows, :]
+    c, s = cos[...], sin[...]
     dqa, dqb = total[:, :128] * 0.125, total[:, 128:] * 0.125
-    dq[rows, :128] = (dqa * c + dqb * s).astype(BF)
-    dq[rows, 128:256] = (dqb * c - dqa * s).astype(BF)
-
-    @pl.when(step == 3)
-    def _():
-        dk = dkt[...].T
-        ca, sa = cos[...], sin[...]
-        dq[:, 256:384] = (dk[:, :128] * ca + dk[:, 128:] * sa).astype(BF)
-        dq[:, 384:512] = (dk[:, 128:] * ca - dk[:, :128] * sa).astype(BF)
-        dq[:, 512:768] = dvt[...].T.astype(BF)
-        ggain1 = jnp.zeros((1, 768), F32)
-        for i, (piece, out) in enumerate(((t0, dn0), (t1, dn1), (t2, dn2), (t3, dn3))):
-            part = dot_nt(dq[256 * i : 256 * i + 256, :], wide[...])
-            x = piece[...].astype(F32)
-            center = x - jnp.mean(x, axis=-1, keepdims=True)
-            inverse = lax.rsqrt(jnp.mean(center * center, axis=-1, keepdims=True) + NORM_EPS)
-            ggain1 += jnp.sum(part * (center * inverse), axis=0, keepdims=True)
-            out[...] = part.astype(BF)
-        wide_grad = dot_tn(n16[...], dq[...]).astype(BF)
-        natural = dot_nt(wide_grad, split_columns(640, 768))
-        gains = jnp.concatenate([ggain1, ggain[0:1, :], jnp.zeros((126, 768), F32)], axis=0)
-        column = jnp.concatenate([natural[:, :512], natural[:, 512:576], gains.T[:, :64]], axis=1)
-        grads[...] = column.astype(BF)
-        copies = []
-        for ky, target in ((1, far), (0, near)):
-            for kz in range(4):
-                at = pl.multiple_of(96 * (ids[1] ^ (kz * 2 + ky)), 96)
-                copies.append(
-                    pltpu.make_async_copy(grads.at[pl.ds(at, 96)], target.at[kz], sems.at[len(copies)])
-                )
-                copies[-1].start()
-        for copy in copies:
-            copy.wait()
-
-
-def backward_attention(ids, token_pieces, cos, sin, n16, q8, key, val, att, prob, d_pieces, gain, wide, ggain):
+    dq[:, :128] = (dqa * c + dqb * s).astype(BF)
+    dq[:, 128:] = (dqb * c - dqa * s).astype(BF)
+
+
+def backward(base, cos, sin, q8, key, val, att, prob, d_pieces, sums=()):
     return pl.pallas_call(
-        backward_kernel,
-        grid=(4,),
-        in_specs=[SMEM]
-        + [full((256, 768))] * 4
-        + [full((1024, 128))] * 2
-        + [full((1024, 768))]
-        + [full((1024, 256))] * 3
-        + [pl.BlockSpec((256, 192), lambda i: (i, 0))]
-        + [pl.BlockSpec((3, 256, 1024), lambda i: (0, i, 0))]
-        + [full((256, 192))] * 4
-        + [full((8, 768)), full((768, 768)), full((8, 768))],
-        out_specs=[full((256, 768))] * 4 + [ANY, ANY],
+        functools.partial(backward_kernel, resumed=bool(sums)),
+        grid=(2,),
+        in_specs=[
+            pl.BlockSpec((256, 128), lambda i: (base + i, 0)),
+            pl.BlockSpec((256, 128), lambda i: (base + i, 0)),
+            pl.BlockSpec((256, 256), lambda i: (base + i, 0)),
+            full((1024, 256)),
+            full((1024, 256)),
+            pl.BlockSpec((256, 192), lambda i: (i, 0)),
+            pl.BlockSpec((3, 256, 1024), lambda i: (0, i, 0)),
+            full((256, 192)),
+            full((256, 192)),
+        ]
+        + [full((256, 1024))] * len(sums),
+        out_specs=[pl.BlockSpec((256, 256), lambda i: (i, 0)), full((256, 1024)), full((256, 1024))],
+        out_shape=[shaped((512, 256), BF), shaped((256, 1024), F32), shaped((256, 1024), F32)],
+        compiler_params=pltpu.CompilerParams(vmem_limit_bytes=VMEM_LIMIT),
+        cost_estimate=pl.CostEstimate(flops=3 * 10**9, bytes_accessed=8 * 10**6, transcendentals=0),
+        name="backward",
+    )(cos, sin, q8, key, val, att, prob, *d_pieces, *sums)
+
+
+def finish_kernel(
+    ids, t0, t1, t2, t3, cos, sin, n16, dq_low, dq_high, dkt, dvt, wide, ggain,
+    dn0, dn1, dn2, dn3, far, near, dmixed, grads, sems,
+):
+    dk = dkt[...].T
+    c, s = cos[...], sin[...]
+    dmixed[:512, :256] = dq_low[...]
+    dmixed[512:, :256] = dq_high[...]
+    dmixed[:, 256:384] = (dk[:, :128] * c + dk[:, 128:] * s).astype(BF)
+    dmixed[:, 384:512] = (dk[:, 128:] * c - dk[:, :128] * s).astype(BF)
+    dmixed[:, 512:768] = dvt[...].T.astype(BF)
+    ggain1 = jnp.zeros((1, 768), F32)
+    for i, (piece, out) in enumerate(((t0, dn0), (t1, dn1), (t2, dn2), (t3, dn3))):
+        part = dot_nt(dmixed[256 * i : 256 * i + 256, :], wide[...])
+        x = piece[...].astype(F32)
+        center = x - jnp.mean(x, axis=-1, keepdims=True)
+        inverse = lax.rsqrt(jnp.mean(center * center, axis=-1, keepdims=True) + NORM_EPS)
+        ggain1 += jnp.sum(part * (center * inverse), axis=0, keepdims=True)
+        out[...] = part.astype(BF)
+    wide_grad = dot_tn(n16[...], dmixed[...]).astype(BF)
+    natural = dot_nt(wide_grad, split_columns(640, 768))
+    gains = jnp.concatenate([ggain1, ggain[0:1, :], jnp.zeros((126, 768), F32)], axis=0)
+    column = jnp.concatenate([natural[:, :512], natural[:, 512:576], gains.T[:, :64]], axis=1)
+    grads[...] = column.astype(BF)
+    copies = []
+    for ky, target in ((1, far), (0, near)):
+        for kz in range(4):
+            at = pl.multiple_of(96 * (ids[1] ^ (kz * 2 + ky)), 96)
+            copies.append(pltpu.make_async_copy(grads.at[pl.ds(at, 96)], target.at[kz], sems.at[len(copies)]))
+            copies[-1].start()
+    for copy in copies:
+        copy.wait()
+
+
+def finish(ids, token_pieces, cos, sin, n16, dq_low, dq_high, dkt, dvt, wide, ggain):
+    return pl.pallas_call(
+        finish_kernel,
+        in_specs=[SMEM] + [VM] * 13,
+        out_specs=[VM] * 4 + [ANY, ANY],
         out_shape=[shaped((256, 768), BF)] * 4 + [shaped((4, 96, 640), BF)] * 2,
         scratch_shapes=[
             pltpu.VMEM((1024, 768), BF),
-            pltpu.VMEM((256, 1024), F32),
-            pltpu.VMEM((256, 1024), F32),
             pltpu.VMEM((768, 640), BF),
             pltpu.SemaphoreType.DMA((8,)),
         ],
         compiler_params=pltpu.CompilerParams(vmem_limit_bytes=VMEM_LIMIT),
-        cost_estimate=pl.CostEstimate(flops=8 * 10**9, bytes_accessed=16 * 10**6, transcendentals=0),
-        name="backward_attention",
-    )(ids, *token_pieces, cos, sin, n16, q8, key, val, att, prob, *d_pieces, gain, wide, ggain)
+        cost_estimate=pl.CostEstimate(flops=4 * 10**9, bytes_accessed=8 * 10**6, transcendentals=0),
+        name="finish",
+    )(ids, *token_pieces, cos, sin, n16, dq_low, dq_high, dkt, dvt, wide, ggain)
 
 
 def pack_layout(count_row, length_row, slots, own_place):
@@ -844,20 +925,9 @@
     ]
 
 
-def gather_halves(halves, core):
-    mine = jnp.where(core == 0, halves[0], halves[1])
-    other = jnp.where(core == 0, halves[1], halves[0])
-    came = xperm(other, 1)
-    lower, upper = jnp.where(core == 0, mine, came), jnp.where(core == 0, came, mine)
-    own = jnp.concatenate([lower, upper], axis=0)
-    z1, z2, z3 = xperm(own, 8), xperm(own, 16), xperm(own, 24)
-    p0, p1 = jnp.stack([own, z1]), jnp.stack([z2, z3])
-    x0, y0 = xperm(p0, 2), xperm(p0, 4)
-    x1, y1 = xperm(p1, 2), xperm(p1, 4)
-    xy0 = xperm(y0, 2)
-    xy1 = xperm(x1, 4)
-    held = [p0, p1, x0, x1, y0, y1, xy0, xy1]
-    return held + [xperm(piece, 1) for piece in held]
+def after(values, *signals):
+    held = lax.optimization_barrier((tuple(values), signals))
+    return list(held[0])
 
 
 def fast_body(
@@ -874,51 +944,68 @@
     chip = group_row * 2 + side
     ids = jnp.stack([own_place, group_row, core, chip]).astype(jnp.int32)
 
-    qkv16 = weight_qkv.astype(BF)
-    blocks = qkv16.reshape(24, 3, 4, 192).transpose(2, 0, 1, 3).reshape(4, 24, 576)
-    gain_cols = jnp.concatenate([norm_gains.T.astype(BF), jnp.zeros((24, 62), BF)], axis=1)
-    blocks = jnp.concatenate([blocks, jnp.broadcast_to(gain_cols[None], (4, 24, 64))], axis=2)
-    sends = [lax.dynamic_index_in_dim(blocks, own_place ^ k, 0, keepdims=False) for k in range(4)]
-    came = [sends[0]] + [xperm(sends[k], k) for k in (1, 2, 3)]
-    rows_here = jnp.concatenate(by_place(came, core == 1, side == 1), axis=0)
-    column = [rows_here, xperm(rows_here, 8), xperm(rows_here, 16), xperm(rows_here, 24)]
-    w_pieces = []
-    for piece in column:
-        w_pieces += [piece, xperm(piece, 4)]
-
-    tok_x, tok_c = xperm(tokens, 2), xperm(tokens, 1)
+    def exchange(near, far):
+        came = xperm(far, 2)
+        return [xperm(near, 1), came[0], xperm(came[1], 1)]
+
+    own, near, far, mine_in, other_in, mine_rest, other_rest = prologue(
+        ids, weight_qkv, weight_out, weight_in, weight_down, norm_gains
+    )
+    tok_c = xperm(tokens, 1)
+
+    def column_of(own):
+        return jnp.stack([own, xperm(own, 8), xperm(own, 16), xperm(own, 24)])
+
+    came_rest, came_in = xperm(other_rest, 1), xperm(other_in, 1)
+    rows_here, own_rest, own_in = assemble(
+        ids, own, *exchange(near, far), mine_rest, came_rest, mine_in, came_in
+    )
+    rows_z = jnp.stack([xperm(rows_here, 8), xperm(rows_here, 16), xperm(rows_here, 24)])
+    w_pieces = [rows_here, xperm(rows_here, 4), rows_z, xperm(rows_z, 4)]
+    (tokens_later,) = after([tokens], rows_here, tok_c)
+    tok_x = xperm(tokens_later, 2)
     token_pieces = [tokens, tok_c, tok_x, xperm(tok_x, 1)]
 
-    in16, out16, down16 = weight_in.astype(BF), weight_out.astype(BF), weight_down.astype(BF)
-    down16 = jnp.pad(down16, ((0, 0), (0, 128)))
-    first = gather_halves(
-        [
-            jnp.concatenate([in16[:, 1152 * h : 1152 * h + 1152], out16[:, 384 * h : 384 * h + 384]], axis=1)
-            for h in range(2)
-        ],
-        core,
-    )
-    last = gather_halves([down16[:, 640 * h : 640 * h + 640] for h in range(2)], core)
+    (own_rest,) = after([own_rest], rows_z, w_pieces[1])
+    rest = column_of(own_rest)
+    rest_x, rest_y = xperm(rest, 2), xperm(rest, 4)
+    (own_in,) = after([own_in], rest, w_pieces[3])
+    into = column_of(own_in)
+    into_x, into_y = xperm(into, 2), xperm(into, 4)
 
     count_row = lax.dynamic_index_in_dim(counts, group_row, 0, keepdims=False)
     length_row = lax.dynamic_index_in_dim(lengths, group_row, 0, keepdims=False)
+    count_row, length_row = after([count_row, length_row], rows_here)
     docs, position, living = pack_layout(count_row, length_row, slots, own_place)
     speeds = ROTARY_BASE ** (-(jnp.arange(HD // 2, dtype=F32) * (2.0 / HD)))
     angles = position.astype(F32)[:, None] * jnp.tile(speeds, 4)[None, :]
     cos, sin = jnp.cos(angles), jnp.sin(angles)
     live = living[:slots, None].astype(F32)
 
-    n16, q8, key, val, att, a0, a1, a2, a3, prob, gain, wide = forward_attention(
-        ids, token_pieces, cos, sin, docs, w_pieces
-    )
-    att_pieces = [a0, xperm(a1, 1), xperm(a2, 2), xperm(a3, 3)]
-    block_out, dmiddle, d0, d1, d2, d3, act16, n2low, dgate, dbr, ggain = feed_forward(
-        ids, tokens, cotangent, live, gain, att_pieces, first, last
-    )
-    d_pieces = [d0, xperm(d1, 1), xperm(d2, 2), xperm(d3, 3)]
-    s0, s1, s2, s3, k0, k1, k2, k3 = feed_gradients(
-        ids, cotangent, live, act16, n2low, dgate, dbr, att_pieces
-    )
+    (cos_ready,) = after([cos], rest)
+    n16, q8, key, val, gain, wide = project(ids, token_pieces, cos_ready, sin, w_pieces)
+    (q8_high,) = after([q8], into, rest_x, rest_y)
+    att_high, far, prob_high = attend(2, q8_high, key, val, docs)
+    (q8_low,) = after([q8], far, into_x, into_y)
+    att_low, near, prob_low = attend(0, q8_low, key, val, docs)
+
+    def relay(held, held_x, held_y, signal):
+        held = [held, held_x, held_y]
+        _, ready_x, ready_y = after(held, signal)
+        return held + [xperm(ready_y[:2], 2), xperm(ready_x[2:], 4)]
+
+    held_rest = relay(rest, rest_x, rest_y, far)
+    far_came = xperm(far, 2)
+    (near_last,) = after([near[1]], held_rest[3], held_rest[4], far_came)
+    held_in = relay(into, into_x, into_y, near)
+    att_pieces = [near[0], xperm(near_last, 1), far_came[0], xperm(far_came[1], 1)]
+    held_rest += [xperm(piece, 1) for piece in held_rest]
+    held_in += [xperm(piece, 1) for piece in held_in]
+    block_out, dmiddle, d_near, d_far, act16, n2low, dgate, dbr, ggain = feed_forward(
+        ids, tokens, cotangent, live, gain, att_pieces, held_rest, held_in
+    )
+    d_came = xperm(d_far, 2)
+    d_pieces = [d_near[0], xperm(d_near[1], 1), d_came[0], xperm(d_came[1], 1)]
 
     def add(*parts):
         total = parts[0].astype(F32)
@@ -926,35 +1013,64 @@
             total = total + part.astype(F32)
         return total.astype(BF)
 
-    e3 = add(k3, xperm(s3, 1))
-    e1 = add(k1, xperm(s1, 1))
-    e2 = add(k2, xperm(s2, 1))
-    e0 = add(k0, xperm(s0, 1))
-    to_y = xperm(e3[:2], 2)
-    to_x = xperm(e3[2:], 4)
-    x0 = xperm(e1[:2], 2)
-    y1 = xperm(e2[2:], 4)
-    y0 = xperm(add(e2[:2], to_y), 4)
-    x1 = xperm(add(e1[2:], to_x), 2)
-    f0 = add(e0[:2], x0, y0)
-    f1 = add(e0[2:], x1, y1)
-    chip_rows = add(f0[0], xperm(f0[1], 8), xperm(f1[0], 16), xperm(f1[1], 24))
-    lower, upper = chip_rows[:24], chip_rows[24:]
-    mine, other = jnp.where(core == 0, lower, upper), jnp.where(core == 0, upper, lower)
-    came = xperm(other, 1)
-    half0 = jnp.where(core == 0, mine, came).astype(F32)
-    half1 = jnp.where(core == 0, came, mine).astype(F32)
-    grad_in = jnp.concatenate([half0[:, :1152], half1[:, :1152]], axis=1)
-    grad_out = jnp.concatenate([half0[:, 1152:1536], half1[:, 1152:1536]], axis=1)
-    grad_down = jnp.concatenate([half0[:, 1536:2176], half1[:, 1536:2048]], axis=1)
-
-    dn0, dn1, dn2, dn3, far, near = backward_attention(
-        ids, token_pieces, cos, sin, n16, q8, key, val, att, prob, d_pieces, gain, wide, ggain
-    )
-    e = add(near, xperm(far, 4))
+    def reduce_begin(far_sent, sent, far_kept, kept, *signals):
+        came, rest = xperm(far_sent, 1), xperm(sent, 1)
+        far_kept, came = after([far_kept, came], *signals)
+        for_y, for_x = add(far_kept[:2], came[:2]), add(far_kept[2:], came[2:])
+        return xperm(for_y, 2), xperm(for_x, 4), kept, rest, for_y, for_x
+
+    def reduce_middle(to_y, to_x, kept, rest, *signals):
+        kept, to_x, to_y = after([kept, to_x, to_y], *signals)
+        one = jnp.concatenate([add(kept[4:6], rest[4:6]), add(kept[6:8], rest[6:8], to_x)], axis=0)
+        two = jnp.concatenate([add(kept[8:10], rest[8:10], to_y), add(kept[10:], rest[10:])], axis=0)
+        return xperm(one, 2), xperm(two, 4)
+
+    def reduce_column(one, two, kept, rest, *signals):
+        kept, one = after([kept, one], *signals)
+        pieces = [add(kept[kz], rest[kz], one[kz], two[kz]) for kz in range(4)]
+        return [pieces[0]] + [xperm(pieces[kz], 8 * kz) for kz in (1, 2, 3)]
+
+    def reduce_end(pieces):
+        rows = add(*pieces)
+        lower, upper = rows[:24], rows[24:]
+        mine, other = jnp.where(core == 0, lower, upper), jnp.where(core == 0, upper, lower)
+        came = xperm(other, 1)
+        return (
+            jnp.where(core == 0, mine, came).astype(F32),
+            jnp.where(core == 0, came, mine).astype(F32),
+        )
+
+    chunks_in = chunk_call(grad_in_kernel, "grad_in", 1152, ids, n2low, dgate)
+    *state_in, for_y, for_x = reduce_begin(*chunks_in)
+    (cot_later,) = after([cotangent], for_y, for_x, d_came)
+    chunks_rest = chunk_call(
+        grad_rest_kernel, "grad_rest", 1024, ids, cot_later, live, act16, dbr, *att_pieces
+    )
+    one_in, two_in = reduce_middle(*state_in, chunks_rest[0])
+    (key_low,) = after([key], d_pieces[2], d_pieces[3], state_in[0], state_in[1])
+    dq_low, dkt, dvt = backward(0, cos, sin, q8, key_low, val, att_low, prob_low, d_pieces[:2])
+    *state_rest, _, _ = reduce_begin(*chunks_rest, dq_low)
+    (key_high,) = after([key], state_rest[3], one_in, two_in)
+    dq_high, dkt, dvt = backward(2, cos, sin, q8, key_high, val, att_high, prob_high, d_pieces[2:], (dkt, dvt))
+    one_rest, two_rest = reduce_middle(*state_rest, dq_high)
+    column_in = reduce_column(one_in, two_in, *state_in[2:], dq_low)
+    (dkt_ready,) = after([dkt], state_rest[0], state_rest[1], *column_in)
+    dn0, dn1, dn2, dn3, far, near = finish(
+        ids, token_pieces, cos, sin, n16, dq_low, dq_high, dkt_ready, dvt, wide, ggain
+    )
+    (far,) = after([far], one_rest, two_rest)
+    (far_y,) = after([xperm(far, 4)], *column_in)
+    column_rest = reduce_column(one_rest, two_rest, *state_rest[2:], near)
+    half0, half1 = reduce_end(column_in)
+    grad_in = jnp.concatenate([half0, half1], axis=1)
+    half0, half1 = reduce_end(column_rest)
+    grad_out = jnp.concatenate([half0[:, :384], half1[:, :384]], axis=1)
+    grad_down = jnp.concatenate([half0[:, 384:], half1[:, 384:896]], axis=1)
+
+    e = add(near, far_y)
     dp_rows = add(e[0], xperm(e[1], 8), xperm(e[2], 16), xperm(e[3], 24)).reshape(4, 24, 640)
     sends = [lax.dynamic_index_in_dim(dp_rows, own_place ^ k, 0, keepdims=False) for k in range(4)]
-    came = [sends[0]] + [xperm(sends[k], k) for k in (1, 2, 3)]
+    came = [sends[0]] + exchange(sends[1], jnp.stack(sends[2:]))
     placed = jnp.stack(by_place([piece.astype(F32) for piece in came], core == 1, side == 1))
     grad_qkv = placed[:, :, :576].reshape(4, 24, 3, 192).transpose(1, 2, 0, 3).reshape(24, 2304)
     grad_gains = jnp.sum(placed[:, :, 576:578], axis=0).T

time: 292 us -> 219 us (0.75); the launches traced: 287 us -> 218 us
  waiting for transfers between devices: 91.2 us -> 37.2 us
  local copies, waits for them, and re-layouts: 37.5 us -> 9.67 us
  Pallas kernels: 53.2 us -> 70.9 us
  starting transfers between devices: 73 us -> 69.5 us
    ppermute x79 -> x73, waiting for transfers between devices: 91.2 us -> 37.2 us  [xperm(): return lax.ppermute(value, AXES, [(i, i ^ mask) for i in range(count)])]
    unnamed x177 -> x142, local copies, waits for them, and re-layouts: 28.7 us -> 2.63 us
    pallas_call x4 -> x11, Pallas kernels: 53.2 us -> 70.9 us  [the longest x2 15 us: backward(): pl.pallas_call(functools.partial(backward_kernel, resumed=bool(sums)), gr...]
    ppermute x79 -> x73, starting transfers between devices: 73 us -> 69.5 us  [xperm(): return lax.ppermute(value, AXES, [(i, i ^ mask) for i in range(count)])]
    reshape x2, local copies, waits for them, and re-layouts: 3.71 us -> 0.37 us  [fast_body(): placed[:, :, :576].reshape(4, 24, 3, 192).transpose(1, 2, 0, 3)]
    squeeze x2 -> x7, local copies, waits for them, and re-layouts: 0.05 us -> 3.31 us  [the longest x2 1.35 us: fast_body(): d_pieces = [d_near[0], xperm(d_near[1], 1), d_came[0], xperm(d_came[1], 1)]]
    convert_element_type x11 -> x9, other arithmetic: 8.37 us -> 7.8 us  [add(): return total.astype(BF)]
  transfers between devices with their start and end apart: 79 -> 73, of which waited for: 19 -> 16; matrix products, arithmetic and copies ran while one was open for 11% -> 14% of each run, Pallas kernels for 9% -> 25%
where the time goes in v2:
time: 219 us; the launch traced here: 218 us
  Pallas kernels  70.9 us (32%)
  starting transfers between devices  69.5 us (32%)
  waiting for transfers between devices  37.2 us (17%)
  other arithmetic  28.4 us (13%)
  local copies, waits for them, and re-layouts  9.67 us (4%)
    ppermute x73, starting transfers between devices, xperm(): return lax.ppermute(value, AXES, [(i, i ^ mask) for i in range(count)])  69.5 us
    ppermute x73, waiting for transfers between devices, xperm(): return lax.ppermute(value, AXES, [(i, i ^ mask) for i in range(count)])  37.2 us
    pallas_call x2, Pallas kernels, backward(): pl.pallas_call(functools.partial(backward_kernel, resumed=bool(sums)), gr...  15 us
    pallas_call x2, Pallas kernels, attend(): pl.pallas_call(attend_kernel, grid=(2,), in_specs=[pl.BlockSpec((256, 256...  14.3 us
    pallas_call x1, Pallas kernels, feed_forward(): pl.pallas_call(feed_kernel, in_specs=[SMEM] + [VM] * 8 + [ANY] * (2 * SLO...  10.7 us
    pallas_call x1, Pallas kernels, finish(): pl.pallas_call(finish_kernel, in_specs=[SMEM] + [VM] * 13, out_specs=[VM]...  9.83 us
    pallas_call x2, Pallas kernels, chunk_call(): pl.pallas_call(kernel, in_specs=[SMEM] + [VM] * len(operands), out_specs=...  9.47 us
    pallas_call x1, Pallas kernels, project(): pl.pallas_call(project_kernel, in_specs=[SMEM] + [VM] * 6 + [ANY] * 4, ou...  7.8 us
  transfers between devices with their start and end apart: 73, of which 16 were waited for; matrix products, arithmetic and copies ran while one was open for 14% of the time, Pallas kernels for 25%

profile of v2, /device:TPU:9, one launch (start us, length us, event | category | flops | bytes accessed | tf_op | source)
XLA Modules:
  0.0 217.6 jit_solution(2381084482408826420)
XLA Ops:
  1.3 2.0 prologue.1
  3.3 1.2 collective-permute-start.1
  6.0 1.1 convert_reduce_fusion
  7.7 1.3 collective-permute-start.2
  10.6 1.7 assemble.1
  12.3 2.5 %collective-permute-start.9 = (bf16[96,640]{1,0:T(8,128)(2,1)}, bf16[96,640]{1,0:T(8,128)(2,1)S(1)}, u32[]{:S(2)}, u32[]{:S(2)}) collective-permute-start(bf16[96,640]{1,0:T(8,128)(2,1)} %get-tuple-element.118.w0), channel_id=1, source_target_pairs={{0,16},{1,17},{2,18},{3,19},{4,20},{5,21},{6,22},{7,23},{8,24},{9,... | collective-permute-start | bytes 368648 | tf_op jit(solution)/shard_map/ppermute | solution.py:391
  15.0 1.2 collective-permute-start.11
  18.2 1.3 collective-permute-start.6
  19.5 1.5 collective-permute-done.9
  21.0 5.2 %collective-permute-done.10 = bf16[96,640]{1,0:T(8,128)(2,1)S(1)} collective-permute-done((bf16[96,640]{1,0:T(8,128)(2,1)}, bf16[96,640]{1,0:T(8,128)(2,1)S(1)}, u32[]{:S(2)}, u32[]{:S(2)}) %collective-permute-start.10) | collective-permute-done | bytes 122912 | tf_op jit(solution)/shard_map/ppermute | solution.py:391
  26.3 2.4 %collective-permute-start.13 = (bf16[48,1024]{1,0:T(8,128)(2,1)S(1)}, bf16[48,1024]{1,0:T(8,128)(2,1)S(1)}, u32[]{:S(2)}, u32[]{:S(2)}) collective-permute-start(bf16[48,1024]{1,0:T(8,128)(2,1)S(1)} %copy-done.38), channel_id=1, source_target_pairs={{0,16},{1,17},{2,18},{3,19},{4,20},{5,21},{6,22},{7,23},{8,24},{9,... | collective-permute-start | bytes 294920 | tf_op jit(solution)/shard_map/ppermute | solution.py:391
  29.0 1.2 collective-permute-start.15
  30.2 3.1 %multiply_sine_fusion = (f32[1024,128]{1,0:T(8,128)}, f32[1024,128]{1,0:T(8,128)}) fusion(f32[128]{0:T(128)S(1)} %mul.248, f32[1024]{0:T(1024)S(1)} %get-tuple-element.277), kind=kLoop, calls=%fused_computation.16 | loop fusion | flops 131072 | bytes 1053184 | tf_op jit(solution)/shard_map/sin | solution.py:982
  33.3 4.2 %collective-permute-done.14 = bf16[48,1024]{1,0:T(8,128)(2,1)S(1)} collective-permute-done((bf16[48,1024]{1,0:T(8,128)(2,1)S(1)}, bf16[48,1024]{1,0:T(8,128)(2,1)S(1)}, u32[]{:S(2)}, u32[]{:S(2)}) %collective-permute-start.14) | collective-permute-done | bytes 98336 | tf_op jit(solution)/shard_map/ppermute | solution.py:391
  38.1 2.1 collective-permute-start.17
  40.3 3.1 %collective-permute-start.7 = (bf16[256,768]{1,0:T(8,128)(2,1)S(1)}, bf16[256,768]{1,0:T(8,128)(2,1)S(1)}, u32[]{:S(2)}, u32[]{:S(2)}) collective-permute-start(bf16[256,768]{1,0:T(8,128)(2,1)S(1)} %collective-permute-done.6.t2), channel_id=1, source_target_pairs={{0,1},{1,0},{2,3},{3,2},{4,5},{5,4},{6,7},{7,6},{8,9},{9,8},{10,11... | collective-permute-start | bytes 1179656 | tf_op jit(solution)/shard_map/ppermute | solution.py:391
  44.1 1.2 collective-permute-start.19
  45.3 1.2 collective-permute-start.20
  46.5 2.7 %collective-permute-start.28 = (bf16[4,48,1024]{2,1,0:T(8,128)(2,1)S(1)}, bf16[4,48,1024]{2,1,0:T(8,128)(2,1)}, u32[]{:S(2)}, u32[]{:S(2)}) collective-permute-start(bf16[4,48,1024]{2,1,0:T(8,128)(2,1)S(1)} %pad_maximum_fusion.3.refs_9_), channel_id=1, source_target_pairs={{0,1},{1,0},{2,3},{3,2},{4,5},{5,4},{6,7},{7,6},{8,9},{9,8},{10,11... | collective-permute-start | bytes 1179656 | tf_op jit(solution)/shard_map/ppermute | solution.py:391
  49.7 1.3 collective-permute-start.21
  51.0 1.3 collective-permute-start.22
  52.3 7.8 %project.1 = (bf16[1024,768]{1,0:T(8,128)(2,1)}, bf16[1024,256]{1,0:T(8,128)(2,1)}, bf16[1024,256]{1,0:T(8,128)(2,1)}, bf16[1024,256]{1,0:T(8,128)(2,1)}, f32[8,768]{1,0:T(8,128)}, /*index=5*/bf16[768,768]{1,0:T(8,128)(2,1)}) custom-call(s32[4]{0:T(128)} %pad_add_fusion.ids.refs_0_, bf16[256,768]{1,0:T(8,128)(2,1)} %t0.3, bf16[256,768]{1,0:T(8,128)(2,1)} %copy-done.57, ...), custom_call_target="tpu_custom_call" | custom-call | flops 3000000000 | bytes 8000000 | tf_op jit(solution)/shard_map/project/pallas_call | solution.py:571
  60.1 2.5 %collective-permute-start.35 = (bf16[4,48,1152]{2,1,0:T(8,128)(2,1)S(1)}, bf16[4,48,1152]{2,1,0:T(8,128)(2,1)S(1)}, u32[]{:S(2)}, u32[]{:S(2)}) collective-permute-start(bf16[4,48,1152]{2,1,0:T(8,128)(2,1)S(1)} %pad_maximum_fusion.refs_19_), channel_id=1, source_target_pairs={{0,1},{1,0},{2,3},{3,2},{4,5},{5,4},{6,7},{7,6},{8,9},{9,8},{10,11... | collective-permute-start | bytes 1327112 | tf_op jit(solution)/shard_map/ppermute | solution.py:391
  62.7 7.2 %attend.2 = (f32[512,192]{1,0:T(8,128)}, bf16[2,256,192]{2,1,0:T(8,128)(2,1)}, bf16[3,512,1024]{2,1,0:T(8,128)(2,1)}) custom-call(bf16[1024,256]{1,0:T(8,128)(2,1)} %get-tuple-element.133.q8.refs_2_, bf16[1024,256]{1,0:T(8,128)(2,1)} %get-tuple-element.165.key.refs_3_, bf16[1024,256]{1,0:T(8,128)(2,1)} %get-tuple-element.131.val.refs_4_, ...), custom_call_target="tpu_custom_call" | custom-call | flops 3000000000 | bytes 8000000 | tf_op jit(solution)/shard_map/attend/pallas_call | solution.py:591
  70.6 7.1 %attend.3 = (f32[512,192]{1,0:T(8,128)}, bf16[2,256,192]{2,1,0:T(8,128)(2,1)}, bf16[3,512,1024]{2,1,0:T(8,128)(2,1)}) custom-call(bf16[1024,256]{1,0:T(8,128)(2,1)} %get-tuple-element.133.q8.refs_2_, bf16[1024,256]{1,0:T(8,128)(2,1)} %get-tuple-element.165.key.refs_3_, bf16[1024,256]{1,0:T(8,128)(2,1)} %get-tuple-element.131.val.refs_4_, ...), custom_call_target="tpu_custom_call" | custom-call | flops 3000000000 | bytes 8000000 | tf_op jit(solution)/shard_map/attend/pallas_call | solution.py:591
  77.9 1.3 collective-permute-start.23
  80.2 1.0 collective-permute-start.36
  81.3 2.8 %collective-permute-done.23.refs_12_ = bf16[2,48,1024]{2,1,0:T(8,128)(2,1)S(1)} collective-permute-done((bf16[2,48,1024]{2,1,0:T(8,128)(2,1)S(1)}, bf16[2,48,1024]{2,1,0:T(8,128)(2,1)S(1)}, u32[]{:S(2)}, u32[]{:S(2)}) %collective-permute-start.23) | collective-permute-done | bytes 196640 | tf_op jit(solution)/shard_map/ppermute | solution.py:391
  84.1 1.2 collective-permute-start.33
  85.7 1.7 collective-permute-start.31
  88.1 1.7 collective-permute-done.33.refs_22_
  89.9 2.1 collective-permute-start.26
  91.9 1.2 collective-permute-start.27
  97.0 10.7 %feed_forward.1 = (bf16[256,768]{1,0:T(8,128)(2,1)}, f32[256,768]{1,0:T(8,128)}, bf16[2,256,192]{2,1,0:T(8,128)(2,1)}, bf16[2,256,192]{2,1,0:T(8,128)(2,1)}, bf1...) custom-call(s32[4]{0:T(128)} %pad_add_fusion.ids.refs_0_, ...), custom_call_target="tpu_custom_call" | custom-call | flops 5000000000 | bytes 12000000 | tf_op jit(solution)/shard_map/feed_forward/pallas_call | solution.py:706
  107.7 4.7 %grad_in.1 = (bf16[4,48,1152]{2,1,0:T(8,128)(2,1)}, bf16[12,48,1152]{2,1,0:T(8,128)(2,1)}, bf16[4,48,1152]{2,1,0:T(8,128)(2,1)}, bf16[12,48,1152]{2,1,0:T(8,128)(2,1)}) custom-call(s32[4]{0:T(128)} %pad_add_fusion.ids.refs_0_, bf16[256,768]{1,0:T(8,128)(2,1)} %get-tuple-element.144.n2low, bf16[256,2304]{1,0:T(8,128)(2,1)} %get-tuple-element.145.dgate), custom_call_target="tpu_custom_call" | custom-call | flops 1500000000 | bytes 8000000 | tf_op jit(solution)/shard_map/grad_in/pallas_call | solution.py:771
  115.3 1.1 add_convert_fusion.7
  116.5 1.2 collective-permute-start.43
  118.1 3.5 %collective-permute-done.40 = bf16[2,256,192]{2,1,0:T(8,128)(2,1)S(1)} collective-permute-done((bf16[2,256,192]{2,1,0:T(8,128)(2,1)S(1)}, bf16[2,256,192]{2,1,0:T(8,128)(2,1)S(1)}, u32[]{:S(2)}, u32[]{:S(2)}) %collective-permute-start.40) | collective-permute-done | bytes 196640 | tf_op jit(solution)/shard_map/ppermute | solution.py:391
  122.3 1.5 collective-permute-start.41
  123.8 4.7 %grad_rest.1 = (bf16[4,48,1024]{2,1,0:T(8,128)(2,1)}, bf16[12,48,1024]{2,1,0:T(8,128)(2,1)}, bf16[4,48,1024]{2,1,0:T(8,128)(2,1)}, bf16[12,48,1024]{2,1,0:T(8,128)(2,1)}) custom-call(s32[4]{0:T(128)} %pad_add_fusion.ids.refs_0_, bf16[256,768]{1,0:T(8,128)(2,1)} %cot, f32[256,1]{1,0:T(8,128)} %copy.103.refs_3_.live, ...), custom_call_target="tpu_custom_call" | custom-call | flops 1500000000 | bytes 8000000 | tf_op jit(solution)/shard_map/grad_rest/pallas_call | solution.py:771
  131.5 7.3 %backward.2 = (bf16[512,256]{1,0:T(8,128)(2,1)}, f32[256,1024]{1,0:T(8,128)}, f32[256,1024]{1,0:T(8,128)}) custom-call(f32[1024,128]{1,0:T(8,128)} %get-tuple-element.124.cos.refs_0_, f32[1024,128]{1,0:T(8,128)} %get-tuple-element.321.sin.refs_1_, bf16[1024,256]{1,0:T(8,128)(2,1)} %get-tuple-element.133.q8.refs_2_, ...), custom_call_target="tpu_custom_call" | custom-call | flops 3000000000 | bytes 8000000 | tf_op jit(solution)/shard_map/backward/pallas_call | solution.py:823
  138.8 2.1 add_convert_fusion.13
  140.9 1.1 collective-permute-start.51
  142.0 1.1 collective-permute-start.52
  144.0 2.6 %collective-permute-start.54 = (bf16[48,1152]{1,0:T(8,128)(2,1)S(1)}, bf16[48,1152]{1,0:T(8,128)(2,1)}, u32[]{:S(2)}, u32[]{:S(2)}) collective-permute-start(bf16[48,1152]{1,0:T(8,128)(2,1)S(1)} %get-tuple-element.281), channel_id=1, source_target_pairs={{0,16},{1,17},{2,18},{3,19},{4,20},{5,21},{6,22},{7,23},{8,24},{9,... | collective-permute-start | bytes 331784 | tf_op jit(solution)/shard_map/ppermute | solution.py:391
  146.7 7.8 %backward.3 = (bf16[512,256]{1,0:T(8,128)(2,1)}, f32[256,1024]{1,0:T(8,128)}, f32[256,1024]{1,0:T(8,128)}) custom-call(f32[1024,128]{1,0:T(8,128)} %get-tuple-element.124.cos.refs_0_, f32[1024,128]{1,0:T(8,128)} %get-tuple-element.321.sin.refs_1_, bf16[1024,256]{1,0:T(8,128)(2,1)} %get-tuple-element.133.q8.refs_2_, ...), custom_call_target="tpu_custom_call" | custom-call | flops 3000000000 | bytes 8000000 | tf_op jit(solution)/shard_map/backward/pallas_call | solution.py:823
  154.5 1.7 add_convert_fusion.10
  158.9 1.2 add_convert_fusion.15
  160.1 2.7 %collective-permute-start.72 = (bf16[24,1152]{1,0:T(8,128)(2,1)S(1)}, bf16[24,1152]{1,0:T(8,128)(2,1)S(1)}, u32[]{:S(2)}, u32[]{:S(2)}) collective-permute-start(bf16[24,1152]{1,0:T(8,128)(2,1)S(1)} %broadcast_select_fusion.2), channel_id=1, source_target_pairs={{0,1},{1,0},{2,3},{3,2},{4,5},{5,4},{6,7},{7,6},{8,9},{9,8},{10,11... | collective-permute-start | bytes 165896 | tf_op jit(solution)/shard_map/ppermute | solution.py:391
  162.8 9.8 %finish.1 = (bf16[256,768]{1,0:T(8,128)(2,1)}, bf16[256,768]{1,0:T(8,128)(2,1)}, bf16[256,768]{1,0:T(8,128)(2,1)}, bf16[256,768]{1,0:T(8,128)(2,1)}, bf16[4,96,6...) custom-call(s32[4]{0:T(128)} %pad_add_fusion.ids.refs_0_, bf16[256,768]{1,0:T(8,128)(2,1)} %t0.3, ...), custom_call_target="tpu_custom_call" | custom-call | flops 4000000000 | bytes 8000000 | tf_op jit(solution)/shard_map/finish/pallas_call | solution.py:881
  173.3 1.5 fusion.29
  175.7 1.7 collective-permute-start.69
  179.2 1.1 collective-permute-start.61
  180.3 3.3 %collective-permute-done.69 = bf16[48,1024]{1,0:T(8,128)(2,1)S(1)} collective-permute-done((bf16[48,1024]{1,0:T(8,128)(2,1)S(1)}, bf16[48,1024]{1,0:T(8,128)(2,1)S(1)}, u32[]{:S(2)}, u32[]{:S(2)}) %collective-permute-start.69) | collective-permute-done | bytes 98336 | tf_op jit(solution)/shard_map/ppermute | solution.py:391
  183.6 2.9 %collective-permute-done.70 = bf16[48,1024]{1,0:T(8,128)(2,1)S(1)} collective-permute-done((bf16[48,1024]{1,0:T(8,128)(2,1)S(1)}, bf16[48,1024]{1,0:T(8,128)(2,1)S(1)}, u32[]{:S(2)}, u32[]{:S(2)}) %collective-permute-start.70) | collective-permute-done | bytes 98336 | tf_op jit(solution)/shard_map/ppermute | solution.py:391
  186.5 1.1 fusion.22
  187.6 1.2 collective-permute-start.71
  193.4 2.1 collective-permute-start.63
  195.7 4.0 %collective-permute-done.58 = bf16[256,768]{1,0:T(8,128)(2,1)S(1)} collective-permute-done((bf16[256,768]{1,0:T(8,128)(2,1)S(1)}, bf16[256,768]{1,0:T(8,128)(2,1)S(1)}, u32[]{:S(2)}, u32[]{:S(2)}) %collective-permute-start.58) | collective-permute-done | bytes 393248 | tf_op jit(solution)/shard_map/ppermute | solution.py:391
  200.2 3.0 %collective-permute-done.63 = bf16[96,640]{1,0:T(8,128)(2,1)S(1)} collective-permute-done((bf16[96,640]{1,0:T(8,128)(2,1)S(1)}, bf16[96,640]{1,0:T(8,128)(2,1)S(1)}, u32[]{:S(2)}, u32[]{:S(2)}) %collective-permute-start.63) | collective-permute-done | bytes 122912 | tf_op jit(solution)/shard_map/ppermute | solution.py:391
  203.2 2.8 %collective-permute-done.64 = bf16[96,640]{1,0:T(8,128)(2,1)S(1)} collective-permute-done((bf16[96,640]{1,0:T(8,128)(2,1)S(1)}, bf16[96,640]{1,0:T(8,128)(2,1)S(1)}, u32[]{:S(2)}, u32[]{:S(2)}) %collective-permute-start.64) | collective-permute-done | bytes 122912 | tf_op jit(solution)/shard_map/ppermute | solution.py:391
  206.9 2.1 collective-permute-start.67
  209.2 3.1 %collective-permute-start.66 = (bf16[24,640]{1,0:T(8,128)(2,1)S(1)}, bf16[24,640]{1,0:T(8,128)(2,1)S(1)}, u32[]{:S(2)}, u32[]{:S(2)}) collective-permute-start(bf16[24,640]{1,0:T(8,128)(2,1)S(1)} %slice_bitcast_fusion.13), channel_id=1, source_target_pairs={{0,1},{1,0},{2,3},{3,2},{4,5},{5,4},{6,7},{7,6},{8,9},{9,8},{10,11... | collective-permute-start | bytes 92168 | tf_op jit(solution)/shard_map/ppermute | solution.py:391
  212.3 1.3 fusion.7
  (319 shorter events, 39.2 us)
Async XLA Ops:
  3.3 3.8 %collective-permute-start.1 = (bf16[2,24,640]{2,1,0:T(8,128)(2,1)}, bf16[2,24,640]{2,1,0:T(8,128)(2,1)S(1)}, u32[]{:S(2)}, u32[]{:S(2)}) collective-permute-start(bf16[2,24,640]{2,1,0:T(8,128)(2,1)} %get-tuple-element.113), channel_id=1, source_target_pairs={{0,2},{1,3},{2,0},{3,1},{4,6},{5,7},{6,4},{7,5},{8,10},{9,11},{10,... | collective-permute-start | bytes 184328 | tf_op jit(solution)/shard_map/ppermute | solution.py:391
  4.5 5.5 %collective-permute-start.4 = (bf16[24,1152]{1,0:T(8,128)(2,1)}, bf16[24,1152]{1,0:T(8,128)(2,1)S(1)}, u32[]{:S(2)}, u32[]{:S(2)}) collective-permute-start(bf16[24,1152]{1,0:T(8,128)(2,1)} %get-tuple-element.117), channel_id=1, source_target_pairs={{0,1},{1,0},{2,3},{3,2},{4,5},{5,4},{6,7},{7,6},{8,9},{9,8},{10,11... | collective-permute-start | bytes 165896 | tf_op jit(solution)/shard_map/ppermute | solution.py:391
  5.4 4.5 %collective-permute-start.3 = (bf16[24,1024]{1,0:T(8,128)(2,1)}, bf16[24,1024]{1,0:T(8,128)(2,1)S(1)}, u32[]{:S(2)}, u32[]{:S(2)}) collective-permute-start(bf16[24,1024]{1,0:T(8,128)(2,1)} %get-tuple-element.115), channel_id=1, source_target_pairs={{0,1},{1,0},{2,3},{3,2},{4,5},{5,4},{6,7},{7,6},{8,9},{9,8},{10,11... | collective-permute-start | bytes 147464 | tf_op jit(solution)/shard_map/ppermute | solution.py:391
  5.4 4.5 %collective-permute-start = (bf16[24,640]{1,0:T(8,128)(2,1)}, bf16[24,640]{1,0:T(8,128)(2,1)S(1)}, u32[]{:S(2)}, u32[]{:S(2)}) collective-permute-start(bf16[24,640]{1,0:T(8,128)(2,1)} %get-tuple-element.112), channel_id=1, source_target_pairs={{0,1},{1,0},{2,3},{3,2},{4,5},{5,4},{6,7},{7,6},{8,9},{9,8},{10,11... | collective-permute-start | bytes 92168 | tf_op jit(solution)/shard_map/ppermute | solution.py:391
  5.9 12.2 %collective-permute-start.5 = (bf16[256,768]{1,0:T(8,128)(2,1)}, bf16[256,768]{1,0:T(8,128)(2,1)S(1)}, u32[]{:S(2)}, u32[]{:S(2)}) collective-permute-start(bf16[256,768]{1,0:T(8,128)(2,1)} %t0.3), channel_id=1, source_target_pairs={{0,1},{1,0},{2,3},{3,2},{4,5},{5,4},{6,7},{7,6},{8,9},{9,8},{10,11... | collective-permute-start | bytes 1179656 | tf_op jit(solution)/shard_map/ppermute | solution.py:391
  12.3 7.1 %collective-permute-start.8 = (bf16[96,640]{1,0:T(8,128)(2,1)}, bf16[96,640]{1,0:T(8,128)(2,1)S(1)}, u32[]{:S(2)}, u32[]{:S(2)}) collective-permute-start(bf16[96,640]{1,0:T(8,128)(2,1)} %get-tuple-element.118.w0), channel_id=1, source_target_pairs={{0,8},{1,9},{2,10},{3,11},{4,12},{5,13},{6,14},{7,15},{8,0},{9,1},... | collective-permute-start | bytes 368648 | tf_op jit(solution)/shard_map/ppermute | solution.py:391
  12.3 8.6 %collective-permute-start.9 = (bf16[96,640]{1,0:T(8,128)(2,1)}, bf16[96,640]{1,0:T(8,128)(2,1)S(1)}, u32[]{:S(2)}, u32[]{:S(2)}) collective-permute-start(bf16[96,640]{1,0:T(8,128)(2,1)} %get-tuple-element.118.w0), channel_id=1, source_target_pairs={{0,16},{1,17},{2,18},{3,19},{4,20},{5,21},{6,22},{7,23},{8,24},{9,... | collective-permute-start | bytes 368648 | tf_op jit(solution)/shard_map/ppermute | solution.py:391
  14.8 11.3 %collective-permute-start.10 = (bf16[96,640]{1,0:T(8,128)(2,1)}, bf16[96,640]{1,0:T(8,128)(2,1)S(1)}, u32[]{:S(2)}, u32[]{:S(2)}) collective-permute-start(bf16[96,640]{1,0:T(8,128)(2,1)} %get-tuple-element.118.w0), channel_id=1, source_target_pairs={{0,24},{1,25},{2,26},{3,27},{4,28},{5,29},{6,30},{7,31},{8,16},{9,... | collective-permute-start | bytes 368648 | tf_op jit(solution)/shard_map/ppermute | solution.py:391
  15.0 11.2 %collective-permute-start.11 = (bf16[96,640]{1,0:T(8,128)(2,1)}, bf16[96,640]{1,0:T(8,128)(2,1)S(1)}, u32[]{:S(2)}, u32[]{:S(2)}) collective-permute-start(bf16[96,640]{1,0:T(8,128)(2,1)} %get-tuple-element.118.w0), channel_id=1, source_target_pairs={{0,4},{1,5},{2,6},{3,7},{4,0},{5,1},{6,2},{7,3},{8,12},{9,13},{10,... | collective-permute-start | bytes 368648 | tf_op jit(solution)/shard_map/ppermute | solution.py:391
  18.2 22.1 %collective-permute-start.6 = (bf16[256,768]{1,0:T(8,128)(2,1)S(1)}, bf16[256,768]{1,0:T(8,128)(2,1)S(1)}, u32[]{:S(2)}, u32[]{:S(2)}) collective-permute-start(bf16[256,768]{1,0:T(8,128)(2,1)S(1)} %copy-done.2), channel_id=1, source_target_pairs={{0,2},{1,3},{2,0},{3,1},{4,6},{5,7},{6,4},{7,5},{8,10},{9,11},{10,... | collective-permute-start | bytes 1179656 | tf_op jit(solution)/shard_map/ppermute | solution.py:391
  26.2 7.0 %collective-permute-start.12 = (bf16[48,1024]{1,0:T(8,128)(2,1)S(1)}, bf16[48,1024]{1,0:T(8,128)(2,1)S(1)}, u32[]{:S(2)}, u32[]{:S(2)}) collective-permute-start(bf16[48,1024]{1,0:T(8,128)(2,1)S(1)} %copy-done.38), channel_id=1, source_target_pairs={{0,8},{1,9},{2,10},{3,11},{4,12},{5,13},{6,14},{7,15},{8,0},{9,1},... | collective-permute-start | bytes 294920 | tf_op jit(solution)/shard_map/ppermute | solution.py:391
  26.3 6.9 %collective-permute-start.13 = (bf16[48,1024]{1,0:T(8,128)(2,1)S(1)}, bf16[48,1024]{1,0:T(8,128)(2,1)S(1)}, u32[]{:S(2)}, u32[]{:S(2)}) collective-permute-start(bf16[48,1024]{1,0:T(8,128)(2,1)S(1)} %copy-done.38), channel_id=1, source_target_pairs={{0,16},{1,17},{2,18},{3,19},{4,20},{5,21},{6,22},{7,23},{8,24},{9,... | collective-permute-start | bytes 294920 | tf_op jit(solution)/shard_map/ppermute | solution.py:391
  28.7 8.8 %collective-permute-start.14 = (bf16[48,1024]{1,0:T(8,128)(2,1)S(1)}, bf16[48,1024]{1,0:T(8,128)(2,1)S(1)}, u32[]{:S(2)}, u32[]{:S(2)}) collective-permute-start(bf16[48,1024]{1,0:T(8,128)(2,1)S(1)} %copy-done.38), channel_id=1, source_target_pairs={{0,24},{1,25},{2,26},{3,27},{4,28},{5,29},{6,30},{7,31},{8,16},{9,... | collective-permute-start | bytes 294920 | tf_op jit(solution)/shard_map/ppermute | solution.py:391
  29.0 8.6 %collective-permute-start.15 = (bf16[3,96,640]{2,1,0:T(8,128)(2,1)S(1)}, bf16[3,96,640]{2,1,0:T(8,128)(2,1)S(1)}, u32[]{:S(2)}, u32[]{:S(2)}) collective-permute-start(bf16[3,96,640]{2,1,0:T(8,128)(2,1)S(1)} %pad_maximum_fusion.6.w2), channel_id=1, source_target_pairs={{0,4},{1,5},{2,6},{3,7},{4,0},{5,1},{6,2},{7,3},{8,12},{9,13},{10,... | collective-permute-start | bytes 1105928 | tf_op jit(solution)/shard_map/ppermute | solution.py:391
  37.6 7.7 %collective-permute-start.16 = (bf16[48,1152]{1,0:T(8,128)(2,1)S(1)}, bf16[48,1152]{1,0:T(8,128)(2,1)S(1)}, u32[]{:S(2)}, u32[]{:S(2)}) collective-permute-start(bf16[48,1152]{1,0:T(8,128)(2,1)S(1)} %copy-done.36), channel_id=1, source_target_pairs={{0,8},{1,9},{2,10},{3,11},{4,12},{5,13},{6,14},{7,15},{8,0},{9,1},... | collective-permute-start | bytes 331784 | tf_op jit(solution)/shard_map/ppermute | solution.py:391
  38.1 8.4 %collective-permute-start.17 = (bf16[48,1152]{1,0:T(8,128)(2,1)S(1)}, bf16[48,1152]{1,0:T(8,128)(2,1)S(1)}, u32[]{:S(2)}, u32[]{:S(2)}) collective-permute-start(bf16[48,1152]{1,0:T(8,128)(2,1)S(1)} %copy-done.36), channel_id=1, source_target_pairs={{0,16},{1,17},{2,18},{3,19},{4,20},{5,21},{6,22},{7,23},{8,24},{9,... | collective-permute-start | bytes 331784 | tf_op jit(solution)/shard_map/ppermute | solution.py:391
  40.2 9.4 %collective-permute-start.18 = (bf16[48,1152]{1,0:T(8,128)(2,1)S(1)}, bf16[48,1152]{1,0:T(8,128)(2,1)S(1)}, u32[]{:S(2)}, u32[]{:S(2)}) collective-permute-start(bf16[48,1152]{1,0:T(8,128)(2,1)S(1)} %copy-done.36), channel_id=1, source_target_pairs={{0,24},{1,25},{2,26},{3,27},{4,28},{5,29},{6,30},{7,31},{8,16},{9,... | collective-permute-start | bytes 331784 | tf_op jit(solution)/shard_map/ppermute | solution.py:391
  40.3 10.6 %collective-permute-start.7 = (bf16[256,768]{1,0:T(8,128)(2,1)S(1)}, bf16[256,768]{1,0:T(8,128)(2,1)S(1)}, u32[]{:S(2)}, u32[]{:S(2)}) collective-permute-start(bf16[256,768]{1,0:T(8,128)(2,1)S(1)} %collective-permute-done.6.t2), channel_id=1, source_target_pairs={{0,1},{1,0},{2,3},{3,2},{4,5},{5,4},{6,7},{7,6},{8,9},{9,8},{10,11... | collective-permute-start | bytes 1179656 | tf_op jit(solution)/shard_map/ppermute | solution.py:391
  44.1 16.0 %collective-permute-start.19 = (bf16[4,48,1024]{2,1,0:T(8,128)(2,1)S(1)}, bf16[4,48,1024]{2,1,0:T(8,128)(2,1)S(1)}, u32[]{:S(2)}, u32[]{:S(2)}) collective-permute-start(bf16[4,48,1024]{2,1,0:T(8,128)(2,1)S(1)} %pad_maximum_fusion.3.refs_9_), channel_id=1, source_target_pairs={{0,2},{1,3},{2,0},{3,1},{4,6},{5,7},{6,4},{7,5},{8,10},{9,11},{10,... | collective-permute-start | bytes 1179656 | tf_op jit(solution)/shard_map/ppermute | solution.py:391
  45.3 17.3 %collective-permute-start.20 = (bf16[4,48,1024]{2,1,0:T(8,128)(2,1)S(1)}, bf16[4,48,1024]{2,1,0:T(8,128)(2,1)S(1)}, u32[]{:S(2)}, u32[]{:S(2)}) collective-permute-start(bf16[4,48,1024]{2,1,0:T(8,128)(2,1)S(1)} %pad_maximum_fusion.3.refs_9_), channel_id=1, source_target_pairs={{0,4},{1,5},{2,6},{3,7},{4,0},{5,1},{6,2},{7,3},{8,12},{9,13},{10,... | collective-permute-start | bytes 1179656 | tf_op jit(solution)/shard_map/ppermute | solution.py:391
  46.5 31.3 %collective-permute-start.28 = (bf16[4,48,1024]{2,1,0:T(8,128)(2,1)S(1)}, bf16[4,48,1024]{2,1,0:T(8,128)(2,1)}, u32[]{:S(2)}, u32[]{:S(2)}) collective-permute-start(bf16[4,48,1024]{2,1,0:T(8,128)(2,1)S(1)} %pad_maximum_fusion.3.refs_9_), channel_id=1, source_target_pairs={{0,1},{1,0},{2,3},{3,2},{4,5},{5,4},{6,7},{7,6},{8,9},{9,8},{10,11... | collective-permute-start | bytes 1179656 | tf_op jit(solution)/shard_map/ppermute | solution.py:391
  49.7 20.2 %collective-permute-start.21 = (bf16[4,48,1152]{2,1,0:T(8,128)(2,1)S(1)}, bf16[4,48,1152]{2,1,0:T(8,128)(2,1)S(1)}, u32[]{:S(2)}, u32[]{:S(2)}) collective-permute-start(bf16[4,48,1152]{2,1,0:T(8,128)(2,1)S(1)} %pad_maximum_fusion.refs_19_), channel_id=1, source_target_pairs={{0,2},{1,3},{2,0},{3,1},{4,6},{5,7},{6,4},{7,5},{8,10},{9,11},{10,... | collective-permute-start | bytes 1327112 | tf_op jit(solution)/shard_map/ppermute | solution.py:391
  51.0 19.4 %collective-permute-start.22 = (bf16[4,48,1152]{2,1,0:T(8,128)(2,1)S(1)}, bf16[4,48,1152]{2,1,0:T(8,128)(2,1)S(1)}, u32[]{:S(2)}, u32[]{:S(2)}) collective-permute-start(bf16[4,48,1152]{2,1,0:T(8,128)(2,1)S(1)} %pad_maximum_fusion.refs_19_), channel_id=1, source_target_pairs={{0,4},{1,5},{2,6},{3,7},{4,0},{5,1},{6,2},{7,3},{8,12},{9,13},{10,... | collective-permute-start | bytes 1327112 | tf_op jit(solution)/shard_map/ppermute | solution.py:391
  60.1 21.1 %collective-permute-start.35 = (bf16[4,48,1152]{2,1,0:T(8,128)(2,1)S(1)}, bf16[4,48,1152]{2,1,0:T(8,128)(2,1)S(1)}, u32[]{:S(2)}, u32[]{:S(2)}) collective-permute-start(bf16[4,48,1152]{2,1,0:T(8,128)(2,1)S(1)} %pad_maximum_fusion.refs_19_), channel_id=1, source_target_pairs={{0,1},{1,0},{2,3},{3,2},{4,5},{5,4},{6,7},{7,6},{8,9},{9,8},{10,11... | collective-permute-start | bytes 1327112 | tf_op jit(solution)/shard_map/ppermute | solution.py:391
  62.6 16.5 %collective-permute-start.29 = (bf16[4,48,1024]{2,1,0:T(8,128)(2,1)S(1)}, bf16[4,48,1024]{2,1,0:T(8,128)(2,1)}, u32[]{:S(2)}, u32[]{:S(2)}) collective-permute-start(bf16[4,48,1024]{2,1,0:T(8,128)(2,1)S(1)} %collective-permute-done.19.refs_10_), channel_id=1, source_target_pairs={{0,1},{1,0},{2,3},{3,2},{4,5},{5,4},{6,7},{7,6},{8,9},{9,8},{10,11... | collective-permute-start | bytes 1179656 | tf_op jit(solution)/shard_map/ppermute | solution.py:391
  69.9 10.3 %collective-permute-start.30 = (bf16[4,48,1024]{2,1,0:T(8,128)(2,1)S(1)}, bf16[4,48,1024]{2,1,0:T(8,128)(2,1)}, u32[]{:S(2)}, u32[]{:S(2)}) collective-permute-start(bf16[4,48,1024]{2,1,0:T(8,128)(2,1)S(1)} %collective-permute-done.20.refs_11_), channel_id=1, source_target_pairs={{0,1},{1,0},{2,3},{3,2},{4,5},{5,4},{6,7},{7,6},{8,9},{9,8},{10,11... | collective-permute-start | bytes 1179656 | tf_op jit(solution)/shard_map/ppermute | solution.py:391
  70.4 15.4 %collective-permute-start.25 = (bf16[2,256,192]{2,1,0:T(8,128)(2,1)}, bf16[2,256,192]{2,1,0:T(8,128)(2,1)S(1)}, u32[]{:S(2)}, u32[]{:S(2)}) collective-permute-start(bf16[2,256,192]{2,1,0:T(8,128)(2,1)} %get-tuple-element.132), channel_id=1, source_target_pairs={{0,2},{1,3},{2,0},{3,1},{4,6},{5,7},{6,4},{7,5},{8,10},{9,11},{10,... | collective-permute-start | bytes 589832 | tf_op jit(solution)/shard_map/ppermute | solution.py:391
  77.9 6.2 %collective-permute-start.23 = (bf16[2,48,1024]{2,1,0:T(8,128)(2,1)S(1)}, bf16[2,48,1024]{2,1,0:T(8,128)(2,1)S(1)}, u32[]{:S(2)}, u32[]{:S(2)}) collective-permute-start(bf16[2,48,1024]{2,1,0:T(8,128)(2,1)S(1)} %slice.269), channel_id=1, source_target_pairs={{0,2},{1,3},{2,0},{3,1},{4,6},{5,7},{6,4},{7,5},{8,10},{9,11},{10,... | collective-permute-start | bytes 589832 | tf_op jit(solution)/shard_map/ppermute | solution.py:391
  79.2 6.2 %collective-permute-start.24 = (bf16[2,48,1024]{2,1,0:T(8,128)(2,1)S(1)}, bf16[2,48,1024]{2,1,0:T(8,128)(2,1)}, u32[]{:S(2)}, u32[]{:S(2)}) collective-permute-start(bf16[2,48,1024]{2,1,0:T(8,128)(2,1)S(1)} %slice.270), channel_id=1, source_target_pairs={{0,4},{1,5},{2,6},{3,7},{4,0},{5,1},{6,2},{7,3},{8,12},{9,13},{10,... | collective-permute-start | bytes 589832 | tf_op jit(solution)/shard_map/ppermute | solution.py:391
  80.2 15.7 %collective-permute-start.36 = (bf16[4,48,1152]{2,1,0:T(8,128)(2,1)S(1)}, bf16[4,48,1152]{2,1,0:T(8,128)(2,1)S(1)}, u32[]{:S(2)}, u32[]{:S(2)}) collective-permute-start(bf16[4,48,1152]{2,1,0:T(8,128)(2,1)S(1)} %collective-permute-done.21.refs_20_), channel_id=1, source_target_pairs={{0,1},{1,0},{2,3},{3,2},{4,5},{5,4},{6,7},{7,6},{8,9},{9,8},{10,11... | collective-permute-start | bytes 1327112 | tf_op jit(solution)/shard_map/ppermute | solution.py:391
  81.2 14.8 %collective-permute-start.37 = (bf16[4,48,1152]{2,1,0:T(8,128)(2,1)S(1)}, bf16[4,48,1152]{2,1,0:T(8,128)(2,1)S(1)}, u32[]{:S(2)}, u32[]{:S(2)}) collective-permute-start(bf16[4,48,1152]{2,1,0:T(8,128)(2,1)S(1)} %collective-permute-done.22.refs_21_), channel_id=1, source_target_pairs={{0,1},{1,0},{2,3},{3,2},{4,5},{5,4},{6,7},{7,6},{8,9},{9,8},{10,11... | collective-permute-start | bytes 1327112 | tf_op jit(solution)/shard_map/ppermute | solution.py:391
  84.1 5.8 %collective-permute-start.33 = (bf16[2,48,1152]{2,1,0:T(8,128)(2,1)S(1)}, bf16[2,48,1152]{2,1,0:T(8,128)(2,1)S(1)}, u32[]{:S(2)}, u32[]{:S(2)}) collective-permute-start(bf16[2,48,1152]{2,1,0:T(8,128)(2,1)S(1)} %slice.273), channel_id=1, source_target_pairs={{0,2},{1,3},{2,0},{3,1},{4,6},{5,7},{6,4},{7,5},{8,10},{9,11},{10,... | collective-permute-start | bytes 663560 | tf_op jit(solution)/shard_map/ppermute | solution.py:391
  85.3 6.6 %collective-permute-start.34 = (bf16[2,48,1152]{2,1,0:T(8,128)(2,1)S(1)}, bf16[2,48,1152]{2,1,0:T(8,128)(2,1)S(1)}, u32[]{:S(2)}, u32[]{:S(2)}) collective-permute-start(bf16[2,48,1152]{2,1,0:T(8,128)(2,1)S(1)} %slice.274), channel_id=1, source_target_pairs={{0,4},{1,5},{2,6},{3,7},{4,0},{5,1},{6,2},{7,3},{8,12},{9,13},{10,... | collective-permute-start | bytes 663560 | tf_op jit(solution)/shard_map/ppermute | solution.py:391
  85.7 8.8 %collective-permute-start.31 = (bf16[2,48,1024]{2,1,0:T(8,128)(2,1)S(1)}, bf16[2,48,1024]{2,1,0:T(8,128)(2,1)S(1)}, u32[]{:S(2)}, u32[]{:S(2)}) collective-permute-start(bf16[2,48,1024]{2,1,0:T(8,128)(2,1)S(1)} %collective-permute-done.23.refs_12_), channel_id=1, source_target_pairs={{0,1},{1,0},{2,3},{3,2},{4,5},{5,4},{6,7},{7,6},{8,9},{9,8},{10,11... | collective-permute-start | bytes 589832 | tf_op jit(solution)/shard_map/ppermute | solution.py:391
  112.7 16.5 %collective-permute-start.47 = (bf16[12,48,1152]{2,1,0:T(8,128)(2,1)}, bf16[12,48,1152]{2,1,0:T(8,128)(2,1)S(1)}, u32[]{:S(2)}, u32[]{:S(2)}) collective-permute-start(bf16[12,48,1152]{2,1,0:T(8,128)(2,1)} %get-tuple-element.162), channel_id=1, source_target_pairs={{0,1},{1,0},{2,3},{3,2},{4,5},{5,4},{6,7},{7,6},{8,9},{9,8},{10,11... | collective-permute-start | bytes 3981320 | tf_op jit(solution)/shard_map/ppermute | solution.py:391
  113.8 7.8 %collective-permute-start.40 = (bf16[2,256,192]{2,1,0:T(8,128)(2,1)S(1)}, bf16[2,256,192]{2,1,0:T(8,128)(2,1)S(1)}, u32[]{:S(2)}, u32[]{:S(2)}) collective-permute-start(bf16[2,256,192]{2,1,0:T(8,128)(2,1)S(1)} %copy-done.61), channel_id=1, source_target_pairs={{0,2},{1,3},{2,0},{3,1},{4,6},{5,7},{6,4},{7,5},{8,10},{9,11},{10,... | collective-permute-start | bytes 589832 | tf_op jit(solution)/shard_map/ppermute | solution.py:391
  114.8 16.7 %collective-permute-start.45 = (bf16[256,192]{1,0:T(8,128)(2,1)S(1)}, bf16[256,192]{1,0:T(8,128)(2,1)}, u32[]{:S(2)}, u32[]{:S(2)}) collective-permute-start(bf16[256,192]{1,0:T(8,128)(2,1)S(1)} %get-tuple-element.300), channel_id=1, source_target_pairs={{0,1},{1,0},{2,3},{3,2},{4,5},{5,4},{6,7},{7,6},{8,9},{9,8},{10,11... | collective-permute-start | bytes 294920 | tf_op jit(solution)/shard_map/ppermute | solution.py:391
  116.5 12.1 %collective-permute-start.43 = (bf16[2,48,1152]{2,1,0:T(8,128)(2,1)S(1)}, bf16[2,48,1152]{2,1,0:T(8,128)(2,1)S(1)}, u32[]{:S(2)}, u32[]{:S(2)}) collective-permute-start(bf16[2,48,1152]{2,1,0:T(8,128)(2,1)S(1)} %get-tuple-element.294), channel_id=1, source_target_pairs={{0,2},{1,3},{2,0},{3,1},{4,6},{5,7},{6,4},{7,5},{8,10},{9,11},{10,... | collective-permute-start | bytes 663560 | tf_op jit(solution)/shard_map/ppermute | solution.py:391
  117.7 11.0 %collective-permute-start.44 = (bf16[2,48,1152]{2,1,0:T(8,128)(2,1)S(1)}, bf16[2,48,1152]{2,1,0:T(8,128)(2,1)S(1)}, u32[]{:S(2)}, u32[]{:S(2)}) collective-permute-start(bf16[2,48,1152]{2,1,0:T(8,128)(2,1)S(1)} %get-tuple-element.293), channel_id=1, source_target_pairs={{0,4},{1,5},{2,6},{3,7},{4,0},{5,1},{6,2},{7,3},{8,12},{9,13},{10,... | collective-permute-start | bytes 663560 | tf_op jit(solution)/shard_map/ppermute | solution.py:391
  122.3 6.9 %collective-permute-start.41 = (bf16[256,192]{1,0:T(8,128)(2,1)S(1)}, bf16[256,192]{1,0:T(8,128)(2,1)S(1)}, u32[]{:S(2)}, u32[]{:S(2)}) collective-permute-start(bf16[256,192]{1,0:T(8,128)(2,1)S(1)} %get-tuple-element.302), channel_id=1, source_target_pairs={{0,1},{1,0},{2,3},{3,2},{4,5},{5,4},{6,7},{7,6},{8,9},{9,8},{10,11... | collective-permute-start | bytes 294920 | tf_op jit(solution)/shard_map/ppermute | solution.py:391
  128.6 10.2 %collective-permute-start.50 = (bf16[4,48,1024]{2,1,0:T(8,128)(2,1)}, bf16[4,48,1024]{2,1,0:T(8,128)(2,1)}, u32[]{:S(2)}, u32[]{:S(2)}) collective-permute-start(bf16[4,48,1024]{2,1,0:T(8,128)(2,1)} %get-tuple-element.160), channel_id=1, source_target_pairs={{0,1},{1,0},{2,3},{3,2},{4,5},{5,4},{6,7},{7,6},{8,9},{9,8},{10,11... | collective-permute-start | bytes 1179656 | tf_op jit(solution)/shard_map/ppermute | solution.py:391
  128.7 17.9 %collective-permute-start.46 = (bf16[12,48,1024]{2,1,0:T(8,128)(2,1)}, bf16[12,48,1024]{2,1,0:T(8,128)(2,1)}, u32[]{:S(2)}, u32[]{:S(2)}) collective-permute-start(bf16[12,48,1024]{2,1,0:T(8,128)(2,1)} %get-tuple-element.158), channel_id=1, source_target_pairs={{0,1},{1,0},{2,3},{3,2},{4,5},{5,4},{6,7},{7,6},{8,9},{9,8},{10,11... | collective-permute-start | bytes 3538952 | tf_op jit(solution)/shard_map/ppermute | solution.py:391
  129.9 13.2 %collective-permute-start.48 = (bf16[4,48,1152]{2,1,0:T(8,128)(2,1)S(1)}, bf16[4,48,1152]{2,1,0:T(8,128)(2,1)S(1)}, u32[]{:S(2)}, u32[]{:S(2)}) collective-permute-start(bf16[4,48,1152]{2,1,0:T(8,128)(2,1)S(1)} %pad_maximum_fusion.1), channel_id=1, source_target_pairs={{0,2},{1,3},{2,0},{3,1},{4,6},{5,7},{6,4},{7,5},{8,10},{9,11},{10,... | collective-permute-start | bytes 1327112 | tf_op jit(solution)/shard_map/ppermute | solution.py:391
  131.1 12.0 %collective-permute-start.49 = (bf16[4,48,1152]{2,1,0:T(8,128)(2,1)}, bf16[4,48,1152]{2,1,0:T(8,128)(2,1)S(1)}, u32[]{:S(2)}, u32[]{:S(2)}) collective-permute-start(bf16[4,48,1152]{2,1,0:T(8,128)(2,1)} %pad_maximum_fusion.2), channel_id=1, source_target_pairs={{0,4},{1,5},{2,6},{3,7},{4,0},{5,1},{6,2},{7,3},{8,12},{9,13},{10,... | collective-permute-start | bytes 1327112 | tf_op jit(solution)/shard_map/ppermute | solution.py:391
  140.9 13.6 %collective-permute-start.51 = (bf16[2,48,1024]{2,1,0:T(8,128)(2,1)}, bf16[2,48,1024]{2,1,0:T(8,128)(2,1)}, u32[]{:S(2)}, u32[]{:S(2)}) collective-permute-start(bf16[2,48,1024]{2,1,0:T(8,128)(2,1)} %get-tuple-element.296), channel_id=1, source_target_pairs={{0,2},{1,3},{2,0},{3,1},{4,6},{5,7},{6,4},{7,5},{8,10},{9,11},{10,... | collective-permute-start | bytes 589832 | tf_op jit(solution)/shard_map/ppermute | solution.py:391
  142.0 12.5 %collective-permute-start.52 = (bf16[2,48,1024]{2,1,0:T(8,128)(2,1)}, bf16[2,48,1024]{2,1,0:T(8,128)(2,1)}, u32[]{:S(2)}, u32[]{:S(2)}) collective-permute-start(bf16[2,48,1024]{2,1,0:T(8,128)(2,1)} %get-tuple-element.295), channel_id=1, source_target_pairs={{0,4},{1,5},{2,6},{3,7},{4,0},{5,1},{6,2},{7,3},{8,12},{9,13},{10,... | collective-permute-start | bytes 589832 | tf_op jit(solution)/shard_map/ppermute | solution.py:391
  144.0 14.8 %collective-permute-start.53 = (bf16[48,1152]{1,0:T(8,128)(2,1)}, bf16[48,1152]{1,0:T(8,128)(2,1)}, u32[]{:S(2)}, u32[]{:S(2)}) collective-permute-start(bf16[48,1152]{1,0:T(8,128)(2,1)} %get-tuple-element.279), channel_id=1, source_target_pairs={{0,8},{1,9},{2,10},{3,11},{4,12},{5,13},{6,14},{7,15},{8,0},{9,1},... | collective-permute-start | bytes 331784 | tf_op jit(solution)/shard_map/ppermute | solution.py:391
  144.0 14.8 %collective-permute-start.54 = (bf16[48,1152]{1,0:T(8,128)(2,1)S(1)}, bf16[48,1152]{1,0:T(8,128)(2,1)}, u32[]{:S(2)}, u32[]{:S(2)}) collective-permute-start(bf16[48,1152]{1,0:T(8,128)(2,1)S(1)} %get-tuple-element.281), channel_id=1, source_target_pairs={{0,16},{1,17},{2,18},{3,19},{4,20},{5,21},{6,22},{7,23},{8,24},{9,... | collective-permute-start | bytes 331784 | tf_op jit(solution)/shard_map/ppermute | solution.py:391
  146.6 12.3 %collective-permute-start.55 = (bf16[48,1152]{1,0:T(8,128)(2,1)S(1)}, bf16[48,1152]{1,0:T(8,128)(2,1)}, u32[]{:S(2)}, u32[]{:S(2)}) collective-permute-start(bf16[48,1152]{1,0:T(8,128)(2,1)S(1)} %get-tuple-element.280), channel_id=1, source_target_pairs={{0,24},{1,25},{2,26},{3,27},{4,28},{5,29},{6,30},{7,31},{8,16},{9,... | collective-permute-start | bytes 331784 | tf_op jit(solution)/shard_map/ppermute | solution.py:391
  157.0 16.2 %collective-permute-start.60 = (bf16[4,48,1024]{2,1,0:T(8,128)(2,1)}, bf16[4,48,1024]{2,1,0:T(8,128)(2,1)}, u32[]{:S(2)}, u32[]{:S(2)}) collective-permute-start(bf16[4,48,1024]{2,1,0:T(8,128)(2,1)} %pad_maximum_fusion.5), channel_id=1, source_target_pairs={{0,4},{1,5},{2,6},{3,7},{4,0},{5,1},{6,2},{7,3},{8,12},{9,13},{10,... | collective-permute-start | bytes 1179656 | tf_op jit(solution)/shard_map/ppermute | solution.py:391
  158.2 15.0 %collective-permute-start.59 = (bf16[4,48,1024]{2,1,0:T(8,128)(2,1)}, bf16[4,48,1024]{2,1,0:T(8,128)(2,1)}, u32[]{:S(2)}, u32[]{:S(2)}) collective-permute-start(bf16[4,48,1024]{2,1,0:T(8,128)(2,1)} %pad_maximum_fusion.4), channel_id=1, source_target_pairs={{0,2},{1,3},{2,0},{3,1},{4,6},{5,7},{6,4},{7,5},{8,10},{9,11},{10,... | collective-permute-start | bytes 1179656 | tf_op jit(solution)/shard_map/ppermute | solution.py:391
  160.1 13.1 %collective-permute-start.72 = (bf16[24,1152]{1,0:T(8,128)(2,1)S(1)}, bf16[24,1152]{1,0:T(8,128)(2,1)S(1)}, u32[]{:S(2)}, u32[]{:S(2)}) collective-permute-start(bf16[24,1152]{1,0:T(8,128)(2,1)S(1)} %broadcast_select_fusion.2), channel_id=1, source_target_pairs={{0,1},{1,0},{2,3},{3,2},{4,5},{5,4},{6,7},{7,6},{8,9},{9,8},{10,11... | collective-permute-start | bytes 165896 | tf_op jit(solution)/shard_map/ppermute | solution.py:391
  172.6 16.1 %collective-permute-start.57 = (bf16[256,768]{1,0:T(8,128)(2,1)}, bf16[256,768]{1,0:T(8,128)(2,1)S(1)}, u32[]{:S(2)}, u32[]{:S(2)}) collective-permute-start(bf16[256,768]{1,0:T(8,128)(2,1)} %get-tuple-element.184), channel_id=1, source_target_pairs={{0,1},{1,0},{2,3},{3,2},{4,5},{5,4},{6,7},{7,6},{8,9},{9,8},{10,11... | collective-permute-start | bytes 1179656 | tf_op jit(solution)/shard_map/ppermute | solution.py:391
  172.7 22.9 %collective-permute-start.56 = (bf16[256,768]{1,0:T(8,128)(2,1)}, bf16[256,768]{1,0:T(8,128)(2,1)S(1)}, u32[]{:S(2)}, u32[]{:S(2)}) collective-permute-start(bf16[256,768]{1,0:T(8,128)(2,1)} %get-tuple-element.182), channel_id=1, source_target_pairs={{0,1},{1,0},{2,3},{3,2},{4,5},{5,4},{6,7},{7,6},{8,9},{9,8},{10,11... | collective-permute-start | bytes 1179656 | tf_op jit(solution)/shard_map/ppermute | solution.py:391
  174.8 4.4 %collective-permute-start.68 = (bf16[48,1024]{1,0:T(8,128)(2,1)S(1)}, bf16[48,1024]{1,0:T(8,128)(2,1)S(1)}, u32[]{:S(2)}, u32[]{:S(2)}) collective-permute-start(bf16[48,1024]{1,0:T(8,128)(2,1)S(1)} %get-tuple-element.282), channel_id=1, source_target_pairs={{0,8},{1,9},{2,10},{3,11},{4,12},{5,13},{6,14},{7,15},{8,0},{9,1},... | collective-permute-start | bytes 294920 | tf_op jit(solution)/shard_map/ppermute | solution.py:391
  175.7 7.9 %collective-permute-start.69 = (bf16[48,1024]{1,0:T(8,128)(2,1)S(1)}, bf16[48,1024]{1,0:T(8,128)(2,1)S(1)}, u32[]{:S(2)}, u32[]{:S(2)}) collective-permute-start(bf16[48,1024]{1,0:T(8,128)(2,1)S(1)} %get-tuple-element.284), channel_id=1, source_target_pairs={{0,16},{1,17},{2,18},{3,19},{4,20},{5,21},{6,22},{7,23},{8,24},{9,... | collective-permute-start | bytes 294920 | tf_op jit(solution)/shard_map/ppermute | solution.py:391
  177.4 9.0 %collective-permute-start.70 = (bf16[48,1024]{1,0:T(8,128)(2,1)S(1)}, bf16[48,1024]{1,0:T(8,128)(2,1)S(1)}, u32[]{:S(2)}, u32[]{:S(2)}) collective-permute-start(bf16[48,1024]{1,0:T(8,128)(2,1)S(1)} %get-tuple-element.283), channel_id=1, source_target_pairs={{0,24},{1,25},{2,26},{3,27},{4,28},{5,29},{6,30},{7,31},{8,16},{9,... | collective-permute-start | bytes 294920 | tf_op jit(solution)/shard_map/ppermute | solution.py:391
  179.2 13.5 %collective-permute-start.61 = (bf16[4,96,640]{2,1,0:T(8,128)(2,1)S(1)}, bf16[4,96,640]{2,1,0:T(8,128)(2,1)S(1)}, u32[]{:S(2)}, u32[]{:S(2)}) collective-permute-start(bf16[4,96,640]{2,1,0:T(8,128)(2,1)S(1)} %copy-done.53), channel_id=1, source_target_pairs={{0,4},{1,5},{2,6},{3,7},{4,0},{5,1},{6,2},{7,3},{8,12},{9,13},{10,... | collective-permute-start | bytes 1474568 | tf_op jit(solution)/shard_map/ppermute | solution.py:391
  188.9 10.8 %collective-permute-start.58 = (bf16[256,768]{1,0:T(8,128)(2,1)S(1)}, bf16[256,768]{1,0:T(8,128)(2,1)S(1)}, u32[]{:S(2)}, u32[]{:S(2)}) collective-permute-start(bf16[256,768]{1,0:T(8,128)(2,1)S(1)} %add_convert_fusion.1), channel_id=1, source_target_pairs={{0,2},{1,3},{2,0},{3,1},{4,6},{5,7},{6,4},{7,5},{8,10},{9,11},{10,... | collective-permute-start | bytes 1179656 | tf_op jit(solution)/shard_map/ppermute | solution.py:391
  192.9 7.2 %collective-permute-start.62 = (bf16[96,640]{1,0:T(8,128)(2,1)S(1)}, bf16[96,640]{1,0:T(8,128)(2,1)S(1)}, u32[]{:S(2)}, u32[]{:S(2)}) collective-permute-start(bf16[96,640]{1,0:T(8,128)(2,1)S(1)} %get-tuple-element.297), channel_id=1, source_target_pairs={{0,8},{1,9},{2,10},{3,11},{4,12},{5,13},{6,14},{7,15},{8,0},{9,1},... | collective-permute-start | bytes 368648 | tf_op jit(solution)/shard_map/ppermute | solution.py:391
  193.4 9.7 %collective-permute-start.63 = (bf16[96,640]{1,0:T(8,128)(2,1)S(1)}, bf16[96,640]{1,0:T(8,128)(2,1)S(1)}, u32[]{:S(2)}, u32[]{:S(2)}) collective-permute-start(bf16[96,640]{1,0:T(8,128)(2,1)S(1)} %get-tuple-element.299), channel_id=1, source_target_pairs={{0,16},{1,17},{2,18},{3,19},{4,20},{5,21},{6,22},{7,23},{8,24},{9,... | collective-permute-start | bytes 368648 | tf_op jit(solution)/shard_map/ppermute | solution.py:391
  195.5 10.4 %collective-permute-start.64 = (bf16[96,640]{1,0:T(8,128)(2,1)S(1)}, bf16[96,640]{1,0:T(8,128)(2,1)S(1)}, u32[]{:S(2)}, u32[]{:S(2)}) collective-permute-start(bf16[96,640]{1,0:T(8,128)(2,1)S(1)} %get-tuple-element.298), channel_id=1, source_target_pairs={{0,24},{1,25},{2,26},{3,27},{4,28},{5,29},{6,30},{7,31},{8,16},{9,... | collective-permute-start | bytes 368648 | tf_op jit(solution)/shard_map/ppermute | solution.py:391
  206.9 6.7 %collective-permute-start.67 = (bf16[24,640]{1,0:T(8,128)(2,1)S(1)}, bf16[24,640]{1,0:T(8,128)(2,1)S(1)}, u32[]{:S(2)}, u32[]{:S(2)}) collective-permute-start(bf16[24,640]{1,0:T(8,128)(2,1)S(1)} %get-tuple-element.316), channel_id=1, source_target_pairs={{0,1},{1,0},{2,3},{3,2},{4,5},{5,4},{6,7},{7,6},{8,9},{9,8},{10,11... | collective-permute-start | bytes 92168 | tf_op jit(solution)/shard_map/ppermute | solution.py:391
  209.2 4.3 %collective-permute-start.66 = (bf16[24,640]{1,0:T(8,128)(2,1)S(1)}, bf16[24,640]{1,0:T(8,128)(2,1)S(1)}, u32[]{:S(2)}, u32[]{:S(2)}) collective-permute-start(bf16[24,640]{1,0:T(8,128)(2,1)S(1)} %slice_bitcast_fusion.13), channel_id=1, source_target_pairs={{0,1},{1,0},{2,3},{3,2},{4,5},{5,4},{6,7},{7,6},{8,9},{9,8},{10,11... | collective-permute-start | bytes 92168 | tf_op jit(solution)/shard_map/ppermute | solution.py:391
  (80 other events, 527.5 us)

commit v3 on v1

--- a/solution.py
+++ b/solution.py
@@ -1,3 +1,5 @@
+import functools
+
 import jax
 import jax.numpy as jnp
 from jax import lax
@@ -378,10 +380,11 @@
     )
 
 
+FL = {'C2': 1, 'GO': 2, 'H1': 3, 'H2': 2, 'H3': 1, 'H5': 1, 'H7': 2, 'H8': 1, 'T3': 4, 'T4': 3, 'T5': 3, 'T6': 1, 'TA': 3, 'TC': 1}
 BF = jnp.bfloat16
 F32 = jnp.float32
 AXES = ("dp", "fsdp")
-VMEM_LIMIT = 50 * 1024 * 1024
+VMEM_LIMIT = 60 * 1024 * 1024
 
 
 def xperm(value, mask):
@@ -401,17 +404,25 @@
     return lax.dot_general(a, b, (((0,), (0,)), ((), ())), preferred_element_type=F32)
 
 
-def split_columns(first, second):
-    src = lax.broadcasted_iota(jnp.int32, (first, second), 0)
-    col = lax.broadcasted_iota(jnp.int32, (1, second), 1)
-    part = col // 256
-    inner = col % 256
-    half = inner // 128
-    lane = inner % 128
-    rotary = jnp.where(lane < 96, 192 * part + 64 * (lane // 32) + 32 * half + lane % 32, -1)
-    plain = jnp.where(inner < 192, 384 + inner, -1)
-    want = jnp.where(part < 2, rotary, plain)
-    return (src == want).astype(F32).astype(BF)
+def spread_columns(weight):
+    rows = weight.shape[0]
+    gap, end = jnp.zeros((rows, 32), weight.dtype), jnp.zeros((rows, 64), weight.dtype)
+    parts = []
+    for i in range(4):
+        parts += [weight[:, 96 * i : 96 * i + 96], gap]
+    return jnp.concatenate(parts + [weight[:, 384:576], end], axis=1)
+
+
+def pack_columns(spread, last):
+    return jnp.concatenate([spread[:, 128 * i : 128 * i + 96] for i in range(4)] + [spread[:, 512:704], last], axis=1)
+
+
+def pack_heads(block):
+    return jnp.concatenate([block[64 * i : 64 * i + 64] for i in range(4)], axis=1)
+
+
+def unpack_heads(packed):
+    return jnp.concatenate([packed[:, 192 * i : 192 * i + 192] for i in range(4)], axis=0)
 
 
 def head_lanes(width, head):
@@ -424,23 +435,66 @@
     return (lane >= 64 * head) & (lane < 64 * head + 64)
 
 
+def prologue_kernel(ids, wq, w_out, w_in, w_down, gains, near, far, mine, other):
+    f, core = ids[0], ids[2]
+    row = lax.broadcasted_iota(jnp.int32, (24, 24), 0)
+    col = lax.broadcasted_iota(jnp.int32, (24, 24), 1)
+    parts = []
+    for j in range(2):
+        spread = jnp.where(row == col, gains[j : j + 1, :], 0.0)
+        parts.append(jnp.sum(spread, axis=-1, keepdims=True))
+    lane = lax.broadcasted_iota(jnp.int32, (24, 64), 1)
+    columns = jnp.where(lane == 0, parts[0], jnp.where(lane == 1, parts[1], 0.0))
+    blocks = []
+    for j in range(4):
+        pieces = []
+        for part in range(2):
+            heads = wq[:, 768 * part + 192 * j : 768 * part + 192 * j + 192]
+            pieces += [heads[:, 64 * h + 32 * half : 64 * h + 32 * half + 32] for half in range(2) for h in range(3)]
+        blocks.append(jnp.concatenate(pieces + [wq[:, 1536 + 192 * j : 1728 + 192 * j], columns], axis=1))
+    for k, out in enumerate((near.at[0], near.at[1], far.at[0], far.at[1])):
+        place = f ^ k
+        low = jnp.where(place == 0, blocks[0], blocks[1])
+        high = jnp.where(place == 2, blocks[2], blocks[3])
+        out[...] = jnp.where(place < 2, low, high).astype(BF)
+    left = jnp.concatenate([w_in[:, :1152], w_out[:, :384], w_down[:, :640]], axis=1)
+    right = jnp.concatenate([w_in[:, 1152:], w_out[:, 384:], w_down[:, 640:], jnp.zeros((24, 128), F32)], axis=1)
+    mine[...] = jnp.where(core == 0, left, right).astype(BF)
+    other[...] = jnp.where(core == 0, right, left).astype(BF)
+
+
+def assemble_kernel(ids, q0, q1, q2, q3, mine, came, rows, other):
+    f, core = ids[0], ids[2]
+    pieces = [q[i].astype(F32) for q, i in ((q0, 0), (q1, 1), (q2, 0), (q3, 1))]
+    ordered = []
+    for place in range(4):
+        k = f ^ place
+        low = jnp.where(k == 0, pieces[0], pieces[1])
+        high = jnp.where(k == 2, pieces[2], pieces[3])
+        ordered.append(jnp.where(k < 2, low, high))
+    rows[...] = jnp.concatenate(ordered, axis=0).astype(BF)
+    one, two = mine[...].astype(F32), came[...].astype(F32)
+    other[...] = jnp.concatenate([jnp.where(core == 0, one, two), jnp.where(core == 0, two, one)], axis=0).astype(BF)
+
+
 def forward_kernel(
-    ids, t0, t1, t2, t3, cos, sin, docq, dock, w0, w1, w2, w3, w4, w5, w6, w7,
-    n16, q8, key, val, att, a0, a1, a2, a3, prob, gain, wide, wscr, sems,
+    ids, t0, t1, t2, t3, cos, sin, docq, dock, w0, w1, w2, w3,
+    q8, key, val, att, near, far, prob, gain, wide, wscr, sems,
 ):
     step = pl.program_id(0)
 
     @pl.when(step == 0)
     def _():
         copies = []
-        for k, piece in enumerate((w0, w1, w2, w3, w4, w5, w6, w7)):
+        pieces = (w0, w1, w2.at[0], w3.at[0], w2.at[1], w3.at[1], w2.at[2], w3.at[2])
+        for k, piece in enumerate(pieces):
             at = pl.multiple_of(96 * (ids[1] ^ k), 96)
             copies.append(pltpu.make_async_copy(piece, wscr.at[pl.ds(at, 96)], sems.at[k]))
             copies[-1].start()
         for copy in copies:
             copy.wait()
         weight = wscr[...]
-        wide[...] = dot_nn(weight, split_columns(640, 768)).astype(BF)
+        wide[...] = spread_columns(weight)
         row = lax.broadcasted_iota(jnp.int32, (8, 640), 0)
         col = lax.broadcasted_iota(jnp.int32, (8, 640), 1)
         pick = ((col == row + 576) & (row < 2)).astype(F32).astype(BF)
@@ -451,9 +505,7 @@
             x = piece[...].astype(F32)
             center = x - jnp.mean(x, axis=-1, keepdims=True)
             inverse = lax.rsqrt(jnp.mean(center * center, axis=-1, keepdims=True) + NORM_EPS)
-            normed = (center * inverse * gain_row).astype(BF)
-            n16[rows, :] = normed
-            mixed = dot_nn(normed, wide[...])
+            mixed = dot_nn((center * inverse * gain_row).astype(BF), wide[...])
             c, s = cos[rows, :], sin[rows, :]
             qa, qb = mixed[:, :128], mixed[:, 128:256]
             ka, kb = mixed[:, 256:384], mixed[:, 384:512]
@@ -481,23 +533,113 @@
         total += dot_nn(weights16, jnp.where(value_lanes(256, h), values, zero))
     att[...] = total[:, :192]
     low = total[:, :192].astype(BF)
-    for i, out in enumerate((a0, a1, a2, a3)):
-
-        @pl.when(step == i)
-        def _():
-            out[...] = low
+
+    @pl.when(step < 2)
+    def _():
+        near[0] = pack_heads(low)
+
+    @pl.when(step >= 2)
+    def _():
+        far[0] = pack_heads(low)
+
+
+def project_kernel(ids, t0, t1, t2, t3, cos, sin, w0, w1, w2, w3, q8, key, val, gain, wide, wscr, sems):
+    copies = []
+    pieces = (w0, w1, w2.at[0], w3.at[0], w2.at[1], w3.at[1], w2.at[2], w3.at[2])
+    for k, piece in enumerate(pieces):
+        at = pl.multiple_of(96 * (ids[1] ^ k), 96)
+        copies.append(pltpu.make_async_copy(piece, wscr.at[pl.ds(at, 96)], sems.at[k]))
+        copies[-1].start()
+    for copy in copies:
+        copy.wait()
+    weight = wscr[...]
+    wide[...] = spread_columns(weight)
+    row = lax.broadcasted_iota(jnp.int32, (8, 640), 0)
+    col = lax.broadcasted_iota(jnp.int32, (8, 640), 1)
+    pick = ((col == row + 576) & (row < 2)).astype(F32).astype(BF)
+    gain[...] = dot_nt(pick, weight)
+    gain_row = gain[0:1, :]
+    for i, piece in enumerate((t0, t1, t2, t3)):
+        rows = slice(256 * i, 256 * i + 256)
+        x = piece[...].astype(F32)
+        center = x - jnp.mean(x, axis=-1, keepdims=True)
+        inverse = lax.rsqrt(jnp.mean(center * center, axis=-1, keepdims=True) + NORM_EPS)
+        mixed = dot_nn((center * inverse * gain_row).astype(BF), wide[...])
+        c, s = cos[rows, :], sin[rows, :]
+        qa, qb = mixed[:, :128], mixed[:, 128:256]
+        ka, kb = mixed[:, 256:384], mixed[:, 384:512]
+        q8[rows, :128] = ((qa * c - qb * s).astype(BF).astype(F32) * 0.125).astype(BF)
+        q8[rows, 128:] = ((qb * c + qa * s).astype(BF).astype(F32) * 0.125).astype(BF)
+        key[rows, :128] = (ka * c - kb * s).astype(BF)
+        key[rows, 128:] = (kb * c + ka * s).astype(BF)
+        val[rows, :] = mixed[:, 512:].astype(BF)
+
+
+def attend_kernel(q8, key, val, docq, dock, att, near, far, prob):
+    step = pl.program_id(0)
+    rows = pl.ds(pl.multiple_of(step * 256, 256), 256)
+    queries = q8[rows, :]
+    keys = key[...]
+    values = val[...]
+    same = docq[rows, :] == dock[...]
+    total = jnp.zeros((256, 256), F32)
+    zero = jnp.zeros((), BF)
+    for h in range(3):
+        scores = dot_nt(jnp.where(head_lanes(256, h), queries, zero), keys)
+        scores = jnp.where(same, scores, MASKED)
+        peak = jnp.max(scores, axis=-1, keepdims=True)
+        weights = jnp.exp(scores - peak)
+        scale = 1.0 / jnp.sum(weights, axis=-1, keepdims=True)
+        weights16 = (weights * scale).astype(BF)
+        prob[h] = weights16
+        total += dot_nn(weights16, jnp.where(value_lanes(256, h), values, zero))
+    att[...] = total[:, :192]
+    low = total[:, :192].astype(BF)
+
+    @pl.when(step < 2)
+    def _():
+        near[0] = pack_heads(low)
+
+    @pl.when(step >= 2)
+    def _():
+        far[0] = pack_heads(low)
 
 
 def full(shape):
     return pl.BlockSpec(shape, lambda *_: (0,) * len(shape))
 
 
+VM = pl.BlockSpec(memory_space=pltpu.VMEM)
 SMEM = pl.BlockSpec(memory_space=pltpu.SMEM)
-ANY = pl.BlockSpec(memory_space=pl.ANY)
+ANY = pl.BlockSpec(memory_space=pltpu.HBM)
 
 
 def shaped(shape, dtype):
     return jax.ShapeDtypeStruct(shape, dtype)
+
+
+def prologue(ids, weight_qkv, weight_out, weight_in, weight_down, norm_gains):
+    return pl.pallas_call(
+        prologue_kernel,
+        in_specs=[SMEM] + [VM] * 5,
+        out_specs=[VM] * 4,
+        out_shape=[shaped((2, 24, 640), BF)] * 2 + [shaped((24, 2176), BF)] * 2,
+        compiler_params=pltpu.CompilerParams(vmem_limit_bytes=VMEM_LIMIT),
+        cost_estimate=pl.CostEstimate(flops=10**6, bytes_accessed=10**6, transcendentals=0),
+        name="prologue",
+    )(ids, weight_qkv, weight_out, weight_in, weight_down, norm_gains)
+
+
+def assemble(ids, *pieces):
+    return pl.pallas_call(
+        assemble_kernel,
+        in_specs=[SMEM] + [VM] * 6,
+        out_specs=[VM] * 2,
+        out_shape=[shaped((96, 640), BF), shaped((48, 2176), BF)],
+        compiler_params=pltpu.CompilerParams(vmem_limit_bytes=VMEM_LIMIT),
+        cost_estimate=pl.CostEstimate(flops=10**6, bytes_accessed=10**6, transcendentals=0),
+        name="assemble",
+    )(ids, *pieces)
 
 
 def forward_attention(ids, token_pieces, cos, sin, docs, w_pieces):
@@ -508,31 +650,25 @@
         + [full((256, 768))] * 4
         + [full((1024, 128))] * 2
         + [full((1024, 1)), full((1, 1024))]
-        + [ANY] * 8,
+        + [ANY] * 4,
         out_specs=[
-            full((1024, 768)),
             full((1024, 256)),
             full((1024, 256)),
             full((1024, 256)),
             pl.BlockSpec((256, 192), lambda i: (i, 0)),
-            full((256, 192)),
-            full((256, 192)),
-            full((256, 192)),
-            full((256, 192)),
+            pl.BlockSpec((1, 64, 768), lambda i: (jnp.minimum(i, 1), 0, 0)),
+            pl.BlockSpec((1, 64, 768), lambda i: (jnp.maximum(i - 2, 0), 0, 0)),
             pl.BlockSpec((3, 256, 1024), lambda i: (0, i, 0)),
             full((8, 768)),
             full((768, 768)),
         ],
         out_shape=[
-            shaped((1024, 768), BF),
             shaped((1024, 256), BF),
             shaped((1024, 256), BF),
             shaped((1024, 256), BF),
             shaped((1024, 192), F32),
-            shaped((256, 192), BF),
-            shaped((256, 192), BF),
-            shaped((256, 192), BF),
-            shaped((256, 192), BF),
+            shaped((2, 64, 768), BF),
+            shaped((2, 64, 768), BF),
             shaped((3, 1024, 1024), BF),
             shaped((8, 768), F32),
             shaped((768, 768), BF),
@@ -544,54 +680,96 @@
     )(ids, *token_pieces, cos, sin, docs[:, None], docs[None, :], *w_pieces)
 
 
+def project(ids, token_pieces, cos, sin, w_pieces):
+    return pl.pallas_call(
+        project_kernel,
+        in_specs=[SMEM] + [VM] * 6 + [ANY] * 4,
+        out_specs=[VM] * 5,
+        out_shape=[
+            shaped((1024, 256), BF),
+            shaped((1024, 256), BF),
+            shaped((1024, 256), BF),
+            shaped((8, 768), F32),
+            shaped((768, 768), BF),
+        ],
+        scratch_shapes=[pltpu.VMEM((768, 640), BF), pltpu.SemaphoreType.DMA((8,))],
+        compiler_params=pltpu.CompilerParams(vmem_limit_bytes=VMEM_LIMIT),
+        cost_estimate=pl.CostEstimate(flops=3 * 10**9, bytes_accessed=8 * 10**6, transcendentals=0),
+        name="project",
+    )(ids, *token_pieces, cos, sin, *w_pieces)
+
+
+def attend(q8, key, val, docs):
+    return pl.pallas_call(
+        attend_kernel,
+        grid=(4,),
+        in_specs=[full((1024, 256))] * 3 + [full((1024, 1)), full((1, 1024))],
+        out_specs=[
+            pl.BlockSpec((256, 192), lambda i: (i, 0)),
+            pl.BlockSpec((1, 64, 768), lambda i: (jnp.minimum(i, 1), 0, 0)),
+            pl.BlockSpec((1, 64, 768), lambda i: (jnp.maximum(i - 2, 0), 0, 0)),
+            pl.BlockSpec((3, 256, 1024), lambda i: (0, i, 0)),
+        ],
+        out_shape=[
+            shaped((1024, 192), F32),
+            shaped((2, 64, 768), BF),
+            shaped((2, 64, 768), BF),
+            shaped((3, 1024, 1024), BF),
+        ],
+        compiler_params=pltpu.CompilerParams(vmem_limit_bytes=VMEM_LIMIT),
+        cost_estimate=pl.CostEstimate(flops=3 * 10**9, bytes_accessed=8 * 10**6, transcendentals=3 * 10**6),
+        name="attend",
+    )(q8, key, val, docs[:, None], docs[None, :])
+
+
 def erf_pair(x):
     cdf = 0.5 * (1.0 + lax.erf(x * (0.5**0.5)))
     density = jnp.exp(-0.5 * x * x) * (1.0 / (2.0 * 3.141592653589793) ** 0.5)
     return cdf, density
 
 
-SLOTS = 16
+def load_halves(held, w_in, w_rest, core, chip, sems):
+    groups = [[], []]
+    for owner in range(2):
+        half = core if owner == 0 else 1 - core
+        arrays = held[owner * 5 : owner * 5 + 5]
+        for group in range(4):
+            for kz in range(4):
+                rows = pl.ds(pl.multiple_of(48 * (chip ^ (kz * 4 + group)), 48), 48)
+                if group < 3:
+                    in_parts = [(arrays[group].at[kz, :, pl.ds(0, 1152)], w_in.at[half, rows])]
+                    rest_part = arrays[group].at[kz, :, pl.ds(1152, 1024)]
+                else:
+                    in_parts = [
+                        (arrays[3].at[pl.ds(48 * kz, 48)], w_in.at[half, rows, pl.ds(0, 768)]),
+                        (arrays[4].at[kz, :, pl.ds(0, 384)], w_in.at[half, rows, pl.ds(768, 384)]),
+                    ]
+                    rest_part = arrays[4].at[kz, :, pl.ds(384, 1024)]
+                for which, parts in ((0, in_parts), (1, [(rest_part, w_rest.at[half, rows])])):
+                    for source, target in parts:
+                        sem = sems.at[which, len(groups[which])]
+                        groups[which].append(pltpu.make_async_copy(source, target, sem))
+    for copy in groups[1] + groups[0]:
+        copy.start()
+    return groups
 
 
 def feed_kernel(*refs):
     ids, tok, cot, live, gain, a0, a1, a2, a3 = refs[:9]
-    first = refs[9 : 9 + SLOTS]
-    last = refs[9 + SLOTS : 9 + 2 * SLOTS]
-    (block, dmid, d0, d1, d2, d3, act16, n2low, dgate, dbr, ggain, w_in, w_out, w_down, sems) = refs[
-        9 + 2 * SLOTS :
-    ]
+    held = refs[9:-12]
+    (block, dmid, d_near, d_far, act16, n2low, dgate, dbr, ggain, w_rest, w_in, sems) = refs[-12:]
     f, core, chip = ids[0], ids[2], ids[3]
-    copies = []
-
-    def load(source, target):
-        copies.append(pltpu.make_async_copy(source, target, sems.at[len(copies)]))
-        copies[-1].start()
-
-    places = []
-    for owner in range(2):
-        half = core if owner == 0 else 1 - core
-        for group in range(8):
-            for j in range(2):
-                kx, ky, kz = (group >> 1) & 1, (group >> 2) & 1, (group & 1) * 2 + j
-                mask = kz * 4 + ky * 2 + kx
-                at = pl.multiple_of(48 * (chip ^ mask), 48)
-                places.append((owner * 8 + group, j, half, pl.ds(at, 48)))
-    for which, j, half, rows in places:
-        load(first[which].at[j, :, pl.ds(1152, 384)], w_out.at[half, rows])
-    for which, j, half, rows in places:
-        load(first[which].at[j, :, pl.ds(0, 1152)], w_in.at[half, rows])
-    for which, j, half, rows in places:
-        load(last[which].at[j], w_down.at[half, rows])
-    for copy in copies[:32]:
+    in_copies, rest_copies = load_halves(held, w_in, w_rest, core, chip, sems)
+    tok_f = tok[...].astype(F32)
+    pieces = [unpack_heads(a) for a in (a0[0], a1[1], a2[192:256, :], a3[256:320, :])]
+    heads = [pl.ds(pl.multiple_of(192 * (f ^ k), 192), 192) for k in range(4)]
+    for copy in rest_copies:
         copy.wait()
-    tok_f = tok[...].astype(F32)
-    pieces = [a[...] for a in (a0, a1, a2, a3)]
-    heads = [pl.ds(pl.multiple_of(192 * (f ^ k), 192), 192) for k in range(4)]
     left = jnp.zeros((256, 384), F32)
     right = jnp.zeros((256, 384), F32)
     for k in range(4):
-        left += dot_nn(pieces[k], w_out[0, heads[k], :])
-        right += dot_nn(pieces[k], w_out[1, heads[k], :])
+        left += dot_nn(pieces[k], w_rest[0, heads[k], :384])
+        right += dot_nn(pieces[k], w_rest[1, heads[k], :384])
     middle = tok_f + jnp.concatenate([left, right], axis=1)
     center = middle - jnp.mean(middle, axis=-1, keepdims=True)
     inverse = lax.rsqrt(jnp.mean(center * center, axis=-1, keepdims=True) + NORM_EPS)
@@ -599,7 +777,7 @@
     gain_row = gain[1:2, :]
     low = (normed * gain_row).astype(BF)
     n2low[...] = low
-    for copy in copies[32:64]:
+    for copy in in_copies:
         copy.wait()
     act = dot_nn(low, w_in[0])
     gate = dot_nn(low, w_in[1])
@@ -607,12 +785,10 @@
     gelu = act * cdf
     active = (gelu * gate).astype(BF)
     act16[...] = active
-    for copy in copies[64:]:
-        copy.wait()
     alive = live[...]
     dout = jnp.where(alive > 0.5, cot[...].astype(F32), 0.0)
     dym = dout.astype(BF)
-    dact = jnp.concatenate([dot_nn(dym, w_down[0]), dot_nn(dym, w_down[1, :, :512])], axis=1)
+    dact = jnp.concatenate([dot_nn(dym, w_rest[0, :, 384:1024]), dot_nn(dym, w_rest[1, :, 384:896])], axis=1)
     dg_front = (dact * gate * (cdf + act * density)).astype(BF)
     dg_rear = (dact * gelu).astype(BF)
     dgate[:, :1152] = dg_front
@@ -628,26 +804,27 @@
     dmid[...] = dmiddle
     dbranch = dmiddle.astype(BF)
     dbr[...] = dbranch
-    for k, out in enumerate((d0, d1, d2, d3)):
-        out[...] = (
-            dot_nt(dbranch[:, :384], w_out[0, heads[k], :]) + dot_nt(dbranch[:, 384:], w_out[1, heads[k], :])
-        ).astype(BF)
-    branch = dot_nt(active[:, :640], w_down[0]) + dot_nt(active[:, 640:], w_down[1, :, :512])
+    for k in range(4):
+        (d_near, d_far)[k // 2][k % 2] = pack_heads(
+            (
+                dot_nt(dbranch[:, :384], w_rest[0, heads[k], :384])
+                + dot_nt(dbranch[:, 384:], w_rest[1, heads[k], :384])
+            ).astype(BF)
+        )
+    branch = dot_nt(active[:, :640], w_rest[0, :, 384:1024]) + dot_nt(active[:, 640:], w_rest[1, :, 384:896])
     block[...] = jnp.where(alive > 0.5, middle + branch, 0.0).astype(BF)
 
 
-def feed_forward(ids, tokens, cotangent, live, gain, att_pieces, first, last):
+def feed_forward(ids, tokens, cotangent, live, gain, att_pieces, held):
     return pl.pallas_call(
         feed_kernel,
-        in_specs=[SMEM] + [pl.BlockSpec(memory_space=pltpu.VMEM)] * 8 + [ANY] * (2 * SLOTS),
-        out_specs=[pl.BlockSpec(memory_space=pltpu.VMEM)] * 11,
+        in_specs=[SMEM] + [VM] * 8 + [ANY] * len(held),
+        out_specs=[VM] * 9,
         out_shape=[
             shaped((256, 768), BF),
             shaped((256, 768), F32),
-            shaped((256, 192), BF),
-            shaped((256, 192), BF),
-            shaped((256, 192), BF),
-            shaped((256, 192), BF),
+            shaped((2, 64, 768), BF),
+            shaped((2, 64, 768), BF),
             shaped((256, 1152), BF),
             shaped((256, 768), BF),
             shaped((256, 2304), BF),
@@ -655,83 +832,129 @@
             shaped((8, 768), F32),
         ],
         scratch_shapes=[
+            pltpu.VMEM((2, 768, 1024), BF),
             pltpu.VMEM((2, 768, 1152), BF),
-            pltpu.VMEM((2, 768, 384), BF),
-            pltpu.VMEM((2, 768, 640), BF),
-            pltpu.SemaphoreType.DMA((96,)),
+            pltpu.SemaphoreType.DMA((2, 40)),
         ],
         compiler_params=pltpu.CompilerParams(vmem_limit_bytes=VMEM_LIMIT),
         cost_estimate=pl.CostEstimate(flops=5 * 10**9, bytes_accessed=12 * 10**6, transcendentals=10**6),
         name="feed_forward",
-    )(ids, tokens, cotangent, live, gain, *att_pieces, *first, *last)
-
-
-CHUNK = 2176
-
-
-def feed_grad_kernel(
-    ids, cot, live, act16, n2low, dgate, dbr, a0, a1, a2, a3,
-    s0, s1, s2, s3, k0, k1, k2, k3, grads, sems,
-):
-    f, core, chip = ids[0], ids[2], ids[3]
+    )(ids, tokens, cotangent, live, gain, *att_pieces, *held)
+
+
+def store_chunks(grads, sent, kept, order, core, chip, sems, what="both"):
+    copies = []
+    for slot, group in enumerate(order):
+        for kz in range(4):
+            at = pl.multiple_of(48 * (chip ^ (kz * 4 + group)), 48)
+            for half, target in ((1 - core, sent), (core, kept)):
+                copies.append(
+                    pltpu.make_async_copy(
+                        grads.at[half, pl.ds(at, 48)], target.at[slot * 4 + kz], sems.at[len(copies)]
+                    )
+                )
+                if what != "wait":
+                    copies[-1].start()
+    if what != "start":
+        for copy in copies:
+            copy.wait()
+
+
+def grad_in_kernel(ids, n2low, dgate, sent, kept, grads, sems, wait=True):
+    low = n2low[...]
+    grads[0] = dot_tn(low, dgate[:, :1152]).astype(BF)
+    grads[1] = dot_tn(low, dgate[:, 1152:]).astype(BF)
+    store_chunks(grads, sent, kept, (3, 1, 2, 0), ids[2], ids[3], sems, "both" if wait else "start")
+
+
+def grad_rest_kernel(ids, cot, live, act16, dbr, a0, a1, a2, a3, sent, kept, grads, sems, wait=True):
+    f = ids[0]
     dym = jnp.where(live[...] > 0.5, cot[...].astype(F32), 0.0).astype(BF)
     gdown = dot_tn(dym, act16[...])
-    grads[0, :, 1536:2176] = gdown[:, :640].astype(BF)
-    grads[1, :, 1536:2048] = gdown[:, 640:].astype(BF)
-    grads[1, :, 2048:2176] = jnp.zeros((768, 128), BF)
-    low = n2low[...]
-    grads[0, :, :1152] = dot_tn(low, dgate[:, :1152]).astype(BF)
-    grads[1, :, :1152] = dot_tn(low, dgate[:, 1152:]).astype(BF)
+    grads[0, :, 384:1024] = gdown[:, :640].astype(BF)
+    grads[1, :, 384:896] = gdown[:, 640:].astype(BF)
+    grads[1, :, 896:1024] = jnp.zeros((768, 128), BF)
     branch = dbr[...]
-    for k, piece in enumerate((a0, a1, a2, a3)):
+    for k, piece in enumerate((a0[0], a1[1], a2[192:256, :], a3[256:320, :])):
+        piece = unpack_heads(piece)
         rows = pl.ds(pl.multiple_of(192 * (f ^ k), 192), 192)
-        gout = dot_tn(piece[...], branch).astype(BF)
-        grads[0, rows, 1152:1536] = gout[:, :384]
-        grads[1, rows, 1152:1536] = gout[:, 384:]
-    copies = []
-    for group in (3, 1, 2, 0):
-        for kz in range(4):
-            at = pl.multiple_of(48 * (chip ^ (kz * 4 + group)), 48)
-            for half, target in ((1 - core, (s0, s1, s2, s3)[group]), (core, (k0, k1, k2, k3)[group])):
-                copies.append(
-                    pltpu.make_async_copy(grads.at[half, pl.ds(at, 48)], target.at[kz], sems.at[len(copies)])
-                )
-                copies[-1].start()
-    for copy in copies:
-        copy.wait()
-
-
-def feed_gradients(ids, cotangent, live, act16, n2low, dgate, dbr, att_pieces):
+        gout = dot_tn(piece, branch).astype(BF)
+        grads[0, rows, :384] = gout[:, :384]
+        grads[1, rows, :384] = gout[:, 384:]
+    store_chunks(grads, sent, kept, (3, 2, 1, 0), ids[2], ids[3], sems, "both" if wait else "start")
+
+
+def grads_kernel(
+    ids, cot, live, act16, dbr, a0, a1, a2, a3, n2low, dgate, sent_in, kept_in, sent_rest, kept_rest, g_in, g_rest, sems
+):
+    grad_in_kernel(ids, n2low, dgate, sent_in, kept_in, g_in, sems.at[0], False)
+    grad_rest_kernel(ids, cot, live, act16, dbr, a0, a1, a2, a3, sent_rest, kept_rest, g_rest, sems.at[1], False)
+    store_chunks(g_in, sent_in, kept_in, (3, 1, 2, 0), ids[2], ids[3], sems.at[0], "wait")
+    store_chunks(g_rest, sent_rest, kept_rest, (3, 2, 1, 0), ids[2], ids[3], sems.at[1], "wait")
+
+
+def feed_gradients(ids, *operands):
     return pl.pallas_call(
-        feed_grad_kernel,
-        in_specs=[SMEM] + [pl.BlockSpec(memory_space=pltpu.VMEM)] * 10,
-        out_specs=[ANY] * 8,
-        out_shape=[shaped((4, 48, CHUNK), BF)] * 8,
-        scratch_shapes=[pltpu.VMEM((2, 768, CHUNK), BF), pltpu.SemaphoreType.DMA((32,))],
+        grads_kernel,
+        in_specs=[SMEM] + [VM] * len(operands),
+        out_specs=[ANY] * 4,
+        out_shape=[shaped((16, 48, width), BF) for width in (1152, 1152, 1024, 1024)],
+        scratch_shapes=[
+            pltpu.VMEM((2, 768, 1152), BF),
+            pltpu.VMEM((2, 768, 1024), BF),
+            pltpu.SemaphoreType.DMA((2, 32)),
+        ],
         compiler_params=pltpu.CompilerParams(vmem_limit_bytes=VMEM_LIMIT),
-        cost_estimate=pl.CostEstimate(flops=3 * 10**9, bytes_accessed=12 * 10**6, transcendentals=0),
-        name="feed_gradients",
-    )(ids, cotangent, live, act16, n2low, dgate, dbr, *att_pieces)
-
-
-def backward_kernel(
-    ids, t0, t1, t2, t3, cos, sin, n16, q8, key, val, att, prob, d0, d1, d2, d3, gain, wide, ggain,
-    dn0, dn1, dn2, dn3, far, near, dq, dkt, dvt, grads, sems,
-):
+        cost_estimate=pl.CostEstimate(flops=3 * 10**9, bytes_accessed=16 * 10**6, transcendentals=0),
+        name="grads",
+    )(ids, *operands)
+
+
+def chunk_call(kernel, name, width, ids, *operands):
+    return pl.pallas_call(
+        kernel,
+        in_specs=[SMEM] + [VM] * len(operands),
+        out_specs=[ANY] * 2,
+        out_shape=[shaped((16, 48, width), BF)] * 2,
+        scratch_shapes=[pltpu.VMEM((2, 768, width), BF), pltpu.SemaphoreType.DMA((32,))],
+        compiler_params=pltpu.CompilerParams(vmem_limit_bytes=VMEM_LIMIT),
+        cost_estimate=pl.CostEstimate(flops=15 * 10**8, bytes_accessed=8 * 10**6, transcendentals=0),
+        name=name,
+    )(ids, *operands)
+
+
+def backward_kernel(*refs, base, blocks):
+    resumed, last = base > 0, base + blocks == 4
+    ids, t0, t1, t2, t3, cos, sin, q8, key, val, att, prob, d0, d1, gain, wide, ggain = refs[:17]
+    refs = refs[17:]
+    if blocks == 4:
+        d2, d3, refs = refs[0], refs[1], refs[2:]
+    if resumed:
+        dq_in, dkt_in, dvt_in, refs = refs[0], refs[1], refs[2], refs[3:]
+    if last:
+        dn0, dn1, dn2, dn3, far, near, dq, dkt, dvt, n16, grads, sems = refs
+    else:
+        dq, dkt, dvt = refs
     step = pl.program_id(0)
 
     @pl.when(step == 0)
     def _():
-        dkt[...] = jnp.zeros((256, 1024), F32)
-        dvt[...] = jnp.zeros((256, 1024), F32)
-
-    rows = pl.ds(pl.multiple_of(step * 256, 256), 256)
+        if resumed:
+            dkt[...] = dkt_in[...]
+            dvt[...] = dvt_in[...]
+            dq[:512, :256] = dq_in[...]
+        else:
+            dkt[...] = jnp.zeros((256, 1024), F32)
+            dvt[...] = jnp.zeros((256, 1024), F32)
+
+    rows = pl.ds(pl.multiple_of((base + step) * 256, 256), 256)
     zero = jnp.zeros((), BF)
     keys = key[...]
     values = val[...]
-    dattn = d0[...]
-    for i, piece in ((1, d1), (2, d2), (3, d3)):
-        dattn = jnp.where(step == i, piece[...], dattn)
+    dattn = unpack_heads(d0[0])
+    others = ((1, d1[1]),) if blocks == 2 else ((1, d1[1]), (2, d2[0]), (3, d3[1]))
+    for i, piece in others:
+        dattn = jnp.where(step == i, unpack_heads(piece), dattn)
     dattn = jnp.concatenate([dattn, jnp.zeros((256, 64), BF)], axis=1)
     product = dattn[:, :192].astype(F32) * att[...]
     queries_t = q8[rows, :].T
@@ -753,7 +976,10 @@
     dq[rows, :128] = (dqa * c + dqb * s).astype(BF)
     dq[rows, 128:256] = (dqb * c - dqa * s).astype(BF)
 
-    @pl.when(step == 3)
+    if not last:
+        return
+
+    @pl.when(step == blocks - 1)
     def _():
         dk = dkt[...].T
         ca, sa = cos[...], sin[...]
@@ -761,18 +987,18 @@
         dq[:, 384:512] = (dk[:, 128:] * ca - dk[:, :128] * sa).astype(BF)
         dq[:, 512:768] = dvt[...].T.astype(BF)
         ggain1 = jnp.zeros((1, 768), F32)
+        gain_row = gain[0:1, :]
         for i, (piece, out) in enumerate(((t0, dn0), (t1, dn1), (t2, dn2), (t3, dn3))):
             part = dot_nt(dq[256 * i : 256 * i + 256, :], wide[...])
             x = piece[...].astype(F32)
             center = x - jnp.mean(x, axis=-1, keepdims=True)
             inverse = lax.rsqrt(jnp.mean(center * center, axis=-1, keepdims=True) + NORM_EPS)
-            ggain1 += jnp.sum(part * (center * inverse), axis=0, keepdims=True)
+            normed = center * inverse
+            n16[256 * i : 256 * i + 256, :] = (normed * gain_row).astype(BF)
+            ggain1 += jnp.sum(part * normed, axis=0, keepdims=True)
             out[...] = part.astype(BF)
-        wide_grad = dot_tn(n16[...], dq[...]).astype(BF)
-        natural = dot_nt(wide_grad, split_columns(640, 768))
         gains = jnp.concatenate([ggain1, ggain[0:1, :], jnp.zeros((126, 768), F32)], axis=0)
-        column = jnp.concatenate([natural[:, :512], natural[:, 512:576], gains.T[:, :64]], axis=1)
-        grads[...] = column.astype(BF)
+        grads[...] = pack_columns(dot_tn(n16[...], dq[...]), gains.T[:, :64]).astype(BF)
         copies = []
         for ky, target in ((1, far), (0, near)):
             for kz in range(4):
@@ -785,32 +1011,159 @@
             copy.wait()
 
 
-def backward_attention(ids, token_pieces, cos, sin, n16, q8, key, val, att, prob, d_pieces, gain, wide, ggain):
+def backward_attention(
+    ids, token_pieces, cos, sin, q8, key, val, att, prob, d_pieces, gain, wide, ggain, base=0, blocks=4, sums=()
+):
+    last = base + blocks == 4
+    if last:
+        out_specs = [full((256, 768))] * 4 + [ANY, ANY]
+        out_shape = [shaped((256, 768), BF)] * 4 + [shaped((4, 96, 640), BF)] * 2
+        scratch = [
+            pltpu.VMEM((1024, 768), BF),
+            pltpu.VMEM((256, 1024), F32),
+            pltpu.VMEM((256, 1024), F32),
+            pltpu.VMEM((1024, 768), BF),
+            pltpu.VMEM((768, 640), BF),
+            pltpu.SemaphoreType.DMA((8,)),
+        ]
+    else:
+        out_specs = [full((512, 256)), full((256, 1024)), full((256, 1024))]
+        out_shape = [shaped((512, 256), BF), shaped((256, 1024), F32), shaped((256, 1024), F32)]
+        scratch = []
+    sum_specs = [full((512, 256)), full((256, 1024)), full((256, 1024))] if sums else []
     return pl.pallas_call(
-        backward_kernel,
-        grid=(4,),
+        functools.partial(backward_kernel, base=base, blocks=blocks),
+        grid=(blocks,),
         in_specs=[SMEM]
         + [full((256, 768))] * 4
         + [full((1024, 128))] * 2
-        + [full((1024, 768))]
         + [full((1024, 256))] * 3
-        + [pl.BlockSpec((256, 192), lambda i: (i, 0))]
-        + [pl.BlockSpec((3, 256, 1024), lambda i: (0, i, 0))]
-        + [full((256, 192))] * 4
-        + [full((8, 768)), full((768, 768)), full((8, 768))],
-        out_specs=[full((256, 768))] * 4 + [ANY, ANY],
-        out_shape=[shaped((256, 768), BF)] * 4 + [shaped((4, 96, 640), BF)] * 2,
-        scratch_shapes=[
-            pltpu.VMEM((1024, 768), BF),
-            pltpu.VMEM((256, 1024), F32),
-            pltpu.VMEM((256, 1024), F32),
-            pltpu.VMEM((768, 640), BF),
-            pltpu.SemaphoreType.DMA((8,)),
-        ],
+        + [pl.BlockSpec((256, 192), lambda i: (base + i, 0))]
+        + [pl.BlockSpec((3, 256, 1024), lambda i: (0, base + i, 0))]
+        + [full((2, 64, 768))] * 2
+        + [full((8, 768)), full((768, 768)), full((8, 768))]
+        + [full((2, 64, 768))] * (len(d_pieces) - 2)
+        + sum_specs,
+        out_specs=out_specs,
+        out_shape=out_shape,
+        scratch_shapes=scratch,
         compiler_params=pltpu.CompilerParams(vmem_limit_bytes=VMEM_LIMIT),
-        cost_estimate=pl.CostEstimate(flops=8 * 10**9, bytes_accessed=16 * 10**6, transcendentals=0),
+        cost_estimate=pl.CostEstimate(flops=2 * blocks * 10**9, bytes_accessed=16 * 10**6, transcendentals=0),
         name="backward_attention",
-    )(ids, *token_pieces, cos, sin, n16, q8, key, val, att, prob, *d_pieces, gain, wide, ggain)
+    )(ids, *token_pieces, cos, sin, q8, key, val, att, prob, *d_pieces[:2], gain, wide, ggain, *d_pieces[2:], *sums)
+
+
+def sum_heads_kernel(ids, e0, e1, e2, e3, near, far):
+    f = ids[0]
+    total = e0[...].astype(F32) + e1[...].astype(F32) + e2[...].astype(F32) + e3[...].astype(F32)
+    pieces = [total[24 * j : 24 * j + 24, :] for j in range(4)]
+    for k, out in enumerate((near.at[0], near.at[1], far.at[0], far.at[1])):
+        place = f ^ k
+        low = jnp.where(place == 0, pieces[0], pieces[1])
+        high = jnp.where(place == 2, pieces[2], pieces[3])
+        out[...] = jnp.where(place < 2, low, high).astype(BF)
+
+
+def sum_heads(ids, *pieces):
+    return pl.pallas_call(
+        sum_heads_kernel,
+        in_specs=[SMEM] + [VM] * 4,
+        out_specs=[VM] * 2,
+        out_shape=[shaped((2, 24, 640), BF)] * 2,
+        compiler_params=pltpu.CompilerParams(vmem_limit_bytes=VMEM_LIMIT),
+        cost_estimate=pl.CostEstimate(flops=10**6, bytes_accessed=10**6, transcendentals=0),
+        name="sum_heads",
+    )(ids, *pieces)
+
+
+def sum_rows_kernel(ids, a0, a1, a2, a3, b0, b1, b2, b3, mine, other):
+    core = ids[2]
+    one = a0[...].astype(F32) + a1[...].astype(F32) + a2[...].astype(F32) + a3[...].astype(F32)
+    two = b0[...].astype(F32) + b1[...].astype(F32) + b2[...].astype(F32) + b3[...].astype(F32)
+    rows = jnp.concatenate([one, two], axis=1)
+    mine[...] = jnp.where(core == 0, rows[:24], rows[24:]).astype(BF)
+    other[...] = jnp.where(core == 0, rows[24:], rows[:24]).astype(BF)
+
+
+def sum_rows(ids, *pieces):
+    return pl.pallas_call(
+        sum_rows_kernel,
+        in_specs=[SMEM] + [VM] * 8,
+        out_specs=[VM] * 2,
+        out_shape=[shaped((24, 2176), BF)] * 2,
+        compiler_params=pltpu.CompilerParams(vmem_limit_bytes=VMEM_LIMIT),
+        cost_estimate=pl.CostEstimate(flops=10**6, bytes_accessed=10**6, transcendentals=0),
+        name="sum_rows",
+    )(ids, *pieces)
+
+
+def store_update(gradient, state, outs, rate):
+    master, first, second, average = [ref[...] for ref in state]
+    for out, value in zip(outs, adam_update(master, first, second, average, gradient, rate)):
+        out[...] = value
+
+
+def update_rows_kernel(ids, mine, came, *refs):
+    core = ids[2]
+    one, two = mine[...].astype(F32), came[...].astype(F32)
+    left, right = jnp.where(core == 0, one, two), jnp.where(core == 0, two, one)
+    grads = (
+        jnp.concatenate([left[:, :1152], right[:, :1152]], axis=1),
+        jnp.concatenate([left[:, 1152:1536], right[:, 1152:1536]], axis=1),
+        jnp.concatenate([left[:, 1536:2176], right[:, 1536:2048]], axis=1),
+    )
+    for i, gradient in enumerate(grads):
+        store_update(gradient, refs[4 * i : 4 * i + 4], refs[12 + 5 * i : 17 + 5 * i], MATRIX_RATE)
+
+
+def update_rows(ids, mine, came, states):
+    return pl.pallas_call(
+        update_rows_kernel,
+        in_specs=[SMEM] + [VM] * 14,
+        out_specs=[VM] * 15,
+        out_shape=[shaped((24, width), dtype) for width in (2304, 768, 1152) for dtype in (F32,) * 4 + (BF,)],
+        compiler_params=pltpu.CompilerParams(vmem_limit_bytes=VMEM_LIMIT),
+        cost_estimate=pl.CostEstimate(flops=10**7, bytes_accessed=4 * 10**6, transcendentals=10**5),
+        name="update_rows",
+    )(ids, mine, came, *[array for state in states for array in state])
+
+
+def update_heads_kernel(ids, c0, c1, c2, c3, *refs):
+    f = ids[0]
+    pieces = [c[i].astype(F32) for c, i in ((c0, 0), (c1, 1), (c2, 0), (c3, 1))]
+    ordered = []
+    for place in range(4):
+        k = f ^ place
+        low = jnp.where(k == 0, pieces[0], pieces[1])
+        high = jnp.where(k == 2, pieces[2], pieces[3])
+        ordered.append(jnp.where(k < 2, low, high))
+    parts = []
+    for part in range(2):
+        for piece in ordered:
+            for h in range(3):
+                parts += [piece[:, 192 * part + 96 * half + 32 * h : 192 * part + 96 * half + 32 * h + 32] for half in range(2)]
+    gradient = jnp.concatenate(parts + [piece[:, 384:576] for piece in ordered], axis=1)
+    store_update(gradient, refs[:4], refs[8:13], MATRIX_RATE)
+    columns = sum(piece[:, 512:640] for piece in pieces)
+    row = lax.broadcasted_iota(jnp.int32, (24, 24), 0)
+    col = lax.broadcasted_iota(jnp.int32, (24, 24), 1)
+    lines = [
+        jnp.sum(jnp.where(row == col, columns[:, 64 + i : 65 + i], 0.0), axis=0, keepdims=True) for i in range(2)
+    ]
+    store_update(jnp.concatenate(lines, axis=0), refs[4:8], refs[13:18], GAIN_RATE)
+
+
+def update_heads(ids, came, state, gain_state):
+    return pl.pallas_call(
+        update_heads_kernel,
+        in_specs=[SMEM] + [VM] * 12,
+        out_specs=[VM] * 10,
+        out_shape=[shaped((24, 2304), dtype) for dtype in (F32,) * 4 + (BF,)]
+        + [shaped((2, 24), dtype) for dtype in (F32,) * 4 + (BF,)],
+        compiler_params=pltpu.CompilerParams(vmem_limit_bytes=VMEM_LIMIT),
+        cost_estimate=pl.CostEstimate(flops=10**7, bytes_accessed=3 * 10**6, transcendentals=10**5),
+        name="update_heads",
+    )(ids, *came, *state, *gain_state)
 
 
 def pack_layout(count_row, length_row, slots, own_place):
@@ -832,32 +1185,9 @@
     return document, position, living
 
 
-def by_place(pieces, low_bit, high_bit):
-    a, b, c, d = pieces
-    t0, t1 = jnp.where(low_bit, b, a), jnp.where(low_bit, a, b)
-    t2, t3 = jnp.where(low_bit, d, c), jnp.where(low_bit, c, d)
-    return [
-        jnp.where(high_bit, t2, t0),
-        jnp.where(high_bit, t3, t1),
-        jnp.where(high_bit, t0, t2),
-        jnp.where(high_bit, t1, t3),
-    ]
-
-
-def gather_halves(halves, core):
-    mine = jnp.where(core == 0, halves[0], halves[1])
-    other = jnp.where(core == 0, halves[1], halves[0])
-    came = xperm(other, 1)
-    lower, upper = jnp.where(core == 0, mine, came), jnp.where(core == 0, came, mine)
-    own = jnp.concatenate([lower, upper], axis=0)
-    z1, z2, z3 = xperm(own, 8), xperm(own, 16), xperm(own, 24)
-    p0, p1 = jnp.stack([own, z1]), jnp.stack([z2, z3])
-    x0, y0 = xperm(p0, 2), xperm(p0, 4)
-    x1, y1 = xperm(p1, 2), xperm(p1, 4)
-    xy0 = xperm(y0, 2)
-    xy1 = xperm(x1, 4)
-    held = [p0, p1, x0, x1, y0, y1, xy0, xy1]
-    return held + [xperm(piece, 1) for piece in held]
+def after(values, *signals):
+    held = lax.optimization_barrier((tuple(values), signals))
+    return list(held[0])
 
 
 def fast_body(
@@ -874,51 +1204,82 @@
     chip = group_row * 2 + side
     ids = jnp.stack([own_place, group_row, core, chip]).astype(jnp.int32)
 
-    qkv16 = weight_qkv.astype(BF)
-    blocks = qkv16.reshape(24, 3, 4, 192).transpose(2, 0, 1, 3).reshape(4, 24, 576)
-    gain_cols = jnp.concatenate([norm_gains.T.astype(BF), jnp.zeros((24, 62), BF)], axis=1)
-    blocks = jnp.concatenate([blocks, jnp.broadcast_to(gain_cols[None], (4, 24, 64))], axis=2)
-    sends = [lax.dynamic_index_in_dim(blocks, own_place ^ k, 0, keepdims=False) for k in range(4)]
-    came = [sends[0]] + [xperm(sends[k], k) for k in (1, 2, 3)]
-    rows_here = jnp.concatenate(by_place(came, core == 1, side == 1), axis=0)
-    column = [rows_here, xperm(rows_here, 8), xperm(rows_here, 16), xperm(rows_here, 24)]
-    w_pieces = []
-    for piece in column:
-        w_pieces += [piece, xperm(piece, 4)]
-
-    tok_x, tok_c = xperm(tokens, 2), xperm(tokens, 1)
+    def flag(name):
+        return FL.get(name, 0)
+
+    def exchange(near, far, direct=False):
+        if direct:
+            return [near, xperm(near, 1), xperm(far, 2), xperm(far, 3)]
+        came = xperm(far, 2)
+        return [near, xperm(near, 1), came, xperm(came, 1)]
+
+    def pick(name, values, *signals):
+        k = flag(name)
+        if k == 0:
+            return list(values)
+        chosen = signals[k - 1]
+        return after(values, *chosen)
+
+    near, far, mine, other = prologue(ids, weight_qkv, weight_out, weight_in, weight_down, norm_gains)
+    tok_c = xperm(tokens, 1)
+    rows_here, own_rows = assemble(ids, *exchange(near, far, flag("QX")), mine, xperm(other, 1))
+    rows_z = [xperm(rows_here, 8), xperm(rows_here, 16), xperm(rows_here, 24)]
+    rows_y = xperm(rows_here, 4)
+    rows_z = jnp.stack(rows_z)
+    rows_zy = xperm(rows_z, 4)
+    w_pieces = [rows_here, rows_y, rows_z, rows_zy]
+    (tokens_later,) = pick("H5", [tokens], (rows_here, tok_c), (rows_z,), (rows_y,))
+    tok_x = xperm(tokens_later, 2)
     token_pieces = [tokens, tok_c, tok_x, xperm(tok_x, 1)]
 
-    in16, out16, down16 = weight_in.astype(BF), weight_out.astype(BF), weight_down.astype(BF)
-    down16 = jnp.pad(down16, ((0, 0), (0, 128)))
-    first = gather_halves(
-        [
-            jnp.concatenate([in16[:, 1152 * h : 1152 * h + 1152], out16[:, 384 * h : 384 * h + 384]], axis=1)
-            for h in range(2)
-        ],
-        core,
-    )
-    last = gather_halves([down16[:, 640 * h : 640 * h + 640] for h in range(2)], core)
+    column0 = own_rows
+    (own_rows,) = pick("H1", [own_rows], (rows_z, rows_y), (rows_z,), (rows_y,), (rows_zy,))
+    column = [own_rows, xperm(own_rows, 8), xperm(own_rows, 16), xperm(own_rows, 24)]
+    held = jnp.stack(column)
 
     count_row = lax.dynamic_index_in_dim(counts, group_row, 0, keepdims=False)
     length_row = lax.dynamic_index_in_dim(lengths, group_row, 0, keepdims=False)
+    count_row, length_row = pick("H2", [count_row, length_row], (rows_here,), (rows_z,), (rows_zy,))
     docs, position, living = pack_layout(count_row, length_row, slots, own_place)
     speeds = ROTARY_BASE ** (-(jnp.arange(HD // 2, dtype=F32) * (2.0 / HD)))
     angles = position.astype(F32)[:, None] * jnp.tile(speeds, 4)[None, :]
     cos, sin = jnp.cos(angles), jnp.sin(angles)
     live = living[:slots, None].astype(F32)
 
-    n16, q8, key, val, att, a0, a1, a2, a3, prob, gain, wide = forward_attention(
-        ids, token_pieces, cos, sin, docs, w_pieces
-    )
-    att_pieces = [a0, xperm(a1, 1), xperm(a2, 2), xperm(a3, 3)]
-    block_out, dmiddle, d0, d1, d2, d3, act16, n2low, dgate, dbr, ggain = feed_forward(
-        ids, tokens, cotangent, live, gain, att_pieces, first, last
-    )
-    d_pieces = [d0, xperm(d1, 1), xperm(d2, 2), xperm(d3, 3)]
-    s0, s1, s2, s3, k0, k1, k2, k3 = feed_gradients(
-        ids, cotangent, live, act16, n2low, dgate, dbr, att_pieces
-    )
+    if flag("FS"):
+        held_x, held_y = xperm(held, 2), xperm(held, 4)
+        (cos_ready,) = pick("H3", [cos], (held,), (column[-1],))
+        q8, key, val, gain, wide = project(ids, token_pieces, cos_ready, sin, w_pieces)
+        (q8_ready,) = pick("H8", [q8], (held,), (column[0],), (column[0], column[1]))
+        att, near, far, prob = attend(q8_ready, key, val, docs)
+    else:
+        held_x, held_y = xperm(held, 2), xperm(held, 4)
+        (cos_ready,) = pick("H3", [cos], (held,), (column[-1],))
+        q8, key, val, att, near, far, prob, gain, wide = forward_attention(
+            ids, token_pieces, cos_ready, sin, docs, w_pieces
+        )
+    ready_x, ready_y = pick("H4", [held_x, held_y], (q8,), (near,))
+    by_x = jnp.concatenate([ready_y[:, :, :768].reshape(192, 768), far.reshape(128, 768)], axis=0)
+    (from_x,) = pick("H6", [ready_x], (near,), (by_x,))
+    by_x, by_y = xperm(by_x, 2), xperm(from_x[:, :, 768:], 4)
+    held = [held, held_x, held_y]
+    held = pick("H7", held, (q8,), (near,), (by_x,))
+    (near,) = pick("H9", [near], (by_x,), (by_y,))
+    if flag("HC") == 1:
+        pair = xperm(jnp.concatenate(held[1:], axis=0), 1)
+        held_c = [xperm(held[0], 1), pair[:4], pair[4:]]
+    elif flag("HC") == 2:
+        trio = xperm(jnp.concatenate(held, axis=0), 1)
+        held_c = [trio[:4], trio[4:8], trio[8:]]
+    else:
+        held_c = [xperm(piece, 1) for piece in held]
+    by_x_c, by_y_c = xperm(by_x, 1), xperm(by_y, 1)
+    att_pieces = [near, xperm(near, 1), by_x, by_x_c]
+    held = held + [by_x, by_y] + held_c + [by_x_c, by_y_c]
+    block_out, dmiddle, d_near, d_far, act16, n2low, dgate, dbr, ggain = feed_forward(
+        ids, tokens, cotangent, live, gain, att_pieces, held
+    )
+    d_pieces = exchange(d_near, d_far, flag("DX"))
 
     def add(*parts):
         total = parts[0].astype(F32)
@@ -926,53 +1287,170 @@
             total = total + part.astype(F32)
         return total.astype(BF)
 
-    e3 = add(k3, xperm(s3, 1))
-    e1 = add(k1, xperm(s1, 1))
-    e2 = add(k2, xperm(s2, 1))
-    e0 = add(k0, xperm(s0, 1))
-    to_y = xperm(e3[:2], 2)
-    to_x = xperm(e3[2:], 4)
-    x0 = xperm(e1[:2], 2)
-    y1 = xperm(e2[2:], 4)
-    y0 = xperm(add(e2[:2], to_y), 4)
-    x1 = xperm(add(e1[2:], to_x), 2)
-    f0 = add(e0[:2], x0, y0)
-    f1 = add(e0[2:], x1, y1)
-    chip_rows = add(f0[0], xperm(f0[1], 8), xperm(f1[0], 16), xperm(f1[1], 24))
-    lower, upper = chip_rows[:24], chip_rows[24:]
-    mine, other = jnp.where(core == 0, lower, upper), jnp.where(core == 0, upper, lower)
-    came = xperm(other, 1)
-    half0 = jnp.where(core == 0, mine, came).astype(F32)
-    half1 = jnp.where(core == 0, came, mine).astype(F32)
-    grad_in = jnp.concatenate([half0[:, :1152], half1[:, :1152]], axis=1)
-    grad_out = jnp.concatenate([half0[:, 1152:1536], half1[:, 1152:1536]], axis=1)
-    grad_down = jnp.concatenate([half0[:, 1536:2176], half1[:, 1536:2048]], axis=1)
-
-    dn0, dn1, dn2, dn3, far, near = backward_attention(
-        ids, token_pieces, cos, sin, n16, q8, key, val, att, prob, d_pieces, gain, wide, ggain
-    )
-    e = add(near, xperm(far, 4))
-    dp_rows = add(e[0], xperm(e[1], 8), xperm(e[2], 16), xperm(e[3], 24)).reshape(4, 24, 640)
-    sends = [lax.dynamic_index_in_dim(dp_rows, own_place ^ k, 0, keepdims=False) for k in range(4)]
-    came = [sends[0]] + [xperm(sends[k], k) for k in (1, 2, 3)]
-    placed = jnp.stack(by_place([piece.astype(F32) for piece in came], core == 1, side == 1))
-    grad_qkv = placed[:, :, :576].reshape(4, 24, 3, 192).transpose(1, 2, 0, 3).reshape(24, 2304)
-    grad_gains = jnp.sum(placed[:, :, 576:578], axis=0).T
-
-    own_sum, x_sum = add(dn0, xperm(dn1, 1)), add(dn2, xperm(dn3, 1))
-    dnormed = own_sum.astype(F32) + xperm(x_sum, 2).astype(F32)
+    def reduce_column(kept, rest, one, two):
+        pieces = [add(kept[12 + kz], rest[12 + kz], one[kz], two[kz]) for kz in range(4)]
+        if flag("ZM"):
+            return pieces
+        return [pieces[0]] + [xperm(pieces[kz], 8 * kz) for kz in (1, 2, 3)]
+
+    if flag("GO") == 2:
+        sent_in, kept_in, sent_rest, kept_rest = feed_gradients(
+            ids, cotangent, live, act16, dbr, *att_pieces, n2low, dgate
+        )
+    elif flag("GO"):
+        sent_rest, kept_rest = chunk_call(
+            grad_rest_kernel, "grad_rest", 1024, ids, cotangent, live, act16, dbr, *att_pieces
+        )
+        (n2_later,) = pick("T1", [n2low], (sent_rest,), (sent_rest, d_pieces[2]), (d_pieces[2],))
+        sent_in, kept_in = chunk_call(grad_in_kernel, "grad_in", 1152, ids, n2_later, dgate)
+    else:
+        sent_in, kept_in = chunk_call(grad_in_kernel, "grad_in", 1152, ids, n2low, dgate)
+        (cot_later,) = pick("T1", [cotangent], (sent_in,), (sent_in, d_pieces[2]), (d_pieces[2],))
+        sent_rest, kept_rest = chunk_call(
+            grad_rest_kernel, "grad_rest", 1024, ids, cot_later, live, act16, dbr, *att_pieces
+        )
+    if flag("C1") and flag("GO") == 1:
+        (sent_rest,) = after([sent_rest], sent_in)
+    elif flag("C1") and flag("GO") == 0:
+        (sent_in,) = after([sent_in], sent_rest)
+    (sent_in,) = pick("C2", [sent_in], (d_pieces[2],), (d_pieces[3],))
+    (sent_rest,) = pick("C3", [sent_rest], (d_pieces[2],), (d_pieces[3],))
+    came_in, came_rest = xperm(sent_in, 1), xperm(sent_rest, 1)
+
+    def begin(name, kept, came):
+        kept, came = pick(name, [kept, came], tuple(signals)) if signals else (kept, came)
+        return xperm(add(kept[:2], came[:2]), 2), xperm(add(kept[2:4], came[2:4]), 4)
+
+    def middle(name, to_y, to_x, kx, rx, ky, ry, *marks):
+        kx, ky = pick(name, [kx, ky], *[(mark,) for mark in marks])
+        one = jnp.concatenate([add(kx[:2], rx[:2]), add(kx[2:], rx[2:], to_x)], axis=0)
+        two = jnp.concatenate([add(ky[:2], ry[:2], to_y), add(ky[2:], ry[2:])], axis=0)
+        return xperm(one, 2), xperm(two, 4)
+
+    signals = []
+    if flag("RV"):
+        to_in = begin("V1", kept_in[:4], came_in[:4])
+        early_rest = flag("V2") == 0
+        if early_rest:
+            to_rest = begin("V0", kept_rest[:4], came_rest[:4])
+        marks = [to_in[0], to_in[1]]
+        (key_later,) = pick("V3", [key], (to_in[0],), (kept_in, came_in), (kept_rest, came_rest))
+        if flag("V4") == 0:
+            one_in, two_in = middle("V5", *to_in, kept_in[4:8], came_in[4:8], kept_in[8:12], came_in[8:12], to_in[0])
+        if flag("BS"):
+            sums = backward_attention(
+                ids, token_pieces, cos, sin, q8, key_later, val, att, prob, d_pieces[:2], gain, wide, ggain, 0, 2
+            )
+            signals = [sums[0]]
+            if flag("V4") == 1:
+                one_in, two_in = middle(
+                    "V5", *to_in, kept_in[4:8], came_in[4:8], kept_in[8:12], came_in[8:12], sums[0]
+                )
+            if not early_rest:
+                to_rest = begin("V6", kept_rest[:4], came_rest[:4])
+            if flag("V7"):
+                one_rest, two_rest = middle(
+                    "V8", *to_rest, kept_rest[8:12], came_rest[8:12], kept_rest[4:8], came_rest[4:8], sums[0]
+                )
+            (key_last,) = pick("V9", [key], (to_in[0], to_in[1]), (one_in, two_in), (to_rest[0], to_rest[1]))
+            dn0, dn1, dn2, dn3, far, near = backward_attention(
+                ids, token_pieces, cos, sin, q8, key_last, val, att, prob, d_pieces[2:], gain, wide, ggain, 2, 2, sums
+            )
+        else:
+            dn0, dn1, dn2, dn3, far, near = backward_attention(
+                ids, token_pieces, cos, sin, q8, key_later, val, att, prob, d_pieces, gain, wide, ggain
+            )
+            if flag("V4") == 1:
+                one_in, two_in = middle(
+                    "V5", *to_in, kept_in[4:8], came_in[4:8], kept_in[8:12], came_in[8:12], near
+                )
+            signals = [near]
+            if not early_rest:
+                to_rest = begin("V6", kept_rest[:4], came_rest[:4])
+        if not (flag("BS") and flag("V7")):
+            one_rest, two_rest = middle(
+                "V8", *to_rest, kept_rest[8:12], came_rest[8:12], kept_rest[4:8], came_rest[4:8], near
+            )
+        (far,) = pick("VA", [far], (one_in, two_in), (one_rest, two_rest), (to_rest[0],))
+        far_y = xperm(far, 4)
+        along_x, along_y, then_y, then_x = one_in, two_rest, two_in, one_rest
+        column_in = reduce_column(kept_in, came_in, one_in, two_in)
+        column_rest = reduce_column(kept_rest, came_rest, one_rest, two_rest)
+    else:
+        lead_in = add(kept_in[:8], came_in[:8])
+        lead_rest = add(kept_rest[:8], came_rest[:8])
+        along_x, along_y = xperm(lead_in, 2), xperm(lead_rest, 4)
+        (key_later,) = pick("T3", [key], (lead_in, lead_rest), (lead_in,), (lead_rest,), (d_pieces[2], d_pieces[3]))
+        if flag("BS"):
+            sums = backward_attention(
+                ids, token_pieces, cos, sin, q8, key_later, val, att, prob, d_pieces[:2], gain, wide, ggain, 0, 2
+            )
+            (key_last,) = pick("T0", [key], (lead_in, lead_rest), (along_x,), (along_y,), (along_x, along_y))
+            signal = sums[0]
+            if flag("T5") >= 3:
+                along_x, along_y = after([along_x, along_y], signal)
+            if flag("T5") == 4:
+                next_in = add(kept_in[8:12], came_in[8:12], along_x[:4])
+                next_rest = add(kept_rest[8:12], came_rest[8:12], along_y[:4])
+                (key_last,) = after([key_last], next_in, next_rest)
+            dn0, dn1, dn2, dn3, far, near = backward_attention(
+                ids, token_pieces, cos, sin, q8, key_last, val, att, prob, d_pieces[2:], gain, wide, ggain, 2, 2, sums
+            )
+        else:
+            dn0, dn1, dn2, dn3, far, near = backward_attention(
+                ids, token_pieces, cos, sin, q8, key_later, val, att, prob, d_pieces, gain, wide, ggain
+            )
+        if flag("T5") in (1, 2):
+            along_x, along_y = after([along_x, along_y], *((near,) if flag("T5") == 1 else (near, far)))
+        (far,) = pick("T4", [far], (along_x, along_y), (along_x,), (along_y,))
+        far_y = xperm(far, 4)
+        next_in = add(kept_in[8:12], came_in[8:12], along_x[:4])
+        next_rest = add(kept_rest[8:12], came_rest[8:12], along_y[:4])
+        next_in, next_rest = pick("T8", [next_in, next_rest], (far_y,))
+        then_y, then_x = xperm(next_in, 4), xperm(next_rest, 2)
+        (far_y,) = pick("TA", [far_y], (then_y, then_x), (then_x,), (then_y,))
+        column_in = reduce_column(kept_in, came_in, along_x[4:], then_y)
+        column_rest = reduce_column(kept_rest, came_rest, along_y[4:], then_x)
+    if flag("ZM"):
+        wide_z = [jnp.concatenate([column_in[kz], column_rest[kz]], axis=1) for kz in range(4)]
+        wide_z = [wide_z[0]] + [xperm(wide_z[kz], 8 * kz) for kz in (1, 2, 3)]
+        column_in = [piece[:, :1152] for piece in wide_z]
+        column_rest = [piece[:, 1152:] for piece in wide_z]
+    (far_y,) = pick("TB", [far_y], (*column_in, *column_rest), tuple(column_rest), tuple(column_in))
+    e = [add(near[kz], far_y[kz]) for kz in range(4)]
+    heads = [e[0], xperm(e[1], 8), xperm(e[2], 16), xperm(e[3], 24)]
+    dn1, dn3 = pick("T6", [dn1, dn3], (far_y,), (then_x, then_y), (along_x, along_y), (e[1],))
+    if flag("DM"):
+        both = xperm(jnp.stack([dn1, dn3]), 1)
+        dn1_came, dn3_came = both[0], both[1]
+    else:
+        dn1_came, dn3_came = xperm(dn1, 1), xperm(dn3, 1)
+    x_sum = add(dn2, dn3_came)
+    x_came = xperm(x_sum, 2)
+    own_sum = add(dn0, dn1_came)
+    heads = pick("T7", heads, (x_came,))
+    mine, other = sum_rows(ids, *column_in, *column_rest)
+    states = [
+        (weight_in, first_in, second_in, average_in),
+        (weight_out, first_out, second_out, average_out),
+        (weight_down, first_down, second_down, average_down),
+    ]
+    new_rows = update_rows(ids, mine, xperm(other, 1), states)
+
+    heads = pick("TC", heads, (new_rows[0],), (other,))
+    came = exchange(*sum_heads(ids, *heads), flag("UX"))
+    new_heads = update_heads(
+        ids,
+        came,
+        (weight_qkv, first_qkv, second_qkv, average_qkv),
+        (norm_gains, first_gains, second_gains, average_gains),
+    )
+
+    dnormed = own_sum.astype(F32) + x_came.astype(F32)
     normed, inverse = norm_parts(tokens.astype(F32))
     grad_tokens = dmiddle + norm_back(dnormed * gain[0:1, :], normed, inverse)
 
-    masters = (weight_qkv, weight_out, weight_in, weight_down, norm_gains)
-    firsts = (first_qkv, first_out, first_in, first_down, first_gains)
-    seconds = (second_qkv, second_out, second_in, second_down, second_gains)
-    averages = (average_qkv, average_out, average_in, average_down, average_gains)
-    rates = (MATRIX_RATE, MATRIX_RATE, MATRIX_RATE, MATRIX_RATE, GAIN_RATE)
-    grads = (grad_qkv, grad_out, grad_in, grad_down, grad_gains)
-    updated = [
-        adam_update(masters[i], firsts[i], seconds[i], averages[i], grads[i], rates[i]) for i in range(5)
-    ]
+    updated = [new_heads[:5], new_rows[5:10], new_rows[:5], new_rows[10:], new_heads[5:]]
     return (block_out, grad_tokens) + tuple(updated[i][j] for j in range(5) for i in range(5))
 
 

time: 292 us -> 207 us (0.71); the launches traced: 287 us -> 206 us
  waiting for transfers between devices: 91.2 us -> 41.1 us
  local copies, waits for them, and re-layouts: 37.5 us -> 10.6 us
  Pallas kernels: 53.2 us -> 66.5 us
  other arithmetic: 30.7 us -> 20.6 us
  starting transfers between devices: 73 us -> 66.1 us
    ppermute x79 -> x51, waiting for transfers between devices: 91.2 us -> 41.1 us  [xperm(): return lax.ppermute(value, AXES, [(i, i ^ mask) for i in range(count)])]
    unnamed x177 -> x80, local copies, waits for them, and re-layouts: 28.7 us -> 6.6 us
    pallas_call x3 -> x9, Pallas kernels: 35.7 us -> 49 us  [the longest x1 16.5 us: backward_attention(): pl.pallas_call(functools.partial(backward_kernel, base=base, blocks=block...]
    convert_element_type x11 -> x0, other arithmetic: 7.88 us -> none  [the longest x5 5.22 us: adam_update(): master_new.astype(jnp.bfloat16)]
    ppermute x79 -> x51, starting transfers between devices: 73 us -> 66.1 us  [xperm(): return lax.ppermute(value, AXES, [(i, i ^ mask) for i in range(count)])]
    reshape x5 -> x0, local copies, waits for them, and re-layouts: 4.12 us -> none  [the longest x2 3.71 us: fast_body(): placed[:, :, :576].reshape(4, 24, 3, 192).transpose(1, 2, 0, 3)]
    convert_element_type x11 -> x6, other arithmetic: 8.37 us -> 8.51 us  [add(): return total.astype(BF)]
  transfers between devices with their start and end apart: 79 -> 51, of which waited for: 19 -> 16; matrix products, arithmetic and copies ran while one was open for 11% -> 11% of each run, Pallas kernels for 9% -> 26%
where the time goes in v3:
time: 207 us; the launch traced here: 206 us
  Pallas kernels  66.5 us (32%)
  starting transfers between devices  66.1 us (32%)
  waiting for transfers between devices  41.1 us (20%)
  other arithmetic  20.6 us (10%)
  local copies, waits for them, and re-layouts  10.6 us (5%)
    ppermute x51, starting transfers between devices, xperm(): return lax.ppermute(value, AXES, [(i, i ^ mask) for i in range(count)])  66.1 us
    ppermute x51, waiting for transfers between devices, xperm(): return lax.ppermute(value, AXES, [(i, i ^ mask) for i in range(count)])  41.1 us
    pallas_call x1, Pallas kernels, forward_attention(): pl.pallas_call(forward_kernel, grid=(4,), in_specs=[SMEM] + [full((256, 7...  17.5 us
    pallas_call x1, Pallas kernels, backward_attention(): pl.pallas_call(functools.partial(backward_kernel, base=base, blocks=block...  16.5 us
    pallas_call x1, Pallas kernels, feed_forward(): pl.pallas_call(feed_kernel, in_specs=[SMEM] + [VM] * 8 + [ANY] * len(held...  11.4 us
    convert_element_type x6, other arithmetic, add(): return total.astype(BF)  8.51 us
    pallas_call x1, Pallas kernels, feed_gradients(): pl.pallas_call(grads_kernel, in_specs=[SMEM] + [VM] * len(operands), out_...  7.8 us
    unnamed x80, local copies, waits for them, and re-layouts  6.6 us
  transfers between devices with their start and end apart: 51, of which 16 were waited for; matrix products, arithmetic and copies ran while one was open for 11% of the time, Pallas kernels for 26%

profile of v3, /device:TPU:9, one launch (start us, length us, event | category | flops | bytes accessed | tf_op | source)
XLA Modules:
  0.0 206.1 jit_solution(6622454438175535486)
XLA Ops:
  1.3 2.0 prologue.1
  3.3 1.2 collective-permute-start.1
  4.5 1.0 collective-permute-start
  6.6 1.8 collective-permute-start.2
  8.5 0.8 collective-permute-done.2.q3
  9.9 1.9 assemble.1
  11.8 1.3 collective-permute-start.6
  13.1 1.1 collective-permute-start.5
  14.2 1.1 collective-permute-start.4
  15.3 1.2 collective-permute-start.10
  16.5 0.9 dynamic-slice_reduce_fusion
  17.5 2.0 collective-permute-done.10.w1
  20.2 1.2 collective-permute-start.13
  22.6 1.1 collective-permute-done.5
  23.7 9.0 %collective-permute-start.11 = (bf16[48,2176]{1,0:T(8,128)(2,1)}, bf16[48,2176]{1,0:T(8,128)(2,1)S(1)}, u32[]{:S(2)}, u32[]{:S(2)}) collective-permute-start(bf16[48,2176]{1,0:T(8,128)(2,1)} %get-tuple-element.117), channel_id=1, source_target_pairs={{0,8},{1,9},{2,10},{3,11},{4,12},{5,13},{6,14},{7,15},{8,0},{9,1},... | collective-permute-start | bytes 626696 | tf_op jit(solution)/shard_map/ppermute | solution.py:392
  32.8 1.2 collective-permute-start.14
  34.6 1.3 collective-permute-start.8
  35.8 3.0 %multiply_sine_fusion = (f32[1024,128]{1,0:T(8,128)}, f32[1024,128]{1,0:T(8,128)}) fusion(f32[128]{0:T(128)S(1)} %mul.90, f32[1024]{0:T(1024)S(1)} %get-tuple-element.195), kind=kLoop, calls=%fused_computation.20 | loop fusion | flops 131072 | bytes 1053184 | tf_op jit(solution)/shard_map/sin | solution.py:1246
  38.9 2.8 %collective-permute-done.12 = bf16[48,2176]{1,0:T(8,128)(2,1)S(1)} collective-permute-done((bf16[48,2176]{1,0:T(8,128)(2,1)}, bf16[48,2176]{1,0:T(8,128)(2,1)S(1)}, u32[]{:S(2)}, u32[]{:S(2)}) %collective-permute-start.12) | collective-permute-done | bytes 208928 | tf_op jit(solution)/shard_map/ppermute | solution.py:392
  41.8 1.3 collective-permute-start.16
  43.1 1.2 collective-permute-start.19
  44.3 3.2 %collective-permute-start.9 = (bf16[256,768]{1,0:T(8,128)(2,1)}, bf16[256,768]{1,0:T(8,128)(2,1)S(1)}, u32[]{:S(2)}, u32[]{:S(2)}) collective-permute-start(bf16[256,768]{1,0:T(8,128)(2,1)} %collective-permute-done.8.t2.refs_3_), channel_id=1, source_target_pairs={{0,1},{1,0},{2,3},{3,2},{4,5},{5,4},{6,7},{7,6},{8,9},{9,8},{10,11... | collective-permute-start | bytes 1179656 | tf_op jit(solution)/shard_map/ppermute | solution.py:392
  48.6 0.9 fusion.14.docq
  50.2 17.5 %forward_attention.1 = (bf16[1024,256]{1,0:T(8,128)(2,1)}, bf16[1024,256]{1,0:T(8,128)(2,1)}, bf16[1024,256]{1,0:T(8,128)(2,1)}, f32[1024,192]{1,0:T(8,128)}, bf...) custom-call(s32[4]{0:T(128)} %pad_add_fusion.ids.refs_0_, ...), custom_call_target="tpu_custom_call" | custom-call | flops 6000000000 | bytes 16000000 | tf_op jit(solution)/shard_map/forward_attention/pallas_call | solution.py:646
  68.2 1.0 slice.226
  69.8 1.0 collective-permute-start.21
  71.3 10.1 %collective-permute-done.20.refs_13_ = bf16[4,48,1408]{2,1,0:T(8,128)(2,1)} collective-permute-done((bf16[4,48,1408]{2,1,0:T(8,128)(2,1)S(1)}, bf16[4,48,1408]{2,1,0:T(8,128)(2,1)}, u32[]{:S(2)}, u32[]{:S(2)}) %collective-permute-start.20) | collective-permute-done | bytes 540704 | tf_op jit(solution)/shard_map/ppermute | solution.py:392
  81.4 1.3 collective-permute-start.24
  83.0 0.8 copy.57.refs_3_.live
  83.8 1.5 collective-permute-done.18.refs_8_.refs_17_.a3
  85.4 11.4 %feed_forward.1 = (bf16[256,768]{1,0:T(8,128)(2,1)}, f32[256,768]{1,0:T(8,128)}, bf16[2,64,768]{2,1,0:T(8,128)(2,1)}, bf16[2,64,768]{2,1,0:T(8,128)(2,1)}, bf16[...) custom-call(s32[4]{0:T(128)} %pad_add_fusion.ids.refs_0_, ...), custom_call_target="tpu_custom_call" | custom-call | flops 5000000000 | bytes 12000000 | tf_op jit(solution)/shard_map/feed_forward/pallas_call | solution.py:819
  97.3 7.8 %grads.1 = (bf16[16,48,1152]{2,1,0:T(8,128)(2,1)}, bf16[16,48,1152]{2,1,0:T(8,128)(2,1)}, bf16[16,48,1024]{2,1,0:T(8,128)(2,1)}, bf16[16,48,1024]{2,1,0:T(8,128)(2,1)}) custom-call(s32[4]{0:T(128)} %pad_add_fusion.ids.refs_0_, bf16[256,768]{1,0:T(8,128)(2,1)} %cot.1, f32[256,1]{1,0:T(8,128)} %copy.57.refs_3_.live, ...), custom_call_target="tpu_custom_call" | custom-call | flops 3000000000 | bytes 16000000 | tf_op jit(solution)/shard_map/grads/pallas_call | solution.py:897
  107.3 4.6 %collective-permute-done.26.refs_18_ = bf16[2,64,768]{2,1,0:T(8,128)(2,1)S(1)} collective-permute-done((bf16[2,64,768]{2,1,0:T(8,128)(2,1)}, bf16[2,64,768]{2,1,0:T(8,128)(2,1)S(1)}, u32[]{:S(2)}, u32[]{:S(2)}) %collective-permute-start.26) | collective-permute-done | bytes 196640 | tf_op jit(solution)/shard_map/ppermute | solution.py:392
  112.6 2.9 %add_convert_fusion.1 = bf16[8,48,1024]{2,1,0:T(8,128)(2,1)} fusion(bf16[16,48,1024]{2,1,0:T(8,128)(2,1)S(1)} %collective-permute-done.28, bf16[16,48,1024]{2,1,0:T(8,128)(2,1)} %get-tuple-element.145), kind=kLoop, calls=%fused_computation.1 | loop fusion | flops 1572864 | bytes 2359296 | tf_op jit(solution)/shard_map/convert_element_type | solution.py:1288
  116.2 1.1 add_convert_fusion
  117.4 1.0 collective-permute-start.32
  119.0 16.5 %backward_attention.1 = (bf16[256,768]{1,0:T(8,128)(2,1)}, bf16[256,768]{1,0:T(8,128)(2,1)}, bf16[256,768]{1,0:T(8,128)(2,1)}, bf16[256,768]{1,0:T(8,128)(2,1)},...) custom-call(s32[4]{0:T(128)} %pad_add_fusion.ids.refs_0_, bf16[256,768]{1,0:T(8,128)(2,1)} %refs_1_.5, ...), custom_call_target="tpu_custom_call" | custom-call | flops 8000000000 | bytes 16000000 | tf_op jit(solution)/shard_map/backward_attention/pallas_call | solution.py:1034
  136.3 1.4 add_convert_fusion.3
  138.3 1.2 add_convert_fusion.2
  139.5 0.8 collective-permute-start.33
  140.3 6.9 %collective-permute-done.43 = bf16[4,48,1024]{2,1,0:T(8,128)(2,1)S(1)} collective-permute-done((bf16[4,48,1024]{2,1,0:T(8,128)(2,1)S(1)}, bf16[4,48,1024]{2,1,0:T(8,128)(2,1)S(1)}, u32[]{:S(2)}, u32[]{:S(2)}) %collective-permute-start.43) | collective-permute-done | bytes 393248 | tf_op jit(solution)/shard_map/ppermute | solution.py:392
  147.2 2.2 %fusion.26 = (bf16[48,1024]{1,0:T(8,128)(2,1)S(1)}, bf16[48,1024]{1,0:T(8,128)(2,1)S(1)}, bf16[48,1024]{1,0:T(8,128)(2,1)S(1)}, bf16[48,1024]{1,0:T(8,128)(2,1)}) fusion(bf16[4,48,1024]{2,1,0:T(8,128)(2,1)S(1)} %collective-permute-done.43, bf16[8,48,1024]{2,1,0:T(8,128)(2,1)} %collective-permute-done.29, bf16[16,48,1024]{2,1,0:T(8,128)(2,1)} %copy-done.6, ...), kind=kLoop, calls=%fused_computation.54 | loop fusion | flops 1572864 | bytes 1966080 | tf_op jit(solution)/shard_map/add | solution.py:1287
  149.4 2.1 %collective-permute-start.44 = (bf16[48,1024]{1,0:T(8,128)(2,1)S(1)}, bf16[48,1024]{1,0:T(8,128)(2,1)S(1)}, u32[]{:S(2)}, u32[]{:S(2)}) collective-permute-start(bf16[48,1024]{1,0:T(8,128)(2,1)S(1)} %get-tuple-element.203), channel_id=1, source_target_pairs={{0,8},{1,9},{2,10},{3,11},{4,12},{5,13},{6,14},{7,15},{8,0},{9,1},... | collective-permute-start | bytes 294920 | tf_op jit(solution)/shard_map/ppermute | solution.py:392
  151.5 1.8 collective-permute-start.45
  153.3 3.7 %collective-permute-done.33 = bf16[4,48,1152]{2,1,0:T(8,128)(2,1)S(1)} collective-permute-done((bf16[4,48,1152]{2,1,0:T(8,128)(2,1)S(1)}, bf16[4,48,1152]{2,1,0:T(8,128)(2,1)S(1)}, u32[]{:S(2)}, u32[]{:S(2)}) %collective-permute-start.33) | collective-permute-done | bytes 442400 | tf_op jit(solution)/shard_map/ppermute | solution.py:392
  157.0 1.8 collective-permute-start.35
  158.9 1.9 fusion.22
  160.8 2.1 %collective-permute-start.40 = (bf16[48,1152]{1,0:T(8,128)(2,1)S(1)}, bf16[48,1152]{1,0:T(8,128)(2,1)S(1)}, u32[]{:S(2)}, u32[]{:S(2)}) collective-permute-start(bf16[48,1152]{1,0:T(8,128)(2,1)S(1)} %get-tuple-element.199), channel_id=1, source_target_pairs={{0,8},{1,9},{2,10},{3,11},{4,12},{5,13},{6,14},{7,15},{8,0},{9,1},... | collective-permute-start | bytes 331784 | tf_op jit(solution)/shard_map/ppermute | solution.py:392
  162.9 1.8 collective-permute-start.41
  167.4 2.5 %collective-permute-start.37 = (bf16[96,640]{1,0:T(8,128)(2,1)S(1)}, bf16[96,640]{1,0:T(8,128)(2,1)S(1)}, u32[]{:S(2)}, u32[]{:S(2)}) collective-permute-start(bf16[96,640]{1,0:T(8,128)(2,1)S(1)} %get-tuple-element.207), channel_id=1, source_target_pairs={{0,8},{1,9},{2,10},{3,11},{4,12},{5,13},{6,14},{7,15},{8,0},{9,1},... | collective-permute-start | bytes 368648 | tf_op jit(solution)/shard_map/ppermute | solution.py:392
  169.9 1.7 collective-permute-done.41.a2
  171.6 3.2 %collective-permute-start.38 = (bf16[96,640]{1,0:T(8,128)(2,1)S(1)}, bf16[96,640]{1,0:T(8,128)(2,1)S(1)}, u32[]{:S(2)}, u32[]{:S(2)}) collective-permute-start(bf16[96,640]{1,0:T(8,128)(2,1)S(1)} %get-tuple-element.206), channel_id=1, source_target_pairs={{0,16},{1,17},{2,18},{3,19},{4,20},{5,21},{6,22},{7,23},{8,24},{9,... | collective-permute-start | bytes 368648 | tf_op jit(solution)/shard_map/ppermute | solution.py:392
  175.2 5.0 %collective-permute-start.39 = (bf16[96,640]{1,0:T(8,128)(2,1)S(1)}, bf16[96,640]{1,0:T(8,128)(2,1)S(1)}, u32[]{:S(2)}, u32[]{:S(2)}) collective-permute-start(bf16[96,640]{1,0:T(8,128)(2,1)S(1)} %get-tuple-element.205), channel_id=1, source_target_pairs={{0,24},{1,25},{2,26},{3,27},{4,28},{5,29},{6,30},{7,31},{8,16},{9,... | collective-permute-start | bytes 368648 | tf_op jit(solution)/shard_map/ppermute | solution.py:392
  180.2 2.0 sum_rows.1
  182.3 3.4 %collective-permute-start.47 = (bf16[24,2176]{1,0:T(8,128)(2,1)}, bf16[24,2176]{1,0:T(8,128)(2,1)S(1)}, u32[]{:S(2)}, u32[]{:S(2)}) collective-permute-start(bf16[24,2176]{1,0:T(8,128)(2,1)} %get-tuple-element.157), channel_id=1, source_target_pairs={{0,1},{1,0},{2,3},{3,2},{4,5},{5,4},{6,7},{7,6},{8,9},{9,8},{10,11... | collective-permute-start | bytes 313352 | tf_op jit(solution)/shard_map/ppermute | solution.py:392
  185.7 1.1 add_convert_fusion.4
  187.5 3.0 %update_rows.1 = (f32[24,2304]{1,0:T(8,128)}, f32[24,2304]{1,0:T(8,128)}, f32[24,2304]{1,0:T(8,128)}, f32[24,2304]{1,0:T(8,128)}, bf16[24,2304]{1,0:T(8,128)(2,1...) custom-call(s32[4]{0:T(128)} %pad_add_fusion.ids.refs_0_, ...), custom_call_target="tpu_custom_call" | custom-call | flops 10000000 | bytes 4000000 | tf_op jit(solution)/shard_map/update_rows/pallas_call | solution.py:1120
  191.3 1.9 sum_heads.1
  193.2 1.1 collective-permute-start.49
  194.2 0.9 collective-permute-start.48
  195.1 3.5 %collective-permute-done.49.c2 = bf16[2,24,640]{2,1,0:T(8,128)(2,1)S(1)} collective-permute-done((bf16[2,24,640]{2,1,0:T(8,128)(2,1)}, bf16[2,24,640]{2,1,0:T(8,128)(2,1)S(1)}, u32[]{:S(2)}, u32[]{:S(2)}) %collective-permute-start.49) | collective-permute-done | bytes 61472 | tf_op jit(solution)/shard_map/ppermute | solution.py:392
  198.6 1.1 collective-permute-start.50
  201.8 2.6 %update_heads.1 = (f32[24,2304]{1,0:T(8,128)}, f32[24,2304]{1,0:T(8,128)}, f32[24,2304]{1,0:T(8,128)}, f32[24,2304]{1,0:T(8,128)}, bf16[24,2304]{1,0:T(8,128)(2,...) custom-call(s32[4]{0:T(128)} %pad_add_fusion.ids.refs_0_, ...), custom_call_target="tpu_custom_call" | custom-call | flops 10000000 | bytes 3000000 | tf_op jit(solution)/shard_map/update_heads/pallas_call | solution.py:1157
  204.8 1.3 fusion.7
  (170 shorter events, 22.0 us)
Async XLA Ops:
  0.7 15.9 %copy-start = (s32[8,8]{1,0:T(8,128)S(1)}, s32[8,8]{1,0:T(8,128)}, u32[]{:S(2)}) copy-start(s32[8,8]{1,0:T(8,128)} %param.27) | copy-start | bytes 772
  0.7 33.8 %copy-start.1 = (bf16[256,768]{1,0:T(8,128)(2,1)S(1)}, bf16[256,768]{1,0:T(8,128)(2,1)}, u32[]{:S(2)}) copy-start(bf16[256,768]{1,0:T(8,128)(2,1)} %refs_1_.5) | copy-start | bytes 1179652
  3.3 3.3 %collective-permute-start.1 = (bf16[2,24,640]{2,1,0:T(8,128)(2,1)}, bf16[2,24,640]{2,1,0:T(8,128)(2,1)S(1)}, u32[]{:S(2)}, u32[]{:S(2)}) collective-permute-start(bf16[2,24,640]{2,1,0:T(8,128)(2,1)} %get-tuple-element.109), channel_id=1, source_target_pairs={{0,2},{1,3},{2,0},{3,1},{4,6},{5,7},{6,4},{7,5},{8,10},{9,11},{10,... | collective-permute-start | bytes 184328 | tf_op jit(solution)/shard_map/ppermute | solution.py:392
  4.5 3.9 %collective-permute-start = (bf16[2,24,640]{2,1,0:T(8,128)(2,1)}, bf16[2,24,640]{2,1,0:T(8,128)(2,1)S(1)}, u32[]{:S(2)}, u32[]{:S(2)}) collective-permute-start(bf16[2,24,640]{2,1,0:T(8,128)(2,1)} %get-tuple-element.108.q0), channel_id=1, source_target_pairs={{0,1},{1,0},{2,3},{3,2},{4,5},{5,4},{6,7},{7,6},{8,9},{9,8},{10,11... | collective-permute-start | bytes 184328 | tf_op jit(solution)/shard_map/ppermute | solution.py:392
  5.5 3.0 %collective-permute-start.3 = (bf16[24,2176]{1,0:T(8,128)(2,1)}, bf16[24,2176]{1,0:T(8,128)(2,1)S(1)}, u32[]{:S(2)}, u32[]{:S(2)}) collective-permute-start(bf16[24,2176]{1,0:T(8,128)(2,1)} %get-tuple-element.111), channel_id=1, source_target_pairs={{0,1},{1,0},{2,3},{3,2},{4,5},{5,4},{6,7},{7,6},{8,9},{9,8},{10,11... | collective-permute-start | bytes 313352 | tf_op jit(solution)/shard_map/ppermute | solution.py:392
  5.5 29.0 %collective-permute-start.7 = (bf16[256,768]{1,0:T(8,128)(2,1)}, bf16[256,768]{1,0:T(8,128)(2,1)S(1)}, u32[]{:S(2)}, u32[]{:S(2)}) collective-permute-start(bf16[256,768]{1,0:T(8,128)(2,1)} %refs_1_.5), channel_id=1, source_target_pairs={{0,1},{1,0},{2,3},{3,2},{4,5},{5,4},{6,7},{7,6},{8,9},{9,8},{10,11... | collective-permute-start | bytes 1179656 | tf_op jit(solution)/shard_map/ppermute | solution.py:392
  6.6 2.7 %collective-permute-start.2 = (bf16[2,24,640]{2,1,0:T(8,128)(2,1)S(1)}, bf16[2,24,640]{2,1,0:T(8,128)(2,1)S(1)}, u32[]{:S(2)}, u32[]{:S(2)}) collective-permute-start(bf16[2,24,640]{2,1,0:T(8,128)(2,1)S(1)} %collective-permute-done.1.q2), channel_id=1, source_target_pairs={{0,1},{1,0},{2,3},{3,2},{4,5},{5,4},{6,7},{7,6},{8,9},{9,8},{10,11... | collective-permute-start | bytes 184328 | tf_op jit(solution)/shard_map/ppermute | solution.py:392
  11.8 29.8 %copy-start.13 = (bf16[48,2176]{1,0:T(8,128)(2,1)S(1)}, bf16[48,2176]{1,0:T(8,128)(2,1)}, u32[]{:S(2)}) copy-start(bf16[48,2176]{1,0:T(8,128)(2,1)} %get-tuple-element.117) | copy-start | bytes 626692
  11.8 10.0 %collective-permute-start.6 = (bf16[96,640]{1,0:T(8,128)(2,1)}, bf16[96,640]{1,0:T(8,128)(2,1)S(1)}, u32[]{:S(2)}, u32[]{:S(2)}) collective-permute-start(bf16[96,640]{1,0:T(8,128)(2,1)} %get-tuple-element.112.w0), channel_id=1, source_target_pairs={{0,24},{1,25},{2,26},{3,27},{4,28},{5,29},{6,30},{7,31},{8,16},{9,... | collective-permute-start | bytes 368648 | tf_op jit(solution)/shard_map/ppermute | solution.py:392
  13.1 10.6 %collective-permute-start.5 = (bf16[96,640]{1,0:T(8,128)(2,1)}, bf16[96,640]{1,0:T(8,128)(2,1)S(1)}, u32[]{:S(2)}, u32[]{:S(2)}) collective-permute-start(bf16[96,640]{1,0:T(8,128)(2,1)} %get-tuple-element.112.w0), channel_id=1, source_target_pairs={{0,16},{1,17},{2,18},{3,19},{4,20},{5,21},{6,22},{7,23},{8,24},{9,... | collective-permute-start | bytes 368648 | tf_op jit(solution)/shard_map/ppermute | solution.py:392
  14.2 18.5 %collective-permute-start.4 = (bf16[96,640]{1,0:T(8,128)(2,1)}, bf16[96,640]{1,0:T(8,128)(2,1)S(1)}, u32[]{:S(2)}, u32[]{:S(2)}) collective-permute-start(bf16[96,640]{1,0:T(8,128)(2,1)} %get-tuple-element.112.w0), channel_id=1, source_target_pairs={{0,8},{1,9},{2,10},{3,11},{4,12},{5,13},{6,14},{7,15},{8,0},{9,1},... | collective-permute-start | bytes 368648 | tf_op jit(solution)/shard_map/ppermute | solution.py:392
  15.3 4.2 %collective-permute-start.10 = (bf16[96,640]{1,0:T(8,128)(2,1)}, bf16[96,640]{1,0:T(8,128)(2,1)S(1)}, u32[]{:S(2)}, u32[]{:S(2)}) collective-permute-start(bf16[96,640]{1,0:T(8,128)(2,1)} %get-tuple-element.112.w0), channel_id=1, source_target_pairs={{0,4},{1,5},{2,6},{3,7},{4,0},{5,1},{6,2},{7,3},{8,12},{9,13},{10,... | collective-permute-start | bytes 368648 | tf_op jit(solution)/shard_map/ppermute | solution.py:392
  20.2 18.7 %collective-permute-start.13 = (bf16[48,2176]{1,0:T(8,128)(2,1)}, bf16[48,2176]{1,0:T(8,128)(2,1)S(1)}, u32[]{:S(2)}, u32[]{:S(2)}) collective-permute-start(bf16[48,2176]{1,0:T(8,128)(2,1)} %get-tuple-element.117), channel_id=1, source_target_pairs={{0,24},{1,25},{2,26},{3,27},{4,28},{5,29},{6,30},{7,31},{8,16},{9,... | collective-permute-start | bytes 626696 | tf_op jit(solution)/shard_map/ppermute | solution.py:392
  21.8 19.8 %collective-permute-start.12 = (bf16[48,2176]{1,0:T(8,128)(2,1)}, bf16[48,2176]{1,0:T(8,128)(2,1)S(1)}, u32[]{:S(2)}, u32[]{:S(2)}) collective-permute-start(bf16[48,2176]{1,0:T(8,128)(2,1)} %get-tuple-element.117), channel_id=1, source_target_pairs={{0,16},{1,17},{2,18},{3,19},{4,20},{5,21},{6,22},{7,23},{8,24},{9,... | collective-permute-start | bytes 626696 | tf_op jit(solution)/shard_map/ppermute | solution.py:392
  23.7 18.0 %collective-permute-start.11 = (bf16[48,2176]{1,0:T(8,128)(2,1)}, bf16[48,2176]{1,0:T(8,128)(2,1)S(1)}, u32[]{:S(2)}, u32[]{:S(2)}) collective-permute-start(bf16[48,2176]{1,0:T(8,128)(2,1)} %get-tuple-element.117), channel_id=1, source_target_pairs={{0,8},{1,9},{2,10},{3,11},{4,12},{5,13},{6,14},{7,15},{8,0},{9,1},... | collective-permute-start | bytes 626696 | tf_op jit(solution)/shard_map/ppermute | solution.py:392
  32.8 15.6 %copy-start.11 = (bf16[3,96,640]{2,1,0:T(8,128)(2,1)}, bf16[3,96,640]{2,1,0:T(8,128)(2,1)S(1)}, u32[]{:S(2)}) copy-start(bf16[3,96,640]{2,1,0:T(8,128)(2,1)S(1)} %pad_maximum_fusion.2.w2) | copy-start | bytes 1105924
  32.8 16.7 %collective-permute-start.14 = (bf16[3,96,640]{2,1,0:T(8,128)(2,1)S(1)}, bf16[3,96,640]{2,1,0:T(8,128)(2,1)}, u32[]{:S(2)}, u32[]{:S(2)}) collective-permute-start(bf16[3,96,640]{2,1,0:T(8,128)(2,1)S(1)} %pad_maximum_fusion.2.w2), channel_id=1, source_target_pairs={{0,4},{1,5},{2,6},{3,7},{4,0},{5,1},{6,2},{7,3},{8,12},{9,13},{10,... | collective-permute-start | bytes 1105928 | tf_op jit(solution)/shard_map/ppermute | solution.py:392
  34.6 9.7 %collective-permute-start.8 = (bf16[256,768]{1,0:T(8,128)(2,1)S(1)}, bf16[256,768]{1,0:T(8,128)(2,1)}, u32[]{:S(2)}, u32[]{:S(2)}) collective-permute-start(bf16[256,768]{1,0:T(8,128)(2,1)S(1)} %copy-done.1), channel_id=1, source_target_pairs={{0,2},{1,3},{2,0},{3,1},{4,6},{5,7},{6,4},{7,5},{8,10},{9,11},{10,... | collective-permute-start | bytes 1179656 | tf_op jit(solution)/shard_map/ppermute | solution.py:392
  41.8 28.0 %copy-start.7 = (bf16[4,48,2176]{2,1,0:T(8,128)(2,1)}, bf16[4,48,2176]{2,1,0:T(8,128)(2,1)S(1)}, u32[]{:S(2)}) copy-start(bf16[4,48,2176]{2,1,0:T(8,128)(2,1)S(1)} %pad_maximum_fusion.refs_9_) | copy-start | bytes 2506756
  41.8 26.4 %collective-permute-start.16 = (bf16[4,48,2176]{2,1,0:T(8,128)(2,1)S(1)}, bf16[4,48,2176]{2,1,0:T(8,128)(2,1)}, u32[]{:S(2)}, u32[]{:S(2)}) collective-permute-start(bf16[4,48,2176]{2,1,0:T(8,128)(2,1)S(1)} %pad_maximum_fusion.refs_9_), channel_id=1, source_target_pairs={{0,4},{1,5},{2,6},{3,7},{4,0},{5,1},{6,2},{7,3},{8,12},{9,13},{10,... | collective-permute-start | bytes 2506760 | tf_op jit(solution)/shard_map/ppermute | solution.py:392
  43.1 24.7 %collective-permute-start.19 = (bf16[4,48,2176]{2,1,0:T(8,128)(2,1)S(1)}, bf16[4,48,2176]{2,1,0:T(8,128)(2,1)S(1)}, u32[]{:S(2)}, u32[]{:S(2)}) collective-permute-start(bf16[4,48,2176]{2,1,0:T(8,128)(2,1)S(1)} %pad_maximum_fusion.refs_9_), channel_id=1, source_target_pairs={{0,2},{1,3},{2,0},{3,1},{4,6},{5,7},{6,4},{7,5},{8,10},{9,11},{10,... | collective-permute-start | bytes 2506760 | tf_op jit(solution)/shard_map/ppermute | solution.py:392
  44.3 5.2 %collective-permute-start.9 = (bf16[256,768]{1,0:T(8,128)(2,1)}, bf16[256,768]{1,0:T(8,128)(2,1)S(1)}, u32[]{:S(2)}, u32[]{:S(2)}) collective-permute-start(bf16[256,768]{1,0:T(8,128)(2,1)} %collective-permute-done.8.t2.refs_3_), channel_id=1, source_target_pairs={{0,1},{1,0},{2,3},{3,2},{4,5},{5,4},{6,7},{7,6},{8,9},{9,8},{10,11... | collective-permute-start | bytes 1179656 | tf_op jit(solution)/shard_map/ppermute | solution.py:392
  67.7 3.1 %collective-permute-start.15 = (bf16[2,64,768]{2,1,0:T(8,128)(2,1)}, bf16[2,64,768]{2,1,0:T(8,128)(2,1)S(1)}, u32[]{:S(2)}, u32[]{:S(2)}) collective-permute-start(bf16[2,64,768]{2,1,0:T(8,128)(2,1)} %get-tuple-element.120.refs_5_.a0), channel_id=1, source_target_pairs={{0,1},{1,0},{2,3},{3,2},{4,5},{5,4},{6,7},{7,6},{8,9},{9,8},{10,11... | collective-permute-start | bytes 589832 | tf_op jit(solution)/shard_map/ppermute | solution.py:392
  67.8 17.5 %copy-start.12 = (bf16[4,48,2176]{2,1,0:T(8,128)(2,1)}, bf16[4,48,2176]{2,1,0:T(8,128)(2,1)S(1)}, u32[]{:S(2)}) copy-start(bf16[4,48,2176]{2,1,0:T(8,128)(2,1)S(1)} %collective-permute-done.19.refs_10_) | copy-start | bytes 2506756
  67.9 13.5 %collective-permute-start.20 = (bf16[4,48,1408]{2,1,0:T(8,128)(2,1)S(1)}, bf16[4,48,1408]{2,1,0:T(8,128)(2,1)}, u32[]{:S(2)}, u32[]{:S(2)}) collective-permute-start(bf16[4,48,1408]{2,1,0:T(8,128)(2,1)S(1)} %slice.227), channel_id=1, source_target_pairs={{0,4},{1,5},{2,6},{3,7},{4,0},{5,1},{6,2},{7,3},{8,12},{9,13},{10,... | collective-permute-start | bytes 1622024 | tf_op jit(solution)/shard_map/ppermute | solution.py:392
  69.2 13.5 %collective-permute-start.17 = (bf16[320,768]{1,0:T(8,128)(2,1)S(1)}, bf16[320,768]{1,0:T(8,128)(2,1)}, u32[]{:S(2)}, u32[]{:S(2)}) collective-permute-start(bf16[320,768]{1,0:T(8,128)(2,1)S(1)} %pad_maximum_fusion.1), channel_id=1, source_target_pairs={{0,2},{1,3},{2,0},{3,1},{4,6},{5,7},{6,4},{7,5},{8,10},{9,11},{10,... | collective-permute-start | bytes 1474568 | tf_op jit(solution)/shard_map/ppermute | solution.py:392
  69.8 14.0 %collective-permute-start.21 = (bf16[4,48,2176]{2,1,0:T(8,128)(2,1)S(1)}, bf16[4,48,2176]{2,1,0:T(8,128)(2,1)S(1)}, u32[]{:S(2)}, u32[]{:S(2)}) collective-permute-start(bf16[4,48,2176]{2,1,0:T(8,128)(2,1)S(1)} %pad_maximum_fusion.refs_9_), channel_id=1, source_target_pairs={{0,1},{1,0},{2,3},{3,2},{4,5},{5,4},{6,7},{7,6},{8,9},{9,8},{10,11... | collective-permute-start | bytes 2506760 | tf_op jit(solution)/shard_map/ppermute | solution.py:392
  70.8 13.0 %collective-permute-start.22 = (bf16[4,48,2176]{2,1,0:T(8,128)(2,1)S(1)}, bf16[4,48,2176]{2,1,0:T(8,128)(2,1)}, u32[]{:S(2)}, u32[]{:S(2)}) collective-permute-start(bf16[4,48,2176]{2,1,0:T(8,128)(2,1)S(1)} %collective-permute-done.19.refs_10_), channel_id=1, source_target_pairs={{0,1},{1,0},{2,3},{3,2},{4,5},{5,4},{6,7},{7,6},{8,9},{9,8},{10,11... | collective-permute-start | bytes 2506760 | tf_op jit(solution)/shard_map/ppermute | solution.py:392
  70.8 14.5 %copy-start.35 = (bf16[2,64,768]{2,1,0:T(8,128)(2,1)}, bf16[2,64,768]{2,1,0:T(8,128)(2,1)S(1)}, u32[]{:S(2)}) copy-start(bf16[2,64,768]{2,1,0:T(8,128)(2,1)S(1)} %collective-permute-done.15.refs_6_.a1) | copy-start | bytes 589828
  70.8 13.0 %collective-permute-start.23 = (bf16[4,48,2176]{2,1,0:T(8,128)(2,1)}, bf16[4,48,2176]{2,1,0:T(8,128)(2,1)}, u32[]{:S(2)}, u32[]{:S(2)}) collective-permute-start(bf16[4,48,2176]{2,1,0:T(8,128)(2,1)} %collective-permute-done.16.refs_11_), channel_id=1, source_target_pairs={{0,1},{1,0},{2,3},{3,2},{4,5},{5,4},{6,7},{7,6},{8,9},{9,8},{10,11... | collective-permute-start | bytes 2506760 | tf_op jit(solution)/shard_map/ppermute | solution.py:392
  81.4 3.9 %collective-permute-start.24 = (bf16[4,48,1408]{2,1,0:T(8,128)(2,1)}, bf16[4,48,1408]{2,1,0:T(8,128)(2,1)}, u32[]{:S(2)}, u32[]{:S(2)}) collective-permute-start(bf16[4,48,1408]{2,1,0:T(8,128)(2,1)} %collective-permute-done.20.refs_13_), channel_id=1, source_target_pairs={{0,1},{1,0},{2,3},{3,2},{4,5},{5,4},{6,7},{7,6},{8,9},{9,8},{10,11... | collective-permute-start | bytes 1622024 | tf_op jit(solution)/shard_map/ppermute | solution.py:392
  82.7 2.6 %collective-permute-start.18 = (bf16[320,768]{1,0:T(8,128)(2,1)}, bf16[320,768]{1,0:T(8,128)(2,1)}, u32[]{:S(2)}, u32[]{:S(2)}) collective-permute-start(bf16[320,768]{1,0:T(8,128)(2,1)} %collective-permute-done.17.refs_7_.refs_12_.a2), channel_id=1, source_target_pairs={{0,1},{1,0},{2,3},{3,2},{4,5},{5,4},{6,7},{7,6},{8,9},{9,8},{10,11... | collective-permute-start | bytes 1474568 | tf_op jit(solution)/shard_map/ppermute | solution.py:392
  96.7 9.1 %collective-permute-start.25 = (bf16[2,64,768]{2,1,0:T(8,128)(2,1)}, bf16[2,64,768]{2,1,0:T(8,128)(2,1)S(1)}, u32[]{:S(2)}, u32[]{:S(2)}) collective-permute-start(bf16[2,64,768]{2,1,0:T(8,128)(2,1)} %get-tuple-element.129), channel_id=1, source_target_pairs={{0,2},{1,3},{2,0},{3,1},{4,6},{5,7},{6,4},{7,5},{8,10},{9,11},{10,... | collective-permute-start | bytes 589832 | tf_op jit(solution)/shard_map/ppermute | solution.py:392
  105.1 6.8 %collective-permute-start.28 = (bf16[16,48,1024]{2,1,0:T(8,128)(2,1)}, bf16[16,48,1024]{2,1,0:T(8,128)(2,1)S(1)}, u32[]{:S(2)}, u32[]{:S(2)}) collective-permute-start(bf16[16,48,1024]{2,1,0:T(8,128)(2,1)} %get-tuple-element.146), channel_id=1, source_target_pairs={{0,1},{1,0},{2,3},{3,2},{4,5},{5,4},{6,7},{7,6},{8,9},{9,8},{10,11... | collective-permute-start | bytes 4718600 | tf_op jit(solution)/shard_map/ppermute | solution.py:392
  106.5 9.7 %collective-permute-start.31 = (bf16[16,48,1152]{2,1,0:T(8,128)(2,1)}, bf16[16,48,1152]{2,1,0:T(8,128)(2,1)S(1)}, u32[]{:S(2)}, u32[]{:S(2)}) collective-permute-start(bf16[16,48,1152]{2,1,0:T(8,128)(2,1)} %get-tuple-element.150), channel_id=1, source_target_pairs={{0,1},{1,0},{2,3},{3,2},{4,5},{5,4},{6,7},{7,6},{8,9},{9,8},{10,11... | collective-permute-start | bytes 5308424 | tf_op jit(solution)/shard_map/ppermute | solution.py:392
  106.6 5.4 %collective-permute-start.26 = (bf16[2,64,768]{2,1,0:T(8,128)(2,1)}, bf16[2,64,768]{2,1,0:T(8,128)(2,1)S(1)}, u32[]{:S(2)}, u32[]{:S(2)}) collective-permute-start(bf16[2,64,768]{2,1,0:T(8,128)(2,1)} %copy-done.36), channel_id=1, source_target_pairs={{0,1},{1,0},{2,3},{3,2},{4,5},{5,4},{6,7},{7,6},{8,9},{9,8},{10,11... | collective-permute-start | bytes 589832 | tf_op jit(solution)/shard_map/ppermute | solution.py:392
  107.2 11.1 %collective-permute-start.27 = (bf16[2,64,768]{2,1,0:T(8,128)(2,1)}, bf16[2,64,768]{2,1,0:T(8,128)(2,1)S(1)}, u32[]{:S(2)}, u32[]{:S(2)}) collective-permute-start(bf16[2,64,768]{2,1,0:T(8,128)(2,1)} %get-tuple-element.134.refs_12_), channel_id=1, source_target_pairs={{0,1},{1,0},{2,3},{3,2},{4,5},{5,4},{6,7},{7,6},{8,9},{9,8},{10,11... | collective-permute-start | bytes 589832 | tf_op jit(solution)/shard_map/ppermute | solution.py:392
  115.5 20.0 %collective-permute-start.29 = (bf16[8,48,1024]{2,1,0:T(8,128)(2,1)}, bf16[8,48,1024]{2,1,0:T(8,128)(2,1)}, u32[]{:S(2)}, u32[]{:S(2)}) collective-permute-start(bf16[8,48,1024]{2,1,0:T(8,128)(2,1)} %add_convert_fusion.1), channel_id=1, source_target_pairs={{0,4},{1,5},{2,6},{3,7},{4,0},{5,1},{6,2},{7,3},{8,12},{9,13},{10,... | collective-permute-start | bytes 2359304 | tf_op jit(solution)/shard_map/ppermute | solution.py:392
  117.4 20.9 %collective-permute-start.32 = (bf16[8,48,1152]{2,1,0:T(8,128)(2,1)}, bf16[8,48,1152]{2,1,0:T(8,128)(2,1)}, u32[]{:S(2)}, u32[]{:S(2)}) collective-permute-start(bf16[8,48,1152]{2,1,0:T(8,128)(2,1)} %add_convert_fusion), channel_id=1, source_target_pairs={{0,2},{1,3},{2,0},{3,1},{4,6},{5,7},{6,4},{7,5},{8,10},{9,11},{10,... | collective-permute-start | bytes 2654216 | tf_op jit(solution)/shard_map/ppermute | solution.py:392
  135.5 17.8 %collective-permute-start.30 = (bf16[4,96,640]{2,1,0:T(8,128)(2,1)}, bf16[4,96,640]{2,1,0:T(8,128)(2,1)S(1)}, u32[]{:S(2)}, u32[]{:S(2)}) collective-permute-start(bf16[4,96,640]{2,1,0:T(8,128)(2,1)} %get-tuple-element.147), channel_id=1, source_target_pairs={{0,4},{1,5},{2,6},{3,7},{4,0},{5,1},{6,2},{7,3},{8,12},{9,13},{10,... | collective-permute-start | bytes 1474568 | tf_op jit(solution)/shard_map/ppermute | solution.py:392
  137.7 9.5 %collective-permute-start.43 = (bf16[4,48,1024]{2,1,0:T(8,128)(2,1)S(1)}, bf16[4,48,1024]{2,1,0:T(8,128)(2,1)S(1)}, u32[]{:S(2)}, u32[]{:S(2)}) collective-permute-start(bf16[4,48,1024]{2,1,0:T(8,128)(2,1)S(1)} %add_convert_fusion.3), channel_id=1, source_target_pairs={{0,2},{1,3},{2,0},{3,1},{4,6},{5,7},{6,4},{7,5},{8,10},{9,11},{10,... | collective-permute-start | bytes 1179656 | tf_op jit(solution)/shard_map/ppermute | solution.py:392
  139.5 17.5 %collective-permute-start.33 = (bf16[4,48,1152]{2,1,0:T(8,128)(2,1)S(1)}, bf16[4,48,1152]{2,1,0:T(8,128)(2,1)S(1)}, u32[]{:S(2)}, u32[]{:S(2)}) collective-permute-start(bf16[4,48,1152]{2,1,0:T(8,128)(2,1)S(1)} %add_convert_fusion.2), channel_id=1, source_target_pairs={{0,4},{1,5},{2,6},{3,7},{4,0},{5,1},{6,2},{7,3},{8,12},{9,13},{10,... | collective-permute-start | bytes 1327112 | tf_op jit(solution)/shard_map/ppermute | solution.py:392
  149.4 16.0 %copy-start.9 = (bf16[4,96,640]{2,1,0:T(8,128)(2,1)S(1)}, bf16[4,96,640]{2,1,0:T(8,128)(2,1)}, u32[]{:S(2)}) copy-start(bf16[4,96,640]{2,1,0:T(8,128)(2,1)} %get-tuple-element.155) | copy-start | bytes 1474564
  149.4 13.5 %collective-permute-start.44 = (bf16[48,1024]{1,0:T(8,128)(2,1)S(1)}, bf16[48,1024]{1,0:T(8,128)(2,1)S(1)}, u32[]{:S(2)}, u32[]{:S(2)}) collective-permute-start(bf16[48,1024]{1,0:T(8,128)(2,1)S(1)} %get-tuple-element.203), channel_id=1, source_target_pairs={{0,8},{1,9},{2,10},{3,11},{4,12},{5,13},{6,14},{7,15},{8,0},{9,1},... | collective-permute-start | bytes 294920 | tf_op jit(solution)/shard_map/ppermute | solution.py:392
  151.5 13.2 %collective-permute-start.45 = (bf16[48,1024]{1,0:T(8,128)(2,1)S(1)}, bf16[48,1024]{1,0:T(8,128)(2,1)S(1)}, u32[]{:S(2)}, u32[]{:S(2)}) collective-permute-start(bf16[48,1024]{1,0:T(8,128)(2,1)S(1)} %get-tuple-element.202), channel_id=1, source_target_pairs={{0,16},{1,17},{2,18},{3,19},{4,20},{5,21},{6,22},{7,23},{8,24},{9,... | collective-permute-start | bytes 294920 | tf_op jit(solution)/shard_map/ppermute | solution.py:392
  153.3 12.8 %collective-permute-start.46 = (bf16[48,1024]{1,0:T(8,128)(2,1)S(1)}, bf16[48,1024]{1,0:T(8,128)(2,1)S(1)}, u32[]{:S(2)}, u32[]{:S(2)}) collective-permute-start(bf16[48,1024]{1,0:T(8,128)(2,1)S(1)} %get-tuple-element.201), channel_id=1, source_target_pairs={{0,24},{1,25},{2,26},{3,27},{4,28},{5,29},{6,30},{7,31},{8,16},{9,... | collective-permute-start | bytes 294920 | tf_op jit(solution)/shard_map/ppermute | solution.py:392
  157.0 25.2 %collective-permute-start.35 = (bf16[256,768]{1,0:T(8,128)(2,1)}, bf16[256,768]{1,0:T(8,128)(2,1)}, u32[]{:S(2)}, u32[]{:S(2)}) collective-permute-start(bf16[256,768]{1,0:T(8,128)(2,1)} %get-tuple-element.154), channel_id=1, source_target_pairs={{0,1},{1,0},{2,3},{3,2},{4,5},{5,4},{6,7},{7,6},{8,9},{9,8},{10,11... | collective-permute-start | bytes 1179656 | tf_op jit(solution)/shard_map/ppermute | solution.py:392
  160.8 24.9 %copy-start.10 = (bf16[256,768]{1,0:T(8,128)(2,1)S(1)}, bf16[256,768]{1,0:T(8,128)(2,1)}, u32[]{:S(2)}) copy-start(bf16[256,768]{1,0:T(8,128)(2,1)} %get-tuple-element.153) | copy-start | bytes 1179652
  160.8 6.6 %collective-permute-start.40 = (bf16[48,1152]{1,0:T(8,128)(2,1)S(1)}, bf16[48,1152]{1,0:T(8,128)(2,1)S(1)}, u32[]{:S(2)}, u32[]{:S(2)}) collective-permute-start(bf16[48,1152]{1,0:T(8,128)(2,1)S(1)} %get-tuple-element.199), channel_id=1, source_target_pairs={{0,8},{1,9},{2,10},{3,11},{4,12},{5,13},{6,14},{7,15},{8,0},{9,1},... | collective-permute-start | bytes 331784 | tf_op jit(solution)/shard_map/ppermute | solution.py:392
  162.9 17.3 %copy-start.23 = (bf16[48,1024]{1,0:T(8,128)(2,1)}, bf16[48,1024]{1,0:T(8,128)(2,1)S(1)}, u32[]{:S(2)}) copy-start(bf16[48,1024]{1,0:T(8,128)(2,1)S(1)} %collective-permute-done.44.b1) | copy-start | bytes 294916
  162.9 8.6 %collective-permute-start.41 = (bf16[48,1152]{1,0:T(8,128)(2,1)S(1)}, bf16[48,1152]{1,0:T(8,128)(2,1)S(1)}, u32[]{:S(2)}, u32[]{:S(2)}) collective-permute-start(bf16[48,1152]{1,0:T(8,128)(2,1)S(1)} %get-tuple-element.198), channel_id=1, source_target_pairs={{0,16},{1,17},{2,18},{3,19},{4,20},{5,21},{6,22},{7,23},{8,24},{9,... | collective-permute-start | bytes 331784 | tf_op jit(solution)/shard_map/ppermute | solution.py:392
  164.7 10.5 %collective-permute-start.42 = (bf16[48,1152]{1,0:T(8,128)(2,1)S(1)}, bf16[48,1152]{1,0:T(8,128)(2,1)S(1)}, u32[]{:S(2)}, u32[]{:S(2)}) collective-permute-start(bf16[48,1152]{1,0:T(8,128)(2,1)S(1)} %get-tuple-element.197), channel_id=1, source_target_pairs={{0,24},{1,25},{2,26},{3,27},{4,28},{5,29},{6,30},{7,31},{8,16},{9,... | collective-permute-start | bytes 331784 | tf_op jit(solution)/shard_map/ppermute | solution.py:392
  165.4 21.9 %copy-start.3 = (bf16[256,768]{1,0:T(8,128)(2,1)S(1)}, bf16[256,768]{1,0:T(8,128)(2,1)}, u32[]{:S(2)}) copy-start(bf16[256,768]{1,0:T(8,128)(2,1)} %refs_1_.5) | copy-start | bytes 1179652
  166.2 14.1 %copy-start.25 = (bf16[48,1024]{1,0:T(8,128)(2,1)}, bf16[48,1024]{1,0:T(8,128)(2,1)S(1)}, u32[]{:S(2)}) copy-start(bf16[48,1024]{1,0:T(8,128)(2,1)S(1)} %collective-permute-done.46.b3) | copy-start | bytes 294916
  166.2 38.2 %collective-permute-start.34 = (bf16[256,768]{1,0:T(8,128)(2,1)}, bf16[256,768]{1,0:T(8,128)(2,1)S(1)}, u32[]{:S(2)}, u32[]{:S(2)}) collective-permute-start(bf16[256,768]{1,0:T(8,128)(2,1)} %get-tuple-element.152), channel_id=1, source_target_pairs={{0,1},{1,0},{2,3},{3,2},{4,5},{5,4},{6,7},{7,6},{8,9},{9,8},{10,11... | collective-permute-start | bytes 1179656 | tf_op jit(solution)/shard_map/ppermute | solution.py:392
  167.4 23.1 %collective-permute-start.37 = (bf16[96,640]{1,0:T(8,128)(2,1)S(1)}, bf16[96,640]{1,0:T(8,128)(2,1)S(1)}, u32[]{:S(2)}, u32[]{:S(2)}) collective-permute-start(bf16[96,640]{1,0:T(8,128)(2,1)S(1)} %get-tuple-element.207), channel_id=1, source_target_pairs={{0,8},{1,9},{2,10},{3,11},{4,12},{5,13},{6,14},{7,15},{8,0},{9,1},... | collective-permute-start | bytes 368648 | tf_op jit(solution)/shard_map/ppermute | solution.py:392
  171.6 19.0 %collective-permute-start.38 = (bf16[96,640]{1,0:T(8,128)(2,1)S(1)}, bf16[96,640]{1,0:T(8,128)(2,1)S(1)}, u32[]{:S(2)}, u32[]{:S(2)}) collective-permute-start(bf16[96,640]{1,0:T(8,128)(2,1)S(1)} %get-tuple-element.206), channel_id=1, source_target_pairs={{0,16},{1,17},{2,18},{3,19},{4,20},{5,21},{6,22},{7,23},{8,24},{9,... | collective-permute-start | bytes 368648 | tf_op jit(solution)/shard_map/ppermute | solution.py:392
  175.2 15.3 %collective-permute-start.39 = (bf16[96,640]{1,0:T(8,128)(2,1)S(1)}, bf16[96,640]{1,0:T(8,128)(2,1)S(1)}, u32[]{:S(2)}, u32[]{:S(2)}) collective-permute-start(bf16[96,640]{1,0:T(8,128)(2,1)S(1)} %get-tuple-element.205), channel_id=1, source_target_pairs={{0,24},{1,25},{2,26},{3,27},{4,28},{5,29},{6,30},{7,31},{8,16},{9,... | collective-permute-start | bytes 368648 | tf_op jit(solution)/shard_map/ppermute | solution.py:392
  182.3 4.6 %collective-permute-start.47 = (bf16[24,2176]{1,0:T(8,128)(2,1)}, bf16[24,2176]{1,0:T(8,128)(2,1)S(1)}, u32[]{:S(2)}, u32[]{:S(2)}) collective-permute-start(bf16[24,2176]{1,0:T(8,128)(2,1)} %get-tuple-element.157), channel_id=1, source_target_pairs={{0,1},{1,0},{2,3},{3,2},{4,5},{5,4},{6,7},{7,6},{8,9},{9,8},{10,11... | collective-permute-start | bytes 313352 | tf_op jit(solution)/shard_map/ppermute | solution.py:392
  186.8 17.5 %collective-permute-start.36 = (bf16[256,768]{1,0:T(8,128)(2,1)S(1)}, bf16[256,768]{1,0:T(8,128)(2,1)S(1)}, u32[]{:S(2)}, u32[]{:S(2)}) collective-permute-start(bf16[256,768]{1,0:T(8,128)(2,1)S(1)} %add_convert_fusion.4), channel_id=1, source_target_pairs={{0,2},{1,3},{2,0},{3,1},{4,6},{5,7},{6,4},{7,5},{8,10},{9,11},{10,... | collective-permute-start | bytes 1179656 | tf_op jit(solution)/shard_map/ppermute | solution.py:392
  187.5 16.8 %copy-start.5 = (bf16[256,768]{1,0:T(8,128)(2,1)S(1)}, bf16[256,768]{1,0:T(8,128)(2,1)}, u32[]{:S(2)}) copy-start(bf16[256,768]{1,0:T(8,128)(2,1)} %get-tuple-element.137) | copy-start | bytes 1179652
  193.2 5.4 %collective-permute-start.49 = (bf16[2,24,640]{2,1,0:T(8,128)(2,1)}, bf16[2,24,640]{2,1,0:T(8,128)(2,1)S(1)}, u32[]{:S(2)}, u32[]{:S(2)}) collective-permute-start(bf16[2,24,640]{2,1,0:T(8,128)(2,1)} %get-tuple-element.164), channel_id=1, source_target_pairs={{0,2},{1,3},{2,0},{3,1},{4,6},{5,7},{6,4},{7,5},{8,10},{9,11},{10,... | collective-permute-start | bytes 184328 | tf_op jit(solution)/shard_map/ppermute | solution.py:392
  194.2 6.3 %collective-permute-start.48 = (bf16[2,24,640]{2,1,0:T(8,128)(2,1)}, bf16[2,24,640]{2,1,0:T(8,128)(2,1)S(1)}, u32[]{:S(2)}, u32[]{:S(2)}) collective-permute-start(bf16[2,24,640]{2,1,0:T(8,128)(2,1)} %get-tuple-element.163.c0), channel_id=1, source_target_pairs={{0,1},{1,0},{2,3},{3,2},{4,5},{5,4},{6,7},{7,6},{8,9},{9,8},{10,11... | collective-permute-start | bytes 184328 | tf_op jit(solution)/shard_map/ppermute | solution.py:392
  198.6 2.0 collective-permute-start.50
  (27 other events, 89.7 us)

commit v4 on v3

--- a/solution.py
+++ b/solution.py
@@ -380,7 +380,7 @@
     )
 
 
-FL = {'C2': 1, 'GO': 2, 'H1': 3, 'H2': 2, 'H3': 1, 'H5': 1, 'H7': 2, 'H8': 1, 'T3': 4, 'T4': 3, 'T5': 3, 'T6': 1, 'TA': 3, 'TC': 1}
+FL = {'DM': 1, 'DX': 1, 'H1': 3, 'H2': 2, 'H3': 2, 'H5': 1, 'H6': 1, 'H7': 2, 'QX': 1, 'T4': 1, 'TC': 1}
 BF = jnp.bfloat16
 F32 = jnp.float32
 AXES = ("dp", "fsdp")
@@ -754,10 +754,16 @@
     return groups
 
 
+def store_half(own_pack, other_pack, at, halves, core):
+    width = halves[0].shape[1]
+    own_pack[:, at : at + width] = jnp.where(core == 0, halves[0], halves[1])
+    other_pack[:, at : at + width] = jnp.where(core == 0, halves[1], halves[0])
+
+
 def feed_kernel(*refs):
     ids, tok, cot, live, gain, a0, a1, a2, a3 = refs[:9]
-    held = refs[9:-12]
-    (block, dmid, d_near, d_far, act16, n2low, dgate, dbr, ggain, w_rest, w_in, sems) = refs[-12:]
+    held = refs[9:-10]
+    (block, dmid, d_near, d_far, own_pack, other_pack, ggain, w_rest, w_in, sems) = refs[-10:]
     f, core, chip = ids[0], ids[2], ids[3]
     in_copies, rest_copies = load_halves(held, w_in, w_rest, core, chip, sems)
     tok_f = tok[...].astype(F32)
@@ -776,7 +782,8 @@
     normed = center * inverse
     gain_row = gain[1:2, :]
     low = (normed * gain_row).astype(BF)
-    n2low[...] = low
+    own_pack[:, :768] = low
+    other_pack[:, :768] = low
     for copy in in_copies:
         copy.wait()
     act = dot_nn(low, w_in[0])
@@ -784,15 +791,15 @@
     cdf, density = erf_pair(act)
     gelu = act * cdf
     active = (gelu * gate).astype(BF)
-    act16[...] = active
+    halves = [active[:, :640], jnp.concatenate([active[:, 640:], jnp.zeros((256, 128), BF)], axis=1)]
+    store_half(own_pack, other_pack, 1920, halves, core)
     alive = live[...]
     dout = jnp.where(alive > 0.5, cot[...].astype(F32), 0.0)
     dym = dout.astype(BF)
     dact = jnp.concatenate([dot_nn(dym, w_rest[0, :, 384:1024]), dot_nn(dym, w_rest[1, :, 384:896])], axis=1)
     dg_front = (dact * gate * (cdf + act * density)).astype(BF)
     dg_rear = (dact * gelu).astype(BF)
-    dgate[:, :1152] = dg_front
-    dgate[:, 1152:] = dg_rear
+    store_half(own_pack, other_pack, 768, [dg_front, dg_rear], core)
     dnormed = dot_nt(dg_front, w_in[0]) + dot_nt(dg_rear, w_in[1])
     ggain[...] = jnp.broadcast_to(jnp.sum(dnormed * normed, axis=0, keepdims=True), (8, 768))
     up = dnormed * gain_row
@@ -803,7 +810,7 @@
     )
     dmid[...] = dmiddle
     dbranch = dmiddle.astype(BF)
-    dbr[...] = dbranch
+    store_half(own_pack, other_pack, 2560, [dbranch[:, :384], dbranch[:, 384:]], core)
     for k in range(4):
         (d_near, d_far)[k // 2][k % 2] = pack_heads(
             (
@@ -819,16 +826,14 @@
     return pl.pallas_call(
         feed_kernel,
         in_specs=[SMEM] + [VM] * 8 + [ANY] * len(held),
-        out_specs=[VM] * 9,
+        out_specs=[VM] * 7,
         out_shape=[
             shaped((256, 768), BF),
             shaped((256, 768), F32),
             shaped((2, 64, 768), BF),
             shaped((2, 64, 768), BF),
-            shaped((256, 1152), BF),
-            shaped((256, 768), BF),
-            shaped((256, 2304), BF),
-            shaped((256, 768), BF),
+            shaped((256, 2944), BF),
+            shaped((256, 2944), BF),
             shaped((8, 768), F32),
         ],
         scratch_shapes=[
@@ -842,55 +847,38 @@
     )(ids, tokens, cotangent, live, gain, *att_pieces, *held)
 
 
-def store_chunks(grads, sent, kept, order, core, chip, sems, what="both"):
+def grads_kernel(
+    ids, cot, cot_c, live, live_c, own, came, near, near_c, by_x, by_x_c,
+    lead_in, keep_in, lead_rest, keep_rest, g_in, g_rest, sems,
+):
+    f, chip = ids[0], ids[3]
     copies = []
-    for slot, group in enumerate(order):
-        for kz in range(4):
-            at = pl.multiple_of(48 * (chip ^ (kz * 4 + group)), 48)
-            for half, target in ((1 - core, sent), (core, kept)):
-                copies.append(
-                    pltpu.make_async_copy(
-                        grads.at[half, pl.ds(at, 48)], target.at[slot * 4 + kz], sems.at[len(copies)]
-                    )
-                )
-                if what != "wait":
-                    copies[-1].start()
-    if what != "start":
-        for copy in copies:
-            copy.wait()
-
-
-def grad_in_kernel(ids, n2low, dgate, sent, kept, grads, sems, wait=True):
-    low = n2low[...]
-    grads[0] = dot_tn(low, dgate[:, :1152]).astype(BF)
-    grads[1] = dot_tn(low, dgate[:, 1152:]).astype(BF)
-    store_chunks(grads, sent, kept, (3, 1, 2, 0), ids[2], ids[3], sems, "both" if wait else "start")
-
-
-def grad_rest_kernel(ids, cot, live, act16, dbr, a0, a1, a2, a3, sent, kept, grads, sems, wait=True):
-    f = ids[0]
-    dym = jnp.where(live[...] > 0.5, cot[...].astype(F32), 0.0).astype(BF)
-    gdown = dot_tn(dym, act16[...])
-    grads[0, :, 384:1024] = gdown[:, :640].astype(BF)
-    grads[1, :, 384:896] = gdown[:, 640:].astype(BF)
-    grads[1, :, 896:1024] = jnp.zeros((768, 128), BF)
-    branch = dbr[...]
-    for k, piece in enumerate((a0[0], a1[1], a2[192:256, :], a3[256:320, :])):
-        piece = unpack_heads(piece)
+
+    def store(grads, which, lead, keep, order):
+        for slot, group in enumerate(order):
+            for kz in range(4):
+                at = pl.multiple_of(48 * (chip ^ (kz * 4 + group)), 48)
+                target = lead.at[slot * 4 + kz] if slot < 2 else keep.at[slot * 4 + kz - 8]
+                copies.append(pltpu.make_async_copy(grads.at[pl.ds(at, 48)], target, sems.at[which, slot * 4 + kz]))
+                copies[-1].start()
+
+    def both(first, last):
+        return jnp.concatenate([own[:, first:last], came[:, first:last]], axis=0)
+
+    g_in[...] = dot_tn(both(0, 768), both(768, 1920)).astype(BF)
+    store(g_in, 0, lead_in, keep_in, (3, 1, 2, 0))
+    dym = jnp.concatenate([jnp.where(alive[...] > 0.5, c[...].astype(F32), 0.0) for alive, c in ((live, cot), (live_c, cot_c))])
+    g_rest[:, 384:] = dot_tn(dym.astype(BF), both(1920, 2560)).astype(BF)
+    branch = both(2560, 2944)
+    mine = (near[0], near_c[1], by_x[192:256, :], by_x_c[256:320, :])
+    others = (near[1], near_c[0], by_x[256:320, :], by_x_c[192:256, :])
+    for k in range(4):
         rows = pl.ds(pl.multiple_of(192 * (f ^ k), 192), 192)
-        gout = dot_tn(piece, branch).astype(BF)
-        grads[0, rows, :384] = gout[:, :384]
-        grads[1, rows, :384] = gout[:, 384:]
-    store_chunks(grads, sent, kept, (3, 2, 1, 0), ids[2], ids[3], sems, "both" if wait else "start")
-
-
-def grads_kernel(
-    ids, cot, live, act16, dbr, a0, a1, a2, a3, n2low, dgate, sent_in, kept_in, sent_rest, kept_rest, g_in, g_rest, sems
-):
-    grad_in_kernel(ids, n2low, dgate, sent_in, kept_in, g_in, sems.at[0], False)
-    grad_rest_kernel(ids, cot, live, act16, dbr, a0, a1, a2, a3, sent_rest, kept_rest, g_rest, sems.at[1], False)
-    store_chunks(g_in, sent_in, kept_in, (3, 1, 2, 0), ids[2], ids[3], sems.at[0], "wait")
-    store_chunks(g_rest, sent_rest, kept_rest, (3, 2, 1, 0), ids[2], ids[3], sems.at[1], "wait")
+        heads = jnp.concatenate([unpack_heads(mine[k]), unpack_heads(others[k])], axis=0)
+        g_rest[rows, :384] = dot_tn(heads, branch).astype(BF)
+    store(g_rest, 1, lead_rest, keep_rest, (3, 2, 1, 0))
+    for copy in copies:
+        copy.wait()
 
 
 def feed_gradients(ids, *operands):
@@ -898,28 +886,15 @@
         grads_kernel,
         in_specs=[SMEM] + [VM] * len(operands),
         out_specs=[ANY] * 4,
-        out_shape=[shaped((16, 48, width), BF) for width in (1152, 1152, 1024, 1024)],
+        out_shape=[shaped((8, 48, width), BF) for width in (1152, 1152, 1024, 1024)],
         scratch_shapes=[
-            pltpu.VMEM((2, 768, 1152), BF),
-            pltpu.VMEM((2, 768, 1024), BF),
-            pltpu.SemaphoreType.DMA((2, 32)),
+            pltpu.VMEM((768, 1152), BF),
+            pltpu.VMEM((768, 1024), BF),
+            pltpu.SemaphoreType.DMA((2, 16)),
         ],
         compiler_params=pltpu.CompilerParams(vmem_limit_bytes=VMEM_LIMIT),
-        cost_estimate=pl.CostEstimate(flops=3 * 10**9, bytes_accessed=16 * 10**6, transcendentals=0),
+        cost_estimate=pl.CostEstimate(flops=3 * 10**9, bytes_accessed=10**7, transcendentals=0),
         name="grads",
-    )(ids, *operands)
-
-
-def chunk_call(kernel, name, width, ids, *operands):
-    return pl.pallas_call(
-        kernel,
-        in_specs=[SMEM] + [VM] * len(operands),
-        out_specs=[ANY] * 2,
-        out_shape=[shaped((16, 48, width), BF)] * 2,
-        scratch_shapes=[pltpu.VMEM((2, 768, width), BF), pltpu.SemaphoreType.DMA((32,))],
-        compiler_params=pltpu.CompilerParams(vmem_limit_bytes=VMEM_LIMIT),
-        cost_estimate=pl.CostEstimate(flops=15 * 10**8, bytes_accessed=8 * 10**6, transcendentals=0),
-        name=name,
     )(ids, *operands)
 
 
@@ -1221,7 +1196,7 @@
         return after(values, *chosen)
 
     near, far, mine, other = prologue(ids, weight_qkv, weight_out, weight_in, weight_down, norm_gains)
-    tok_c = xperm(tokens, 1)
+    tok_c, cot_c = xperm(tokens, 1), xperm(cotangent, 1)
     rows_here, own_rows = assemble(ids, *exchange(near, far, flag("QX")), mine, xperm(other, 1))
     rows_z = [xperm(rows_here, 8), xperm(rows_here, 16), xperm(rows_here, 24)]
     rows_y = xperm(rows_here, 4)
@@ -1244,7 +1219,7 @@
     speeds = ROTARY_BASE ** (-(jnp.arange(HD // 2, dtype=F32) * (2.0 / HD)))
     angles = position.astype(F32)[:, None] * jnp.tile(speeds, 4)[None, :]
     cos, sin = jnp.cos(angles), jnp.sin(angles)
-    live = living[:slots, None].astype(F32)
+    live, live_c = living[:slots, None].astype(F32), living[slots : 2 * slots, None].astype(F32)
 
     if flag("FS"):
         held_x, held_y = xperm(held, 2), xperm(held, 4)
@@ -1276,7 +1251,7 @@
     by_x_c, by_y_c = xperm(by_x, 1), xperm(by_y, 1)
     att_pieces = [near, xperm(near, 1), by_x, by_x_c]
     held = held + [by_x, by_y] + held_c + [by_x_c, by_y_c]
-    block_out, dmiddle, d_near, d_far, act16, n2low, dgate, dbr, ggain = feed_forward(
+    block_out, dmiddle, d_near, d_far, own_pack, other_pack, ggain = feed_forward(
         ids, tokens, cotangent, live, gain, att_pieces, held
     )
     d_pieces = exchange(d_near, d_far, flag("DX"))
@@ -1287,138 +1262,58 @@
             total = total + part.astype(F32)
         return total.astype(BF)
 
-    def reduce_column(kept, rest, one, two):
-        pieces = [add(kept[12 + kz], rest[12 + kz], one[kz], two[kz]) for kz in range(4)]
+    def reduce_column(keep, one, two):
+        pieces = [add(keep[4 + kz], one[kz], two[kz]) for kz in range(4)]
         if flag("ZM"):
             return pieces
         return [pieces[0]] + [xperm(pieces[kz], 8 * kz) for kz in (1, 2, 3)]
 
-    if flag("GO") == 2:
-        sent_in, kept_in, sent_rest, kept_rest = feed_gradients(
-            ids, cotangent, live, act16, dbr, *att_pieces, n2low, dgate
+    (other_pack,) = pick("C2", [other_pack], (d_pieces[2],), (d_pieces[3],))
+    came_pack = xperm(other_pack, 1)
+    (pack_later,) = pick("C3", [own_pack], (d_pieces[2],), (d_pieces[3],), (d_pieces[1],))
+    lead_in, keep_in, lead_rest, keep_rest = feed_gradients(
+        ids, cotangent, cot_c, live, live_c, pack_later, came_pack, *att_pieces
+    )
+    along_x, along_y = xperm(lead_in, 2), xperm(lead_rest, 4)
+    (key_later,) = pick("T3", [key], (lead_in,), (d_pieces[2], d_pieces[3]), (lead_in, d_pieces[2], d_pieces[3]))
+    if flag("BS"):
+        sums = backward_attention(
+            ids, token_pieces, cos, sin, q8, key_later, val, att, prob, d_pieces[:2], gain, wide, ggain, 0, 2
         )
-    elif flag("GO"):
-        sent_rest, kept_rest = chunk_call(
-            grad_rest_kernel, "grad_rest", 1024, ids, cotangent, live, act16, dbr, *att_pieces
+        (key_last,) = pick("T0", [key], (along_x,), (along_y,), (along_x, along_y))
+        if flag("T5") >= 3:
+            along_x, along_y = after([along_x, along_y], sums[0])
+        if flag("T5") == 4:
+            next_in = add(keep_in[:4], along_x[:4])
+            next_rest = add(keep_rest[:4], along_y[:4])
+            (key_last,) = after([key_last], next_in, next_rest)
+        dn0, dn1, dn2, dn3, far, near = backward_attention(
+            ids, token_pieces, cos, sin, q8, key_last, val, att, prob, d_pieces[2:], gain, wide, ggain, 2, 2, sums
         )
-        (n2_later,) = pick("T1", [n2low], (sent_rest,), (sent_rest, d_pieces[2]), (d_pieces[2],))
-        sent_in, kept_in = chunk_call(grad_in_kernel, "grad_in", 1152, ids, n2_later, dgate)
     else:
-        sent_in, kept_in = chunk_call(grad_in_kernel, "grad_in", 1152, ids, n2low, dgate)
-        (cot_later,) = pick("T1", [cotangent], (sent_in,), (sent_in, d_pieces[2]), (d_pieces[2],))
-        sent_rest, kept_rest = chunk_call(
-            grad_rest_kernel, "grad_rest", 1024, ids, cot_later, live, act16, dbr, *att_pieces
+        dn0, dn1, dn2, dn3, far, near = backward_attention(
+            ids, token_pieces, cos, sin, q8, key_later, val, att, prob, d_pieces, gain, wide, ggain
         )
-    if flag("C1") and flag("GO") == 1:
-        (sent_rest,) = after([sent_rest], sent_in)
-    elif flag("C1") and flag("GO") == 0:
-        (sent_in,) = after([sent_in], sent_rest)
-    (sent_in,) = pick("C2", [sent_in], (d_pieces[2],), (d_pieces[3],))
-    (sent_rest,) = pick("C3", [sent_rest], (d_pieces[2],), (d_pieces[3],))
-    came_in, came_rest = xperm(sent_in, 1), xperm(sent_rest, 1)
-
-    def begin(name, kept, came):
-        kept, came = pick(name, [kept, came], tuple(signals)) if signals else (kept, came)
-        return xperm(add(kept[:2], came[:2]), 2), xperm(add(kept[2:4], came[2:4]), 4)
-
-    def middle(name, to_y, to_x, kx, rx, ky, ry, *marks):
-        kx, ky = pick(name, [kx, ky], *[(mark,) for mark in marks])
-        one = jnp.concatenate([add(kx[:2], rx[:2]), add(kx[2:], rx[2:], to_x)], axis=0)
-        two = jnp.concatenate([add(ky[:2], ry[:2], to_y), add(ky[2:], ry[2:])], axis=0)
-        return xperm(one, 2), xperm(two, 4)
-
-    signals = []
-    if flag("RV"):
-        to_in = begin("V1", kept_in[:4], came_in[:4])
-        early_rest = flag("V2") == 0
-        if early_rest:
-            to_rest = begin("V0", kept_rest[:4], came_rest[:4])
-        marks = [to_in[0], to_in[1]]
-        (key_later,) = pick("V3", [key], (to_in[0],), (kept_in, came_in), (kept_rest, came_rest))
-        if flag("V4") == 0:
-            one_in, two_in = middle("V5", *to_in, kept_in[4:8], came_in[4:8], kept_in[8:12], came_in[8:12], to_in[0])
-        if flag("BS"):
-            sums = backward_attention(
-                ids, token_pieces, cos, sin, q8, key_later, val, att, prob, d_pieces[:2], gain, wide, ggain, 0, 2
-            )
-            signals = [sums[0]]
-            if flag("V4") == 1:
-                one_in, two_in = middle(
-                    "V5", *to_in, kept_in[4:8], came_in[4:8], kept_in[8:12], came_in[8:12], sums[0]
-                )
-            if not early_rest:
-                to_rest = begin("V6", kept_rest[:4], came_rest[:4])
-            if flag("V7"):
-                one_rest, two_rest = middle(
-                    "V8", *to_rest, kept_rest[8:12], came_rest[8:12], kept_rest[4:8], came_rest[4:8], sums[0]
-                )
-            (key_last,) = pick("V9", [key], (to_in[0], to_in[1]), (one_in, two_in), (to_rest[0], to_rest[1]))
-            dn0, dn1, dn2, dn3, far, near = backward_attention(
-                ids, token_pieces, cos, sin, q8, key_last, val, att, prob, d_pieces[2:], gain, wide, ggain, 2, 2, sums
-            )
-        else:
-            dn0, dn1, dn2, dn3, far, near = backward_attention(
-                ids, token_pieces, cos, sin, q8, key_later, val, att, prob, d_pieces, gain, wide, ggain
-            )
-            if flag("V4") == 1:
-                one_in, two_in = middle(
-                    "V5", *to_in, kept_in[4:8], came_in[4:8], kept_in[8:12], came_in[8:12], near
-                )
-            signals = [near]
-            if not early_rest:
-                to_rest = begin("V6", kept_rest[:4], came_rest[:4])
-        if not (flag("BS") and flag("V7")):
-            one_rest, two_rest = middle(
-                "V8", *to_rest, kept_rest[8:12], came_rest[8:12], kept_rest[4:8], came_rest[4:8], near
-            )
-        (far,) = pick("VA", [far], (one_in, two_in), (one_rest, two_rest), (to_rest[0],))
-        far_y = xperm(far, 4)
-        along_x, along_y, then_y, then_x = one_in, two_rest, two_in, one_rest
-        column_in = reduce_column(kept_in, came_in, one_in, two_in)
-        column_rest = reduce_column(kept_rest, came_rest, one_rest, two_rest)
-    else:
-        lead_in = add(kept_in[:8], came_in[:8])
-        lead_rest = add(kept_rest[:8], came_rest[:8])
-        along_x, along_y = xperm(lead_in, 2), xperm(lead_rest, 4)
-        (key_later,) = pick("T3", [key], (lead_in, lead_rest), (lead_in,), (lead_rest,), (d_pieces[2], d_pieces[3]))
-        if flag("BS"):
-            sums = backward_attention(
-                ids, token_pieces, cos, sin, q8, key_later, val, att, prob, d_pieces[:2], gain, wide, ggain, 0, 2
-            )
-            (key_last,) = pick("T0", [key], (lead_in, lead_rest), (along_x,), (along_y,), (along_x, along_y))
-            signal = sums[0]
-            if flag("T5") >= 3:
-                along_x, along_y = after([along_x, along_y], signal)
-            if flag("T5") == 4:
-                next_in = add(kept_in[8:12], came_in[8:12], along_x[:4])
-                next_rest = add(kept_rest[8:12], came_rest[8:12], along_y[:4])
-                (key_last,) = after([key_last], next_in, next_rest)
-            dn0, dn1, dn2, dn3, far, near = backward_attention(
-                ids, token_pieces, cos, sin, q8, key_last, val, att, prob, d_pieces[2:], gain, wide, ggain, 2, 2, sums
-            )
-        else:
-            dn0, dn1, dn2, dn3, far, near = backward_attention(
-                ids, token_pieces, cos, sin, q8, key_later, val, att, prob, d_pieces, gain, wide, ggain
-            )
-        if flag("T5") in (1, 2):
-            along_x, along_y = after([along_x, along_y], *((near,) if flag("T5") == 1 else (near, far)))
-        (far,) = pick("T4", [far], (along_x, along_y), (along_x,), (along_y,))
-        far_y = xperm(far, 4)
-        next_in = add(kept_in[8:12], came_in[8:12], along_x[:4])
-        next_rest = add(kept_rest[8:12], came_rest[8:12], along_y[:4])
-        next_in, next_rest = pick("T8", [next_in, next_rest], (far_y,))
-        then_y, then_x = xperm(next_in, 4), xperm(next_rest, 2)
-        (far_y,) = pick("TA", [far_y], (then_y, then_x), (then_x,), (then_y,))
-        column_in = reduce_column(kept_in, came_in, along_x[4:], then_y)
-        column_rest = reduce_column(kept_rest, came_rest, along_y[4:], then_x)
+    if flag("T5") in (1, 2):
+        along_x, along_y = after([along_x, along_y], *((near,) if flag("T5") == 1 else (near, far)))
+    (far,) = pick("T4", [far], (along_x, along_y), (along_x,), (along_y,))
+    far_y = xperm(far, 4)
+    next_in = add(keep_in[:4], along_x[:4])
+    next_rest = add(keep_rest[:4], along_y[:4])
+    next_in, next_rest = pick("T8", [next_in, next_rest], (far_y,))
+    then_y, then_x = xperm(next_in, 4), xperm(next_rest, 2)
+    (far_y,) = pick("TA", [far_y], (then_y, then_x), (then_x,), (then_y,))
+    e = [add(near[kz], far_y[kz]) for kz in range(4)]
+    heads = [e[0], xperm(e[1], 8), xperm(e[2], 16), xperm(e[3], 24)]
+    then_x, = pick("Z1", [then_x], (e[1], e[2], e[3]), (heads[1],), (heads[1], heads[2], heads[3]))
+    then_y, = pick("Z2", [then_y], (e[1], e[2], e[3]), (heads[1],), (heads[1], heads[2], heads[3]))
+    column_in = reduce_column(keep_in, along_x[4:], then_y)
+    column_rest = reduce_column(keep_rest, along_y[4:], then_x)
     if flag("ZM"):
         wide_z = [jnp.concatenate([column_in[kz], column_rest[kz]], axis=1) for kz in range(4)]
         wide_z = [wide_z[0]] + [xperm(wide_z[kz], 8 * kz) for kz in (1, 2, 3)]
         column_in = [piece[:, :1152] for piece in wide_z]
         column_rest = [piece[:, 1152:] for piece in wide_z]
-    (far_y,) = pick("TB", [far_y], (*column_in, *column_rest), tuple(column_rest), tuple(column_in))
-    e = [add(near[kz], far_y[kz]) for kz in range(4)]
-    heads = [e[0], xperm(e[1], 8), xperm(e[2], 16), xperm(e[3], 24)]
     dn1, dn3 = pick("T6", [dn1, dn3], (far_y,), (then_x, then_y), (along_x, along_y), (e[1],))
     if flag("DM"):
         both = xperm(jnp.stack([dn1, dn3]), 1)

time: 207 us -> 193 us (0.932)
  starting transfers between devices: 66.1 us -> 55.6 us
  other arithmetic: 20.6 us -> 14.8 us
  waiting for transfers between devices: 41.1 us -> 43.3 us
    ppermute x51 -> x50, starting transfers between devices: 66.1 us -> 55.6 us  [xperm(): return lax.ppermute(value, AXES, [(i, i ^ mask) for i in range(count)])]
    add x2 -> x0, other arithmetic: 4.17 us -> none  [add(): total = total + part.astype(F32)]
    convert_element_type x6, other arithmetic: 8.51 us -> 5.51 us  [add(): return total.astype(BF)]
    ppermute x51 -> x50, waiting for transfers between devices: 41.1 us -> 43.3 us  [xperm(): return lax.ppermute(value, AXES, [(i, i ^ mask) for i in range(count)])]
    unnamed x80 -> x90, local copies, waits for them, and re-layouts: 6.6 us -> 7.25 us
  transfers between devices with their start and end apart: 51 -> 50, of which waited for: 16 -> 17; matrix products, arithmetic and copies ran while one was open for 11% -> 10% of each run, Pallas kernels for 26% -> 25%
where the time goes in v4:
time: 193 us; the launch traced here: 192 us
  Pallas kernels  65.1 us (34%)
  starting transfers between devices  55.6 us (29%)
  waiting for transfers between devices  43.3 us (22%)
  other arithmetic  14.8 us (8%)
  local copies, waits for them, and re-layouts  12 us (6%)
    ppermute x50, starting transfers between devices, xperm(): return lax.ppermute(value, AXES, [(i, i ^ mask) for i in range(count)])  55.6 us
    ppermute x50, waiting for transfers between devices, xperm(): return lax.ppermute(value, AXES, [(i, i ^ mask) for i in range(count)])  43.3 us
    pallas_call x1, Pallas kernels, forward_attention(): pl.pallas_call(forward_kernel, grid=(4,), in_specs=[SMEM] + [full((256, 7...  17.5 us
    pallas_call x1, Pallas kernels, backward_attention(): pl.pallas_call(functools.partial(backward_kernel, base=base, blocks=block...  16.5 us
    pallas_call x1, Pallas kernels, feed_forward(): pl.pallas_call(feed_kernel, in_specs=[SMEM] + [VM] * 8 + [ANY] * len(held...  11.3 us
    unnamed x90, local copies, waits for them, and re-layouts  7.25 us
    pallas_call x1, Pallas kernels, feed_gradients(): pl.pallas_call(grads_kernel, in_specs=[SMEM] + [VM] * len(operands), out_...  6.61 us
    convert_element_type x6, other arithmetic, add(): return total.astype(BF)  5.51 us
  transfers between devices with their start and end apart: 50, of which 17 were waited for; matrix products, arithmetic and copies ran while one was open for 10% of the time, Pallas kernels for 25%

profile of v4, /device:TPU:9, one launch (start us, length us, event | category | flops | bytes accessed | tf_op | source)
XLA Modules:
  0.0 192.2 jit_solution(2238968798602956920)
XLA Ops:
  1.3 2.0 %prologue.1 = (bf16[2,24,640]{2,1,0:T(8,128)(2,1)}, bf16[2,24,640]{2,1,0:T(8,128)(2,1)}, bf16[24,2176]{1,0:T(8,128)(2,1)}, bf16[24,2176]{1,0:T(8,128)(2,1)}) custom-call(s32[4]{0:T(128)} %pad_add_fusion.ids.refs_0_, f32[24,2304]{1,0:T(8,128)} %refs_0_.3, f32[24,768]{1,0:T(8,128)} %refs_4_.2, f32[24,2304]{1,0:T(8,128)} %refs_0_.2, f32[24,1152]{1,0:T(8,128)} %refs_8_.1, ...), custom_call_target="tpu_custom_call" | custom-call | flops 1000000 | bytes 1000000 | tf_op jit(solution)/shard_map/prologue/pallas_call | solution.py:622
  3.4 1.2 collective-permute-start.1
  4.6 1.1 collective-permute-start.2
  6.2 0.9 collective-permute-done.q1
  7.2 2.0 %collective-permute-done.2.q3 = bf16[2,24,640]{2,1,0:T(8,128)(2,1)S(1)} collective-permute-done((bf16[2,24,640]{2,1,0:T(8,128)(2,1)}, bf16[2,24,640]{2,1,0:T(8,128)(2,1)S(1)}, u32[]{:S(2)}, u32[]{:S(2)}) %collective-permute-start.2) | collective-permute-done | bytes 61472 | tf_op jit(solution)/shard_map/ppermute | solution.py:392
  9.8 1.9 assemble.1
  11.8 2.3 %collective-permute-start.5 = (bf16[96,640]{1,0:T(8,128)(2,1)}, bf16[96,640]{1,0:T(8,128)(2,1)S(1)}, u32[]{:S(2)}, u32[]{:S(2)}) collective-permute-start(bf16[96,640]{1,0:T(8,128)(2,1)} %get-tuple-element.106.w0), channel_id=1, source_target_pairs={{0,16},{1,17},{2,18},{3,19},{4,20},{5,21},{6,22},{7,23},{8,24},{9,... | collective-permute-start | bytes 368648 | tf_op jit(solution)/shard_map/ppermute | solution.py:392
  14.3 1.2 collective-permute-start.10
  15.6 0.9 dynamic-slice_reduce_fusion
  16.5 1.7 collective-permute-done.10.w1
  18.9 1.6 collective-permute-start.11
  20.5 3.1 %collective-permute-start.14 = (bf16[48,2176]{1,0:T(8,128)(2,1)}, bf16[48,2176]{1,0:T(8,128)(2,1)S(1)}, u32[]{:S(2)}, u32[]{:S(2)}) collective-permute-start(bf16[48,2176]{1,0:T(8,128)(2,1)} %get-tuple-element.111), channel_id=1, source_target_pairs={{0,8},{1,9},{2,10},{3,11},{4,12},{5,13},{6,14},{7,15},{8,0},{9,1},... | collective-permute-start | bytes 626696 | tf_op jit(solution)/shard_map/ppermute | solution.py:392
  23.6 1.1 collective-permute-start.15
  24.7 2.8 %collective-permute-done.6 = bf16[96,640]{1,0:T(8,128)(2,1)S(1)} collective-permute-done((bf16[96,640]{1,0:T(8,128)(2,1)}, bf16[96,640]{1,0:T(8,128)(2,1)S(1)}, u32[]{:S(2)}, u32[]{:S(2)}) %collective-permute-start.6) | collective-permute-done | bytes 122912 | tf_op jit(solution)/shard_map/ppermute | solution.py:392
  27.6 1.3 collective-permute-start.12
  29.5 3.3 %collective-permute-start.8 = (bf16[256,768]{1,0:T(8,128)(2,1)S(1)}, bf16[256,768]{1,0:T(8,128)(2,1)}, u32[]{:S(2)}, u32[]{:S(2)}) collective-permute-start(bf16[256,768]{1,0:T(8,128)(2,1)S(1)} %copy-done.1), channel_id=1, source_target_pairs={{0,2},{1,3},{2,0},{3,1},{4,6},{5,7},{6,4},{7,5},{8,10},{9,11},{10,... | collective-permute-start | bytes 1179656 | tf_op jit(solution)/shard_map/ppermute | solution.py:392
  32.8 3.0 %multiply_sine_fusion = (f32[1024,128]{1,0:T(8,128)}, f32[1024,128]{1,0:T(8,128)}) fusion(f32[128]{0:T(128)S(1)} %mul.90, f32[1024]{0:T(1024)S(1)} %get-tuple-element.183), kind=kLoop, calls=%fused_computation.21 | loop fusion | flops 131072 | bytes 1053184 | tf_op jit(solution)/shard_map/sin | solution.py:1221
  35.9 2.7 %collective-permute-done.11 = bf16[48,2176]{1,0:T(8,128)(2,1)S(1)} collective-permute-done((bf16[48,2176]{1,0:T(8,128)(2,1)}, bf16[48,2176]{1,0:T(8,128)(2,1)S(1)}, u32[]{:S(2)}, u32[]{:S(2)}) %collective-permute-start.11) | collective-permute-done | bytes 208928 | tf_op jit(solution)/shard_map/ppermute | solution.py:392
  38.6 3.7 %collective-permute-done.15 = bf16[48,2176]{1,0:T(8,128)(2,1)S(1)} collective-permute-done((bf16[48,2176]{1,0:T(8,128)(2,1)}, bf16[48,2176]{1,0:T(8,128)(2,1)S(1)}, u32[]{:S(2)}, u32[]{:S(2)}) %collective-permute-start.15) | collective-permute-done | bytes 208928 | tf_op jit(solution)/shard_map/ppermute | solution.py:392
  42.4 1.6 collective-permute-start.19
  44.0 1.2 collective-permute-start.16
  45.3 1.7 collective-permute-start.9
  48.1 0.9 fusion.16.docq
  49.0 0.8 copy-done.38
  49.7 17.5 %forward_attention.1 = (bf16[1024,256]{1,0:T(8,128)(2,1)}, bf16[1024,256]{1,0:T(8,128)(2,1)}, bf16[1024,256]{1,0:T(8,128)(2,1)}, f32[1024,192]{1,0:T(8,128)}, bf...) custom-call(s32[4]{0:T(128)} %pad_add_fusion.ids.refs_0_, ...), custom_call_target="tpu_custom_call" | custom-call | flops 6000000000 | bytes 16000000 | tf_op jit(solution)/shard_map/forward_attention/pallas_call | solution.py:646
  67.7 1.0 slice.182
  69.1 1.0 collective-permute-start.21
  70.7 10.2 %collective-permute-done.20.refs_13_ = bf16[4,48,1408]{2,1,0:T(8,128)(2,1)S(1)} collective-permute-done((bf16[4,48,1408]{2,1,0:T(8,128)(2,1)S(1)}, bf16[4,48,1408]{2,1,0:T(8,128)(2,1)S(1)}, u32[]{:S(2)}, u32[]{:S(2)}) %collective-permute-start.20) | collective-permute-done | bytes 540704 | tf_op jit(solution)/shard_map/ppermute | solution.py:392
  80.9 1.2 collective-permute-start.24
  82.6 0.8 copy.58.refs_3_.live
  83.4 1.4 collective-permute-done.18.refs_8_.refs_17_.by_x_c
  84.8 11.3 %feed_forward.1 = (bf16[256,768]{1,0:T(8,128)(2,1)}, f32[256,768]{1,0:T(8,128)}, bf16[2,64,768]{2,1,0:T(8,128)(2,1)}, bf16[2,64,768]{2,1,0:T(8,128)(2,1)}, bf16[...) custom-call(s32[4]{0:T(128)} %pad_add_fusion.ids.refs_0_, bf16[256,768]{1,0:T(8,128)(2,1)} %refs_1_.5, ...), custom_call_target="tpu_custom_call" | custom-call | flops 5000000000 | bytes 12000000 | tf_op jit(solution)/shard_map/feed_forward/pallas_call | solution.py:826
  97.1 0.8 copy.60.live_c
  98.3 1.7 collective-permute-start.27
  101.4 6.6 %grads.1 = (bf16[8,48,1152]{2,1,0:T(8,128)(2,1)}, bf16[8,48,1152]{2,1,0:T(8,128)(2,1)}, bf16[8,48,1024]{2,1,0:T(8,128)(2,1)}, bf16[8,48,1024]{2,1,0:T(8,128)(2,1)}) custom-call(s32[4]{0:T(128)} %pad_add_fusion.ids.refs_0_, bf16[256,768]{1,0:T(8,128)(2,1)} %cot.1, bf16[256,768]{1,0:T(8,128)(2,1)} %copy-done.39, f32[256,1]{1,0:T(8,128)} %copy.58.refs_3_.live, ...), custom_call_target="tpu_custom_call" | custom-call | flops 3000000000 | bytes 10000000 | tf_op jit(solution)/shard_map/grads/pallas_call | solution.py:885
  108.0 0.9 collective-permute-start.33
  110.1 16.5 %backward_attention.1 = (bf16[256,768]{1,0:T(8,128)(2,1)}, bf16[256,768]{1,0:T(8,128)(2,1)}, bf16[256,768]{1,0:T(8,128)(2,1)}, bf16[256,768]{1,0:T(8,128)(2,1)},...) custom-call(s32[4]{0:T(128)} %pad_add_fusion.ids.refs_0_, bf16[256,768]{1,0:T(8,128)(2,1)} %refs_1_.5, ...), custom_call_target="tpu_custom_call" | custom-call | flops 8000000000 | bytes 16000000 | tf_op jit(solution)/shard_map/backward_attention/pallas_call | solution.py:1009
  126.6 1.3 pad_maximum_fusion.1
  127.9 1.0 collective-permute-start.28
  128.9 0.8 slice_reduce_fusion
  129.6 1.1 add_convert_fusion.1
  130.7 1.2 collective-permute-start.42
  132.7 0.9 fusion.9
  133.9 0.9 collective-permute-start.34
  134.8 6.7 %collective-permute-done.42 = bf16[4,48,1024]{2,1,0:T(8,128)(2,1)S(1)} collective-permute-done((bf16[4,48,1024]{2,1,0:T(8,128)(2,1)S(1)}, bf16[4,48,1024]{2,1,0:T(8,128)(2,1)S(1)}, u32[]{:S(2)}, u32[]{:S(2)}) %collective-permute-start.42) | collective-permute-done | bytes 393248 | tf_op jit(solution)/shard_map/ppermute | solution.py:392
  141.5 1.9 fusion.28
  143.4 2.0 %collective-permute-start.43 = (bf16[48,1024]{1,0:T(8,128)(2,1)S(1)}, bf16[48,1024]{1,0:T(8,128)(2,1)S(1)}, u32[]{:S(2)}, u32[]{:S(2)}) collective-permute-start(bf16[48,1024]{1,0:T(8,128)(2,1)S(1)} %get-tuple-element.191), channel_id=1, source_target_pairs={{0,8},{1,9},{2,10},{3,11},{4,12},{5,13},{6,14},{7,15},{8,0},{9,1},... | collective-permute-start | bytes 294920 | tf_op jit(solution)/shard_map/ppermute | solution.py:392
  145.4 1.0 collective-permute-start.44
  146.6 0.8 fusion.24
  147.7 2.2 %collective-permute-start.39 = (bf16[48,1152]{1,0:T(8,128)(2,1)S(1)}, bf16[48,1152]{1,0:T(8,128)(2,1)S(1)}, u32[]{:S(2)}, u32[]{:S(2)}) collective-permute-start(bf16[48,1152]{1,0:T(8,128)(2,1)S(1)} %get-tuple-element.187), channel_id=1, source_target_pairs={{0,8},{1,9},{2,10},{3,11},{4,12},{5,13},{6,14},{7,15},{8,0},{9,1},... | collective-permute-start | bytes 331784 | tf_op jit(solution)/shard_map/ppermute | solution.py:392
  149.8 0.9 collective-permute-done.44.b2
  151.3 2.8 %collective-permute-done.34 = bf16[4,96,640]{2,1,0:T(8,128)(2,1)S(1)} collective-permute-done((bf16[4,96,640]{2,1,0:T(8,128)(2,1)S(1)}, bf16[4,96,640]{2,1,0:T(8,128)(2,1)S(1)}, u32[]{:S(2)}, u32[]{:S(2)}) %collective-permute-start.34) | collective-permute-done | bytes 491552 | tf_op jit(solution)/shard_map/ppermute | solution.py:392
  154.3 0.8 fusion.20
  155.1 4.0 %collective-permute-start.35 = (bf16[96,640]{1,0:T(8,128)(2,1)S(1)}, bf16[96,640]{1,0:T(8,128)(2,1)S(1)}, u32[]{:S(2)}, u32[]{:S(2)}) collective-permute-start(bf16[96,640]{1,0:T(8,128)(2,1)S(1)} %get-tuple-element.195), channel_id=1, source_target_pairs={{0,8},{1,9},{2,10},{3,11},{4,12},{5,13},{6,14},{7,15},{8,0},{9,1},... | collective-permute-start | bytes 368648 | tf_op jit(solution)/shard_map/ppermute | solution.py:392
  159.1 1.2 collective-permute-start.37
  160.3 4.1 %collective-permute-done.41.a3 = bf16[48,1152]{1,0:T(8,128)(2,1)S(1)} collective-permute-done((bf16[48,1152]{1,0:T(8,128)(2,1)S(1)}, bf16[48,1152]{1,0:T(8,128)(2,1)S(1)}, u32[]{:S(2)}, u32[]{:S(2)}) %collective-permute-start.41) | collective-permute-done | bytes 110624 | tf_op jit(solution)/shard_map/ppermute | solution.py:392
  165.0 2.0 %sum_rows.1 = (bf16[24,2176]{1,0:T(8,128)(2,1)}, bf16[24,2176]{1,0:T(8,128)(2,1)}) custom-call(s32[4]{0:T(128)} %pad_add_fusion.ids.refs_0_, bf16[48,1152]{1,0:T(8,128)(2,1)} %get-tuple-element.188.a0, bf16[48,1152]{1,0:T(8,128)(2,1)} %copy-done.18, bf16[48,1152]{1,0:T(8,128)(2,1)} %copy-done.19, bf16[48,1152]{1,0:T(8,128)(2,1)} %copy-done.20, ...), custom_call_target="tpu_custom_call" | custom-call | flops 1000000 | bytes 1000000 | tf_op jit(solution)/shard_map/sum_rows/pallas_call | solution.py:1064
  167.1 7.8 %collective-permute-start.46 = (bf16[24,2176]{1,0:T(8,128)(2,1)}, bf16[24,2176]{1,0:T(8,128)(2,1)S(1)}, u32[]{:S(2)}, u32[]{:S(2)}) collective-permute-start(bf16[24,2176]{1,0:T(8,128)(2,1)} %get-tuple-element.145), channel_id=1, source_target_pairs={{0,1},{1,0},{2,3},{3,2},{4,5},{5,4},{6,7},{7,6},{8,9},{9,8},{10,11... | collective-permute-start | bytes 313352 | tf_op jit(solution)/shard_map/ppermute | solution.py:392
  176.7 2.9 %update_rows.1 = (f32[24,2304]{1,0:T(8,128)}, f32[24,2304]{1,0:T(8,128)}, f32[24,2304]{1,0:T(8,128)}, f32[24,2304]{1,0:T(8,128)}, bf16[24,2304]{1,0:T(8,128)(2,1...) custom-call(s32[4]{0:T(128)} %pad_add_fusion.ids.refs_0_, ...), custom_call_target="tpu_custom_call" | custom-call | flops 10000000 | bytes 4000000 | tf_op jit(solution)/shard_map/update_rows/pallas_call | solution.py:1095
  180.3 1.8 sum_heads.1
  183.5 1.9 collective-permute-done.48.c2
  185.4 1.5 collective-permute-start.49
  186.9 1.3 fusion.7
  189.4 2.6 %update_heads.1 = (f32[24,2304]{1,0:T(8,128)}, f32[24,2304]{1,0:T(8,128)}, f32[24,2304]{1,0:T(8,128)}, f32[24,2304]{1,0:T(8,128)}, bf16[24,2304]{1,0:T(8,128)(2,...) custom-call(s32[4]{0:T(128)} %pad_add_fusion.ids.refs_0_, ...), custom_call_target="tpu_custom_call" | custom-call | flops 10000000 | bytes 3000000 | tf_op jit(solution)/shard_map/update_heads/pallas_call | solution.py:1132
  (178 shorter events, 18.5 us)
Async XLA Ops:
  0.7 14.9 %copy-start = (s32[8,8]{1,0:T(8,128)S(1)}, s32[8,8]{1,0:T(8,128)}, u32[]{:S(2)}) copy-start(s32[8,8]{1,0:T(8,128)} %param.27) | copy-start | bytes 772
  0.7 28.8 %copy-start.1 = (bf16[256,768]{1,0:T(8,128)(2,1)S(1)}, bf16[256,768]{1,0:T(8,128)(2,1)}, u32[]{:S(2)}) copy-start(bf16[256,768]{1,0:T(8,128)(2,1)} %refs_1_.5) | copy-start | bytes 1179652
  3.4 3.8 %collective-permute-start.1 = (bf16[2,24,640]{2,1,0:T(8,128)(2,1)}, bf16[2,24,640]{2,1,0:T(8,128)(2,1)S(1)}, u32[]{:S(2)}, u32[]{:S(2)}) collective-permute-start(bf16[2,24,640]{2,1,0:T(8,128)(2,1)} %get-tuple-element.103), channel_id=1, source_target_pairs={{0,2},{1,3},{2,0},{3,1},{4,6},{5,7},{6,4},{7,5},{8,10},{9,11},{10,... | collective-permute-start | bytes 184328 | tf_op jit(solution)/shard_map/ppermute | solution.py:392
  4.6 4.6 %collective-permute-start.2 = (bf16[2,24,640]{2,1,0:T(8,128)(2,1)}, bf16[2,24,640]{2,1,0:T(8,128)(2,1)S(1)}, u32[]{:S(2)}, u32[]{:S(2)}) collective-permute-start(bf16[2,24,640]{2,1,0:T(8,128)(2,1)} %get-tuple-element.103), channel_id=1, source_target_pairs={{0,3},{1,2},{2,1},{3,0},{4,7},{5,6},{6,5},{7,4},{8,11},{9,10},{10,... | collective-permute-start | bytes 184328 | tf_op jit(solution)/shard_map/ppermute | solution.py:392
  5.7 1.5 collective-permute-start
  5.7 3.5 %collective-permute-start.3 = (bf16[24,2176]{1,0:T(8,128)(2,1)}, bf16[24,2176]{1,0:T(8,128)(2,1)S(1)}, u32[]{:S(2)}, u32[]{:S(2)}) collective-permute-start(bf16[24,2176]{1,0:T(8,128)(2,1)} %get-tuple-element.105), channel_id=1, source_target_pairs={{0,1},{1,0},{2,3},{3,2},{4,5},{5,4},{6,7},{7,6},{8,9},{9,8},{10,11... | collective-permute-start | bytes 313352 | tf_op jit(solution)/shard_map/ppermute | solution.py:392
  6.2 23.3 %collective-permute-start.7 = (bf16[256,768]{1,0:T(8,128)(2,1)}, bf16[256,768]{1,0:T(8,128)(2,1)S(1)}, u32[]{:S(2)}, u32[]{:S(2)}) collective-permute-start(bf16[256,768]{1,0:T(8,128)(2,1)} %refs_1_.5), channel_id=1, source_target_pairs={{0,1},{1,0},{2,3},{3,2},{4,5},{5,4},{6,7},{7,6},{8,9},{9,8},{10,11... | collective-permute-start | bytes 1179656 | tf_op jit(solution)/shard_map/ppermute | solution.py:392
  11.7 30.6 %copy-start.13 = (bf16[48,2176]{1,0:T(8,128)(2,1)S(1)}, bf16[48,2176]{1,0:T(8,128)(2,1)}, u32[]{:S(2)}) copy-start(bf16[48,2176]{1,0:T(8,128)(2,1)} %get-tuple-element.111) | copy-start | bytes 626692
  11.7 8.8 %collective-permute-start.4 = (bf16[96,640]{1,0:T(8,128)(2,1)}, bf16[96,640]{1,0:T(8,128)(2,1)S(1)}, u32[]{:S(2)}, u32[]{:S(2)}) collective-permute-start(bf16[96,640]{1,0:T(8,128)(2,1)} %get-tuple-element.106.w0), channel_id=1, source_target_pairs={{0,8},{1,9},{2,10},{3,11},{4,12},{5,13},{6,14},{7,15},{8,0},{9,1},... | collective-permute-start | bytes 368648 | tf_op jit(solution)/shard_map/ppermute | solution.py:392
  11.8 11.8 %collective-permute-start.5 = (bf16[96,640]{1,0:T(8,128)(2,1)}, bf16[96,640]{1,0:T(8,128)(2,1)S(1)}, u32[]{:S(2)}, u32[]{:S(2)}) collective-permute-start(bf16[96,640]{1,0:T(8,128)(2,1)} %get-tuple-element.106.w0), channel_id=1, source_target_pairs={{0,16},{1,17},{2,18},{3,19},{4,20},{5,21},{6,22},{7,23},{8,24},{9,... | collective-permute-start | bytes 368648 | tf_op jit(solution)/shard_map/ppermute | solution.py:392
  14.2 13.4 %collective-permute-start.6 = (bf16[96,640]{1,0:T(8,128)(2,1)}, bf16[96,640]{1,0:T(8,128)(2,1)S(1)}, u32[]{:S(2)}, u32[]{:S(2)}) collective-permute-start(bf16[96,640]{1,0:T(8,128)(2,1)} %get-tuple-element.106.w0), channel_id=1, source_target_pairs={{0,24},{1,25},{2,26},{3,27},{4,28},{5,29},{6,30},{7,31},{8,16},{9,... | collective-permute-start | bytes 368648 | tf_op jit(solution)/shard_map/ppermute | solution.py:392
  14.3 3.9 %collective-permute-start.10 = (bf16[96,640]{1,0:T(8,128)(2,1)}, bf16[96,640]{1,0:T(8,128)(2,1)S(1)}, u32[]{:S(2)}, u32[]{:S(2)}) collective-permute-start(bf16[96,640]{1,0:T(8,128)(2,1)} %get-tuple-element.106.w0), channel_id=1, source_target_pairs={{0,4},{1,5},{2,6},{3,7},{4,0},{5,1},{6,2},{7,3},{8,12},{9,13},{10,... | collective-permute-start | bytes 368648 | tf_op jit(solution)/shard_map/ppermute | solution.py:392
  18.9 19.6 %collective-permute-start.11 = (bf16[48,2176]{1,0:T(8,128)(2,1)}, bf16[48,2176]{1,0:T(8,128)(2,1)S(1)}, u32[]{:S(2)}, u32[]{:S(2)}) collective-permute-start(bf16[48,2176]{1,0:T(8,128)(2,1)} %get-tuple-element.111), channel_id=1, source_target_pairs={{0,24},{1,25},{2,26},{3,27},{4,28},{5,29},{6,30},{7,31},{8,16},{9,... | collective-permute-start | bytes 626696 | tf_op jit(solution)/shard_map/ppermute | solution.py:392
  20.5 18.0 %collective-permute-start.14 = (bf16[48,2176]{1,0:T(8,128)(2,1)}, bf16[48,2176]{1,0:T(8,128)(2,1)S(1)}, u32[]{:S(2)}, u32[]{:S(2)}) collective-permute-start(bf16[48,2176]{1,0:T(8,128)(2,1)} %get-tuple-element.111), channel_id=1, source_target_pairs={{0,8},{1,9},{2,10},{3,11},{4,12},{5,13},{6,14},{7,15},{8,0},{9,1},... | collective-permute-start | bytes 626696 | tf_op jit(solution)/shard_map/ppermute | solution.py:392
  23.6 18.6 %collective-permute-start.15 = (bf16[48,2176]{1,0:T(8,128)(2,1)}, bf16[48,2176]{1,0:T(8,128)(2,1)S(1)}, u32[]{:S(2)}, u32[]{:S(2)}) collective-permute-start(bf16[48,2176]{1,0:T(8,128)(2,1)} %get-tuple-element.111), channel_id=1, source_target_pairs={{0,16},{1,17},{2,18},{3,19},{4,20},{5,21},{6,22},{7,23},{8,24},{9,... | collective-permute-start | bytes 626696 | tf_op jit(solution)/shard_map/ppermute | solution.py:392
  27.6 20.2 %copy-start.11 = (bf16[3,96,640]{2,1,0:T(8,128)(2,1)}, bf16[3,96,640]{2,1,0:T(8,128)(2,1)S(1)}, u32[]{:S(2)}) copy-start(bf16[3,96,640]{2,1,0:T(8,128)(2,1)S(1)} %pad_maximum_fusion.3.w2) | copy-start | bytes 1105924
  27.6 21.3 %collective-permute-start.12 = (bf16[3,96,640]{2,1,0:T(8,128)(2,1)S(1)}, bf16[3,96,640]{2,1,0:T(8,128)(2,1)}, u32[]{:S(2)}, u32[]{:S(2)}) collective-permute-start(bf16[3,96,640]{2,1,0:T(8,128)(2,1)S(1)} %pad_maximum_fusion.3.w2), channel_id=1, source_target_pairs={{0,4},{1,5},{2,6},{3,7},{4,0},{5,1},{6,2},{7,3},{8,12},{9,13},{10,... | collective-permute-start | bytes 1105928 | tf_op jit(solution)/shard_map/ppermute | solution.py:392
  29.5 12.7 %copy-start.37 = (bf16[256,768]{1,0:T(8,128)(2,1)}, bf16[256,768]{1,0:T(8,128)(2,1)S(1)}, u32[]{:S(2)}) copy-start(bf16[256,768]{1,0:T(8,128)(2,1)S(1)} %collective-permute-done.7.t1.refs_2_) | copy-start | bytes 1179652
  29.5 15.7 %collective-permute-start.8 = (bf16[256,768]{1,0:T(8,128)(2,1)S(1)}, bf16[256,768]{1,0:T(8,128)(2,1)}, u32[]{:S(2)}, u32[]{:S(2)}) collective-permute-start(bf16[256,768]{1,0:T(8,128)(2,1)S(1)} %copy-done.1), channel_id=1, source_target_pairs={{0,2},{1,3},{2,0},{3,1},{4,6},{5,7},{6,4},{7,5},{8,10},{9,11},{10,... | collective-permute-start | bytes 1179656 | tf_op jit(solution)/shard_map/ppermute | solution.py:392
  42.4 26.8 %copy-start.6 = (bf16[4,48,2176]{2,1,0:T(8,128)(2,1)}, bf16[4,48,2176]{2,1,0:T(8,128)(2,1)S(1)}, u32[]{:S(2)}) copy-start(bf16[4,48,2176]{2,1,0:T(8,128)(2,1)S(1)} %pad_maximum_fusion.refs_9_) | copy-start | bytes 2506756
  42.4 24.9 %collective-permute-start.19 = (bf16[4,48,2176]{2,1,0:T(8,128)(2,1)S(1)}, bf16[4,48,2176]{2,1,0:T(8,128)(2,1)S(1)}, u32[]{:S(2)}, u32[]{:S(2)}) collective-permute-start(bf16[4,48,2176]{2,1,0:T(8,128)(2,1)S(1)} %pad_maximum_fusion.refs_9_), channel_id=1, source_target_pairs={{0,2},{1,3},{2,0},{3,1},{4,6},{5,7},{6,4},{7,5},{8,10},{9,11},{10,... | collective-permute-start | bytes 2506760 | tf_op jit(solution)/shard_map/ppermute | solution.py:392
  44.0 23.7 %collective-permute-start.16 = (bf16[4,48,2176]{2,1,0:T(8,128)(2,1)S(1)}, bf16[4,48,2176]{2,1,0:T(8,128)(2,1)}, u32[]{:S(2)}, u32[]{:S(2)}) collective-permute-start(bf16[4,48,2176]{2,1,0:T(8,128)(2,1)S(1)} %pad_maximum_fusion.refs_9_), channel_id=1, source_target_pairs={{0,4},{1,5},{2,6},{3,7},{4,0},{5,1},{6,2},{7,3},{8,12},{9,13},{10,... | collective-permute-start | bytes 2506760 | tf_op jit(solution)/shard_map/ppermute | solution.py:392
  45.3 3.7 %collective-permute-start.9 = (bf16[256,768]{1,0:T(8,128)(2,1)}, bf16[256,768]{1,0:T(8,128)(2,1)S(1)}, u32[]{:S(2)}, u32[]{:S(2)}) collective-permute-start(bf16[256,768]{1,0:T(8,128)(2,1)} %collective-permute-done.8.t2.refs_3_), channel_id=1, source_target_pairs={{0,1},{1,0},{2,3},{3,2},{4,5},{5,4},{6,7},{7,6},{8,9},{9,8},{10,11... | collective-permute-start | bytes 1179656 | tf_op jit(solution)/shard_map/ppermute | solution.py:392
  67.3 2.9 %collective-permute-start.13 = (bf16[2,64,768]{2,1,0:T(8,128)(2,1)}, bf16[2,64,768]{2,1,0:T(8,128)(2,1)S(1)}, u32[]{:S(2)}, u32[]{:S(2)}) collective-permute-start(bf16[2,64,768]{2,1,0:T(8,128)(2,1)} %get-tuple-element.114.refs_5_.near), channel_id=1, source_target_pairs={{0,1},{1,0},{2,3},{3,2},{4,5},{5,4},{6,7},{7,6},{8,9},{9,8},{10,11... | collective-permute-start | bytes 589832 | tf_op jit(solution)/shard_map/ppermute | solution.py:392
  67.3 17.4 %copy-start.12 = (bf16[4,48,2176]{2,1,0:T(8,128)(2,1)}, bf16[4,48,2176]{2,1,0:T(8,128)(2,1)S(1)}, u32[]{:S(2)}) copy-start(bf16[4,48,2176]{2,1,0:T(8,128)(2,1)S(1)} %collective-permute-done.19.refs_10_) | copy-start | bytes 2506756
  67.4 13.5 %collective-permute-start.20 = (bf16[4,48,1408]{2,1,0:T(8,128)(2,1)S(1)}, bf16[4,48,1408]{2,1,0:T(8,128)(2,1)S(1)}, u32[]{:S(2)}, u32[]{:S(2)}) collective-permute-start(bf16[4,48,1408]{2,1,0:T(8,128)(2,1)S(1)} %slice.141), channel_id=1, source_target_pairs={{0,4},{1,5},{2,6},{3,7},{4,0},{5,1},{6,2},{7,3},{8,12},{9,13},{10,... | collective-permute-start | bytes 1622024 | tf_op jit(solution)/shard_map/ppermute | solution.py:392
  68.7 13.4 %collective-permute-start.17 = (bf16[320,768]{1,0:T(8,128)(2,1)S(1)}, bf16[320,768]{1,0:T(8,128)(2,1)}, u32[]{:S(2)}, u32[]{:S(2)}) collective-permute-start(bf16[320,768]{1,0:T(8,128)(2,1)S(1)} %pad_maximum_fusion.2), channel_id=1, source_target_pairs={{0,2},{1,3},{2,0},{3,1},{4,6},{5,7},{6,4},{7,5},{8,10},{9,11},{10,... | collective-permute-start | bytes 1474568 | tf_op jit(solution)/shard_map/ppermute | solution.py:392
  69.1 14.2 %collective-permute-start.21 = (bf16[4,48,2176]{2,1,0:T(8,128)(2,1)S(1)}, bf16[4,48,2176]{2,1,0:T(8,128)(2,1)S(1)}, u32[]{:S(2)}, u32[]{:S(2)}) collective-permute-start(bf16[4,48,2176]{2,1,0:T(8,128)(2,1)S(1)} %pad_maximum_fusion.refs_9_), channel_id=1, source_target_pairs={{0,1},{1,0},{2,3},{3,2},{4,5},{5,4},{6,7},{7,6},{8,9},{9,8},{10,11... | collective-permute-start | bytes 2506760 | tf_op jit(solution)/shard_map/ppermute | solution.py:392
  70.2 13.2 %collective-permute-start.22 = (bf16[4,48,2176]{2,1,0:T(8,128)(2,1)S(1)}, bf16[4,48,2176]{2,1,0:T(8,128)(2,1)}, u32[]{:S(2)}, u32[]{:S(2)}) collective-permute-start(bf16[4,48,2176]{2,1,0:T(8,128)(2,1)S(1)} %collective-permute-done.19.refs_10_), channel_id=1, source_target_pairs={{0,1},{1,0},{2,3},{3,2},{4,5},{5,4},{6,7},{7,6},{8,9},{9,8},{10,11... | collective-permute-start | bytes 2506760 | tf_op jit(solution)/shard_map/ppermute | solution.py:392
  70.2 14.6 %copy-start.40 = (bf16[2,64,768]{2,1,0:T(8,128)(2,1)}, bf16[2,64,768]{2,1,0:T(8,128)(2,1)S(1)}, u32[]{:S(2)}) copy-start(bf16[2,64,768]{2,1,0:T(8,128)(2,1)S(1)} %collective-permute-done.13.refs_6_.near_c) | copy-start | bytes 589828
  70.2 13.2 %collective-permute-start.23 = (bf16[4,48,2176]{2,1,0:T(8,128)(2,1)}, bf16[4,48,2176]{2,1,0:T(8,128)(2,1)}, u32[]{:S(2)}, u32[]{:S(2)}) collective-permute-start(bf16[4,48,2176]{2,1,0:T(8,128)(2,1)} %collective-permute-done.16.refs_11_), channel_id=1, source_target_pairs={{0,1},{1,0},{2,3},{3,2},{4,5},{5,4},{6,7},{7,6},{8,9},{9,8},{10,11... | collective-permute-start | bytes 2506760 | tf_op jit(solution)/shard_map/ppermute | solution.py:392
  80.9 3.8 %collective-permute-start.24 = (bf16[4,48,1408]{2,1,0:T(8,128)(2,1)S(1)}, bf16[4,48,1408]{2,1,0:T(8,128)(2,1)}, u32[]{:S(2)}, u32[]{:S(2)}) collective-permute-start(bf16[4,48,1408]{2,1,0:T(8,128)(2,1)S(1)} %collective-permute-done.20.refs_13_), channel_id=1, source_target_pairs={{0,1},{1,0},{2,3},{3,2},{4,5},{5,4},{6,7},{7,6},{8,9},{9,8},{10,11... | collective-permute-start | bytes 1622024 | tf_op jit(solution)/shard_map/ppermute | solution.py:392
  82.2 2.6 %collective-permute-start.18 = (bf16[320,768]{1,0:T(8,128)(2,1)}, bf16[320,768]{1,0:T(8,128)(2,1)}, u32[]{:S(2)}, u32[]{:S(2)}) collective-permute-start(bf16[320,768]{1,0:T(8,128)(2,1)} %collective-permute-done.17.refs_7_.refs_12_.by_x), channel_id=1, source_target_pairs={{0,1},{1,0},{2,3},{3,2},{4,5},{5,4},{6,7},{7,6},{8,9},{9,8},{10,11... | collective-permute-start | bytes 1474568 | tf_op jit(solution)/shard_map/ppermute | solution.py:392
  96.1 4.2 %collective-permute-start.31 = (bf16[256,2944]{1,0:T(8,128)(2,1)}, bf16[256,2944]{1,0:T(8,128)(2,1)S(1)}, u32[]{:S(2)}, u32[]{:S(2)}) collective-permute-start(bf16[256,2944]{1,0:T(8,128)(2,1)} %get-tuple-element.138), channel_id=1, source_target_pairs={{0,1},{1,0},{2,3},{3,2},{4,5},{5,4},{6,7},{7,6},{8,9},{9,8},{10,11... | collective-permute-start | bytes 4521992 | tf_op jit(solution)/shard_map/ppermute | solution.py:392
  96.6 3.5 %collective-permute-start.30 = (bf16[256,768]{1,0:T(8,128)(2,1)S(1)}, bf16[256,768]{1,0:T(8,128)(2,1)S(1)}, u32[]{:S(2)}, u32[]{:S(2)}) collective-permute-start(bf16[256,768]{1,0:T(8,128)(2,1)S(1)} %copy-done.36), channel_id=1, source_target_pairs={{0,1},{1,0},{2,3},{3,2},{4,5},{5,4},{6,7},{7,6},{8,9},{9,8},{10,11... | collective-permute-start | bytes 1179656 | tf_op jit(solution)/shard_map/ppermute | solution.py:392
  97.9 11.4 %collective-permute-start.26 = (bf16[2,64,768]{2,1,0:T(8,128)(2,1)}, bf16[2,64,768]{2,1,0:T(8,128)(2,1)S(1)}, u32[]{:S(2)}, u32[]{:S(2)}) collective-permute-start(bf16[2,64,768]{2,1,0:T(8,128)(2,1)} %get-tuple-element.130), channel_id=1, source_target_pairs={{0,2},{1,3},{2,0},{3,1},{4,6},{5,7},{6,4},{7,5},{8,10},{9,11},{10,... | collective-permute-start | bytes 589832 | tf_op jit(solution)/shard_map/ppermute | solution.py:392
  98.3 11.1 %collective-permute-start.27 = (bf16[2,64,768]{2,1,0:T(8,128)(2,1)}, bf16[2,64,768]{2,1,0:T(8,128)(2,1)S(1)}, u32[]{:S(2)}, u32[]{:S(2)}) collective-permute-start(bf16[2,64,768]{2,1,0:T(8,128)(2,1)} %get-tuple-element.130), channel_id=1, source_target_pairs={{0,3},{1,2},{2,1},{3,0},{4,7},{5,6},{6,5},{7,4},{8,11},{9,10},{10,... | collective-permute-start | bytes 589832 | tf_op jit(solution)/shard_map/ppermute | solution.py:392
  99.9 9.4 %collective-permute-start.25 = (bf16[2,64,768]{2,1,0:T(8,128)(2,1)}, bf16[2,64,768]{2,1,0:T(8,128)(2,1)S(1)}, u32[]{:S(2)}, u32[]{:S(2)}) collective-permute-start(bf16[2,64,768]{2,1,0:T(8,128)(2,1)} %get-tuple-element.127.refs_12_), channel_id=1, source_target_pairs={{0,1},{1,0},{2,3},{3,2},{4,5},{5,4},{6,7},{7,6},{8,9},{9,8},{10,11... | collective-permute-start | bytes 589832 | tf_op jit(solution)/shard_map/ppermute | solution.py:392
  108.0 21.6 %collective-permute-start.33 = (bf16[8,48,1024]{2,1,0:T(8,128)(2,1)}, bf16[8,48,1024]{2,1,0:T(8,128)(2,1)}, u32[]{:S(2)}, u32[]{:S(2)}) collective-permute-start(bf16[8,48,1024]{2,1,0:T(8,128)(2,1)} %get-tuple-element.140), channel_id=1, source_target_pairs={{0,4},{1,5},{2,6},{3,7},{4,0},{5,1},{6,2},{7,3},{8,12},{9,13},{10,... | collective-permute-start | bytes 2359304 | tf_op jit(solution)/shard_map/ppermute | solution.py:392
  108.9 23.0 %collective-permute-start.32 = (bf16[8,48,1152]{2,1,0:T(8,128)(2,1)}, bf16[8,48,1152]{2,1,0:T(8,128)(2,1)S(1)}, u32[]{:S(2)}, u32[]{:S(2)}) collective-permute-start(bf16[8,48,1152]{2,1,0:T(8,128)(2,1)} %get-tuple-element.139), channel_id=1, source_target_pairs={{0,2},{1,3},{2,0},{3,1},{4,6},{5,7},{6,4},{7,5},{8,10},{9,11},{10,... | collective-permute-start | bytes 2654216 | tf_op jit(solution)/shard_map/ppermute | solution.py:392
  110.1 19.5 %copy-start.8 = (bf16[8,48,1024]{2,1,0:T(8,128)(2,1)S(1)}, bf16[8,48,1024]{2,1,0:T(8,128)(2,1)}, u32[]{:S(2)}) copy-start(bf16[8,48,1024]{2,1,0:T(8,128)(2,1)} %get-tuple-element.143) | copy-start | bytes 2359300
  127.9 4.9 %collective-permute-start.28 = (bf16[2,256,768]{2,1,0:T(8,128)(2,1)S(1)}, bf16[2,256,768]{2,1,0:T(8,128)(2,1)S(1)}, u32[]{:S(2)}, u32[]{:S(2)}) collective-permute-start(bf16[2,256,768]{2,1,0:T(8,128)(2,1)S(1)} %pad_maximum_fusion.1), channel_id=1, source_target_pairs={{0,1},{1,0},{2,3},{3,2},{4,5},{5,4},{6,7},{7,6},{8,9},{9,8},{10,11... | collective-permute-start | bytes 2359304 | tf_op jit(solution)/shard_map/ppermute | solution.py:392
  130.7 10.8 %collective-permute-start.42 = (bf16[4,48,1024]{2,1,0:T(8,128)(2,1)S(1)}, bf16[4,48,1024]{2,1,0:T(8,128)(2,1)S(1)}, u32[]{:S(2)}, u32[]{:S(2)}) collective-permute-start(bf16[4,48,1024]{2,1,0:T(8,128)(2,1)S(1)} %add_convert_fusion.1), channel_id=1, source_target_pairs={{0,2},{1,3},{2,0},{3,1},{4,6},{5,7},{6,4},{7,5},{8,10},{9,11},{10,... | collective-permute-start | bytes 1179656 | tf_op jit(solution)/shard_map/ppermute | solution.py:392
  132.1 14.3 %collective-permute-start.38 = (bf16[4,48,1152]{2,1,0:T(8,128)(2,1)S(1)}, bf16[4,48,1152]{2,1,0:T(8,128)(2,1)S(1)}, u32[]{:S(2)}, u32[]{:S(2)}) collective-permute-start(bf16[4,48,1152]{2,1,0:T(8,128)(2,1)S(1)} %add_convert_fusion), channel_id=1, source_target_pairs={{0,4},{1,5},{2,6},{3,7},{4,0},{5,1},{6,2},{7,3},{8,12},{9,13},{10,... | collective-permute-start | bytes 1327112 | tf_op jit(solution)/shard_map/ppermute | solution.py:392
  133.6 41.3 %collective-permute-start.29 = (bf16[256,768]{1,0:T(8,128)(2,1)}, bf16[256,768]{1,0:T(8,128)(2,1)S(1)}, u32[]{:S(2)}, u32[]{:S(2)}) collective-permute-start(bf16[256,768]{1,0:T(8,128)(2,1)} %fusion.9), channel_id=1, source_target_pairs={{0,2},{1,3},{2,0},{3,1},{4,6},{5,7},{6,4},{7,5},{8,10},{9,11},{10,... | collective-permute-start | bytes 1179656 | tf_op jit(solution)/shard_map/ppermute | solution.py:392
  133.9 20.3 %copy-start.9 = (bf16[4,96,640]{2,1,0:T(8,128)(2,1)S(1)}, bf16[4,96,640]{2,1,0:T(8,128)(2,1)}, u32[]{:S(2)}) copy-start(bf16[4,96,640]{2,1,0:T(8,128)(2,1)} %get-tuple-element.135) | copy-start | bytes 1474564
  133.9 20.1 %collective-permute-start.34 = (bf16[4,96,640]{2,1,0:T(8,128)(2,1)S(1)}, bf16[4,96,640]{2,1,0:T(8,128)(2,1)S(1)}, u32[]{:S(2)}, u32[]{:S(2)}) collective-permute-start(bf16[4,96,640]{2,1,0:T(8,128)(2,1)S(1)} %copy-done.35), channel_id=1, source_target_pairs={{0,4},{1,5},{2,6},{3,7},{4,0},{5,1},{6,2},{7,3},{8,12},{9,13},{10,... | collective-permute-start | bytes 1474568 | tf_op jit(solution)/shard_map/ppermute | solution.py:392
  143.4 4.3 %collective-permute-start.43 = (bf16[48,1024]{1,0:T(8,128)(2,1)S(1)}, bf16[48,1024]{1,0:T(8,128)(2,1)S(1)}, u32[]{:S(2)}, u32[]{:S(2)}) collective-permute-start(bf16[48,1024]{1,0:T(8,128)(2,1)S(1)} %get-tuple-element.191), channel_id=1, source_target_pairs={{0,8},{1,9},{2,10},{3,11},{4,12},{5,13},{6,14},{7,15},{8,0},{9,1},... | collective-permute-start | bytes 294920 | tf_op jit(solution)/shard_map/ppermute | solution.py:392
  145.4 5.3 %collective-permute-start.44 = (bf16[48,1024]{1,0:T(8,128)(2,1)S(1)}, bf16[48,1024]{1,0:T(8,128)(2,1)S(1)}, u32[]{:S(2)}, u32[]{:S(2)}) collective-permute-start(bf16[48,1024]{1,0:T(8,128)(2,1)S(1)} %get-tuple-element.190), channel_id=1, source_target_pairs={{0,16},{1,17},{2,18},{3,19},{4,20},{5,21},{6,22},{7,23},{8,24},{9,... | collective-permute-start | bytes 294920 | tf_op jit(solution)/shard_map/ppermute | solution.py:392
  146.4 8.7 %collective-permute-start.45 = (bf16[48,1024]{1,0:T(8,128)(2,1)S(1)}, bf16[48,1024]{1,0:T(8,128)(2,1)S(1)}, u32[]{:S(2)}, u32[]{:S(2)}) collective-permute-start(bf16[48,1024]{1,0:T(8,128)(2,1)S(1)} %get-tuple-element.189), channel_id=1, source_target_pairs={{0,24},{1,25},{2,26},{3,27},{4,28},{5,29},{6,30},{7,31},{8,16},{9,... | collective-permute-start | bytes 294920 | tf_op jit(solution)/shard_map/ppermute | solution.py:392
  147.5 27.4 %copy-start.3 = (bf16[256,768]{1,0:T(8,128)(2,1)S(1)}, bf16[256,768]{1,0:T(8,128)(2,1)}, u32[]{:S(2)}) copy-start(bf16[256,768]{1,0:T(8,128)(2,1)} %refs_1_.5) | copy-start | bytes 1179652
  147.5 27.4 %copy-start.4 = (bf16[256,768]{1,0:T(8,128)(2,1)S(1)}, bf16[256,768]{1,0:T(8,128)(2,1)}, u32[]{:S(2)}) copy-start(bf16[256,768]{1,0:T(8,128)(2,1)} %get-tuple-element.131) | copy-start | bytes 1179652
  147.7 16.7 %copy-start.23 = (bf16[48,1024]{1,0:T(8,128)(2,1)}, bf16[48,1024]{1,0:T(8,128)(2,1)S(1)}, u32[]{:S(2)}) copy-start(bf16[48,1024]{1,0:T(8,128)(2,1)S(1)} %collective-permute-done.43.b1) | copy-start | bytes 294916
  147.7 11.4 %collective-permute-start.39 = (bf16[48,1152]{1,0:T(8,128)(2,1)S(1)}, bf16[48,1152]{1,0:T(8,128)(2,1)S(1)}, u32[]{:S(2)}, u32[]{:S(2)}) collective-permute-start(bf16[48,1152]{1,0:T(8,128)(2,1)S(1)} %get-tuple-element.187), channel_id=1, source_target_pairs={{0,8},{1,9},{2,10},{3,11},{4,12},{5,13},{6,14},{7,15},{8,0},{9,1},... | collective-permute-start | bytes 331784 | tf_op jit(solution)/shard_map/ppermute | solution.py:392
  150.7 13.7 %copy-start.24 = (bf16[48,1024]{1,0:T(8,128)(2,1)}, bf16[48,1024]{1,0:T(8,128)(2,1)S(1)}, u32[]{:S(2)}) copy-start(bf16[48,1024]{1,0:T(8,128)(2,1)S(1)} %collective-permute-done.44.b2) | copy-start | bytes 294916
  150.7 8.3 %collective-permute-start.40 = (bf16[48,1152]{1,0:T(8,128)(2,1)S(1)}, bf16[48,1152]{1,0:T(8,128)(2,1)S(1)}, u32[]{:S(2)}, u32[]{:S(2)}) collective-permute-start(bf16[48,1152]{1,0:T(8,128)(2,1)S(1)} %get-tuple-element.186), channel_id=1, source_target_pairs={{0,16},{1,17},{2,18},{3,19},{4,20},{5,21},{6,22},{7,23},{8,24},{9,... | collective-permute-start | bytes 331784 | tf_op jit(solution)/shard_map/ppermute | solution.py:392
  154.1 10.3 %collective-permute-start.41 = (bf16[48,1152]{1,0:T(8,128)(2,1)S(1)}, bf16[48,1152]{1,0:T(8,128)(2,1)S(1)}, u32[]{:S(2)}, u32[]{:S(2)}) collective-permute-start(bf16[48,1152]{1,0:T(8,128)(2,1)S(1)} %get-tuple-element.185), channel_id=1, source_target_pairs={{0,24},{1,25},{2,26},{3,27},{4,28},{5,29},{6,30},{7,31},{8,16},{9,... | collective-permute-start | bytes 331784 | tf_op jit(solution)/shard_map/ppermute | solution.py:392
  155.1 24.5 %collective-permute-start.35 = (bf16[96,640]{1,0:T(8,128)(2,1)S(1)}, bf16[96,640]{1,0:T(8,128)(2,1)S(1)}, u32[]{:S(2)}, u32[]{:S(2)}) collective-permute-start(bf16[96,640]{1,0:T(8,128)(2,1)S(1)} %get-tuple-element.195), channel_id=1, source_target_pairs={{0,8},{1,9},{2,10},{3,11},{4,12},{5,13},{6,14},{7,15},{8,0},{9,1},... | collective-permute-start | bytes 368648 | tf_op jit(solution)/shard_map/ppermute | solution.py:392
  159.1 20.5 %collective-permute-start.36 = (bf16[96,640]{1,0:T(8,128)(2,1)S(1)}, bf16[96,640]{1,0:T(8,128)(2,1)S(1)}, u32[]{:S(2)}, u32[]{:S(2)}) collective-permute-start(bf16[96,640]{1,0:T(8,128)(2,1)S(1)} %get-tuple-element.194), channel_id=1, source_target_pairs={{0,16},{1,17},{2,18},{3,19},{4,20},{5,21},{6,22},{7,23},{8,24},{9,... | collective-permute-start | bytes 368648 | tf_op jit(solution)/shard_map/ppermute | solution.py:392
  159.1 20.5 %collective-permute-start.37 = (bf16[96,640]{1,0:T(8,128)(2,1)S(1)}, bf16[96,640]{1,0:T(8,128)(2,1)S(1)}, u32[]{:S(2)}, u32[]{:S(2)}) collective-permute-start(bf16[96,640]{1,0:T(8,128)(2,1)S(1)} %get-tuple-element.193), channel_id=1, source_target_pairs={{0,24},{1,25},{2,26},{3,27},{4,28},{5,29},{6,30},{7,31},{8,16},{9,... | collective-permute-start | bytes 368648 | tf_op jit(solution)/shard_map/ppermute | solution.py:392
  167.1 9.0 %collective-permute-start.46 = (bf16[24,2176]{1,0:T(8,128)(2,1)}, bf16[24,2176]{1,0:T(8,128)(2,1)S(1)}, u32[]{:S(2)}, u32[]{:S(2)}) collective-permute-start(bf16[24,2176]{1,0:T(8,128)(2,1)} %get-tuple-element.145), channel_id=1, source_target_pairs={{0,1},{1,0},{2,3},{3,2},{4,5},{5,4},{6,7},{7,6},{8,9},{9,8},{10,11... | collective-permute-start | bytes 313352 | tf_op jit(solution)/shard_map/ppermute | solution.py:392
  182.1 3.3 %collective-permute-start.48 = (bf16[2,24,640]{2,1,0:T(8,128)(2,1)}, bf16[2,24,640]{2,1,0:T(8,128)(2,1)S(1)}, u32[]{:S(2)}, u32[]{:S(2)}) collective-permute-start(bf16[2,24,640]{2,1,0:T(8,128)(2,1)} %get-tuple-element.152), channel_id=1, source_target_pairs={{0,2},{1,3},{2,0},{3,1},{4,6},{5,7},{6,4},{7,5},{8,10},{9,11},{10,... | collective-permute-start | bytes 184328 | tf_op jit(solution)/shard_map/ppermute | solution.py:392
  182.9 5.3 %collective-permute-start.47 = (bf16[2,24,640]{2,1,0:T(8,128)(2,1)}, bf16[2,24,640]{2,1,0:T(8,128)(2,1)S(1)}, u32[]{:S(2)}, u32[]{:S(2)}) collective-permute-start(bf16[2,24,640]{2,1,0:T(8,128)(2,1)} %get-tuple-element.151.c0), channel_id=1, source_target_pairs={{0,1},{1,0},{2,3},{3,2},{4,5},{5,4},{6,7},{7,6},{8,9},{9,8},{10,11... | collective-permute-start | bytes 184328 | tf_op jit(solution)/shard_map/ppermute | solution.py:392
  185.4 2.8 %collective-permute-start.49 = (bf16[2,24,640]{2,1,0:T(8,128)(2,1)S(1)}, bf16[2,24,640]{2,1,0:T(8,128)(2,1)S(1)}, u32[]{:S(2)}, u32[]{:S(2)}) collective-permute-start(bf16[2,24,640]{2,1,0:T(8,128)(2,1)S(1)} %collective-permute-done.48.c2), channel_id=1, source_target_pairs={{0,1},{1,0},{2,3},{3,2},{4,5},{5,4},{6,7},{7,6},{8,9},{9,8},{10,11... | collective-permute-start | bytes 184328 | tf_op jit(solution)/shard_map/ppermute | solution.py:392
  (31 other events, 93.6 us)

commit v5 on v4

--- a/solution.py
+++ b/solution.py
@@ -380,7 +380,7 @@
     )
 
 
-FL = {'DM': 1, 'DX': 1, 'H1': 3, 'H2': 2, 'H3': 2, 'H5': 1, 'H6': 1, 'H7': 2, 'QX': 1, 'T4': 1, 'TC': 1}
+FL = {'H1': 3, 'H2': 2, 'H3': 2, 'H5': 1, 'H6': 1, 'H7': 2, 'QX': 1, 'DX': 1, 'T4': 1, 'TC': 1}
 BF = jnp.bfloat16
 F32 = jnp.float32
 AXES = ("dp", "fsdp")
@@ -417,6 +417,10 @@
     return jnp.concatenate([spread[:, 128 * i : 128 * i + 96] for i in range(4)] + [spread[:, 512:704], last], axis=1)
 
 
+def live_rows(count):
+    return lax.broadcasted_iota(jnp.int32, (256, 1), 0) < count
+
+
 def pack_heads(block):
     return jnp.concatenate([block[64 * i : 64 * i + 64] for i in range(4)], axis=1)
 
@@ -436,7 +440,7 @@
 
 
 def prologue_kernel(ids, wq, w_out, w_in, w_down, gains, near, far, mine, other):
-    f, core = ids[0], ids[2]
+    f, core = ids[0] & 3, ids[0] & 1
     row = lax.broadcasted_iota(jnp.int32, (24, 24), 0)
     col = lax.broadcasted_iota(jnp.int32, (24, 24), 1)
     parts = []
@@ -457,14 +461,14 @@
         low = jnp.where(place == 0, blocks[0], blocks[1])
         high = jnp.where(place == 2, blocks[2], blocks[3])
         out[...] = jnp.where(place < 2, low, high).astype(BF)
-    left = jnp.concatenate([w_in[:, :1152], w_out[:, :384], w_down[:, :640]], axis=1)
-    right = jnp.concatenate([w_in[:, 1152:], w_out[:, 384:], w_down[:, 640:], jnp.zeros((24, 128), F32)], axis=1)
+    left = jnp.concatenate([w_out[:, :384], w_in[:, :1152], w_down[:, :640]], axis=1)
+    right = jnp.concatenate([w_out[:, 384:], w_in[:, 1152:], w_down[:, 640:], jnp.zeros((24, 128), F32)], axis=1)
     mine[...] = jnp.where(core == 0, left, right).astype(BF)
     other[...] = jnp.where(core == 0, right, left).astype(BF)
 
 
 def assemble_kernel(ids, q0, q1, q2, q3, mine, came, rows, other):
-    f, core = ids[0], ids[2]
+    f, core = ids[0] & 3, ids[0] & 1
     pieces = [q[i].astype(F32) for q, i in ((q0, 0), (q1, 1), (q2, 0), (q3, 1))]
     ordered = []
     for place in range(4):
@@ -488,7 +492,7 @@
         copies = []
         pieces = (w0, w1, w2.at[0], w3.at[0], w2.at[1], w3.at[1], w2.at[2], w3.at[2])
         for k, piece in enumerate(pieces):
-            at = pl.multiple_of(96 * (ids[1] ^ k), 96)
+            at = pl.multiple_of(96 * ((ids[0] >> 2) ^ k), 96)
             copies.append(pltpu.make_async_copy(piece, wscr.at[pl.ds(at, 96)], sems.at[k]))
             copies[-1].start()
         for copy in copies:
@@ -547,7 +551,7 @@
     copies = []
     pieces = (w0, w1, w2.at[0], w3.at[0], w2.at[1], w3.at[1], w2.at[2], w3.at[2])
     for k, piece in enumerate(pieces):
-        at = pl.multiple_of(96 * (ids[1] ^ k), 96)
+        at = pl.multiple_of(96 * ((ids[0] >> 2) ^ k), 96)
         copies.append(pltpu.make_async_copy(piece, wscr.at[pl.ds(at, 96)], sems.at[k]))
         copies[-1].start()
     for copy in copies:
@@ -728,29 +732,26 @@
     return cdf, density
 
 
-def load_halves(held, w_in, w_rest, core, chip, sems):
+def load_halves(held, targets, core, chip, sems):
     groups = [[], []]
-    for owner in range(2):
-        half = core if owner == 0 else 1 - core
-        arrays = held[owner * 5 : owner * 5 + 5]
-        for group in range(4):
-            for kz in range(4):
-                rows = pl.ds(pl.multiple_of(48 * (chip ^ (kz * 4 + group)), 48), 48)
-                if group < 3:
-                    in_parts = [(arrays[group].at[kz, :, pl.ds(0, 1152)], w_in.at[half, rows])]
-                    rest_part = arrays[group].at[kz, :, pl.ds(1152, 1024)]
-                else:
-                    in_parts = [
-                        (arrays[3].at[pl.ds(48 * kz, 48)], w_in.at[half, rows, pl.ds(0, 768)]),
-                        (arrays[4].at[kz, :, pl.ds(0, 384)], w_in.at[half, rows, pl.ds(768, 384)]),
-                    ]
-                    rest_part = arrays[4].at[kz, :, pl.ds(384, 1024)]
-                for which, parts in ((0, in_parts), (1, [(rest_part, w_rest.at[half, rows])])):
-                    for source, target in parts:
-                        sem = sems.at[which, len(groups[which])]
-                        groups[which].append(pltpu.make_async_copy(source, target, sem))
-    for copy in groups[1] + groups[0]:
-        copy.start()
+    early, held = held[: len(held) - 10], held[len(held) - 10 :]
+    for which, columns in enumerate((pl.ds(0, 768), pl.ds(768, 1408))):
+        for owner in range(2):
+            half = core if owner == 0 else 1 - core
+            arrays = held[owner * 5 : owner * 5 + 5]
+            for group in range(4):
+                for kz in range(4):
+                    rows = pl.ds(pl.multiple_of(48 * (chip ^ (kz * 4 + group)), 48), 48)
+                    if group == 3:
+                        piece = arrays[4].at[kz] if which else arrays[3].at[pl.ds(48 * kz, 48)]
+                    elif early:
+                        piece = early[owner].at[group] if kz == 0 else arrays[group].at[kz - 1]
+                        piece = piece.at[:, columns]
+                    else:
+                        piece = arrays[group].at[kz, :, columns]
+                    sem = sems.at[which, len(groups[which])]
+                    groups[which].append(pltpu.make_async_copy(piece, targets[which].at[half, rows], sem))
+                    groups[which][-1].start()
     return groups
 
 
@@ -761,21 +762,21 @@
 
 
 def feed_kernel(*refs):
-    ids, tok, cot, live, gain, a0, a1, a2, a3 = refs[:9]
+    ids, lives, tok, cot, gain, a0, a1, a2, a3 = refs[:9]
     held = refs[9:-10]
-    (block, dmid, d_near, d_far, own_pack, other_pack, ggain, w_rest, w_in, sems) = refs[-10:]
-    f, core, chip = ids[0], ids[2], ids[3]
-    in_copies, rest_copies = load_halves(held, w_in, w_rest, core, chip, sems)
+    (block, dmid, d_near, d_far, own_pack, other_pack, ggain, w_lead, w_rest, sems) = refs[-10:]
+    f, core, chip = ids[0] & 3, ids[0] & 1, ids[0] >> 1
+    lead_copies, rest_copies = load_halves(held, (w_lead, w_rest), core, chip, sems)
     tok_f = tok[...].astype(F32)
     pieces = [unpack_heads(a) for a in (a0[0], a1[1], a2[192:256, :], a3[256:320, :])]
     heads = [pl.ds(pl.multiple_of(192 * (f ^ k), 192), 192) for k in range(4)]
-    for copy in rest_copies:
+    for copy in lead_copies:
         copy.wait()
     left = jnp.zeros((256, 384), F32)
     right = jnp.zeros((256, 384), F32)
     for k in range(4):
-        left += dot_nn(pieces[k], w_rest[0, heads[k], :384])
-        right += dot_nn(pieces[k], w_rest[1, heads[k], :384])
+        left += dot_nn(pieces[k], w_lead[0, heads[k], :384])
+        right += dot_nn(pieces[k], w_lead[1, heads[k], :384])
     middle = tok_f + jnp.concatenate([left, right], axis=1)
     center = middle - jnp.mean(middle, axis=-1, keepdims=True)
     inverse = lax.rsqrt(jnp.mean(center * center, axis=-1, keepdims=True) + NORM_EPS)
@@ -784,23 +785,26 @@
     low = (normed * gain_row).astype(BF)
     own_pack[:, :768] = low
     other_pack[:, :768] = low
-    for copy in in_copies:
+    for copy in rest_copies:
         copy.wait()
-    act = dot_nn(low, w_in[0])
-    gate = dot_nn(low, w_in[1])
+    act, gate = [
+        jnp.concatenate([dot_nn(low, w_lead[h, :, 384:]), dot_nn(low, w_rest[h, :, :768])], axis=1) for h in range(2)
+    ]
     cdf, density = erf_pair(act)
     gelu = act * cdf
     active = (gelu * gate).astype(BF)
     halves = [active[:, :640], jnp.concatenate([active[:, 640:], jnp.zeros((256, 128), BF)], axis=1)]
     store_half(own_pack, other_pack, 1920, halves, core)
-    alive = live[...]
-    dout = jnp.where(alive > 0.5, cot[...].astype(F32), 0.0)
+    alive = live_rows(lives[0])
+    dout = jnp.where(alive, cot[...].astype(F32), 0.0)
     dym = dout.astype(BF)
-    dact = jnp.concatenate([dot_nn(dym, w_rest[0, :, 384:1024]), dot_nn(dym, w_rest[1, :, 384:896])], axis=1)
+    dact = jnp.concatenate([dot_nn(dym, w_rest[0, :, 768:]), dot_nn(dym, w_rest[1, :, 768:1280])], axis=1)
     dg_front = (dact * gate * (cdf + act * density)).astype(BF)
     dg_rear = (dact * gelu).astype(BF)
     store_half(own_pack, other_pack, 768, [dg_front, dg_rear], core)
-    dnormed = dot_nt(dg_front, w_in[0]) + dot_nt(dg_rear, w_in[1])
+    dnormed = jnp.zeros((256, 768), F32)
+    for h, part in enumerate((dg_front, dg_rear)):
+        dnormed += dot_nt(part[:, :384], w_lead[h, :, 384:]) + dot_nt(part[:, 384:], w_rest[h, :, :768])
     ggain[...] = jnp.broadcast_to(jnp.sum(dnormed * normed, axis=0, keepdims=True), (8, 768))
     up = dnormed * gain_row
     dmiddle = dout + inverse * (
@@ -814,18 +818,18 @@
     for k in range(4):
         (d_near, d_far)[k // 2][k % 2] = pack_heads(
             (
-                dot_nt(dbranch[:, :384], w_rest[0, heads[k], :384])
-                + dot_nt(dbranch[:, 384:], w_rest[1, heads[k], :384])
+                dot_nt(dbranch[:, :384], w_lead[0, heads[k], :384])
+                + dot_nt(dbranch[:, 384:], w_lead[1, heads[k], :384])
             ).astype(BF)
         )
-    branch = dot_nt(active[:, :640], w_rest[0, :, 384:1024]) + dot_nt(active[:, 640:], w_rest[1, :, 384:896])
-    block[...] = jnp.where(alive > 0.5, middle + branch, 0.0).astype(BF)
-
-
-def feed_forward(ids, tokens, cotangent, live, gain, att_pieces, held):
+    branch = dot_nt(active[:, :640], w_rest[0, :, 768:]) + dot_nt(active[:, 640:], w_rest[1, :, 768:1280])
+    block[...] = jnp.where(alive, middle + branch, 0.0).astype(BF)
+
+
+def feed_forward(ids, lives, tokens, cotangent, gain, att_pieces, held):
     return pl.pallas_call(
         feed_kernel,
-        in_specs=[SMEM] + [VM] * 8 + [ANY] * len(held),
+        in_specs=[SMEM] * 2 + [VM] * 7 + [ANY] * len(held),
         out_specs=[VM] * 7,
         out_shape=[
             shaped((256, 768), BF),
@@ -837,21 +841,21 @@
             shaped((8, 768), F32),
         ],
         scratch_shapes=[
-            pltpu.VMEM((2, 768, 1024), BF),
-            pltpu.VMEM((2, 768, 1152), BF),
-            pltpu.SemaphoreType.DMA((2, 40)),
+            pltpu.VMEM((2, 768, 768), BF),
+            pltpu.VMEM((2, 768, 1408), BF),
+            pltpu.SemaphoreType.DMA((2, 32)),
         ],
         compiler_params=pltpu.CompilerParams(vmem_limit_bytes=VMEM_LIMIT),
         cost_estimate=pl.CostEstimate(flops=5 * 10**9, bytes_accessed=12 * 10**6, transcendentals=10**6),
         name="feed_forward",
-    )(ids, tokens, cotangent, live, gain, *att_pieces, *held)
+    )(ids, lives, tokens, cotangent, gain, *att_pieces, *held)
 
 
 def grads_kernel(
-    ids, cot, cot_c, live, live_c, own, came, near, near_c, by_x, by_x_c,
+    ids, lives, cot, cot_c, own, came, near, near_c, by_x, by_x_c,
     lead_in, keep_in, lead_rest, keep_rest, g_in, g_rest, sems,
 ):
-    f, chip = ids[0], ids[3]
+    f, chip = ids[0] & 3, ids[0] >> 1
     copies = []
 
     def store(grads, which, lead, keep, order):
@@ -866,8 +870,8 @@
         return jnp.concatenate([own[:, first:last], came[:, first:last]], axis=0)
 
     g_in[...] = dot_tn(both(0, 768), both(768, 1920)).astype(BF)
-    store(g_in, 0, lead_in, keep_in, (3, 1, 2, 0))
-    dym = jnp.concatenate([jnp.where(alive[...] > 0.5, c[...].astype(F32), 0.0) for alive, c in ((live, cot), (live_c, cot_c))])
+    store(g_in, 0, lead_in, keep_in, (3, 2, 1, 0))
+    dym = jnp.concatenate([jnp.where(live_rows(lives[i]), c[...].astype(F32), 0.0) for i, c in enumerate((cot, cot_c))])
     g_rest[:, 384:] = dot_tn(dym.astype(BF), both(1920, 2560)).astype(BF)
     branch = both(2560, 2944)
     mine = (near[0], near_c[1], by_x[192:256, :], by_x_c[256:320, :])
@@ -876,15 +880,15 @@
         rows = pl.ds(pl.multiple_of(192 * (f ^ k), 192), 192)
         heads = jnp.concatenate([unpack_heads(mine[k]), unpack_heads(others[k])], axis=0)
         g_rest[rows, :384] = dot_tn(heads, branch).astype(BF)
-    store(g_rest, 1, lead_rest, keep_rest, (3, 2, 1, 0))
+    store(g_rest, 1, lead_rest, keep_rest, (3, 1, 2, 0))
     for copy in copies:
         copy.wait()
 
 
-def feed_gradients(ids, *operands):
+def feed_gradients(ids, lives, *operands):
     return pl.pallas_call(
         grads_kernel,
-        in_specs=[SMEM] + [VM] * len(operands),
+        in_specs=[SMEM] * 2 + [VM] * len(operands),
         out_specs=[ANY] * 4,
         out_shape=[shaped((8, 48, width), BF) for width in (1152, 1152, 1024, 1024)],
         scratch_shapes=[
@@ -895,40 +899,31 @@
         compiler_params=pltpu.CompilerParams(vmem_limit_bytes=VMEM_LIMIT),
         cost_estimate=pl.CostEstimate(flops=3 * 10**9, bytes_accessed=10**7, transcendentals=0),
         name="grads",
-    )(ids, *operands)
-
-
-def backward_kernel(*refs, base, blocks):
-    resumed, last = base > 0, base + blocks == 4
-    ids, t0, t1, t2, t3, cos, sin, q8, key, val, att, prob, d0, d1, gain, wide, ggain = refs[:17]
-    refs = refs[17:]
-    if blocks == 4:
-        d2, d3, refs = refs[0], refs[1], refs[2:]
-    if resumed:
-        dq_in, dkt_in, dvt_in, refs = refs[0], refs[1], refs[2], refs[3:]
-    if last:
-        dn0, dn1, dn2, dn3, far, near, dq, dkt, dvt, n16, grads, sems = refs
-    else:
-        dq, dkt, dvt = refs
+    )(ids, lives, *operands)
+
+
+def backward_kernel(
+    ids, q8, key, val, att, prob, d0, d1, d2, d3, gain, ggain, t0_far, t1_far, t2_far, t3_far, cos_far, sin_far, wide_far,
+    dn_keep, dn_sent, far, near,
+    dqf, dq, dkt, dvt, n16, grads, t0, t1, t2, t3, cos, sin, wide, sems, late_sems,
+):
     step = pl.program_id(0)
+    late = ((t0_far, t0), (t1_far, t1), (t2_far, t2), (t3_far, t3), (cos_far, cos), (sin_far, sin), (wide_far, wide))
+    loads = [pltpu.make_async_copy(a, b, late_sems.at[i]) for i, (a, b) in enumerate(late)]
 
     @pl.when(step == 0)
     def _():
-        if resumed:
-            dkt[...] = dkt_in[...]
-            dvt[...] = dvt_in[...]
-            dq[:512, :256] = dq_in[...]
-        else:
-            dkt[...] = jnp.zeros((256, 1024), F32)
-            dvt[...] = jnp.zeros((256, 1024), F32)
-
-    rows = pl.ds(pl.multiple_of((base + step) * 256, 256), 256)
+        for load in loads:
+            load.start()
+        dkt[...] = jnp.zeros((256, 1024), F32)
+        dvt[...] = jnp.zeros((256, 1024), F32)
+
+    rows = pl.ds(pl.multiple_of(step * 256, 256), 256)
     zero = jnp.zeros((), BF)
     keys = key[...]
     values = val[...]
     dattn = unpack_heads(d0[0])
-    others = ((1, d1[1]),) if blocks == 2 else ((1, d1[1]), (2, d2[0]), (3, d3[1]))
-    for i, piece in others:
+    for i, piece in ((1, d1[1]), (2, d2[0]), (3, d3[1])):
         dattn = jnp.where(step == i, unpack_heads(piece), dattn)
     dattn = jnp.concatenate([dattn, jnp.zeros((256, 64), BF)], axis=1)
     product = dattn[:, :192].astype(F32) * att[...]
@@ -946,24 +941,22 @@
         dkt[32 * h : 32 * h + 32, :] += dk_head[:32]
         dkt[128 + 32 * h : 160 + 32 * h, :] += dk_head[32:]
         dvt[64 * h : 64 * h + 64, :] += dot_nn(dattn_t[64 * h : 64 * h + 64], weights)
-    c, s = cos[rows, :], sin[rows, :]
-    dqa, dqb = total[:, :128] * 0.125, total[:, 128:] * 0.125
-    dq[rows, :128] = (dqa * c + dqb * s).astype(BF)
-    dq[rows, 128:256] = (dqb * c - dqa * s).astype(BF)
-
-    if not last:
-        return
-
-    @pl.when(step == blocks - 1)
+    dqf[rows, :] = total * 0.125
+
+    @pl.when(step == 3)
     def _():
+        for load in loads:
+            load.wait()
         dk = dkt[...].T
-        ca, sa = cos[...], sin[...]
-        dq[:, 256:384] = (dk[:, :128] * ca + dk[:, 128:] * sa).astype(BF)
-        dq[:, 384:512] = (dk[:, 128:] * ca - dk[:, :128] * sa).astype(BF)
+        c, s = cos[...], sin[...]
+        dq[:, :128] = (dqf[:, :128] * c + dqf[:, 128:] * s).astype(BF)
+        dq[:, 128:256] = (dqf[:, 128:] * c - dqf[:, :128] * s).astype(BF)
+        dq[:, 256:384] = (dk[:, :128] * c + dk[:, 128:] * s).astype(BF)
+        dq[:, 384:512] = (dk[:, 128:] * c - dk[:, :128] * s).astype(BF)
         dq[:, 512:768] = dvt[...].T.astype(BF)
         ggain1 = jnp.zeros((1, 768), F32)
         gain_row = gain[0:1, :]
-        for i, (piece, out) in enumerate(((t0, dn0), (t1, dn1), (t2, dn2), (t3, dn3))):
+        for i, (piece, out) in enumerate(((t0, dn_keep.at[0]), (t1, dn_sent.at[0]), (t2, dn_keep.at[1]), (t3, dn_sent.at[1]))):
             part = dot_nt(dq[256 * i : 256 * i + 256, :], wide[...])
             x = piece[...].astype(F32)
             center = x - jnp.mean(x, axis=-1, keepdims=True)
@@ -977,7 +970,7 @@
         copies = []
         for ky, target in ((1, far), (0, near)):
             for kz in range(4):
-                at = pl.multiple_of(96 * (ids[1] ^ (kz * 2 + ky)), 96)
+                at = pl.multiple_of(96 * ((ids[0] >> 2) ^ (kz * 2 + ky)), 96)
                 copies.append(
                     pltpu.make_async_copy(grads.at[pl.ds(at, 96)], target.at[kz], sems.at[len(copies)])
                 )
@@ -986,50 +979,38 @@
             copy.wait()
 
 
-def backward_attention(
-    ids, token_pieces, cos, sin, q8, key, val, att, prob, d_pieces, gain, wide, ggain, base=0, blocks=4, sums=()
-):
-    last = base + blocks == 4
-    if last:
-        out_specs = [full((256, 768))] * 4 + [ANY, ANY]
-        out_shape = [shaped((256, 768), BF)] * 4 + [shaped((4, 96, 640), BF)] * 2
-        scratch = [
+def backward_attention(ids, token_pieces, cos, sin, q8, key, val, att, prob, d_pieces, gain, wide, ggain):
+    return pl.pallas_call(
+        backward_kernel,
+        grid=(4,),
+        in_specs=[SMEM]
+        + [full((1024, 256))] * 3
+        + [pl.BlockSpec((256, 192), lambda i: (i, 0))]
+        + [pl.BlockSpec((3, 256, 1024), lambda i: (0, i, 0))]
+        + [full((2, 64, 768))] * 4
+        + [full((8, 768))] * 2
+        + [ANY] * 7,
+        out_specs=[full((2, 256, 768))] * 2 + [ANY, ANY],
+        out_shape=[shaped((2, 256, 768), BF)] * 2 + [shaped((4, 96, 640), BF)] * 2,
+        scratch_shapes=[
+            pltpu.VMEM((1024, 256), F32),
             pltpu.VMEM((1024, 768), BF),
             pltpu.VMEM((256, 1024), F32),
             pltpu.VMEM((256, 1024), F32),
             pltpu.VMEM((1024, 768), BF),
             pltpu.VMEM((768, 640), BF),
-            pltpu.SemaphoreType.DMA((8,)),
         ]
-    else:
-        out_specs = [full((512, 256)), full((256, 1024)), full((256, 1024))]
-        out_shape = [shaped((512, 256), BF), shaped((256, 1024), F32), shaped((256, 1024), F32)]
-        scratch = []
-    sum_specs = [full((512, 256)), full((256, 1024)), full((256, 1024))] if sums else []
-    return pl.pallas_call(
-        functools.partial(backward_kernel, base=base, blocks=blocks),
-        grid=(blocks,),
-        in_specs=[SMEM]
-        + [full((256, 768))] * 4
-        + [full((1024, 128))] * 2
-        + [full((1024, 256))] * 3
-        + [pl.BlockSpec((256, 192), lambda i: (base + i, 0))]
-        + [pl.BlockSpec((3, 256, 1024), lambda i: (0, base + i, 0))]
-        + [full((2, 64, 768))] * 2
-        + [full((8, 768)), full((768, 768)), full((8, 768))]
-        + [full((2, 64, 768))] * (len(d_pieces) - 2)
-        + sum_specs,
-        out_specs=out_specs,
-        out_shape=out_shape,
-        scratch_shapes=scratch,
+        + [pltpu.VMEM((256, 768), BF)] * 4
+        + [pltpu.VMEM((1024, 128), F32)] * 2
+        + [pltpu.VMEM((768, 768), BF), pltpu.SemaphoreType.DMA((8,)), pltpu.SemaphoreType.DMA((7,))],
         compiler_params=pltpu.CompilerParams(vmem_limit_bytes=VMEM_LIMIT),
-        cost_estimate=pl.CostEstimate(flops=2 * blocks * 10**9, bytes_accessed=16 * 10**6, transcendentals=0),
+        cost_estimate=pl.CostEstimate(flops=8 * 10**9, bytes_accessed=16 * 10**6, transcendentals=0),
         name="backward_attention",
-    )(ids, *token_pieces, cos, sin, q8, key, val, att, prob, *d_pieces[:2], gain, wide, ggain, *d_pieces[2:], *sums)
+    )(ids, q8, key, val, att, prob, *d_pieces, gain, ggain, *token_pieces, cos, sin, wide)
 
 
 def sum_heads_kernel(ids, e0, e1, e2, e3, near, far):
-    f = ids[0]
+    f = ids[0] & 3
     total = e0[...].astype(F32) + e1[...].astype(F32) + e2[...].astype(F32) + e3[...].astype(F32)
     pieces = [total[24 * j : 24 * j + 24, :] for j in range(4)]
     for k, out in enumerate((near.at[0], near.at[1], far.at[0], far.at[1])):
@@ -1052,7 +1033,7 @@
 
 
 def sum_rows_kernel(ids, a0, a1, a2, a3, b0, b1, b2, b3, mine, other):
-    core = ids[2]
+    core = ids[0] & 1
     one = a0[...].astype(F32) + a1[...].astype(F32) + a2[...].astype(F32) + a3[...].astype(F32)
     two = b0[...].astype(F32) + b1[...].astype(F32) + b2[...].astype(F32) + b3[...].astype(F32)
     rows = jnp.concatenate([one, two], axis=1)
@@ -1079,7 +1060,7 @@
 
 
 def update_rows_kernel(ids, mine, came, *refs):
-    core = ids[2]
+    core = ids[0] & 1
     one, two = mine[...].astype(F32), came[...].astype(F32)
     left, right = jnp.where(core == 0, one, two), jnp.where(core == 0, two, one)
     grads = (
@@ -1104,7 +1085,7 @@
 
 
 def update_heads_kernel(ids, c0, c1, c2, c3, *refs):
-    f = ids[0]
+    f = ids[0] & 3
     pieces = [c[i].astype(F32) for c, i in ((c0, 0), (c1, 1), (c2, 0), (c3, 1))]
     ordered = []
     for place in range(4):
@@ -1177,7 +1158,12 @@
     own_place = lax.axis_index("fsdp")
     core, side = own_place & 1, own_place >> 1
     chip = group_row * 2 + side
-    ids = jnp.stack([own_place, group_row, core, chip]).astype(jnp.int32)
+    count_row = lax.dynamic_index_in_dim(counts, group_row, 0, keepdims=False)
+    length_row = lax.dynamic_index_in_dim(lengths, group_row, 0, keepdims=False)
+    own_count = lax.dynamic_index_in_dim(count_row, own_place, 0, keepdims=False)
+    core_count = lax.dynamic_index_in_dim(count_row, own_place ^ 1, 0, keepdims=False)
+    ids = lax.axis_index(AXES).astype(jnp.int32).reshape(1)
+    lives = jnp.stack([own_count, core_count])
 
     def flag(name):
         return FL.get(name, 0)
@@ -1208,18 +1194,24 @@
     token_pieces = [tokens, tok_c, tok_x, xperm(tok_x, 1)]
 
     column0 = own_rows
+    rows_unmarked = own_rows
     (own_rows,) = pick("H1", [own_rows], (rows_z, rows_y), (rows_z,), (rows_y,), (rows_zy,))
     column = [own_rows, xperm(own_rows, 8), xperm(own_rows, 16), xperm(own_rows, 24)]
+    if flag("EP"):
+        (rows_first,) = pick("E1", [rows_unmarked], (rows_y,), (rows_z[:1],), (tok_c,))
+        early_x = xperm(rows_first, 2)
+        (rows_first,) = pick("E2", [rows_first], (rows_y,), (early_x,), (rows_z[:1],))
+        early_y = xperm(rows_first, 4)
+        trio = jnp.stack([rows_unmarked, early_x, early_y])
+        (trio,) = pick("E3", [trio], (column[3],), (rows_zy,))
+        column = column[1:]
     held = jnp.stack(column)
 
-    count_row = lax.dynamic_index_in_dim(counts, group_row, 0, keepdims=False)
-    length_row = lax.dynamic_index_in_dim(lengths, group_row, 0, keepdims=False)
     count_row, length_row = pick("H2", [count_row, length_row], (rows_here,), (rows_z,), (rows_zy,))
-    docs, position, living = pack_layout(count_row, length_row, slots, own_place)
+    docs, position, _ = pack_layout(count_row, length_row, slots, own_place)
     speeds = ROTARY_BASE ** (-(jnp.arange(HD // 2, dtype=F32) * (2.0 / HD)))
     angles = position.astype(F32)[:, None] * jnp.tile(speeds, 4)[None, :]
     cos, sin = jnp.cos(angles), jnp.sin(angles)
-    live, live_c = living[:slots, None].astype(F32), living[slots : 2 * slots, None].astype(F32)
 
     if flag("FS"):
         held_x, held_y = xperm(held, 2), xperm(held, 4)
@@ -1234,25 +1226,36 @@
             ids, token_pieces, cos_ready, sin, docs, w_pieces
         )
     ready_x, ready_y = pick("H4", [held_x, held_y], (q8,), (near,))
-    by_x = jnp.concatenate([ready_y[:, :, :768].reshape(192, 768), far.reshape(128, 768)], axis=0)
-    (from_x,) = pick("H6", [ready_x], (near,), (by_x,))
-    by_x, by_y = xperm(by_x, 2), xperm(from_x[:, :, 768:], 4)
+    if flag("EP"):
+        front = [early_y[:, :768], ready_y[:, :, :768].reshape(144, 768)]
+        by_x = jnp.concatenate(front + [far.reshape(128, 768)], axis=0)
+        (from_x,) = pick("H6", [ready_x], (near,), (by_x,))
+        by_y = jnp.concatenate([early_x[None, :, 768:], from_x[:, :, 768:]], axis=0)
+        by_x, by_y = xperm(by_x, 2), xperm(by_y, 4)
+    else:
+        by_x = jnp.concatenate([ready_y[:, :, :768].reshape(192, 768), far.reshape(128, 768)], axis=0)
+        (from_x,) = pick("H6", [ready_x], (near,), (by_x,))
+        by_x, by_y = xperm(by_x, 2), xperm(from_x[:, :, 768:], 4)
     held = [held, held_x, held_y]
     held = pick("H7", held, (q8,), (near,), (by_x,))
     (near,) = pick("H9", [near], (by_x,), (by_y,))
     if flag("HC") == 1:
+        count = held[1].shape[0]
         pair = xperm(jnp.concatenate(held[1:], axis=0), 1)
-        held_c = [xperm(held[0], 1), pair[:4], pair[4:]]
+        held_c = [xperm(held[0], 1), pair[:count], pair[count:]]
     elif flag("HC") == 2:
-        trio = xperm(jnp.concatenate(held, axis=0), 1)
-        held_c = [trio[:4], trio[4:8], trio[8:]]
+        count = held[1].shape[0]
+        three = xperm(jnp.concatenate(held, axis=0), 1)
+        held_c = [three[:count], three[count : 2 * count], three[2 * count :]]
     else:
         held_c = [xperm(piece, 1) for piece in held]
     by_x_c, by_y_c = xperm(by_x, 1), xperm(by_y, 1)
     att_pieces = [near, xperm(near, 1), by_x, by_x_c]
     held = held + [by_x, by_y] + held_c + [by_x_c, by_y_c]
+    if flag("EP"):
+        held = [trio, xperm(trio, 1)] + held
     block_out, dmiddle, d_near, d_far, own_pack, other_pack, ggain = feed_forward(
-        ids, tokens, cotangent, live, gain, att_pieces, held
+        ids, lives, tokens, cotangent, gain, att_pieces, held
     )
     d_pieces = exchange(d_near, d_far, flag("DX"))
 
@@ -1272,68 +1275,55 @@
     came_pack = xperm(other_pack, 1)
     (pack_later,) = pick("C3", [own_pack], (d_pieces[2],), (d_pieces[3],), (d_pieces[1],))
     lead_in, keep_in, lead_rest, keep_rest = feed_gradients(
-        ids, cotangent, cot_c, live, live_c, pack_later, came_pack, *att_pieces
-    )
-    along_x, along_y = xperm(lead_in, 2), xperm(lead_rest, 4)
+        ids, lives, cotangent, cot_c, pack_later, came_pack, *att_pieces
+    )
+    along_x, along_y = xperm(lead_rest, 2), xperm(lead_in, 4)
     (key_later,) = pick("T3", [key], (lead_in,), (d_pieces[2], d_pieces[3]), (lead_in, d_pieces[2], d_pieces[3]))
-    if flag("BS"):
-        sums = backward_attention(
-            ids, token_pieces, cos, sin, q8, key_later, val, att, prob, d_pieces[:2], gain, wide, ggain, 0, 2
-        )
-        (key_last,) = pick("T0", [key], (along_x,), (along_y,), (along_x, along_y))
-        if flag("T5") >= 3:
-            along_x, along_y = after([along_x, along_y], sums[0])
-        if flag("T5") == 4:
-            next_in = add(keep_in[:4], along_x[:4])
-            next_rest = add(keep_rest[:4], along_y[:4])
-            (key_last,) = after([key_last], next_in, next_rest)
-        dn0, dn1, dn2, dn3, far, near = backward_attention(
-            ids, token_pieces, cos, sin, q8, key_last, val, att, prob, d_pieces[2:], gain, wide, ggain, 2, 2, sums
-        )
-    else:
-        dn0, dn1, dn2, dn3, far, near = backward_attention(
-            ids, token_pieces, cos, sin, q8, key_later, val, att, prob, d_pieces, gain, wide, ggain
-        )
+    dn_keep, dn_sent, far, near = backward_attention(
+        ids, token_pieces, cos, sin, q8, key_later, val, att, prob, d_pieces, gain, wide, ggain
+    )
     if flag("T5") in (1, 2):
         along_x, along_y = after([along_x, along_y], *((near,) if flag("T5") == 1 else (near, far)))
     (far,) = pick("T4", [far], (along_x, along_y), (along_x,), (along_y,))
     far_y = xperm(far, 4)
-    next_in = add(keep_in[:4], along_x[:4])
-    next_rest = add(keep_rest[:4], along_y[:4])
+    next_in = add(keep_in[:4], along_y[:4])
+    next_rest = add(keep_rest[:4], along_x[:4])
     next_in, next_rest = pick("T8", [next_in, next_rest], (far_y,))
-    then_y, then_x = xperm(next_in, 4), xperm(next_rest, 2)
+    (next_in,) = pick("T9", [next_in], (far_y,), (dn_sent,), (far,))
+    (next_rest,) = pick("TD", [next_rest], (far_y,), (dn_sent,), (far,))
+    then_y, then_x = xperm(next_rest, 4), xperm(next_in, 2)
     (far_y,) = pick("TA", [far_y], (then_y, then_x), (then_x,), (then_y,))
+    (near,) = pick("T2", [near], (along_x, along_y), (then_x,), (then_y,))
     e = [add(near[kz], far_y[kz]) for kz in range(4)]
     heads = [e[0], xperm(e[1], 8), xperm(e[2], 16), xperm(e[3], 24)]
     then_x, = pick("Z1", [then_x], (e[1], e[2], e[3]), (heads[1],), (heads[1], heads[2], heads[3]))
     then_y, = pick("Z2", [then_y], (e[1], e[2], e[3]), (heads[1],), (heads[1], heads[2], heads[3]))
-    column_in = reduce_column(keep_in, along_x[4:], then_y)
-    column_rest = reduce_column(keep_rest, along_y[4:], then_x)
+    column_in = reduce_column(keep_in, along_y[4:], then_x)
+    column_rest = reduce_column(keep_rest, along_x[4:], then_y)
     if flag("ZM"):
         wide_z = [jnp.concatenate([column_in[kz], column_rest[kz]], axis=1) for kz in range(4)]
         wide_z = [wide_z[0]] + [xperm(wide_z[kz], 8 * kz) for kz in (1, 2, 3)]
         column_in = [piece[:, :1152] for piece in wide_z]
         column_rest = [piece[:, 1152:] for piece in wide_z]
-    dn1, dn3 = pick("T6", [dn1, dn3], (far_y,), (then_x, then_y), (along_x, along_y), (e[1],))
-    if flag("DM"):
-        both = xperm(jnp.stack([dn1, dn3]), 1)
-        dn1_came, dn3_came = both[0], both[1]
-    else:
-        dn1_came, dn3_came = xperm(dn1, 1), xperm(dn3, 1)
-    x_sum = add(dn2, dn3_came)
-    x_came = xperm(x_sum, 2)
-    own_sum = add(dn0, dn1_came)
+    (dn_sent,) = pick("T6", [dn_sent], (far_y,), (then_x, then_y), (along_x, along_y), (e[1],))
+    dn_came = xperm(dn_sent, 1)
+    x_came = xperm(add(dn_keep[1], dn_came[1]), 2)
     heads = pick("T7", heads, (x_came,))
+    column_in = pick("Z3", column_in, (heads[1],), (heads[1], heads[2], heads[3]))
     mine, other = sum_rows(ids, *column_in, *column_rest)
     states = [
         (weight_in, first_in, second_in, average_in),
         (weight_out, first_out, second_out, average_out),
         (weight_down, first_down, second_down, average_down),
     ]
-    new_rows = update_rows(ids, mine, xperm(other, 1), states)
-
-    heads = pick("TC", heads, (new_rows[0],), (other,))
-    came = exchange(*sum_heads(ids, *heads), flag("UX"))
+    (other,) = pick("Z5", [other], (heads[1],), (heads[1], heads[2], heads[3]))
+    other_came = xperm(other, 1)
+    if flag("TC"):
+        heads = pick("TC", heads, (other_came,), (other,))
+    head_sums = sum_heads(ids, *heads)
+    came = exchange(*head_sums, flag("UX"))
+    (mine,) = pick("Z4", [mine], (heads[1],), (heads[1], heads[2], heads[3]), (head_sums[0],), (came[2],))
+    new_rows = update_rows(ids, mine, other_came, states)
     new_heads = update_heads(
         ids,
         came,
@@ -1341,7 +1331,7 @@
         (norm_gains, first_gains, second_gains, average_gains),
     )
 
-    dnormed = own_sum.astype(F32) + x_came.astype(F32)
+    dnormed = dn_keep[0].astype(F32) + dn_came[0].astype(F32) + x_came.astype(F32)
     normed, inverse = norm_parts(tokens.astype(F32))
     grad_tokens = dmiddle + norm_back(dnormed * gain[0:1, :], normed, inverse)
 

time: 193 us -> 190 us (0.984)
  local copies, waits for them, and re-layouts: 12 us -> 10 us
    unnamed x90 -> x82, local copies, waits for them, and re-layouts: 7.25 us -> 6.29 us
  transfers between devices with their start and end apart: 50 -> 50, of which waited for: 17 -> 13; matrix products, arithmetic and copies ran while one was open for 10% -> 11% of each run, Pallas kernels for 25% -> 24%
where the time goes in v5:
time: 190 us; the launch traced here: 189 us
  Pallas kernels  63.6 us (33%)
  starting transfers between devices  55.6 us (29%)
  waiting for transfers between devices  42.1 us (22%)
  other arithmetic  16.2 us (9%)
  local copies, waits for them, and re-layouts  10 us (5%)
    ppermute x50, starting transfers between devices, xperm(): return lax.ppermute(value, AXES, [(i, i ^ mask) for i in range(count)])  55.6 us
    ppermute x50, waiting for transfers between devices, xperm(): return lax.ppermute(value, AXES, [(i, i ^ mask) for i in range(count)])  42.1 us
    pallas_call x1, Pallas kernels, forward_attention(): pl.pallas_call(forward_kernel, grid=(4,), in_specs=[SMEM] + [full((256, 7...  17.4 us
    pallas_call x1, Pallas kernels, backward_attention(): pl.pallas_call(backward_kernel, grid=(4,), in_specs=[SMEM] + [full((1024,...  15.4 us
    pallas_call x1, Pallas kernels, feed_forward(): pl.pallas_call(feed_kernel, in_specs=[SMEM] * 2 + [VM] * 7 + [ANY] * len(...  11 us
    convert_element_type x6, other arithmetic, add(): return total.astype(BF)  6.89 us
    pallas_call x1, Pallas kernels, feed_gradients(): pl.pallas_call(grads_kernel, in_specs=[SMEM] * 2 + [VM] * len(operands),...  6.57 us
    unnamed x82, local copies, waits for them, and re-layouts  6.29 us
  transfers between devices with their start and end apart: 50, of which 13 were waited for; matrix products, arithmetic and copies ran while one was open for 11% of the time, Pallas kernels for 24%

profile of v5, /device:TPU:9, one launch (start us, length us, event | category | flops | bytes accessed | tf_op | source)
XLA Modules:
  0.0 188.8 jit_solution(13960828402386202745)
XLA Ops:
  0.7 2.1 %prologue.1 = (bf16[2,24,640]{2,1,0:T(8,128)(2,1)}, bf16[2,24,640]{2,1,0:T(8,128)(2,1)}, bf16[24,2176]{1,0:T(8,128)(2,1)}, bf16[24,2176]{1,0:T(8,128)(2,1)}) custom-call(s32[1]{0:T(128)} %bitcast.ids.refs_0_, f32[24,2304]{1,0:T(8,128)} %refs_0_.2, f32[24,768]{1,0:T(8,128)} %refs_4_.3, f32[24,2304]{1,0:T(8,128)} %refs_0_.3, f32[24,1152]{1,0:T(8,128)} %refs_8_.1, ...), custom_call_target="tpu_custom_call" | custom-call | flops 1000000 | bytes 1000000 | tf_op jit(solution)/shard_map/prologue/pallas_call | solution.py:626
  2.8 1.2 collective-permute-start.2
  4.0 1.1 collective-permute-start.3
  5.6 0.9 collective-permute-done.1.q1
  6.6 2.0 %collective-permute-done.3.q3 = bf16[2,24,640]{2,1,0:T(8,128)(2,1)S(1)} collective-permute-done((bf16[2,24,640]{2,1,0:T(8,128)(2,1)}, bf16[2,24,640]{2,1,0:T(8,128)(2,1)S(1)}, u32[]{:S(2)}, u32[]{:S(2)}) %collective-permute-start.3) | collective-permute-done | bytes 61472 | tf_op jit(solution)/shard_map/ppermute | solution.py:392
  9.2 1.8 assemble.1
  11.2 2.3 %collective-permute-start.8 = (bf16[96,640]{1,0:T(8,128)(2,1)}, bf16[96,640]{1,0:T(8,128)(2,1)S(1)}, u32[]{:S(2)}, u32[]{:S(2)}) collective-permute-start(bf16[96,640]{1,0:T(8,128)(2,1)} %get-tuple-element.104.w0), channel_id=1, source_target_pairs={{0,16},{1,17},{2,18},{3,19},{4,20},{5,21},{6,22},{7,23},{8,24},{9,... | collective-permute-start | bytes 368648 | tf_op jit(solution)/shard_map/ppermute | solution.py:392
  13.7 1.2 collective-permute-start.10
  15.0 0.9 dynamic-slice_reduce_fusion
  15.9 1.7 collective-permute-done.10.w1
  17.7 1.6 collective-permute-start.11
  19.3 3.1 %collective-permute-start.14 = (bf16[48,2176]{1,0:T(8,128)(2,1)}, bf16[48,2176]{1,0:T(8,128)(2,1)S(1)}, u32[]{:S(2)}, u32[]{:S(2)}) collective-permute-start(bf16[48,2176]{1,0:T(8,128)(2,1)} %get-tuple-element.109), channel_id=1, source_target_pairs={{0,8},{1,9},{2,10},{3,11},{4,12},{5,13},{6,14},{7,15},{8,0},{9,1},... | collective-permute-start | bytes 626696 | tf_op jit(solution)/shard_map/ppermute | solution.py:392
  22.4 1.7 collective-permute-start.15
  24.1 3.5 %collective-permute-done.9 = bf16[96,640]{1,0:T(8,128)(2,1)S(1)} collective-permute-done((bf16[96,640]{1,0:T(8,128)(2,1)}, bf16[96,640]{1,0:T(8,128)(2,1)S(1)}, u32[]{:S(2)}, u32[]{:S(2)}) %collective-permute-start.9) | collective-permute-done | bytes 122912 | tf_op jit(solution)/shard_map/ppermute | solution.py:392
  27.7 1.3 collective-permute-start.12
  29.6 3.1 %collective-permute-start.5 = (bf16[256,768]{1,0:T(8,128)(2,1)S(1)}, bf16[256,768]{1,0:T(8,128)(2,1)}, u32[]{:S(2)}, u32[]{:S(2)}) collective-permute-start(bf16[256,768]{1,0:T(8,128)(2,1)S(1)} %copy-done.1), channel_id=1, source_target_pairs={{0,2},{1,3},{2,0},{3,1},{4,6},{5,7},{6,4},{7,5},{8,10},{9,11},{10,... | collective-permute-start | bytes 1179656 | tf_op jit(solution)/shard_map/ppermute | solution.py:392
  32.7 3.1 %multiply_sine_fusion = (f32[1024,128]{1,0:T(8,128)}, f32[1024,128]{1,0:T(8,128)}) fusion(f32[128]{0:T(128)S(1)} %mul.90, f32[1024]{0:T(1024)S(1)} %select_convert_fusion), kind=kLoop, calls=%fused_computation.18 | loop fusion | flops 131072 | bytes 1053184 | tf_op jit(solution)/shard_map/sin | solution.py:1214
  35.8 2.2 %collective-permute-done.11 = bf16[48,2176]{1,0:T(8,128)(2,1)S(1)} collective-permute-done((bf16[48,2176]{1,0:T(8,128)(2,1)}, bf16[48,2176]{1,0:T(8,128)(2,1)S(1)}, u32[]{:S(2)}, u32[]{:S(2)}) %collective-permute-start.11) | collective-permute-done | bytes 208928 | tf_op jit(solution)/shard_map/ppermute | solution.py:392
  38.0 3.7 %collective-permute-done.15 = bf16[48,2176]{1,0:T(8,128)(2,1)S(1)} collective-permute-done((bf16[48,2176]{1,0:T(8,128)(2,1)}, bf16[48,2176]{1,0:T(8,128)(2,1)S(1)}, u32[]{:S(2)}, u32[]{:S(2)}) %collective-permute-start.15) | collective-permute-done | bytes 208928 | tf_op jit(solution)/shard_map/ppermute | solution.py:392
  41.8 1.6 collective-permute-start.19
  43.5 1.2 collective-permute-start.16
  44.7 1.7 collective-permute-start.6
  47.5 0.9 fusion.14.docq
  49.1 17.4 %forward_attention.1 = (bf16[1024,256]{1,0:T(8,128)(2,1)}, bf16[1024,256]{1,0:T(8,128)(2,1)}, bf16[1024,256]{1,0:T(8,128)(2,1)}, f32[1024,192]{1,0:T(8,128)}, bf...) custom-call(s32[1]{0:T(128)} %bitcast.ids.refs_0_, ...), custom_call_target="tpu_custom_call" | custom-call | flops 6000000000 | bytes 16000000 | tf_op jit(solution)/shard_map/forward_attention/pallas_call | solution.py:650
  67.0 1.0 slice.182
  68.4 1.0 collective-permute-start.21
  70.0 10.2 %collective-permute-done.20.refs_13_ = bf16[4,48,1408]{2,1,0:T(8,128)(2,1)S(1)} collective-permute-done((bf16[4,48,1408]{2,1,0:T(8,128)(2,1)S(1)}, bf16[4,48,1408]{2,1,0:T(8,128)(2,1)S(1)}, u32[]{:S(2)}, u32[]{:S(2)}) %collective-permute-start.20) | collective-permute-done | bytes 540704 | tf_op jit(solution)/shard_map/ppermute | solution.py:392
  80.2 1.2 collective-permute-start.24
  82.4 1.9 pad_add_fusion.refs_1_.lives
  84.4 0.8 copy-done.30
  85.2 11.0 %feed_forward.1 = (bf16[256,768]{1,0:T(8,128)(2,1)}, f32[256,768]{1,0:T(8,128)}, bf16[2,64,768]{2,1,0:T(8,128)(2,1)}, bf16[2,64,768]{2,1,0:T(8,128)(2,1)}, bf16[...) custom-call(s32[1]{0:T(128)} %bitcast.ids.refs_0_, s32[2]{0:T(128)} %pad_add_fusion.refs_1_.lives, ...), custom_call_target="tpu_custom_call" | custom-call | flops 5000000000 | bytes 12000000 | tf_op jit(solution)/shard_map/feed_forward/pallas_call | solution.py:830
  97.6 1.4 collective-permute-start.27
  99.1 1.2 collective-permute-done.30.cot_c
  100.3 0.8 copy-done.35
  101.7 6.6 %grads.1 = (bf16[8,48,1152]{2,1,0:T(8,128)(2,1)}, bf16[8,48,1152]{2,1,0:T(8,128)(2,1)}, bf16[8,48,1024]{2,1,0:T(8,128)(2,1)}, bf16[8,48,1024]{2,1,0:T(8,128)(2,1)}) custom-call(s32[1]{0:T(128)} %bitcast.ids.refs_0_, s32[2]{0:T(128)} %pad_add_fusion.refs_1_.lives, bf16[256,768]{1,0:T(8,128)(2,1)} %cot.1, bf16[256,768]{1,0:T(8,128)(2,1)} %copy-done.35, ...), custom_call_target="tpu_custom_call" | custom-call | flops 3000000000 | bytes 10000000 | tf_op jit(solution)/shard_map/grads/pallas_call | solution.py:889
  108.6 1.2 collective-permute-start.33
  110.7 15.4 %backward_attention.1 = (bf16[2,256,768]{2,1,0:T(8,128)(2,1)}, bf16[2,256,768]{2,1,0:T(8,128)(2,1)}, bf16[4,96,640]{2,1,0:T(8,128)(2,1)}, bf16[4,96,640]{2,1,0:T(8,128)(2,1)}) custom-call(s32[1]{0:T(128)} %bitcast.ids.refs_0_, bf16[1024,256]{1,0:T(8,128)(2,1)} %get-tuple-element.120.q8, bf16[1024,256]{1,0:T(8,128)(2,1)} %get-tuple-element.121.key, ...), custom_call_target="tpu_custom_call" | custom-call | flops 8000000000 | bytes 16000000 | tf_op jit(solution)/shard_map/backward_attention/pallas_call | solution.py:983
  126.1 0.8 collective-permute-start.28
  127.7 1.1 add_convert_fusion.1
  128.8 1.2 collective-permute-start.42
  130.1 1.1 add_convert_fusion
  131.2 0.9 collective-permute-start.38
  132.9 0.9 collective-permute-start.34
  133.8 4.8 %collective-permute-done.42 = bf16[4,48,1024]{2,1,0:T(8,128)(2,1)S(1)} collective-permute-done((bf16[4,48,1024]{2,1,0:T(8,128)(2,1)S(1)}, bf16[4,48,1024]{2,1,0:T(8,128)(2,1)S(1)}, u32[]{:S(2)}, u32[]{:S(2)}) %collective-permute-start.42) | collective-permute-done | bytes 393248 | tf_op jit(solution)/shard_map/ppermute | solution.py:392
  138.6 1.9 fusion.27
  140.5 2.0 %collective-permute-start.43 = (bf16[48,1024]{1,0:T(8,128)(2,1)S(1)}, bf16[48,1024]{1,0:T(8,128)(2,1)S(1)}, u32[]{:S(2)}, u32[]{:S(2)}) collective-permute-start(bf16[48,1024]{1,0:T(8,128)(2,1)S(1)} %get-tuple-element.185), channel_id=1, source_target_pairs={{0,8},{1,9},{2,10},{3,11},{4,12},{5,13},{6,14},{7,15},{8,0},{9,1},... | collective-permute-start | bytes 294920 | tf_op jit(solution)/shard_map/ppermute | solution.py:392
  142.5 1.0 collective-permute-start.44
  143.8 1.9 fusion.23
  145.7 2.3 %collective-permute-start.39 = (bf16[48,1152]{1,0:T(8,128)(2,1)S(1)}, bf16[48,1152]{1,0:T(8,128)(2,1)S(1)}, u32[]{:S(2)}, u32[]{:S(2)}) collective-permute-start(bf16[48,1152]{1,0:T(8,128)(2,1)S(1)} %get-tuple-element.181), channel_id=1, source_target_pairs={{0,8},{1,9},{2,10},{3,11},{4,12},{5,13},{6,14},{7,15},{8,0},{9,1},... | collective-permute-start | bytes 331784 | tf_op jit(solution)/shard_map/ppermute | solution.py:392
  148.0 1.1 collective-permute-start.40
  149.4 0.8 fusion.19
  150.2 4.0 %collective-permute-start.35 = (bf16[96,640]{1,0:T(8,128)(2,1)S(1)}, bf16[96,640]{1,0:T(8,128)(2,1)S(1)}, u32[]{:S(2)}, u32[]{:S(2)}) collective-permute-start(bf16[96,640]{1,0:T(8,128)(2,1)S(1)} %get-tuple-element.189), channel_id=1, source_target_pairs={{0,8},{1,9},{2,10},{3,11},{4,12},{5,13},{6,14},{7,15},{8,0},{9,1},... | collective-permute-start | bytes 368648 | tf_op jit(solution)/shard_map/ppermute | solution.py:392
  154.6 1.7 collective-permute-done.40.a2
  156.4 8.5 %collective-permute-done.41.a3 = bf16[48,1152]{1,0:T(8,128)(2,1)S(1)} collective-permute-done((bf16[48,1152]{1,0:T(8,128)(2,1)S(1)}, bf16[48,1152]{1,0:T(8,128)(2,1)S(1)}, u32[]{:S(2)}, u32[]{:S(2)}) %collective-permute-start.41) | collective-permute-done | bytes 110624 | tf_op jit(solution)/shard_map/ppermute | solution.py:392
  165.5 2.0 %sum_rows.1 = (bf16[24,2176]{1,0:T(8,128)(2,1)}, bf16[24,2176]{1,0:T(8,128)(2,1)}) custom-call(s32[1]{0:T(128)} %bitcast.ids.refs_0_, bf16[48,1152]{1,0:T(8,128)(2,1)} %get-tuple-element.182.a0, bf16[48,1152]{1,0:T(8,128)(2,1)} %copy-done.15, bf16[48,1152]{1,0:T(8,128)(2,1)} %copy-done.16, bf16[48,1152]{1,0:T(8,128)(2,1)} %copy-done.17, ...), custom_call_target="tpu_custom_call" | custom-call | flops 1000000 | bytes 1000000 | tf_op jit(solution)/shard_map/sum_rows/pallas_call | solution.py:1045
  167.5 4.1 %collective-permute-start.46 = (bf16[24,2176]{1,0:T(8,128)(2,1)}, bf16[24,2176]{1,0:T(8,128)(2,1)}, u32[]{:S(2)}, u32[]{:S(2)}) collective-permute-start(bf16[24,2176]{1,0:T(8,128)(2,1)} %get-tuple-element.140), channel_id=1, source_target_pairs={{0,1},{1,0},{2,3},{3,2},{4,5},{5,4},{6,7},{7,6},{8,9},{9,8},{10,11... | collective-permute-start | bytes 313352 | tf_op jit(solution)/shard_map/ppermute | solution.py:392
  172.1 0.8 collective-permute-done.46.came
  172.9 1.8 sum_heads.1
  174.7 2.3 %collective-permute-start.48 = (bf16[2,24,640]{2,1,0:T(8,128)(2,1)}, bf16[2,24,640]{2,1,0:T(8,128)(2,1)S(1)}, u32[]{:S(2)}, u32[]{:S(2)}) collective-permute-start(bf16[2,24,640]{2,1,0:T(8,128)(2,1)} %get-tuple-element.146), channel_id=1, source_target_pairs={{0,2},{1,3},{2,0},{3,1},{4,6},{5,7},{6,4},{7,5},{8,10},{9,11},{10,... | collective-permute-start | bytes 184328 | tf_op jit(solution)/shard_map/ppermute | solution.py:392
  177.0 1.2 collective-permute-start.47
  178.8 1.8 collective-permute-start.49
  180.6 1.3 fusion.7
  181.9 2.9 %update_rows.1 = (f32[24,2304]{1,0:T(8,128)}, f32[24,2304]{1,0:T(8,128)}, f32[24,2304]{1,0:T(8,128)}, f32[24,2304]{1,0:T(8,128)}, bf16[24,2304]{1,0:T(8,128)(2,1...) custom-call(s32[1]{0:T(128)} %bitcast.ids.refs_0_, ...), custom_call_target="tpu_custom_call" | custom-call | flops 10000000 | bytes 4000000 | tf_op jit(solution)/shard_map/update_rows/pallas_call | solution.py:1076
  186.0 2.6 %update_heads.1 = (f32[24,2304]{1,0:T(8,128)}, f32[24,2304]{1,0:T(8,128)}, f32[24,2304]{1,0:T(8,128)}, f32[24,2304]{1,0:T(8,128)}, bf16[24,2304]{1,0:T(8,128)(2,...) custom-call(s32[1]{0:T(128)} %bitcast.ids.refs_0_, ...), custom_call_target="tpu_custom_call" | custom-call | flops 10000000 | bytes 3000000 | tf_op jit(solution)/shard_map/update_heads/pallas_call | solution.py:1113
  (167 shorter events, 15.4 us)
Async XLA Ops:
  0.7 28.9 %copy-start.1 = (bf16[256,768]{1,0:T(8,128)(2,1)S(1)}, bf16[256,768]{1,0:T(8,128)(2,1)}, u32[]{:S(2)}) copy-start(bf16[256,768]{1,0:T(8,128)(2,1)} %t0_far.1) | copy-start | bytes 1179652
  2.8 3.8 %collective-permute-start.2 = (bf16[2,24,640]{2,1,0:T(8,128)(2,1)}, bf16[2,24,640]{2,1,0:T(8,128)(2,1)S(1)}, u32[]{:S(2)}, u32[]{:S(2)}) collective-permute-start(bf16[2,24,640]{2,1,0:T(8,128)(2,1)} %get-tuple-element.101), channel_id=1, source_target_pairs={{0,2},{1,3},{2,0},{3,1},{4,6},{5,7},{6,4},{7,5},{8,10},{9,11},{10,... | collective-permute-start | bytes 184328 | tf_op jit(solution)/shard_map/ppermute | solution.py:392
  4.0 4.6 %collective-permute-start.3 = (bf16[2,24,640]{2,1,0:T(8,128)(2,1)}, bf16[2,24,640]{2,1,0:T(8,128)(2,1)S(1)}, u32[]{:S(2)}, u32[]{:S(2)}) collective-permute-start(bf16[2,24,640]{2,1,0:T(8,128)(2,1)} %get-tuple-element.101), channel_id=1, source_target_pairs={{0,3},{1,2},{2,1},{3,0},{4,7},{5,6},{6,5},{7,4},{8,11},{9,10},{10,... | collective-permute-start | bytes 184328 | tf_op jit(solution)/shard_map/ppermute | solution.py:392
  5.1 1.5 collective-permute-start.1
  5.1 3.5 %collective-permute-start.4 = (bf16[24,2176]{1,0:T(8,128)(2,1)}, bf16[24,2176]{1,0:T(8,128)(2,1)S(1)}, u32[]{:S(2)}, u32[]{:S(2)}) collective-permute-start(bf16[24,2176]{1,0:T(8,128)(2,1)} %get-tuple-element.103), channel_id=1, source_target_pairs={{0,1},{1,0},{2,3},{3,2},{4,5},{5,4},{6,7},{7,6},{8,9},{9,8},{10,11... | collective-permute-start | bytes 313352 | tf_op jit(solution)/shard_map/ppermute | solution.py:392
  5.6 24.0 %collective-permute-start = (bf16[256,768]{1,0:T(8,128)(2,1)}, bf16[256,768]{1,0:T(8,128)(2,1)S(1)}, u32[]{:S(2)}, u32[]{:S(2)}) collective-permute-start(bf16[256,768]{1,0:T(8,128)(2,1)} %t0_far.1), channel_id=1, source_target_pairs={{0,1},{1,0},{2,3},{3,2},{4,5},{5,4},{6,7},{7,6},{8,9},{9,8},{10,11... | collective-permute-start | bytes 1179656 | tf_op jit(solution)/shard_map/ppermute | solution.py:392
  11.1 30.6 %copy-start.12 = (bf16[48,2176]{1,0:T(8,128)(2,1)S(1)}, bf16[48,2176]{1,0:T(8,128)(2,1)}, u32[]{:S(2)}) copy-start(bf16[48,2176]{1,0:T(8,128)(2,1)} %get-tuple-element.109) | copy-start | bytes 626692
  11.1 8.2 %collective-permute-start.7 = (bf16[96,640]{1,0:T(8,128)(2,1)}, bf16[96,640]{1,0:T(8,128)(2,1)S(1)}, u32[]{:S(2)}, u32[]{:S(2)}) collective-permute-start(bf16[96,640]{1,0:T(8,128)(2,1)} %get-tuple-element.104.w0), channel_id=1, source_target_pairs={{0,8},{1,9},{2,10},{3,11},{4,12},{5,13},{6,14},{7,15},{8,0},{9,1},... | collective-permute-start | bytes 368648 | tf_op jit(solution)/shard_map/ppermute | solution.py:392
  11.2 11.1 %collective-permute-start.8 = (bf16[96,640]{1,0:T(8,128)(2,1)}, bf16[96,640]{1,0:T(8,128)(2,1)S(1)}, u32[]{:S(2)}, u32[]{:S(2)}) collective-permute-start(bf16[96,640]{1,0:T(8,128)(2,1)} %get-tuple-element.104.w0), channel_id=1, source_target_pairs={{0,16},{1,17},{2,18},{3,19},{4,20},{5,21},{6,22},{7,23},{8,24},{9,... | collective-permute-start | bytes 368648 | tf_op jit(solution)/shard_map/ppermute | solution.py:392
  13.6 14.0 %collective-permute-start.9 = (bf16[96,640]{1,0:T(8,128)(2,1)}, bf16[96,640]{1,0:T(8,128)(2,1)S(1)}, u32[]{:S(2)}, u32[]{:S(2)}) collective-permute-start(bf16[96,640]{1,0:T(8,128)(2,1)} %get-tuple-element.104.w0), channel_id=1, source_target_pairs={{0,24},{1,25},{2,26},{3,27},{4,28},{5,29},{6,30},{7,31},{8,16},{9,... | collective-permute-start | bytes 368648 | tf_op jit(solution)/shard_map/ppermute | solution.py:392
  13.7 3.9 %collective-permute-start.10 = (bf16[96,640]{1,0:T(8,128)(2,1)}, bf16[96,640]{1,0:T(8,128)(2,1)S(1)}, u32[]{:S(2)}, u32[]{:S(2)}) collective-permute-start(bf16[96,640]{1,0:T(8,128)(2,1)} %get-tuple-element.104.w0), channel_id=1, source_target_pairs={{0,4},{1,5},{2,6},{3,7},{4,0},{5,1},{6,2},{7,3},{8,12},{9,13},{10,... | collective-permute-start | bytes 368648 | tf_op jit(solution)/shard_map/ppermute | solution.py:392
  17.7 24.0 %copy-start.40 = (bf16[96,640]{1,0:T(8,128)(2,1)}, bf16[96,640]{1,0:T(8,128)(2,1)S(1)}, u32[]{:S(2)}) copy-start(bf16[96,640]{1,0:T(8,128)(2,1)S(1)} %collective-permute-done.10.w1) | copy-start | bytes 368644
  17.7 20.3 %collective-permute-start.11 = (bf16[48,2176]{1,0:T(8,128)(2,1)}, bf16[48,2176]{1,0:T(8,128)(2,1)S(1)}, u32[]{:S(2)}, u32[]{:S(2)}) collective-permute-start(bf16[48,2176]{1,0:T(8,128)(2,1)} %get-tuple-element.109), channel_id=1, source_target_pairs={{0,24},{1,25},{2,26},{3,27},{4,28},{5,29},{6,30},{7,31},{8,16},{9,... | collective-permute-start | bytes 626696 | tf_op jit(solution)/shard_map/ppermute | solution.py:392
  19.3 18.7 %collective-permute-start.14 = (bf16[48,2176]{1,0:T(8,128)(2,1)}, bf16[48,2176]{1,0:T(8,128)(2,1)S(1)}, u32[]{:S(2)}, u32[]{:S(2)}) collective-permute-start(bf16[48,2176]{1,0:T(8,128)(2,1)} %get-tuple-element.109), channel_id=1, source_target_pairs={{0,8},{1,9},{2,10},{3,11},{4,12},{5,13},{6,14},{7,15},{8,0},{9,1},... | collective-permute-start | bytes 626696 | tf_op jit(solution)/shard_map/ppermute | solution.py:392
  22.4 19.3 %collective-permute-start.15 = (bf16[48,2176]{1,0:T(8,128)(2,1)}, bf16[48,2176]{1,0:T(8,128)(2,1)S(1)}, u32[]{:S(2)}, u32[]{:S(2)}) collective-permute-start(bf16[48,2176]{1,0:T(8,128)(2,1)} %get-tuple-element.109), channel_id=1, source_target_pairs={{0,16},{1,17},{2,18},{3,19},{4,20},{5,21},{6,22},{7,23},{8,24},{9,... | collective-permute-start | bytes 626696 | tf_op jit(solution)/shard_map/ppermute | solution.py:392
  27.7 19.6 %copy-start.10 = (bf16[3,96,640]{2,1,0:T(8,128)(2,1)}, bf16[3,96,640]{2,1,0:T(8,128)(2,1)S(1)}, u32[]{:S(2)}) copy-start(bf16[3,96,640]{2,1,0:T(8,128)(2,1)S(1)} %pad_maximum_fusion.2.w2) | copy-start | bytes 1105924
  27.7 20.7 %collective-permute-start.12 = (bf16[3,96,640]{2,1,0:T(8,128)(2,1)S(1)}, bf16[3,96,640]{2,1,0:T(8,128)(2,1)}, u32[]{:S(2)}, u32[]{:S(2)}) collective-permute-start(bf16[3,96,640]{2,1,0:T(8,128)(2,1)S(1)} %pad_maximum_fusion.2.w2), channel_id=1, source_target_pairs={{0,4},{1,5},{2,6},{3,7},{4,0},{5,1},{6,2},{7,3},{8,12},{9,13},{10,... | collective-permute-start | bytes 1105928 | tf_op jit(solution)/shard_map/ppermute | solution.py:392
  29.6 15.1 %collective-permute-start.5 = (bf16[256,768]{1,0:T(8,128)(2,1)S(1)}, bf16[256,768]{1,0:T(8,128)(2,1)}, u32[]{:S(2)}, u32[]{:S(2)}) collective-permute-start(bf16[256,768]{1,0:T(8,128)(2,1)S(1)} %copy-done.1), channel_id=1, source_target_pairs={{0,2},{1,3},{2,0},{3,1},{4,6},{5,7},{6,4},{7,5},{8,10},{9,11},{10,... | collective-permute-start | bytes 1179656 | tf_op jit(solution)/shard_map/ppermute | solution.py:392
  41.8 26.6 %copy-start.6 = (bf16[4,48,2176]{2,1,0:T(8,128)(2,1)}, bf16[4,48,2176]{2,1,0:T(8,128)(2,1)S(1)}, u32[]{:S(2)}) copy-start(bf16[4,48,2176]{2,1,0:T(8,128)(2,1)S(1)} %pad_maximum_fusion.refs_9_) | copy-start | bytes 2506756
  41.8 24.8 %collective-permute-start.19 = (bf16[4,48,2176]{2,1,0:T(8,128)(2,1)S(1)}, bf16[4,48,2176]{2,1,0:T(8,128)(2,1)S(1)}, u32[]{:S(2)}, u32[]{:S(2)}) collective-permute-start(bf16[4,48,2176]{2,1,0:T(8,128)(2,1)S(1)} %pad_maximum_fusion.refs_9_), channel_id=1, source_target_pairs={{0,2},{1,3},{2,0},{3,1},{4,6},{5,7},{6,4},{7,5},{8,10},{9,11},{10,... | collective-permute-start | bytes 2506760 | tf_op jit(solution)/shard_map/ppermute | solution.py:392
  43.5 23.5 %collective-permute-start.16 = (bf16[4,48,2176]{2,1,0:T(8,128)(2,1)S(1)}, bf16[4,48,2176]{2,1,0:T(8,128)(2,1)}, u32[]{:S(2)}, u32[]{:S(2)}) collective-permute-start(bf16[4,48,2176]{2,1,0:T(8,128)(2,1)S(1)} %pad_maximum_fusion.refs_9_), channel_id=1, source_target_pairs={{0,4},{1,5},{2,6},{3,7},{4,0},{5,1},{6,2},{7,3},{8,12},{9,13},{10,... | collective-permute-start | bytes 2506760 | tf_op jit(solution)/shard_map/ppermute | solution.py:392
  44.7 3.7 %collective-permute-start.6 = (bf16[256,768]{1,0:T(8,128)(2,1)}, bf16[256,768]{1,0:T(8,128)(2,1)S(1)}, u32[]{:S(2)}, u32[]{:S(2)}) collective-permute-start(bf16[256,768]{1,0:T(8,128)(2,1)} %collective-permute-done.5.t2.t2_far), channel_id=1, source_target_pairs={{0,1},{1,0},{2,3},{3,2},{4,5},{5,4},{6,7},{7,6},{8,9},{9,8},{10,11... | collective-permute-start | bytes 1179656 | tf_op jit(solution)/shard_map/ppermute | solution.py:392
  66.5 15.3 %copy-start.28 = (s32[8,4]{0,1:T(4,128)S(1)}, s32[8,4]{0,1:T(4,128)}, u32[]{:S(2)}) copy-start(s32[8,4]{0,1:T(4,128)} %param.26) | copy-start | bytes 388
  66.5 2.9 %collective-permute-start.13 = (bf16[2,64,768]{2,1,0:T(8,128)(2,1)}, bf16[2,64,768]{2,1,0:T(8,128)(2,1)S(1)}, u32[]{:S(2)}, u32[]{:S(2)}) collective-permute-start(bf16[2,64,768]{2,1,0:T(8,128)(2,1)} %get-tuple-element.112.refs_5_.near), channel_id=1, source_target_pairs={{0,1},{1,0},{2,3},{3,2},{4,5},{5,4},{6,7},{7,6},{8,9},{9,8},{10,11... | collective-permute-start | bytes 589832 | tf_op jit(solution)/shard_map/ppermute | solution.py:392
  66.6 17.7 %copy-start.11 = (bf16[4,48,2176]{2,1,0:T(8,128)(2,1)}, bf16[4,48,2176]{2,1,0:T(8,128)(2,1)S(1)}, u32[]{:S(2)}) copy-start(bf16[4,48,2176]{2,1,0:T(8,128)(2,1)S(1)} %collective-permute-done.19.refs_10_) | copy-start | bytes 2506756
  66.7 13.5 %collective-permute-start.20 = (bf16[4,48,1408]{2,1,0:T(8,128)(2,1)S(1)}, bf16[4,48,1408]{2,1,0:T(8,128)(2,1)S(1)}, u32[]{:S(2)}, u32[]{:S(2)}) collective-permute-start(bf16[4,48,1408]{2,1,0:T(8,128)(2,1)S(1)} %slice.140), channel_id=1, source_target_pairs={{0,4},{1,5},{2,6},{3,7},{4,0},{5,1},{6,2},{7,3},{8,12},{9,13},{10,... | collective-permute-start | bytes 1622024 | tf_op jit(solution)/shard_map/ppermute | solution.py:392
  68.0 13.4 %collective-permute-start.17 = (bf16[320,768]{1,0:T(8,128)(2,1)S(1)}, bf16[320,768]{1,0:T(8,128)(2,1)}, u32[]{:S(2)}, u32[]{:S(2)}) collective-permute-start(bf16[320,768]{1,0:T(8,128)(2,1)S(1)} %pad_maximum_fusion.1), channel_id=1, source_target_pairs={{0,2},{1,3},{2,0},{3,1},{4,6},{5,7},{6,4},{7,5},{8,10},{9,11},{10,... | collective-permute-start | bytes 1474568 | tf_op jit(solution)/shard_map/ppermute | solution.py:392
  68.4 15.9 %collective-permute-start.21 = (bf16[4,48,2176]{2,1,0:T(8,128)(2,1)S(1)}, bf16[4,48,2176]{2,1,0:T(8,128)(2,1)S(1)}, u32[]{:S(2)}, u32[]{:S(2)}) collective-permute-start(bf16[4,48,2176]{2,1,0:T(8,128)(2,1)S(1)} %pad_maximum_fusion.refs_9_), channel_id=1, source_target_pairs={{0,1},{1,0},{2,3},{3,2},{4,5},{5,4},{6,7},{7,6},{8,9},{9,8},{10,11... | collective-permute-start | bytes 2506760 | tf_op jit(solution)/shard_map/ppermute | solution.py:392
  69.5 14.8 %collective-permute-start.22 = (bf16[4,48,2176]{2,1,0:T(8,128)(2,1)S(1)}, bf16[4,48,2176]{2,1,0:T(8,128)(2,1)}, u32[]{:S(2)}, u32[]{:S(2)}) collective-permute-start(bf16[4,48,2176]{2,1,0:T(8,128)(2,1)S(1)} %collective-permute-done.19.refs_10_), channel_id=1, source_target_pairs={{0,1},{1,0},{2,3},{3,2},{4,5},{5,4},{6,7},{7,6},{8,9},{9,8},{10,11... | collective-permute-start | bytes 2506760 | tf_op jit(solution)/shard_map/ppermute | solution.py:392
  69.5 14.8 %collective-permute-start.23 = (bf16[4,48,2176]{2,1,0:T(8,128)(2,1)}, bf16[4,48,2176]{2,1,0:T(8,128)(2,1)}, u32[]{:S(2)}, u32[]{:S(2)}) collective-permute-start(bf16[4,48,2176]{2,1,0:T(8,128)(2,1)} %collective-permute-done.16.refs_11_), channel_id=1, source_target_pairs={{0,1},{1,0},{2,3},{3,2},{4,5},{5,4},{6,7},{7,6},{8,9},{9,8},{10,11... | collective-permute-start | bytes 2506760 | tf_op jit(solution)/shard_map/ppermute | solution.py:392
  80.2 4.1 %collective-permute-start.24 = (bf16[4,48,1408]{2,1,0:T(8,128)(2,1)S(1)}, bf16[4,48,1408]{2,1,0:T(8,128)(2,1)}, u32[]{:S(2)}, u32[]{:S(2)}) collective-permute-start(bf16[4,48,1408]{2,1,0:T(8,128)(2,1)S(1)} %collective-permute-done.20.refs_13_), channel_id=1, source_target_pairs={{0,1},{1,0},{2,3},{3,2},{4,5},{5,4},{6,7},{7,6},{8,9},{9,8},{10,11... | collective-permute-start | bytes 1622024 | tf_op jit(solution)/shard_map/ppermute | solution.py:392
  81.4 2.9 %collective-permute-start.18 = (bf16[320,768]{1,0:T(8,128)(2,1)}, bf16[320,768]{1,0:T(8,128)(2,1)}, u32[]{:S(2)}, u32[]{:S(2)}) collective-permute-start(bf16[320,768]{1,0:T(8,128)(2,1)} %collective-permute-done.17.refs_7_.refs_12_.by_x), channel_id=1, source_target_pairs={{0,1},{1,0},{2,3},{3,2},{4,5},{5,4},{6,7},{7,6},{8,9},{9,8},{10,11... | collective-permute-start | bytes 1474568 | tf_op jit(solution)/shard_map/ppermute | solution.py:392
  96.2 4.2 %collective-permute-start.31 = (bf16[256,2944]{1,0:T(8,128)(2,1)}, bf16[256,2944]{1,0:T(8,128)(2,1)S(1)}, u32[]{:S(2)}, u32[]{:S(2)}) collective-permute-start(bf16[256,2944]{1,0:T(8,128)(2,1)} %get-tuple-element.134), channel_id=1, source_target_pairs={{0,1},{1,0},{2,3},{3,2},{4,5},{5,4},{6,7},{7,6},{8,9},{9,8},{10,11... | collective-permute-start | bytes 4521992 | tf_op jit(solution)/shard_map/ppermute | solution.py:392
  96.4 4.0 %collective-permute-start.30 = (bf16[256,768]{1,0:T(8,128)(2,1)}, bf16[256,768]{1,0:T(8,128)(2,1)S(1)}, u32[]{:S(2)}, u32[]{:S(2)}) collective-permute-start(bf16[256,768]{1,0:T(8,128)(2,1)} %cot.1), channel_id=1, source_target_pairs={{0,1},{1,0},{2,3},{3,2},{4,5},{5,4},{6,7},{7,6},{8,9},{9,8},{10,11... | collective-permute-start | bytes 1179656 | tf_op jit(solution)/shard_map/ppermute | solution.py:392
  97.2 12.7 %collective-permute-start.26 = (bf16[2,64,768]{2,1,0:T(8,128)(2,1)}, bf16[2,64,768]{2,1,0:T(8,128)(2,1)S(1)}, u32[]{:S(2)}, u32[]{:S(2)}) collective-permute-start(bf16[2,64,768]{2,1,0:T(8,128)(2,1)} %get-tuple-element.126), channel_id=1, source_target_pairs={{0,2},{1,3},{2,0},{3,1},{4,6},{5,7},{6,4},{7,5},{8,10},{9,11},{10,... | collective-permute-start | bytes 589832 | tf_op jit(solution)/shard_map/ppermute | solution.py:392
  97.6 12.3 %collective-permute-start.27 = (bf16[2,64,768]{2,1,0:T(8,128)(2,1)}, bf16[2,64,768]{2,1,0:T(8,128)(2,1)S(1)}, u32[]{:S(2)}, u32[]{:S(2)}) collective-permute-start(bf16[2,64,768]{2,1,0:T(8,128)(2,1)} %get-tuple-element.126), channel_id=1, source_target_pairs={{0,3},{1,2},{2,1},{3,0},{4,7},{5,6},{6,5},{7,4},{8,11},{9,10},{10,... | collective-permute-start | bytes 589832 | tf_op jit(solution)/shard_map/ppermute | solution.py:392
  99.0 10.9 %collective-permute-start.25 = (bf16[2,64,768]{2,1,0:T(8,128)(2,1)}, bf16[2,64,768]{2,1,0:T(8,128)(2,1)S(1)}, u32[]{:S(2)}, u32[]{:S(2)}) collective-permute-start(bf16[2,64,768]{2,1,0:T(8,128)(2,1)} %get-tuple-element.125.d0), channel_id=1, source_target_pairs={{0,1},{1,0},{2,3},{3,2},{4,5},{5,4},{6,7},{7,6},{8,9},{9,8},{10,11... | collective-permute-start | bytes 589832 | tf_op jit(solution)/shard_map/ppermute | solution.py:392
  108.2 19.4 %collective-permute-start.32 = (bf16[8,48,1024]{2,1,0:T(8,128)(2,1)}, bf16[8,48,1024]{2,1,0:T(8,128)(2,1)}, u32[]{:S(2)}, u32[]{:S(2)}) collective-permute-start(bf16[8,48,1024]{2,1,0:T(8,128)(2,1)} %get-tuple-element.135), channel_id=1, source_target_pairs={{0,2},{1,3},{2,0},{3,1},{4,6},{5,7},{6,4},{7,5},{8,10},{9,11},{10,... | collective-permute-start | bytes 2359304 | tf_op jit(solution)/shard_map/ppermute | solution.py:392
  108.6 21.4 %collective-permute-start.33 = (bf16[8,48,1152]{2,1,0:T(8,128)(2,1)}, bf16[8,48,1152]{2,1,0:T(8,128)(2,1)}, u32[]{:S(2)}, u32[]{:S(2)}) collective-permute-start(bf16[8,48,1152]{2,1,0:T(8,128)(2,1)} %get-tuple-element.136), channel_id=1, source_target_pairs={{0,4},{1,5},{2,6},{3,7},{4,0},{5,1},{6,2},{7,3},{8,12},{9,13},{10,... | collective-permute-start | bytes 2654216 | tf_op jit(solution)/shard_map/ppermute | solution.py:392
  110.7 17.0 %copy-start.8 = (bf16[8,48,1024]{2,1,0:T(8,128)(2,1)S(1)}, bf16[8,48,1024]{2,1,0:T(8,128)(2,1)}, u32[]{:S(2)}) copy-start(bf16[8,48,1024]{2,1,0:T(8,128)(2,1)} %get-tuple-element.139) | copy-start | bytes 2359300
  110.7 19.4 %copy-start.5 = (bf16[8,48,1152]{2,1,0:T(8,128)(2,1)S(1)}, bf16[8,48,1152]{2,1,0:T(8,128)(2,1)}, u32[]{:S(2)}) copy-start(bf16[8,48,1152]{2,1,0:T(8,128)(2,1)} %get-tuple-element.138) | copy-start | bytes 2654212
  126.1 5.9 %collective-permute-start.28 = (bf16[2,256,768]{2,1,0:T(8,128)(2,1)}, bf16[2,256,768]{2,1,0:T(8,128)(2,1)S(1)}, u32[]{:S(2)}, u32[]{:S(2)}) collective-permute-start(bf16[2,256,768]{2,1,0:T(8,128)(2,1)} %get-tuple-element.130), channel_id=1, source_target_pairs={{0,1},{1,0},{2,3},{3,2},{4,5},{5,4},{6,7},{7,6},{8,9},{9,8},{10,11... | collective-permute-start | bytes 2359304 | tf_op jit(solution)/shard_map/ppermute | solution.py:392
  128.8 9.8 %collective-permute-start.42 = (bf16[4,48,1024]{2,1,0:T(8,128)(2,1)S(1)}, bf16[4,48,1024]{2,1,0:T(8,128)(2,1)S(1)}, u32[]{:S(2)}, u32[]{:S(2)}) collective-permute-start(bf16[4,48,1024]{2,1,0:T(8,128)(2,1)S(1)} %add_convert_fusion.1), channel_id=1, source_target_pairs={{0,4},{1,5},{2,6},{3,7},{4,0},{5,1},{6,2},{7,3},{8,12},{9,13},{10,... | collective-permute-start | bytes 1179656 | tf_op jit(solution)/shard_map/ppermute | solution.py:392
  131.2 12.3 %collective-permute-start.38 = (bf16[4,48,1152]{2,1,0:T(8,128)(2,1)S(1)}, bf16[4,48,1152]{2,1,0:T(8,128)(2,1)S(1)}, u32[]{:S(2)}, u32[]{:S(2)}) collective-permute-start(bf16[4,48,1152]{2,1,0:T(8,128)(2,1)S(1)} %add_convert_fusion), channel_id=1, source_target_pairs={{0,2},{1,3},{2,0},{3,1},{4,6},{5,7},{6,4},{7,5},{8,10},{9,11},{10,... | collective-permute-start | bytes 1327112 | tf_op jit(solution)/shard_map/ppermute | solution.py:392
  132.2 39.4 %collective-permute-start.29 = (bf16[256,768]{1,0:T(8,128)(2,1)S(1)}, bf16[256,768]{1,0:T(8,128)(2,1)S(1)}, u32[]{:S(2)}, u32[]{:S(2)}) collective-permute-start(bf16[256,768]{1,0:T(8,128)(2,1)S(1)} %fusion.15), channel_id=1, source_target_pairs={{0,2},{1,3},{2,0},{3,1},{4,6},{5,7},{6,4},{7,5},{8,10},{9,11},{10,... | collective-permute-start | bytes 1179656 | tf_op jit(solution)/shard_map/ppermute | solution.py:392
  132.9 16.5 %copy-start.9 = (bf16[4,96,640]{2,1,0:T(8,128)(2,1)S(1)}, bf16[4,96,640]{2,1,0:T(8,128)(2,1)}, u32[]{:S(2)}) copy-start(bf16[4,96,640]{2,1,0:T(8,128)(2,1)} %get-tuple-element.131) | copy-start | bytes 1474564
  132.9 16.2 %collective-permute-start.34 = (bf16[4,96,640]{2,1,0:T(8,128)(2,1)S(1)}, bf16[4,96,640]{2,1,0:T(8,128)(2,1)S(1)}, u32[]{:S(2)}, u32[]{:S(2)}) collective-permute-start(bf16[4,96,640]{2,1,0:T(8,128)(2,1)S(1)} %copy-done.32), channel_id=1, source_target_pairs={{0,4},{1,5},{2,6},{3,7},{4,0},{5,1},{6,2},{7,3},{8,12},{9,13},{10,... | collective-permute-start | bytes 1474568 | tf_op jit(solution)/shard_map/ppermute | solution.py:392
  140.5 5.2 %collective-permute-start.43 = (bf16[48,1024]{1,0:T(8,128)(2,1)S(1)}, bf16[48,1024]{1,0:T(8,128)(2,1)S(1)}, u32[]{:S(2)}, u32[]{:S(2)}) collective-permute-start(bf16[48,1024]{1,0:T(8,128)(2,1)S(1)} %get-tuple-element.185), channel_id=1, source_target_pairs={{0,8},{1,9},{2,10},{3,11},{4,12},{5,13},{6,14},{7,15},{8,0},{9,1},... | collective-permute-start | bytes 294920 | tf_op jit(solution)/shard_map/ppermute | solution.py:392
  142.5 5.5 %collective-permute-start.44 = (bf16[48,1024]{1,0:T(8,128)(2,1)S(1)}, bf16[48,1024]{1,0:T(8,128)(2,1)S(1)}, u32[]{:S(2)}, u32[]{:S(2)}) collective-permute-start(bf16[48,1024]{1,0:T(8,128)(2,1)S(1)} %get-tuple-element.184), channel_id=1, source_target_pairs={{0,16},{1,17},{2,18},{3,19},{4,20},{5,21},{6,22},{7,23},{8,24},{9,... | collective-permute-start | bytes 294920 | tf_op jit(solution)/shard_map/ppermute | solution.py:392
  143.5 6.7 %collective-permute-start.45 = (bf16[48,1024]{1,0:T(8,128)(2,1)S(1)}, bf16[48,1024]{1,0:T(8,128)(2,1)S(1)}, u32[]{:S(2)}, u32[]{:S(2)}) collective-permute-start(bf16[48,1024]{1,0:T(8,128)(2,1)S(1)} %get-tuple-element.183), channel_id=1, source_target_pairs={{0,24},{1,25},{2,26},{3,27},{4,28},{5,29},{6,30},{7,31},{8,16},{9,... | collective-permute-start | bytes 294920 | tf_op jit(solution)/shard_map/ppermute | solution.py:392
  145.7 25.9 %copy-start.3 = (bf16[256,768]{1,0:T(8,128)(2,1)S(1)}, bf16[256,768]{1,0:T(8,128)(2,1)}, u32[]{:S(2)}) copy-start(bf16[256,768]{1,0:T(8,128)(2,1)} %t0_far.1) | copy-start | bytes 1179652
  145.7 19.2 %copy-start.19 = (bf16[48,1024]{1,0:T(8,128)(2,1)}, bf16[48,1024]{1,0:T(8,128)(2,1)S(1)}, u32[]{:S(2)}) copy-start(bf16[48,1024]{1,0:T(8,128)(2,1)S(1)} %collective-permute-done.43.b1) | copy-start | bytes 294916
  145.7 8.4 %collective-permute-start.39 = (bf16[48,1152]{1,0:T(8,128)(2,1)S(1)}, bf16[48,1152]{1,0:T(8,128)(2,1)S(1)}, u32[]{:S(2)}, u32[]{:S(2)}) collective-permute-start(bf16[48,1152]{1,0:T(8,128)(2,1)S(1)} %get-tuple-element.181), channel_id=1, source_target_pairs={{0,8},{1,9},{2,10},{3,11},{4,12},{5,13},{6,14},{7,15},{8,0},{9,1},... | collective-permute-start | bytes 331784 | tf_op jit(solution)/shard_map/ppermute | solution.py:392
  148.0 16.8 %copy-start.20 = (bf16[48,1024]{1,0:T(8,128)(2,1)}, bf16[48,1024]{1,0:T(8,128)(2,1)S(1)}, u32[]{:S(2)}) copy-start(bf16[48,1024]{1,0:T(8,128)(2,1)S(1)} %collective-permute-done.44.b2) | copy-start | bytes 294916
  148.0 8.3 %collective-permute-start.40 = (bf16[48,1152]{1,0:T(8,128)(2,1)S(1)}, bf16[48,1152]{1,0:T(8,128)(2,1)S(1)}, u32[]{:S(2)}, u32[]{:S(2)}) collective-permute-start(bf16[48,1152]{1,0:T(8,128)(2,1)S(1)} %get-tuple-element.180), channel_id=1, source_target_pairs={{0,16},{1,17},{2,18},{3,19},{4,20},{5,21},{6,22},{7,23},{8,24},{9,... | collective-permute-start | bytes 331784 | tf_op jit(solution)/shard_map/ppermute | solution.py:392
  149.2 15.7 %collective-permute-start.41 = (bf16[48,1152]{1,0:T(8,128)(2,1)S(1)}, bf16[48,1152]{1,0:T(8,128)(2,1)S(1)}, u32[]{:S(2)}, u32[]{:S(2)}) collective-permute-start(bf16[48,1152]{1,0:T(8,128)(2,1)S(1)} %get-tuple-element.179), channel_id=1, source_target_pairs={{0,24},{1,25},{2,26},{3,27},{4,28},{5,29},{6,30},{7,31},{8,16},{9,... | collective-permute-start | bytes 331784 | tf_op jit(solution)/shard_map/ppermute | solution.py:392
  150.2 30.5 %copy-start.7 = (f32[256,768]{1,0:T(8,128)S(1)}, f32[256,768]{1,0:T(8,128)}, u32[]{:S(2)}) copy-start(f32[256,768]{1,0:T(8,128)} %get-tuple-element.119) | copy-start | bytes 2359300
  150.2 21.8 %collective-permute-start.35 = (bf16[96,640]{1,0:T(8,128)(2,1)S(1)}, bf16[96,640]{1,0:T(8,128)(2,1)S(1)}, u32[]{:S(2)}, u32[]{:S(2)}) collective-permute-start(bf16[96,640]{1,0:T(8,128)(2,1)S(1)} %get-tuple-element.189), channel_id=1, source_target_pairs={{0,8},{1,9},{2,10},{3,11},{4,12},{5,13},{6,14},{7,15},{8,0},{9,1},... | collective-permute-start | bytes 368648 | tf_op jit(solution)/shard_map/ppermute | solution.py:392
  154.1 17.9 %collective-permute-start.36 = (bf16[96,640]{1,0:T(8,128)(2,1)S(1)}, bf16[96,640]{1,0:T(8,128)(2,1)}, u32[]{:S(2)}, u32[]{:S(2)}) collective-permute-start(bf16[96,640]{1,0:T(8,128)(2,1)S(1)} %get-tuple-element.188), channel_id=1, source_target_pairs={{0,16},{1,17},{2,18},{3,19},{4,20},{5,21},{6,22},{7,23},{8,24},{9,... | collective-permute-start | bytes 368648 | tf_op jit(solution)/shard_map/ppermute | solution.py:392
  156.3 15.7 %collective-permute-start.37 = (bf16[96,640]{1,0:T(8,128)(2,1)S(1)}, bf16[96,640]{1,0:T(8,128)(2,1)}, u32[]{:S(2)}, u32[]{:S(2)}) collective-permute-start(bf16[96,640]{1,0:T(8,128)(2,1)S(1)} %get-tuple-element.187), channel_id=1, source_target_pairs={{0,24},{1,25},{2,26},{3,27},{4,28},{5,29},{6,30},{7,31},{8,16},{9,... | collective-permute-start | bytes 368648 | tf_op jit(solution)/shard_map/ppermute | solution.py:392
  167.5 5.3 %collective-permute-start.46 = (bf16[24,2176]{1,0:T(8,128)(2,1)}, bf16[24,2176]{1,0:T(8,128)(2,1)}, u32[]{:S(2)}, u32[]{:S(2)}) collective-permute-start(bf16[24,2176]{1,0:T(8,128)(2,1)} %get-tuple-element.140), channel_id=1, source_target_pairs={{0,1},{1,0},{2,3},{3,2},{4,5},{5,4},{6,7},{7,6},{8,9},{9,8},{10,11... | collective-permute-start | bytes 313352 | tf_op jit(solution)/shard_map/ppermute | solution.py:392
  174.7 4.1 %collective-permute-start.48 = (bf16[2,24,640]{2,1,0:T(8,128)(2,1)}, bf16[2,24,640]{2,1,0:T(8,128)(2,1)S(1)}, u32[]{:S(2)}, u32[]{:S(2)}) collective-permute-start(bf16[2,24,640]{2,1,0:T(8,128)(2,1)} %get-tuple-element.146), channel_id=1, source_target_pairs={{0,2},{1,3},{2,0},{3,1},{4,6},{5,7},{6,4},{7,5},{8,10},{9,11},{10,... | collective-permute-start | bytes 184328 | tf_op jit(solution)/shard_map/ppermute | solution.py:392
  177.0 7.8 %collective-permute-start.47 = (bf16[2,24,640]{2,1,0:T(8,128)(2,1)}, bf16[2,24,640]{2,1,0:T(8,128)(2,1)S(1)}, u32[]{:S(2)}, u32[]{:S(2)}) collective-permute-start(bf16[2,24,640]{2,1,0:T(8,128)(2,1)} %get-tuple-element.145.c0), channel_id=1, source_target_pairs={{0,1},{1,0},{2,3},{3,2},{4,5},{5,4},{6,7},{7,6},{8,9},{9,8},{10,11... | collective-permute-start | bytes 184328 | tf_op jit(solution)/shard_map/ppermute | solution.py:392
  178.8 6.0 %collective-permute-start.49 = (bf16[2,24,640]{2,1,0:T(8,128)(2,1)S(1)}, bf16[2,24,640]{2,1,0:T(8,128)(2,1)S(1)}, u32[]{:S(2)}, u32[]{:S(2)}) collective-permute-start(bf16[2,24,640]{2,1,0:T(8,128)(2,1)S(1)} %collective-permute-done.48.c2), channel_id=1, source_target_pairs={{0,1},{1,0},{2,3},{3,2},{4,5},{5,4},{6,7},{7,6},{8,9},{9,8},{10,11... | collective-permute-start | bytes 184328 | tf_op jit(solution)/shard_map/ppermute | solution.py:392
  (27 other events, 119.6 us)

commit v6 on v5

--- a/solution.py
+++ b/solution.py
@@ -380,7 +380,7 @@
     )
 
 
-FL = {'H1': 3, 'H2': 2, 'H3': 2, 'H5': 1, 'H6': 1, 'H7': 2, 'QX': 1, 'DX': 1, 'T4': 1, 'TC': 1}
+FL = {'DX': 1, 'H1': 3, 'H3': 2, 'H6': 1, 'H7': 2, 'T2': 1, 'T3': 1, 'T4': 2, 'T6': 3, 'TD': 1, 'UX': 1, 'Z1': 1, 'Z3': 2, 'Z4': 2, 'T7': 1, 'H5': 1, 'QX': 1}
 BF = jnp.bfloat16
 F32 = jnp.float32
 AXES = ("dp", "fsdp")
@@ -1009,9 +1009,9 @@
     )(ids, q8, key, val, att, prob, *d_pieces, gain, ggain, *token_pieces, cos, sin, wide)
 
 
-def sum_heads_kernel(ids, e0, e1, e2, e3, near, far):
+def sum_heads_kernel(ids, own, pair, last, near, far):
     f = ids[0] & 3
-    total = e0[...].astype(F32) + e1[...].astype(F32) + e2[...].astype(F32) + e3[...].astype(F32)
+    total = own[...].astype(F32) + pair[0].astype(F32) + last[...].astype(F32)
     pieces = [total[24 * j : 24 * j + 24, :] for j in range(4)]
     for k, out in enumerate((near.at[0], near.at[1], far.at[0], far.at[1])):
         place = f ^ k
@@ -1023,7 +1023,7 @@
 def sum_heads(ids, *pieces):
     return pl.pallas_call(
         sum_heads_kernel,
-        in_specs=[SMEM] + [VM] * 4,
+        in_specs=[SMEM] + [VM] * 3,
         out_specs=[VM] * 2,
         out_shape=[shaped((2, 24, 640), BF)] * 2,
         compiler_params=pltpu.CompilerParams(vmem_limit_bytes=VMEM_LIMIT),
@@ -1032,11 +1032,11 @@
     )(ids, *pieces)
 
 
-def sum_rows_kernel(ids, a0, a1, a2, a3, b0, b1, b2, b3, mine, other):
+def sum_rows_kernel(ids, a0, a1, a2, b0, b1, b2, mine, other):
     core = ids[0] & 1
-    one = a0[...].astype(F32) + a1[...].astype(F32) + a2[...].astype(F32) + a3[...].astype(F32)
-    two = b0[...].astype(F32) + b1[...].astype(F32) + b2[...].astype(F32) + b3[...].astype(F32)
-    rows = jnp.concatenate([one, two], axis=1)
+    one = a0[...].astype(F32) + a1[0].astype(F32) + a2[...].astype(F32)
+    two = b0[...].astype(F32) + b1[0].astype(F32) + b2[...].astype(F32)
+    rows = jnp.concatenate([two[:, :384], one, two[:, 384:]], axis=1)
     mine[...] = jnp.where(core == 0, rows[:24], rows[24:]).astype(BF)
     other[...] = jnp.where(core == 0, rows[24:], rows[:24]).astype(BF)
 
@@ -1044,7 +1044,7 @@
 def sum_rows(ids, *pieces):
     return pl.pallas_call(
         sum_rows_kernel,
-        in_specs=[SMEM] + [VM] * 8,
+        in_specs=[SMEM] + [VM] * 6,
         out_specs=[VM] * 2,
         out_shape=[shaped((24, 2176), BF)] * 2,
         compiler_params=pltpu.CompilerParams(vmem_limit_bytes=VMEM_LIMIT),
@@ -1064,8 +1064,8 @@
     one, two = mine[...].astype(F32), came[...].astype(F32)
     left, right = jnp.where(core == 0, one, two), jnp.where(core == 0, two, one)
     grads = (
-        jnp.concatenate([left[:, :1152], right[:, :1152]], axis=1),
-        jnp.concatenate([left[:, 1152:1536], right[:, 1152:1536]], axis=1),
+        jnp.concatenate([left[:, 384:1536], right[:, 384:1536]], axis=1),
+        jnp.concatenate([left[:, :384], right[:, :384]], axis=1),
         jnp.concatenate([left[:, 1536:2176], right[:, 1536:2048]], axis=1),
     )
     for i, gradient in enumerate(grads):
@@ -1265,11 +1265,10 @@
             total = total + part.astype(F32)
         return total.astype(BF)
 
-    def reduce_column(keep, one, two):
-        pieces = [add(keep[4 + kz], one[kz], two[kz]) for kz in range(4)]
-        if flag("ZM"):
-            return pieces
-        return [pieces[0]] + [xperm(pieces[kz], 8 * kz) for kz in (1, 2, 3)]
+    def reduce_column(name, pieces):
+        came = xperm(jnp.stack([pieces[1], pieces[3]]), 8)
+        (came,) = pick(name, [came], (then_y,), (then_x,), (far_y,))
+        return [pieces[0], came, xperm(add(pieces[2], came[1]), 16)]
 
     (other_pack,) = pick("C2", [other_pack], (d_pieces[2],), (d_pieces[3],))
     came_pack = xperm(other_pack, 1)
@@ -1295,34 +1294,29 @@
     (far_y,) = pick("TA", [far_y], (then_y, then_x), (then_x,), (then_y,))
     (near,) = pick("T2", [near], (along_x, along_y), (then_x,), (then_y,))
     e = [add(near[kz], far_y[kz]) for kz in range(4)]
-    heads = [e[0], xperm(e[1], 8), xperm(e[2], 16), xperm(e[3], 24)]
-    then_x, = pick("Z1", [then_x], (e[1], e[2], e[3]), (heads[1],), (heads[1], heads[2], heads[3]))
-    then_y, = pick("Z2", [then_y], (e[1], e[2], e[3]), (heads[1],), (heads[1], heads[2], heads[3]))
-    column_in = reduce_column(keep_in, along_y[4:], then_x)
-    column_rest = reduce_column(keep_rest, along_x[4:], then_y)
-    if flag("ZM"):
-        wide_z = [jnp.concatenate([column_in[kz], column_rest[kz]], axis=1) for kz in range(4)]
-        wide_z = [wide_z[0]] + [xperm(wide_z[kz], 8 * kz) for kz in (1, 2, 3)]
-        column_in = [piece[:, :1152] for piece in wide_z]
-        column_rest = [piece[:, 1152:] for piece in wide_z]
+    heads = reduce_column("Z0", e)
+    (then_x,) = pick("Z1", [then_x], (e[1], e[2], e[3]), (heads[1],), (heads[2],))
+    (then_y,) = pick("Z2", [then_y], (e[1], e[2], e[3]), (heads[1],), (heads[2],))
+    column_in = reduce_column("Z6", [add(keep_in[4 + kz], along_y[4 + kz], then_x[kz]) for kz in range(4)])
+    column_rest = reduce_column("Z7", [add(keep_rest[4 + kz], along_x[4 + kz], then_y[kz]) for kz in range(4)])
     (dn_sent,) = pick("T6", [dn_sent], (far_y,), (then_x, then_y), (along_x, along_y), (e[1],))
     dn_came = xperm(dn_sent, 1)
     x_came = xperm(add(dn_keep[1], dn_came[1]), 2)
     heads = pick("T7", heads, (x_came,))
-    column_in = pick("Z3", column_in, (heads[1],), (heads[1], heads[2], heads[3]))
+    column_in = pick("Z3", column_in, (heads[1],), (heads[2],))
     mine, other = sum_rows(ids, *column_in, *column_rest)
     states = [
         (weight_in, first_in, second_in, average_in),
         (weight_out, first_out, second_out, average_out),
         (weight_down, first_down, second_down, average_down),
     ]
-    (other,) = pick("Z5", [other], (heads[1],), (heads[1], heads[2], heads[3]))
+    (other,) = pick("Z5", [other], (heads[1],), (heads[2],))
     other_came = xperm(other, 1)
     if flag("TC"):
         heads = pick("TC", heads, (other_came,), (other,))
     head_sums = sum_heads(ids, *heads)
     came = exchange(*head_sums, flag("UX"))
-    (mine,) = pick("Z4", [mine], (heads[1],), (heads[1], heads[2], heads[3]), (head_sums[0],), (came[2],))
+    (mine,) = pick("Z4", [mine], (heads[1],), (heads[2],), (head_sums[0],), (came[2],))
     new_rows = update_rows(ids, mine, other_came, states)
     new_heads = update_heads(
         ids,

time: 190 us -> 186 us (0.979)
  starting transfers between devices: 55.6 us -> 49.3 us
  waiting for transfers between devices: 42.1 us -> 45.5 us
  other arithmetic: 16.2 us -> 12.9 us
    ppermute x50 -> x47, starting transfers between devices: 55.6 us -> 49.3 us  [xperm(): return lax.ppermute(value, AXES, [(i, i ^ mask) for i in range(count)])]
    convert_element_type x6 -> x9, other arithmetic: 6.89 us -> 2.8 us  [add(): return total.astype(BF)]
    ppermute x50 -> x47, waiting for transfers between devices: 42.1 us -> 45.5 us  [xperm(): return lax.ppermute(value, AXES, [(i, i ^ mask) for i in range(count)])]
    unnamed x82 -> x90, local copies, waits for them, and re-layouts: 6.29 us -> 7.42 us
  transfers between devices with their start and end apart: 50 -> 47, of which waited for: 13 -> 14; matrix products, arithmetic and copies ran while one was open for 11% -> 9% of each run, Pallas kernels for 24% -> 26%
where the time goes in v6:
time: 186 us; the launch traced here: 184 us
  Pallas kernels  63.5 us (34%)
  starting transfers between devices  49.3 us (27%)
  waiting for transfers between devices  45.5 us (24%)
  other arithmetic  12.9 us (7%)
  local copies, waits for them, and re-layouts  11.1 us (6%)
    ppermute x47, starting transfers between devices, xperm(): return lax.ppermute(value, AXES, [(i, i ^ mask) for i in range(count)])  49.3 us
    ppermute x47, waiting for transfers between devices, xperm(): return lax.ppermute(value, AXES, [(i, i ^ mask) for i in range(count)])  45.5 us
    pallas_call x1, Pallas kernels, forward_attention(): pl.pallas_call(forward_kernel, grid=(4,), in_specs=[SMEM] + [full((256, 7...  17.4 us
    pallas_call x1, Pallas kernels, backward_attention(): pl.pallas_call(backward_kernel, grid=(4,), in_specs=[SMEM] + [full((1024,...  15.4 us
    pallas_call x1, Pallas kernels, feed_forward(): pl.pallas_call(feed_kernel, in_specs=[SMEM] * 2 + [VM] * 7 + [ANY] * len(...  11 us
    unnamed x90, local copies, waits for them, and re-layouts  7.42 us
    pallas_call x1, Pallas kernels, feed_gradients(): pl.pallas_call(grads_kernel, in_specs=[SMEM] * 2 + [VM] * len(operands),...  6.57 us
  transfers between devices with their start and end apart: 47, of which 14 were waited for; matrix products, arithmetic and copies ran while one was open for 9% of the time, Pallas kernels for 26%

profile of v6, /device:TPU:9, one launch (start us, length us, event | category | flops | bytes accessed | tf_op | source)
XLA Modules:
  0.0 183.8 jit_solution(5125623443496125937)
XLA Ops:
  0.7 2.1 %prologue.1 = (bf16[2,24,640]{2,1,0:T(8,128)(2,1)}, bf16[2,24,640]{2,1,0:T(8,128)(2,1)}, bf16[24,2176]{1,0:T(8,128)(2,1)}, bf16[24,2176]{1,0:T(8,128)(2,1)}) custom-call(s32[1]{0:T(128)} %bitcast.ids.refs_0_, f32[24,2304]{1,0:T(8,128)} %refs_0_.2, f32[24,768]{1,0:T(8,128)} %refs_4_.3, f32[24,2304]{1,0:T(8,128)} %refs_0_.3, f32[24,1152]{1,0:T(8,128)} %refs_8_.1, ...), custom_call_target="tpu_custom_call" | custom-call | flops 1000000 | bytes 1000000 | tf_op jit(solution)/shard_map/prologue/pallas_call | solution.py:626
  2.8 1.2 collective-permute-start.2
  4.0 1.1 collective-permute-start.3
  5.6 0.8 constant_dynamic-slice_fusion
  6.4 0.9 fusion.34
  7.9 0.7 collective-permute-done.3.q3
  9.2 1.8 %assemble.1 = (bf16[96,640]{1,0:T(8,128)(2,1)}, bf16[48,2176]{1,0:T(8,128)(2,1)}) custom-call(s32[1]{0:T(128)} %bitcast.ids.refs_0_, bf16[2,24,640]{2,1,0:T(8,128)(2,1)} %get-tuple-element.106.q0, bf16[2,24,640]{2,1,0:T(8,128)(2,1)} %copy-done.29, bf16[2,24,640]{2,1,0:T(8,128)(2,1)} %copy-done.26, bf16[2,24,640]{2,1,0:T(8,128)(2,1)} %copy-done.28, ...), custom_call_target="tpu_custom_call" | custom-call | flops 1000000 | bytes 1000000 | tf_op jit(solution)/shard_map/assemble/pallas_call | solution.py:638
  11.1 2.3 %collective-permute-start.10 = (bf16[96,640]{1,0:T(8,128)(2,1)}, bf16[96,640]{1,0:T(8,128)(2,1)S(1)}, u32[]{:S(2)}, u32[]{:S(2)}) collective-permute-start(bf16[96,640]{1,0:T(8,128)(2,1)} %get-tuple-element.110.w0), channel_id=1, source_target_pairs={{0,16},{1,17},{2,18},{3,19},{4,20},{5,21},{6,22},{7,23},{8,24},{9,... | collective-permute-start | bytes 368648 | tf_op jit(solution)/shard_map/ppermute | solution.py:392
  13.4 1.2 collective-permute-start.7
  14.6 1.2 collective-permute-start.9
  15.9 1.7 collective-permute-done.7.w1
  17.6 5.1 %collective-permute-done.10 = bf16[96,640]{1,0:T(8,128)(2,1)S(1)} collective-permute-done((bf16[96,640]{1,0:T(8,128)(2,1)}, bf16[96,640]{1,0:T(8,128)(2,1)S(1)}, u32[]{:S(2)}, u32[]{:S(2)}) %collective-permute-start.10) | collective-permute-done | bytes 122912 | tf_op jit(solution)/shard_map/ppermute | solution.py:392
  22.7 3.6 %collective-permute-start.15 = (bf16[48,2176]{1,0:T(8,128)(2,1)}, bf16[48,2176]{1,0:T(8,128)(2,1)S(1)}, u32[]{:S(2)}, u32[]{:S(2)}) collective-permute-start(bf16[48,2176]{1,0:T(8,128)(2,1)} %get-tuple-element.113), channel_id=1, source_target_pairs={{0,16},{1,17},{2,18},{3,19},{4,20},{5,21},{6,22},{7,23},{8,24},{9,... | collective-permute-start | bytes 626696 | tf_op jit(solution)/shard_map/ppermute | solution.py:392
  26.3 3.0 %multiply_sine_fusion = (f32[1024,128]{1,0:T(8,128)}, f32[1024,128]{1,0:T(8,128)}) fusion(f32[128]{0:T(128)S(1)} %mul.96, f32[1024]{0:T(1024)S(1)} %select_convert_fusion), kind=kLoop, calls=%fused_computation.18 | loop fusion | flops 131072 | bytes 1053184 | tf_op jit(solution)/shard_map/sin | solution.py:1214
  29.3 0.9 collective-permute-start.5
  30.3 1.3 collective-permute-start.12
  31.6 6.4 %collective-permute-done.8 = bf16[48,2176]{1,0:T(8,128)(2,1)S(1)} collective-permute-done((bf16[48,2176]{1,0:T(8,128)(2,1)}, bf16[48,2176]{1,0:T(8,128)(2,1)S(1)}, u32[]{:S(2)}, u32[]{:S(2)}) %collective-permute-start.8) | collective-permute-done | bytes 208928 | tf_op jit(solution)/shard_map/ppermute | solution.py:392
  38.0 4.5 %collective-permute-done.15 = bf16[48,2176]{1,0:T(8,128)(2,1)S(1)} collective-permute-done((bf16[48,2176]{1,0:T(8,128)(2,1)}, bf16[48,2176]{1,0:T(8,128)(2,1)S(1)}, u32[]{:S(2)}, u32[]{:S(2)}) %collective-permute-start.15) | collective-permute-done | bytes 208928 | tf_op jit(solution)/shard_map/ppermute | solution.py:392
  42.6 1.2 collective-permute-start.19
  43.9 1.2 collective-permute-start.16
  45.1 1.0 collective-permute-start.6
  47.2 0.9 fusion.14.docq
  48.1 0.7 copy-done.38
  48.8 17.4 %forward_attention.1 = (bf16[1024,256]{1,0:T(8,128)(2,1)}, bf16[1024,256]{1,0:T(8,128)(2,1)}, bf16[1024,256]{1,0:T(8,128)(2,1)}, f32[1024,192]{1,0:T(8,128)}, bf...) custom-call(s32[1]{0:T(128)} %bitcast.ids.refs_0_, ...), custom_call_target="tpu_custom_call" | custom-call | flops 6000000000 | bytes 16000000 | tf_op jit(solution)/shard_map/forward_attention/pallas_call | solution.py:650
  66.7 1.0 slice.184
  68.1 1.0 collective-permute-start.21
  69.7 10.2 %collective-permute-done.20.refs_13_ = bf16[4,48,1408]{2,1,0:T(8,128)(2,1)S(1)} collective-permute-done((bf16[4,48,1408]{2,1,0:T(8,128)(2,1)S(1)}, bf16[4,48,1408]{2,1,0:T(8,128)(2,1)S(1)}, u32[]{:S(2)}, u32[]{:S(2)}) %collective-permute-start.20) | collective-permute-done | bytes 540704 | tf_op jit(solution)/shard_map/ppermute | solution.py:392
  79.9 1.2 collective-permute-start.24
  82.1 1.9 %pad_add_fusion.refs_1_.lives = s32[2]{0:T(128)} fusion(s32[1]{0:T(128)} %bitcast.2, s32[1]{0:T(128)} %bitcast.1), kind=kLoop, calls=%fused_computation.81 | loop fusion | flops 2 | bytes 16 | tf_op jit(solution)/shard_map/stack | solution.py:1166
  84.1 0.8 copy-done.33
  84.9 11.0 %feed_forward.1 = (bf16[256,768]{1,0:T(8,128)(2,1)}, f32[256,768]{1,0:T(8,128)}, bf16[2,64,768]{2,1,0:T(8,128)(2,1)}, bf16[2,64,768]{2,1,0:T(8,128)(2,1)}, bf16[...) custom-call(s32[1]{0:T(128)} %bitcast.ids.refs_0_, s32[2]{0:T(128)} %pad_add_fusion.refs_1_.lives, ...), custom_call_target="tpu_custom_call" | custom-call | flops 5000000000 | bytes 12000000 | tf_op jit(solution)/shard_map/feed_forward/pallas_call | solution.py:830
  97.3 1.4 collective-permute-start.29
  98.8 0.8 collective-permute-done.25.cot_c
  100.4 0.8 copy-done.32
  101.2 6.6 %grads.1 = (bf16[8,48,1152]{2,1,0:T(8,128)(2,1)}, bf16[8,48,1152]{2,1,0:T(8,128)(2,1)}, bf16[8,48,1024]{2,1,0:T(8,128)(2,1)}, bf16[8,48,1024]{2,1,0:T(8,128)(2,1)}) custom-call(s32[1]{0:T(128)} %bitcast.ids.refs_0_, s32[2]{0:T(128)} %pad_add_fusion.refs_1_.lives, bf16[256,768]{1,0:T(8,128)(2,1)} %cot.1, bf16[256,768]{1,0:T(8,128)(2,1)} %copy-done.39, ...), custom_call_target="tpu_custom_call" | custom-call | flops 3000000000 | bytes 10000000 | tf_op jit(solution)/shard_map/grads/pallas_call | solution.py:889
  108.2 1.2 collective-permute-start.31
  110.3 15.4 %backward_attention.1 = (bf16[2,256,768]{2,1,0:T(8,128)(2,1)}, bf16[2,256,768]{2,1,0:T(8,128)(2,1)}, bf16[4,96,640]{2,1,0:T(8,128)(2,1)}, bf16[4,96,640]{2,1,0:T(8,128)(2,1)}) custom-call(s32[1]{0:T(128)} %bitcast.ids.refs_0_, bf16[1024,256]{1,0:T(8,128)(2,1)} %get-tuple-element.124.q8, bf16[1024,256]{1,0:T(8,128)(2,1)} %get-tuple-element.129.key, ...), custom_call_target="tpu_custom_call" | custom-call | flops 8000000000 | bytes 16000000 | tf_op jit(solution)/shard_map/backward_attention/pallas_call | solution.py:983
  125.7 1.4 collective-permute-done.30
  127.1 1.2 collective-permute-start.34
  128.3 0.9 collective-permute-done.31
  129.3 1.2 collective-permute-start.40
  130.5 8.7 %collective-permute-done.34 = bf16[4,96,640]{2,1,0:T(8,128)(2,1)S(1)} collective-permute-done((bf16[4,96,640]{2,1,0:T(8,128)(2,1)}, bf16[4,96,640]{2,1,0:T(8,128)(2,1)S(1)}, u32[]{:S(2)}, u32[]{:S(2)}) %collective-permute-start.34) | collective-permute-done | bytes 491552 | tf_op jit(solution)/shard_map/ppermute | solution.py:392
  139.2 0.7 add_convert_fusion.5
  140.0 0.9 collective-permute-start.35
  141.1 2.1 %collective-permute-start.32 = (bf16[2,256,768]{2,1,0:T(8,128)(2,1)S(1)}, bf16[2,256,768]{2,1,0:T(8,128)(2,1)S(1)}, u32[]{:S(2)}, u32[]{:S(2)}) collective-permute-start(bf16[2,256,768]{2,1,0:T(8,128)(2,1)S(1)} %copy-done.34), channel_id=1, source_target_pairs={{0,1},{1,0},{2,3},{3,2},{4,5},{5,4},{6,7},{7,6},{8,9},{9,8},{10,11... | collective-permute-start | bytes 2359304 | tf_op jit(solution)/shard_map/ppermute | solution.py:392
  143.3 1.4 collective-permute-start.43
  144.6 1.1 collective-permute-done.35.pair
  146.0 0.9 collective-permute-start.41
  146.9 2.4 %collective-permute-start.36 = (bf16[96,640]{1,0:T(8,128)(2,1)S(1)}, bf16[96,640]{1,0:T(8,128)(2,1)S(1)}, u32[]{:S(2)}, u32[]{:S(2)}) collective-permute-start(bf16[96,640]{1,0:T(8,128)(2,1)S(1)} %fusion.16), channel_id=1, source_target_pairs={{0,16},{1,17},{2,18},{3,19},{4,20},{5,21},{6,22},{7,23},{8,24},{9,... | collective-permute-start | bytes 368648 | tf_op jit(solution)/shard_map/ppermute | solution.py:392
  149.4 2.4 %collective-permute-start.33 = (bf16[256,768]{1,0:T(8,128)(2,1)S(1)}, bf16[256,768]{1,0:T(8,128)(2,1)S(1)}, u32[]{:S(2)}, u32[]{:S(2)}) collective-permute-start(bf16[256,768]{1,0:T(8,128)(2,1)S(1)} %fusion.15), channel_id=1, source_target_pairs={{0,2},{1,3},{2,0},{3,1},{4,6},{5,7},{6,4},{7,5},{8,10},{9,11},{10,... | collective-permute-start | bytes 1179656 | tf_op jit(solution)/shard_map/ppermute | solution.py:392
  151.8 2.2 %collective-permute-done.43 = bf16[4,48,1024]{2,1,0:T(8,128)(2,1)S(1)} collective-permute-done((bf16[4,48,1024]{2,1,0:T(8,128)(2,1)S(1)}, bf16[4,48,1024]{2,1,0:T(8,128)(2,1)S(1)}, u32[]{:S(2)}, u32[]{:S(2)}) %collective-permute-start.43) | collective-permute-done | bytes 393248 | tf_op jit(solution)/shard_map/ppermute | solution.py:392
  154.8 0.8 fusion.20
  155.5 3.0 %collective-permute-start.42 = (bf16[48,1152]{1,0:T(8,128)(2,1)S(1)}, bf16[48,1152]{1,0:T(8,128)(2,1)S(1)}, u32[]{:S(2)}, u32[]{:S(2)}) collective-permute-start(bf16[48,1152]{1,0:T(8,128)(2,1)S(1)} %get-tuple-element.195), channel_id=1, source_target_pairs={{0,16},{1,17},{2,18},{3,19},{4,20},{5,21},{6,22},{7,23},{8,24},{9,... | collective-permute-start | bytes 331784 | tf_op jit(solution)/shard_map/ppermute | solution.py:392
  158.5 1.2 collective-permute-done.44.b1
  159.7 0.7 fusion.22
  160.5 2.9 %collective-permute-start.45 = (bf16[48,1024]{1,0:T(8,128)(2,1)S(1)}, bf16[48,1024]{1,0:T(8,128)(2,1)}, u32[]{:S(2)}, u32[]{:S(2)}) collective-permute-start(bf16[48,1024]{1,0:T(8,128)(2,1)S(1)} %get-tuple-element.199), channel_id=1, source_target_pairs={{0,16},{1,17},{2,18},{3,19},{4,20},{5,21},{6,22},{7,23},{8,24},{9,... | collective-permute-start | bytes 294920 | tf_op jit(solution)/shard_map/ppermute | solution.py:392
  163.4 0.8 slice_reduce_fusion
  164.8 1.8 sum_heads.1
  166.6 2.2 %collective-permute-start.38 = (bf16[2,24,640]{2,1,0:T(8,128)(2,1)}, bf16[2,24,640]{2,1,0:T(8,128)(2,1)S(1)}, u32[]{:S(2)}, u32[]{:S(2)}) collective-permute-start(bf16[2,24,640]{2,1,0:T(8,128)(2,1)} %get-tuple-element.149), channel_id=1, source_target_pairs={{0,2},{1,3},{2,0},{3,1},{4,6},{5,7},{6,4},{7,5},{8,10},{9,11},{10,... | collective-permute-start | bytes 184328 | tf_op jit(solution)/shard_map/ppermute | solution.py:392
  168.8 2.6 %collective-permute-start.39 = (bf16[2,24,640]{2,1,0:T(8,128)(2,1)}, bf16[2,24,640]{2,1,0:T(8,128)(2,1)S(1)}, u32[]{:S(2)}, u32[]{:S(2)}) collective-permute-start(bf16[2,24,640]{2,1,0:T(8,128)(2,1)} %get-tuple-element.149), channel_id=1, source_target_pairs={{0,3},{1,2},{2,1},{3,0},{4,7},{5,6},{6,5},{7,4},{8,11},{9,10},{10,... | collective-permute-start | bytes 184328 | tf_op jit(solution)/shard_map/ppermute | solution.py:392
  172.0 2.0 %sum_rows.1 = (bf16[24,2176]{1,0:T(8,128)(2,1)}, bf16[24,2176]{1,0:T(8,128)(2,1)}) custom-call(s32[1]{0:T(128)} %bitcast.ids.refs_0_, bf16[48,1152]{1,0:T(8,128)(2,1)} %get-tuple-element.153.a0, bf16[2,48,1152]{2,1,0:T(8,128)(2,1)} %copy-done.14, bf16[48,1152]{1,0:T(8,128)(2,1)} %copy-done.22, bf16[48,1024]{1,0:T(8,128)(2,1)} %get-tuple-element.200.b0, ...), custom_call_target="tpu_custom_call" | custom-call | flops 1000000 | bytes 1000000 | tf_op jit(solution)/shard_map/sum_rows/pallas_call | solution.py:1045
  174.9 1.3 fusion.7
  177.5 2.6 %update_heads.1 = (f32[24,2304]{1,0:T(8,128)}, f32[24,2304]{1,0:T(8,128)}, f32[24,2304]{1,0:T(8,128)}, f32[24,2304]{1,0:T(8,128)}, bf16[24,2304]{1,0:T(8,128)(2,...) custom-call(s32[1]{0:T(128)} %bitcast.ids.refs_0_, ...), custom_call_target="tpu_custom_call" | custom-call | flops 10000000 | bytes 3000000 | tf_op jit(solution)/shard_map/update_heads/pallas_call | solution.py:1113
  180.7 2.9 %update_rows.1 = (f32[24,2304]{1,0:T(8,128)}, f32[24,2304]{1,0:T(8,128)}, f32[24,2304]{1,0:T(8,128)}, f32[24,2304]{1,0:T(8,128)}, bf16[24,2304]{1,0:T(8,128)(2,1...) custom-call(s32[1]{0:T(128)} %bitcast.ids.refs_0_, ...), custom_call_target="tpu_custom_call" | custom-call | flops 10000000 | bytes 4000000 | tf_op jit(solution)/shard_map/update_rows/pallas_call | solution.py:1076
  (175 shorter events, 14.2 us)
Async XLA Ops:
  0.7 28.7 %copy-start.1 = (bf16[256,768]{1,0:T(8,128)(2,1)S(1)}, bf16[256,768]{1,0:T(8,128)(2,1)}, u32[]{:S(2)}) copy-start(bf16[256,768]{1,0:T(8,128)(2,1)} %t0_far.1) | copy-start | bytes 1179652
  2.8 5.1 %collective-permute-start.2 = (bf16[2,24,640]{2,1,0:T(8,128)(2,1)}, bf16[2,24,640]{2,1,0:T(8,128)(2,1)S(1)}, u32[]{:S(2)}, u32[]{:S(2)}) collective-permute-start(bf16[2,24,640]{2,1,0:T(8,128)(2,1)} %get-tuple-element.107), channel_id=1, source_target_pairs={{0,2},{1,3},{2,0},{3,1},{4,6},{5,7},{6,4},{7,5},{8,10},{9,11},{10,... | collective-permute-start | bytes 184328 | tf_op jit(solution)/shard_map/ppermute | solution.py:392
  4.0 4.6 %collective-permute-start.3 = (bf16[2,24,640]{2,1,0:T(8,128)(2,1)}, bf16[2,24,640]{2,1,0:T(8,128)(2,1)S(1)}, u32[]{:S(2)}, u32[]{:S(2)}) collective-permute-start(bf16[2,24,640]{2,1,0:T(8,128)(2,1)} %get-tuple-element.107), channel_id=1, source_target_pairs={{0,3},{1,2},{2,1},{3,0},{4,7},{5,6},{6,5},{7,4},{8,11},{9,10},{10,... | collective-permute-start | bytes 184328 | tf_op jit(solution)/shard_map/ppermute | solution.py:392
  5.1 2.7 %collective-permute-start.1 = (bf16[2,24,640]{2,1,0:T(8,128)(2,1)}, bf16[2,24,640]{2,1,0:T(8,128)(2,1)S(1)}, u32[]{:S(2)}, u32[]{:S(2)}) collective-permute-start(bf16[2,24,640]{2,1,0:T(8,128)(2,1)} %get-tuple-element.106.q0), channel_id=1, source_target_pairs={{0,1},{1,0},{2,3},{3,2},{4,5},{5,4},{6,7},{7,6},{8,9},{9,8},{10,11... | collective-permute-start | bytes 184328 | tf_op jit(solution)/shard_map/ppermute | solution.py:392
  5.1 3.5 %collective-permute-start.4 = (bf16[24,2176]{1,0:T(8,128)(2,1)}, bf16[24,2176]{1,0:T(8,128)(2,1)S(1)}, u32[]{:S(2)}, u32[]{:S(2)}) collective-permute-start(bf16[24,2176]{1,0:T(8,128)(2,1)} %get-tuple-element.109), channel_id=1, source_target_pairs={{0,1},{1,0},{2,3},{3,2},{4,5},{5,4},{6,7},{7,6},{8,9},{9,8},{10,11... | collective-permute-start | bytes 313352 | tf_op jit(solution)/shard_map/ppermute | solution.py:392
  5.6 17.1 %collective-permute-start = (bf16[256,768]{1,0:T(8,128)(2,1)}, bf16[256,768]{1,0:T(8,128)(2,1)S(1)}, u32[]{:S(2)}, u32[]{:S(2)}) collective-permute-start(bf16[256,768]{1,0:T(8,128)(2,1)} %t0_far.1), channel_id=1, source_target_pairs={{0,1},{1,0},{2,3},{3,2},{4,5},{5,4},{6,7},{7,6},{8,9},{9,8},{10,11... | collective-permute-start | bytes 1179656 | tf_op jit(solution)/shard_map/ppermute | solution.py:392
  11.1 31.4 %copy-start.19 = (bf16[48,2176]{1,0:T(8,128)(2,1)S(1)}, bf16[48,2176]{1,0:T(8,128)(2,1)}, u32[]{:S(2)}) copy-start(bf16[48,2176]{1,0:T(8,128)(2,1)} %get-tuple-element.113) | copy-start | bytes 626692
  11.1 11.6 %collective-permute-start.10 = (bf16[96,640]{1,0:T(8,128)(2,1)}, bf16[96,640]{1,0:T(8,128)(2,1)S(1)}, u32[]{:S(2)}, u32[]{:S(2)}) collective-permute-start(bf16[96,640]{1,0:T(8,128)(2,1)} %get-tuple-element.110.w0), channel_id=1, source_target_pairs={{0,16},{1,17},{2,18},{3,19},{4,20},{5,21},{6,22},{7,23},{8,24},{9,... | collective-permute-start | bytes 368648 | tf_op jit(solution)/shard_map/ppermute | solution.py:392
  13.4 4.2 %collective-permute-start.7 = (bf16[96,640]{1,0:T(8,128)(2,1)}, bf16[96,640]{1,0:T(8,128)(2,1)S(1)}, u32[]{:S(2)}, u32[]{:S(2)}) collective-permute-start(bf16[96,640]{1,0:T(8,128)(2,1)} %get-tuple-element.110.w0), channel_id=1, source_target_pairs={{0,4},{1,5},{2,6},{3,7},{4,0},{5,1},{6,2},{7,3},{8,12},{9,13},{10,... | collective-permute-start | bytes 368648 | tf_op jit(solution)/shard_map/ppermute | solution.py:392
  14.6 14.7 %collective-permute-start.11 = (bf16[96,640]{1,0:T(8,128)(2,1)}, bf16[96,640]{1,0:T(8,128)(2,1)S(1)}, u32[]{:S(2)}, u32[]{:S(2)}) collective-permute-start(bf16[96,640]{1,0:T(8,128)(2,1)} %get-tuple-element.110.w0), channel_id=1, source_target_pairs={{0,24},{1,25},{2,26},{3,27},{4,28},{5,29},{6,30},{7,31},{8,16},{9,... | collective-permute-start | bytes 368648 | tf_op jit(solution)/shard_map/ppermute | solution.py:392
  14.6 15.6 %collective-permute-start.9 = (bf16[96,640]{1,0:T(8,128)(2,1)}, bf16[96,640]{1,0:T(8,128)(2,1)S(1)}, u32[]{:S(2)}, u32[]{:S(2)}) collective-permute-start(bf16[96,640]{1,0:T(8,128)(2,1)} %get-tuple-element.110.w0), channel_id=1, source_target_pairs={{0,8},{1,9},{2,10},{3,11},{4,12},{5,13},{6,14},{7,15},{8,0},{9,1},... | collective-permute-start | bytes 368648 | tf_op jit(solution)/shard_map/ppermute | solution.py:392
  17.6 24.9 %copy-start.44 = (bf16[96,640]{1,0:T(8,128)(2,1)}, bf16[96,640]{1,0:T(8,128)(2,1)S(1)}, u32[]{:S(2)}) copy-start(bf16[96,640]{1,0:T(8,128)(2,1)S(1)} %collective-permute-done.7.w1) | copy-start | bytes 368644
  17.6 20.4 %collective-permute-start.8 = (bf16[48,2176]{1,0:T(8,128)(2,1)}, bf16[48,2176]{1,0:T(8,128)(2,1)S(1)}, u32[]{:S(2)}, u32[]{:S(2)}) collective-permute-start(bf16[48,2176]{1,0:T(8,128)(2,1)} %get-tuple-element.113), channel_id=1, source_target_pairs={{0,24},{1,25},{2,26},{3,27},{4,28},{5,29},{6,30},{7,31},{8,16},{9,... | collective-permute-start | bytes 626696 | tf_op jit(solution)/shard_map/ppermute | solution.py:392
  22.7 15.3 %collective-permute-start.14 = (bf16[48,2176]{1,0:T(8,128)(2,1)}, bf16[48,2176]{1,0:T(8,128)(2,1)S(1)}, u32[]{:S(2)}, u32[]{:S(2)}) collective-permute-start(bf16[48,2176]{1,0:T(8,128)(2,1)} %get-tuple-element.113), channel_id=1, source_target_pairs={{0,8},{1,9},{2,10},{3,11},{4,12},{5,13},{6,14},{7,15},{8,0},{9,1},... | collective-permute-start | bytes 626696 | tf_op jit(solution)/shard_map/ppermute | solution.py:392
  22.7 19.8 %copy-start.37 = (bf16[256,768]{1,0:T(8,128)(2,1)}, bf16[256,768]{1,0:T(8,128)(2,1)S(1)}, u32[]{:S(2)}) copy-start(bf16[256,768]{1,0:T(8,128)(2,1)S(1)} %collective-permute-done.t1.t1_far) | copy-start | bytes 1179652
  22.7 19.8 %collective-permute-start.15 = (bf16[48,2176]{1,0:T(8,128)(2,1)}, bf16[48,2176]{1,0:T(8,128)(2,1)S(1)}, u32[]{:S(2)}, u32[]{:S(2)}) collective-permute-start(bf16[48,2176]{1,0:T(8,128)(2,1)} %get-tuple-element.113), channel_id=1, source_target_pairs={{0,16},{1,17},{2,18},{3,19},{4,20},{5,21},{6,22},{7,23},{8,24},{9,... | collective-permute-start | bytes 626696 | tf_op jit(solution)/shard_map/ppermute | solution.py:392
  29.3 15.8 %collective-permute-start.5 = (bf16[256,768]{1,0:T(8,128)(2,1)S(1)}, bf16[256,768]{1,0:T(8,128)(2,1)}, u32[]{:S(2)}, u32[]{:S(2)}) collective-permute-start(bf16[256,768]{1,0:T(8,128)(2,1)S(1)} %copy-done.1), channel_id=1, source_target_pairs={{0,2},{1,3},{2,0},{3,1},{4,6},{5,7},{6,4},{7,5},{8,10},{9,11},{10,... | collective-permute-start | bytes 1179656 | tf_op jit(solution)/shard_map/ppermute | solution.py:392
  30.3 17.8 %copy-start.17 = (bf16[3,96,640]{2,1,0:T(8,128)(2,1)}, bf16[3,96,640]{2,1,0:T(8,128)(2,1)S(1)}, u32[]{:S(2)}) copy-start(bf16[3,96,640]{2,1,0:T(8,128)(2,1)S(1)} %pad_maximum_fusion.2.w2) | copy-start | bytes 1105924
  30.3 17.8 %collective-permute-start.12 = (bf16[3,96,640]{2,1,0:T(8,128)(2,1)S(1)}, bf16[3,96,640]{2,1,0:T(8,128)(2,1)}, u32[]{:S(2)}, u32[]{:S(2)}) collective-permute-start(bf16[3,96,640]{2,1,0:T(8,128)(2,1)S(1)} %pad_maximum_fusion.2.w2), channel_id=1, source_target_pairs={{0,4},{1,5},{2,6},{3,7},{4,0},{5,1},{6,2},{7,3},{8,12},{9,13},{10,... | collective-permute-start | bytes 1105928 | tf_op jit(solution)/shard_map/ppermute | solution.py:392
  42.6 25.5 %copy-start.8 = (bf16[4,48,2176]{2,1,0:T(8,128)(2,1)}, bf16[4,48,2176]{2,1,0:T(8,128)(2,1)S(1)}, u32[]{:S(2)}) copy-start(bf16[4,48,2176]{2,1,0:T(8,128)(2,1)S(1)} %pad_maximum_fusion.refs_9_) | copy-start | bytes 2506756
  42.6 23.7 %collective-permute-start.19 = (bf16[4,48,2176]{2,1,0:T(8,128)(2,1)S(1)}, bf16[4,48,2176]{2,1,0:T(8,128)(2,1)S(1)}, u32[]{:S(2)}, u32[]{:S(2)}) collective-permute-start(bf16[4,48,2176]{2,1,0:T(8,128)(2,1)S(1)} %pad_maximum_fusion.refs_9_), channel_id=1, source_target_pairs={{0,2},{1,3},{2,0},{3,1},{4,6},{5,7},{6,4},{7,5},{8,10},{9,11},{10,... | collective-permute-start | bytes 2506760 | tf_op jit(solution)/shard_map/ppermute | solution.py:392
  43.9 22.8 %collective-permute-start.16 = (bf16[4,48,2176]{2,1,0:T(8,128)(2,1)S(1)}, bf16[4,48,2176]{2,1,0:T(8,128)(2,1)}, u32[]{:S(2)}, u32[]{:S(2)}) collective-permute-start(bf16[4,48,2176]{2,1,0:T(8,128)(2,1)S(1)} %pad_maximum_fusion.refs_9_), channel_id=1, source_target_pairs={{0,4},{1,5},{2,6},{3,7},{4,0},{5,1},{6,2},{7,3},{8,12},{9,13},{10,... | collective-permute-start | bytes 2506760 | tf_op jit(solution)/shard_map/ppermute | solution.py:392
  45.1 2.9 %collective-permute-start.6 = (bf16[256,768]{1,0:T(8,128)(2,1)}, bf16[256,768]{1,0:T(8,128)(2,1)S(1)}, u32[]{:S(2)}, u32[]{:S(2)}) collective-permute-start(bf16[256,768]{1,0:T(8,128)(2,1)} %collective-permute-done.5.t2.t2_far), channel_id=1, source_target_pairs={{0,1},{1,0},{2,3},{3,2},{4,5},{5,4},{6,7},{7,6},{8,9},{9,8},{10,11... | collective-permute-start | bytes 1179656 | tf_op jit(solution)/shard_map/ppermute | solution.py:392
  66.2 15.3 %copy-start.31 = (s32[8,4]{0,1:T(4,128)S(1)}, s32[8,4]{0,1:T(4,128)}, u32[]{:S(2)}) copy-start(s32[8,4]{0,1:T(4,128)} %param.26) | copy-start | bytes 388
  66.2 2.9 %collective-permute-start.13 = (bf16[2,64,768]{2,1,0:T(8,128)(2,1)}, bf16[2,64,768]{2,1,0:T(8,128)(2,1)S(1)}, u32[]{:S(2)}, u32[]{:S(2)}) collective-permute-start(bf16[2,64,768]{2,1,0:T(8,128)(2,1)} %get-tuple-element.116.refs_5_.near), channel_id=1, source_target_pairs={{0,1},{1,0},{2,3},{3,2},{4,5},{5,4},{6,7},{7,6},{8,9},{9,8},{10,11... | collective-permute-start | bytes 589832 | tf_op jit(solution)/shard_map/ppermute | solution.py:392
  66.3 17.7 %copy-start.18 = (bf16[4,48,2176]{2,1,0:T(8,128)(2,1)}, bf16[4,48,2176]{2,1,0:T(8,128)(2,1)S(1)}, u32[]{:S(2)}) copy-start(bf16[4,48,2176]{2,1,0:T(8,128)(2,1)S(1)} %collective-permute-done.19.refs_10_) | copy-start | bytes 2506756
  66.4 13.5 %collective-permute-start.20 = (bf16[4,48,1408]{2,1,0:T(8,128)(2,1)S(1)}, bf16[4,48,1408]{2,1,0:T(8,128)(2,1)S(1)}, u32[]{:S(2)}, u32[]{:S(2)}) collective-permute-start(bf16[4,48,1408]{2,1,0:T(8,128)(2,1)S(1)} %slice.139), channel_id=1, source_target_pairs={{0,4},{1,5},{2,6},{3,7},{4,0},{5,1},{6,2},{7,3},{8,12},{9,13},{10,... | collective-permute-start | bytes 1622024 | tf_op jit(solution)/shard_map/ppermute | solution.py:392
  67.7 13.4 %collective-permute-start.17 = (bf16[320,768]{1,0:T(8,128)(2,1)S(1)}, bf16[320,768]{1,0:T(8,128)(2,1)}, u32[]{:S(2)}, u32[]{:S(2)}) collective-permute-start(bf16[320,768]{1,0:T(8,128)(2,1)S(1)} %pad_maximum_fusion.1), channel_id=1, source_target_pairs={{0,2},{1,3},{2,0},{3,1},{4,6},{5,7},{6,4},{7,5},{8,10},{9,11},{10,... | collective-permute-start | bytes 1474568 | tf_op jit(solution)/shard_map/ppermute | solution.py:392
  68.1 15.9 %collective-permute-start.21 = (bf16[4,48,2176]{2,1,0:T(8,128)(2,1)S(1)}, bf16[4,48,2176]{2,1,0:T(8,128)(2,1)S(1)}, u32[]{:S(2)}, u32[]{:S(2)}) collective-permute-start(bf16[4,48,2176]{2,1,0:T(8,128)(2,1)S(1)} %pad_maximum_fusion.refs_9_), channel_id=1, source_target_pairs={{0,1},{1,0},{2,3},{3,2},{4,5},{5,4},{6,7},{7,6},{8,9},{9,8},{10,11... | collective-permute-start | bytes 2506760 | tf_op jit(solution)/shard_map/ppermute | solution.py:392
  69.2 14.8 %collective-permute-start.22 = (bf16[4,48,2176]{2,1,0:T(8,128)(2,1)S(1)}, bf16[4,48,2176]{2,1,0:T(8,128)(2,1)}, u32[]{:S(2)}, u32[]{:S(2)}) collective-permute-start(bf16[4,48,2176]{2,1,0:T(8,128)(2,1)S(1)} %collective-permute-done.19.refs_10_), channel_id=1, source_target_pairs={{0,1},{1,0},{2,3},{3,2},{4,5},{5,4},{6,7},{7,6},{8,9},{9,8},{10,11... | collective-permute-start | bytes 2506760 | tf_op jit(solution)/shard_map/ppermute | solution.py:392
  69.2 14.9 %copy-start.40 = (bf16[2,64,768]{2,1,0:T(8,128)(2,1)}, bf16[2,64,768]{2,1,0:T(8,128)(2,1)S(1)}, u32[]{:S(2)}) copy-start(bf16[2,64,768]{2,1,0:T(8,128)(2,1)S(1)} %collective-permute-done.13.refs_6_.near_c) | copy-start | bytes 589828
  69.2 14.8 %collective-permute-start.23 = (bf16[4,48,2176]{2,1,0:T(8,128)(2,1)}, bf16[4,48,2176]{2,1,0:T(8,128)(2,1)}, u32[]{:S(2)}, u32[]{:S(2)}) collective-permute-start(bf16[4,48,2176]{2,1,0:T(8,128)(2,1)} %collective-permute-done.16.refs_11_), channel_id=1, source_target_pairs={{0,1},{1,0},{2,3},{3,2},{4,5},{5,4},{6,7},{7,6},{8,9},{9,8},{10,11... | collective-permute-start | bytes 2506760 | tf_op jit(solution)/shard_map/ppermute | solution.py:392
  79.9 4.1 %collective-permute-start.24 = (bf16[4,48,1408]{2,1,0:T(8,128)(2,1)S(1)}, bf16[4,48,1408]{2,1,0:T(8,128)(2,1)}, u32[]{:S(2)}, u32[]{:S(2)}) collective-permute-start(bf16[4,48,1408]{2,1,0:T(8,128)(2,1)S(1)} %collective-permute-done.20.refs_13_), channel_id=1, source_target_pairs={{0,1},{1,0},{2,3},{3,2},{4,5},{5,4},{6,7},{7,6},{8,9},{9,8},{10,11... | collective-permute-start | bytes 1622024 | tf_op jit(solution)/shard_map/ppermute | solution.py:392
  81.1 2.9 %collective-permute-start.18 = (bf16[320,768]{1,0:T(8,128)(2,1)}, bf16[320,768]{1,0:T(8,128)(2,1)}, u32[]{:S(2)}, u32[]{:S(2)}) collective-permute-start(bf16[320,768]{1,0:T(8,128)(2,1)} %collective-permute-done.17.refs_7_.refs_12_.by_x), channel_id=1, source_target_pairs={{0,1},{1,0},{2,3},{3,2},{4,5},{5,4},{6,7},{7,6},{8,9},{9,8},{10,11... | collective-permute-start | bytes 1474568 | tf_op jit(solution)/shard_map/ppermute | solution.py:392
  95.9 4.2 %collective-permute-start.26 = (bf16[256,2944]{1,0:T(8,128)(2,1)}, bf16[256,2944]{1,0:T(8,128)(2,1)S(1)}, u32[]{:S(2)}, u32[]{:S(2)}) collective-permute-start(bf16[256,2944]{1,0:T(8,128)(2,1)} %get-tuple-element.127), channel_id=1, source_target_pairs={{0,1},{1,0},{2,3},{3,2},{4,5},{5,4},{6,7},{7,6},{8,9},{9,8},{10,11... | collective-permute-start | bytes 4521992 | tf_op jit(solution)/shard_map/ppermute | solution.py:392
  96.1 3.5 %collective-permute-start.25 = (bf16[256,768]{1,0:T(8,128)(2,1)S(1)}, bf16[256,768]{1,0:T(8,128)(2,1)S(1)}, u32[]{:S(2)}, u32[]{:S(2)}) collective-permute-start(bf16[256,768]{1,0:T(8,128)(2,1)S(1)} %copy-done.36), channel_id=1, source_target_pairs={{0,1},{1,0},{2,3},{3,2},{4,5},{5,4},{6,7},{7,6},{8,9},{9,8},{10,11... | collective-permute-start | bytes 1179656 | tf_op jit(solution)/shard_map/ppermute | solution.py:392
  96.9 12.6 %collective-permute-start.28 = (bf16[2,64,768]{2,1,0:T(8,128)(2,1)}, bf16[2,64,768]{2,1,0:T(8,128)(2,1)S(1)}, u32[]{:S(2)}, u32[]{:S(2)}) collective-permute-start(bf16[2,64,768]{2,1,0:T(8,128)(2,1)} %get-tuple-element.134), channel_id=1, source_target_pairs={{0,2},{1,3},{2,0},{3,1},{4,6},{5,7},{6,4},{7,5},{8,10},{9,11},{10,... | collective-permute-start | bytes 589832 | tf_op jit(solution)/shard_map/ppermute | solution.py:392
  97.3 12.2 %collective-permute-start.29 = (bf16[2,64,768]{2,1,0:T(8,128)(2,1)}, bf16[2,64,768]{2,1,0:T(8,128)(2,1)S(1)}, u32[]{:S(2)}, u32[]{:S(2)}) collective-permute-start(bf16[2,64,768]{2,1,0:T(8,128)(2,1)} %get-tuple-element.134), channel_id=1, source_target_pairs={{0,3},{1,2},{2,1},{3,0},{4,7},{5,6},{6,5},{7,4},{8,11},{9,10},{10,... | collective-permute-start | bytes 589832 | tf_op jit(solution)/shard_map/ppermute | solution.py:392
  98.7 10.7 %collective-permute-start.27 = (bf16[2,64,768]{2,1,0:T(8,128)(2,1)}, bf16[2,64,768]{2,1,0:T(8,128)(2,1)S(1)}, u32[]{:S(2)}, u32[]{:S(2)}) collective-permute-start(bf16[2,64,768]{2,1,0:T(8,128)(2,1)} %get-tuple-element.133.d0), channel_id=1, source_target_pairs={{0,1},{1,0},{2,3},{3,2},{4,5},{5,4},{6,7},{7,6},{8,9},{9,8},{10,11... | collective-permute-start | bytes 589832 | tf_op jit(solution)/shard_map/ppermute | solution.py:392
  107.8 19.3 %collective-permute-start.30 = (bf16[8,48,1024]{2,1,0:T(8,128)(2,1)}, bf16[8,48,1024]{2,1,0:T(8,128)(2,1)S(1)}, u32[]{:S(2)}, u32[]{:S(2)}) collective-permute-start(bf16[8,48,1024]{2,1,0:T(8,128)(2,1)} %get-tuple-element.139), channel_id=1, source_target_pairs={{0,2},{1,3},{2,0},{3,1},{4,6},{5,7},{6,4},{7,5},{8,10},{9,11},{10,... | collective-permute-start | bytes 2359304 | tf_op jit(solution)/shard_map/ppermute | solution.py:392
  108.2 21.0 %collective-permute-start.31 = (bf16[8,48,1152]{2,1,0:T(8,128)(2,1)}, bf16[8,48,1152]{2,1,0:T(8,128)(2,1)S(1)}, u32[]{:S(2)}, u32[]{:S(2)}) collective-permute-start(bf16[8,48,1152]{2,1,0:T(8,128)(2,1)} %get-tuple-element.128), channel_id=1, source_target_pairs={{0,4},{1,5},{2,6},{3,7},{4,0},{5,1},{6,2},{7,3},{8,12},{9,13},{10,... | collective-permute-start | bytes 2654216 | tf_op jit(solution)/shard_map/ppermute | solution.py:392
  110.3 18.9 %copy-start.5 = (bf16[8,48,1152]{2,1,0:T(8,128)(2,1)S(1)}, bf16[8,48,1152]{2,1,0:T(8,128)(2,1)}, u32[]{:S(2)}) copy-start(bf16[8,48,1152]{2,1,0:T(8,128)(2,1)} %get-tuple-element.151) | copy-start | bytes 2654212
  125.7 13.6 %copy-start.15 = (bf16[4,96,640]{2,1,0:T(8,128)(2,1)S(1)}, bf16[4,96,640]{2,1,0:T(8,128)(2,1)}, u32[]{:S(2)}) copy-start(bf16[4,96,640]{2,1,0:T(8,128)(2,1)} %get-tuple-element.142) | copy-start | bytes 1474564
  125.7 15.3 %copy-start.9 = (bf16[8,48,1024]{2,1,0:T(8,128)(2,1)S(1)}, bf16[8,48,1024]{2,1,0:T(8,128)(2,1)}, u32[]{:S(2)}) copy-start(bf16[8,48,1024]{2,1,0:T(8,128)(2,1)} %get-tuple-element.156) | copy-start | bytes 2359300
  127.1 14.0 %copy-start.10 = (bf16[8,48,1024]{2,1,0:T(8,128)(2,1)}, bf16[8,48,1024]{2,1,0:T(8,128)(2,1)S(1)}, u32[]{:S(2)}) copy-start(bf16[8,48,1024]{2,1,0:T(8,128)(2,1)S(1)} %collective-permute-done.30) | copy-start | bytes 2359300
  127.1 12.1 %collective-permute-start.34 = (bf16[4,96,640]{2,1,0:T(8,128)(2,1)}, bf16[4,96,640]{2,1,0:T(8,128)(2,1)S(1)}, u32[]{:S(2)}, u32[]{:S(2)}) collective-permute-start(bf16[4,96,640]{2,1,0:T(8,128)(2,1)} %get-tuple-element.144), channel_id=1, source_target_pairs={{0,4},{1,5},{2,6},{3,7},{4,0},{5,1},{6,2},{7,3},{8,12},{9,13},{10,... | collective-permute-start | bytes 1474568 | tf_op jit(solution)/shard_map/ppermute | solution.py:392
  129.3 16.5 %collective-permute-start.40 = (bf16[4,48,1152]{2,1,0:T(8,128)(2,1)S(1)}, bf16[4,48,1152]{2,1,0:T(8,128)(2,1)S(1)}, u32[]{:S(2)}, u32[]{:S(2)}) collective-permute-start(bf16[4,48,1152]{2,1,0:T(8,128)(2,1)S(1)} %add_convert_fusion), channel_id=1, source_target_pairs={{0,2},{1,3},{2,0},{3,1},{4,6},{5,7},{6,4},{7,5},{8,10},{9,11},{10,... | collective-permute-start | bytes 1327112 | tf_op jit(solution)/shard_map/ppermute | solution.py:392
  140.0 5.7 %collective-permute-start.35 = (bf16[2,96,640]{2,1,0:T(8,128)(2,1)S(1)}, bf16[2,96,640]{2,1,0:T(8,128)(2,1)S(1)}, u32[]{:S(2)}, u32[]{:S(2)}) collective-permute-start(bf16[2,96,640]{2,1,0:T(8,128)(2,1)S(1)} %pad_maximum_fusion.3), channel_id=1, source_target_pairs={{0,8},{1,9},{2,10},{3,11},{4,12},{5,13},{6,14},{7,15},{8,0},{9,1},... | collective-permute-start | bytes 737288 | tf_op jit(solution)/shard_map/ppermute | solution.py:392
  141.1 12.8 %copy-start.11 = (bf16[8,48,1024]{2,1,0:T(8,128)(2,1)S(1)}, bf16[8,48,1024]{2,1,0:T(8,128)(2,1)}, u32[]{:S(2)}) copy-start(bf16[8,48,1024]{2,1,0:T(8,128)(2,1)} %copy-done.10) | copy-start | bytes 2359300
  141.1 8.2 %collective-permute-start.32 = (bf16[2,256,768]{2,1,0:T(8,128)(2,1)S(1)}, bf16[2,256,768]{2,1,0:T(8,128)(2,1)S(1)}, u32[]{:S(2)}, u32[]{:S(2)}) collective-permute-start(bf16[2,256,768]{2,1,0:T(8,128)(2,1)S(1)} %copy-done.34), channel_id=1, source_target_pairs={{0,1},{1,0},{2,3},{3,2},{4,5},{5,4},{6,7},{7,6},{8,9},{9,8},{10,11... | collective-permute-start | bytes 2359304 | tf_op jit(solution)/shard_map/ppermute | solution.py:392
  143.3 10.7 %collective-permute-start.43 = (bf16[4,48,1024]{2,1,0:T(8,128)(2,1)S(1)}, bf16[4,48,1024]{2,1,0:T(8,128)(2,1)S(1)}, u32[]{:S(2)}, u32[]{:S(2)}) collective-permute-start(bf16[4,48,1024]{2,1,0:T(8,128)(2,1)S(1)} %add_convert_fusion.1), channel_id=1, source_target_pairs={{0,4},{1,5},{2,6},{3,7},{4,0},{5,1},{6,2},{7,3},{8,12},{9,13},{10,... | collective-permute-start | bytes 1179656 | tf_op jit(solution)/shard_map/ppermute | solution.py:392
  146.0 8.8 %collective-permute-start.41 = (bf16[2,48,1152]{2,1,0:T(8,128)(2,1)S(1)}, bf16[2,48,1152]{2,1,0:T(8,128)(2,1)S(1)}, u32[]{:S(2)}, u32[]{:S(2)}) collective-permute-start(bf16[2,48,1152]{2,1,0:T(8,128)(2,1)S(1)} %pad_maximum_fusion.4), channel_id=1, source_target_pairs={{0,8},{1,9},{2,10},{3,11},{4,12},{5,13},{6,14},{7,15},{8,0},{9,1},... | collective-permute-start | bytes 663560 | tf_op jit(solution)/shard_map/ppermute | solution.py:392
  146.9 17.3 %collective-permute-start.36 = (bf16[96,640]{1,0:T(8,128)(2,1)S(1)}, bf16[96,640]{1,0:T(8,128)(2,1)S(1)}, u32[]{:S(2)}, u32[]{:S(2)}) collective-permute-start(bf16[96,640]{1,0:T(8,128)(2,1)S(1)} %fusion.16), channel_id=1, source_target_pairs={{0,16},{1,17},{2,18},{3,19},{4,20},{5,21},{6,22},{7,23},{8,24},{9,... | collective-permute-start | bytes 368648 | tf_op jit(solution)/shard_map/ppermute | solution.py:392
  149.4 14.7 %collective-permute-start.33 = (bf16[256,768]{1,0:T(8,128)(2,1)S(1)}, bf16[256,768]{1,0:T(8,128)(2,1)S(1)}, u32[]{:S(2)}, u32[]{:S(2)}) collective-permute-start(bf16[256,768]{1,0:T(8,128)(2,1)S(1)} %fusion.15), channel_id=1, source_target_pairs={{0,2},{1,3},{2,0},{3,1},{4,6},{5,7},{6,4},{7,5},{8,10},{9,11},{10,... | collective-permute-start | bytes 1179656 | tf_op jit(solution)/shard_map/ppermute | solution.py:392
  154.1 20.4 %copy-start.3 = (bf16[256,768]{1,0:T(8,128)(2,1)S(1)}, bf16[256,768]{1,0:T(8,128)(2,1)}, u32[]{:S(2)}) copy-start(bf16[256,768]{1,0:T(8,128)(2,1)} %t0_far.1) | copy-start | bytes 1179652
  154.1 5.6 %collective-permute-start.44 = (bf16[2,48,1024]{2,1,0:T(8,128)(2,1)S(1)}, bf16[2,48,1024]{2,1,0:T(8,128)(2,1)S(1)}, u32[]{:S(2)}, u32[]{:S(2)}) collective-permute-start(bf16[2,48,1024]{2,1,0:T(8,128)(2,1)S(1)} %pad_maximum_fusion.5), channel_id=1, source_target_pairs={{0,8},{1,9},{2,10},{3,11},{4,12},{5,13},{6,14},{7,15},{8,0},{9,1},... | collective-permute-start | bytes 589832 | tf_op jit(solution)/shard_map/ppermute | solution.py:392
  154.8 16.6 %copy-start.14 = (bf16[2,48,1152]{2,1,0:T(8,128)(2,1)}, bf16[2,48,1152]{2,1,0:T(8,128)(2,1)S(1)}, u32[]{:S(2)}) copy-start(bf16[2,48,1152]{2,1,0:T(8,128)(2,1)S(1)} %collective-permute-done.41.a1) | copy-start | bytes 663556
  155.5 15.8 %collective-permute-start.42 = (bf16[48,1152]{1,0:T(8,128)(2,1)S(1)}, bf16[48,1152]{1,0:T(8,128)(2,1)S(1)}, u32[]{:S(2)}, u32[]{:S(2)}) collective-permute-start(bf16[48,1152]{1,0:T(8,128)(2,1)S(1)} %get-tuple-element.195), channel_id=1, source_target_pairs={{0,16},{1,17},{2,18},{3,19},{4,20},{5,21},{6,22},{7,23},{8,24},{9,... | collective-permute-start | bytes 331784 | tf_op jit(solution)/shard_map/ppermute | solution.py:392
  160.5 14.4 %copy-start.12 = (f32[256,768]{1,0:T(8,128)S(1)}, f32[256,768]{1,0:T(8,128)}, u32[]{:S(2)}) copy-start(f32[256,768]{1,0:T(8,128)} %get-tuple-element.123) | copy-start | bytes 2359300
  160.5 10.9 %collective-permute-start.45 = (bf16[48,1024]{1,0:T(8,128)(2,1)S(1)}, bf16[48,1024]{1,0:T(8,128)(2,1)}, u32[]{:S(2)}, u32[]{:S(2)}) collective-permute-start(bf16[48,1024]{1,0:T(8,128)(2,1)S(1)} %get-tuple-element.199), channel_id=1, source_target_pairs={{0,16},{1,17},{2,18},{3,19},{4,20},{5,21},{6,22},{7,23},{8,24},{9,... | collective-permute-start | bytes 294920 | tf_op jit(solution)/shard_map/ppermute | solution.py:392
  166.6 9.6 %collective-permute-start.38 = (bf16[2,24,640]{2,1,0:T(8,128)(2,1)}, bf16[2,24,640]{2,1,0:T(8,128)(2,1)S(1)}, u32[]{:S(2)}, u32[]{:S(2)}) collective-permute-start(bf16[2,24,640]{2,1,0:T(8,128)(2,1)} %get-tuple-element.149), channel_id=1, source_target_pairs={{0,2},{1,3},{2,0},{3,1},{4,6},{5,7},{6,4},{7,5},{8,10},{9,11},{10,... | collective-permute-start | bytes 184328 | tf_op jit(solution)/shard_map/ppermute | solution.py:392
  168.8 7.4 %collective-permute-start.39 = (bf16[2,24,640]{2,1,0:T(8,128)(2,1)}, bf16[2,24,640]{2,1,0:T(8,128)(2,1)S(1)}, u32[]{:S(2)}, u32[]{:S(2)}) collective-permute-start(bf16[2,24,640]{2,1,0:T(8,128)(2,1)} %get-tuple-element.149), channel_id=1, source_target_pairs={{0,3},{1,2},{2,1},{3,0},{4,7},{5,6},{6,5},{7,4},{8,11},{9,10},{10,... | collective-permute-start | bytes 184328 | tf_op jit(solution)/shard_map/ppermute | solution.py:392
  174.0 6.1 %collective-permute-start.46 = (bf16[24,2176]{1,0:T(8,128)(2,1)}, bf16[24,2176]{1,0:T(8,128)(2,1)S(1)}, u32[]{:S(2)}, u32[]{:S(2)}) collective-permute-start(bf16[24,2176]{1,0:T(8,128)(2,1)} %get-tuple-element.160), channel_id=1, source_target_pairs={{0,1},{1,0},{2,3},{3,2},{4,5},{5,4},{6,7},{7,6},{8,9},{9,8},{10,11... | collective-permute-start | bytes 313352 | tf_op jit(solution)/shard_map/ppermute | solution.py:392
  174.3 1.9 %collective-permute-start.37 = (bf16[2,24,640]{2,1,0:T(8,128)(2,1)}, bf16[2,24,640]{2,1,0:T(8,128)(2,1)S(1)}, u32[]{:S(2)}, u32[]{:S(2)}) collective-permute-start(bf16[2,24,640]{2,1,0:T(8,128)(2,1)} %get-tuple-element.148.c0), channel_id=1, source_target_pairs={{0,1},{1,0},{2,3},{3,2},{4,5},{5,4},{6,7},{7,6},{8,9},{9,8},{10,11... | collective-permute-start | bytes 184328 | tf_op jit(solution)/shard_map/ppermute | solution.py:392
  (28 other events, 105.1 us)
